TPU v7x, 128 devices: a whole 4x4x4 slice. The times are simulated.
128 devices in a mesh: seq: 16 (over x, y), db: 8 (over z, core).
Axes of the slice: x: 4, y: 4, z: 4, core: 2. Of those that a mesh axis runs over, the one named last changes fastest.
Arguments:
- decoder: bfloat16 [16384, 4096], P('seq'), may hold values from -6 to 6
- w_query: bfloat16 [4096, 4096], P(None, 'db'), may hold values from -0.09375 to 0.09375
- w_key: bfloat16 [896, 4096], P(None, 'db'), may hold values from -0.1875 to 0.1875
- w_value: bfloat16 [896, 4096], P(None, 'db'), may hold values from -0.1875 to 0.1875
- w_out: bfloat16 [4096, 4096], P('db'), may hold values from -0.09375 to 0.09375
- database: bfloat16 [384, 128, 896], P('seq'), may hold values from -240 to 240
- nb_shard: int32 [256, 2], replicated, may hold values from 0 to 15, as said below
- nb_slot: int32 [256, 2], replicated, may hold values from 0 to 23
Outputs:
- attended: bfloat16 [16384, 4096], P(('seq', 'db'))
Inputs may be any that keep to these rules, and one draw needn't show every extreme that they name: `nb_shard`: the 32 entries of each 16 consecutive spans name any one shard at most 3 times, and one shard exactly 3 times.
All inputs are finite; a program needn't handle non-finite values.
Results may differ from a plain program's by a relative error of at most 0.022.
The roundings to bfloat16 on the way count: a program that leaves them out, or rounds other values in their place, can miss the bound.
Values may be sent and summed in bfloat16 or wider, within the bound.
No kernel may reach another device: no remote copies, remote signals or barrier semaphores. Data moves between devices by JAX's collectives and lax.ppermute only.
A program may use at most 128 MiB of HBM per device.

v0:
```python
import math

import jax
import jax.numpy as jnp
from jax import lax
from jax.sharding import PartitionSpec as P

HS = 128
CL = 64
NB_LEN = 128
NEIGH = 2


def shifted(value, axis, steps):
    count = lax.axis_size(axis)
    first, last = (max(0, -steps), min(count, count - steps))
    return lax.ppermute(value, axis, [(source, source + steps) for source in range(first, last)])


def attend(queries, keys, values):
    blocks, qlen, width = queries.shape
    heads_here = width // HS
    q_heads = queries.reshape(blocks, qlen, heads_here, HS)
    k_heads = keys.reshape(blocks, keys.shape[1], heads_here, HS)
    v_heads = values.reshape(blocks, values.shape[1], heads_here, HS)
    scores = jnp.einsum("bqhd,bkhd->bhqk", q_heads, k_heads, preferred_element_type=jnp.float32) * (
        1.0 / math.sqrt(HS)
    )
    probs = jax.nn.softmax(scores, axis=-1).astype(jnp.bfloat16)
    context = jnp.einsum("bhqk,bkhd->bqhd", probs, v_heads, preferred_element_type=jnp.float32)
    return context.reshape(blocks, qlen, width).astype(jnp.bfloat16)


def bucket_places(shards):
    count = shards.shape[1]
    same_shard = shards[:, :, None] == shards[:, None, :]
    earlier = jnp.arange(count)[None, :] < jnp.arange(count)[:, None]
    return jnp.sum((same_shard & earlier[None]).astype(jnp.int32), axis=2)


def body(decoder, w_query, w_key, w_value, w_out, database, nb_shard, nb_slot):
    n_seq = lax.axis_size("seq")
    seq_index = lax.axis_index("seq")
    tok_rows = decoder.shape[0]
    spans_dev = tok_rows // CL
    width = w_query.shape[1]
    requests = NEIGH * spans_dev
    capacity = (requests + n_seq - 1) // n_seq + 1
    source = decoder.astype(jnp.float32)
    scale = lax.rsqrt(jnp.mean(source * source, axis=-1, keepdims=True) + 1e-05)
    normed = (source * scale).astype(jnp.bfloat16)
    queries = jnp.dot(normed, w_query, preferred_element_type=jnp.float32).astype(jnp.bfloat16)
    shard_lists = nb_shard.reshape(n_seq, requests)
    slot_lists = nb_slot.reshape(n_seq, requests)
    places = bucket_places(shard_lists)
    mine = shard_lists == seq_index
    picked = mine[:, None, :] & (places[:, None, :] == jnp.arange(capacity)[None, :, None])
    send_slot = jnp.sum(jnp.where(picked, slot_lists[:, None, :], 0), axis=2)
    outgoing = database[send_slot]
    received = lax.all_to_all(outgoing, "seq", split_axis=0, concat_axis=0, tiled=True)
    my_shards = lax.dynamic_index_in_dim(shard_lists, seq_index, 0, keepdims=False)
    my_places = lax.dynamic_index_in_dim(places, seq_index, 0, keepdims=False)
    row_index = my_shards * capacity + my_places
    flat_received = received.reshape(n_seq * capacity, NB_LEN, received.shape[3])
    neighbour_rows = flat_received[row_index].reshape(spans_dev, NEIGH * NB_LEN, received.shape[3])
    keys = jnp.einsum(
        "cne,eh->cnh", neighbour_rows, w_key, preferred_element_type=jnp.float32
    ).astype(jnp.bfloat16)
    values = jnp.einsum(
        "cne,eh->cnh", neighbour_rows, w_value, preferred_element_type=jnp.float32
    ).astype(jnp.bfloat16)
    incoming = shifted(queries[: CL - 1], "seq", -1)
    aligned_queries = jnp.concatenate([queries[CL - 1 :], incoming], axis=0).reshape(
        spans_dev, CL, width
    )
    aligned = attend(aligned_queries, keys, values).reshape(tok_rows, width)
    leading = shifted(aligned[tok_rows - CL + 1 :], "seq", 1)
    context = jnp.concatenate([leading, aligned[: tok_rows - CL + 1]], axis=0)
    return lax.psum_scatter(
        jnp.dot(context, w_out, preferred_element_type=jnp.float32).astype(jnp.bfloat16),
        "db",
        scatter_dimension=0,
        tiled=True,
    )


def solution(mesh):
    return jax.shard_map(
        body,
        mesh=mesh,
        in_specs=(
            P("seq", None),
            P(None, "db"),
            P(None, "db"),
            P(None, "db"),
            P("db", None),
            P("seq", None, None),
            P(),
            P(),
        ),
        out_specs=P(("seq", "db"), None),
        check_vma=False,
    )
```

profile of v0, /device:TPU:1, one launch (start us, length us, event | category | flops | bytes accessed | tf_op | source)
XLA Modules:
  0.0 338.6 jit_solution(11156047391492927584)
XLA Ops:
  6.5 0.0 copy-start
  6.5 0.9 copy.20
  7.4 0.1 reshape.95
  7.6 0.5 convert_reduce_fusion
  8.0 0.8 copy.21
  8.8 0.1 broadcast_in_dim.10
  9.0 0.1 select_reduce_fusion
  9.1 0.1 copy.22
  9.2 0.1 reshape.102
  9.3 9.7 %gather_fusion = bf16[48,128,896]{2,1,0:T(8,128)(2,1)} fusion(bf16[24,128,896]{2,1,0:T(8,128)(2,1)} %param.13, s32[1024]{0:T(1024)S(1)} %pad_clamp_fusion.1), kind=kCustom, calls=%fused_computation | custom fusion | bytes 22020288 | tf_op jit(solution)/shard_map/gather | solution.py:59
  19.1 7.6 %all-to-all-start = ((bf16[16,3,128,896]{3,2,1,0:T(8,128)(2,1)}), bf16[16,3,128,896]{3,2,1,0:T(8,128)(2,1)}, u32[]{:S(2)}, u32[]{:S(2)}) async-start(bf16[16,3,128,896]{3,2,1,0:T(8,128)(2,1)} %bitcast.42), calls=%async_computation | async-start | bytes 22020096 | tf_op jit(solution)/shard_map/all_to_all | solution.py:60
  26.7 0.0 reduce-scatter.2.cloned.1.call-start
  26.7 0.0 copy-start.4
  26.7 5.2 %fusion.1 = f32[1024]{0:T(1024)S(1)} fusion(bf16[1024,4096]{1,0:T(8,128)(2,1)} %param.8), kind=kLoop, calls=%fused_computation.5 | loop fusion | flops 12581888 | bytes 8392704 | tf_op jit(solution)/shard_map/reduce_sum | solution.py:50
  32.0 0.0 copy-done.4
  32.0 7.2 %fusion.20 = bf16[1024,512]{1,0:T(8,128)(2,1)S(1)} fusion(bf16[4096,512]{1,0:T(8,128)(2,1)S(1)} %copy-done.4, bf16[1024,4096]{1,0:T(8,128)(2,1)} %param.8, f32[1024]{0:T(1024)S(1)} %add_rsqrt_fusion), kind=kOutput, calls=%fused_computation.25 | convolution fusion | flops 4308074496 | bytes 13635584 | tf_op jit(solution)/shard_map/dot_general | solution.py:52
  39.2 1.5 collective-permute-start
  40.7 0.2 slice.20
  40.9 83.4 %collective-permute-done = bf16[63,512]{1,0:T(8,128)(2,1)S(1)} collective-permute-done((bf16[63,512]{1,0:T(8,128)(2,1)S(1)}, bf16[63,512]{1,0:T(8,128)(2,1)S(1)}, u32[]{:S(2)}, u32[]{:S(2)}) %collective-permute-start) | collective-permute-done | bytes 64544 | tf_op jit(solution)/shard_map/ppermute | solution.py:17
  124.3 0.1 pad_maximum_fusion
  124.4 0.3 reshape_reshape.3
  124.7 93.7 %all-to-all-done = bf16[16,3,128,896]{3,2,1,0:T(8,128)(2,1)} async-done(((bf16[16,3,128,896]{3,2,1,0:T(8,128)(2,1)}), bf16[16,3,128,896]{3,2,1,0:T(8,128)(2,1)}, u32[]{:S(2)}, u32[]{:S(2)}) %all-to-all-start) | async-done | bytes 11010080 | tf_op jit(solution)/shard_map/all_to_all | solution.py:60
  218.4 8.5 %gather_fusion.1 = bf16[32,128,896]{2,1,0:T(8,128)(2,1)} fusion(bf16[48,128,896]{2,1,0:T(8,128)(2,1)} %bitcast.2, s32[1024]{0:T(1024)S(1)} %pad_clamp_fusion), kind=kCustom, calls=%fused_computation.1 | custom fusion | bytes 14680192 | tf_op jit(solution)/shard_map/gather | solution.py:65
  226.9 0.0 copy-done
  226.9 7.8 %convert_bitcast_fusion = bf16[16,32,4,8,128]{4,3,2,1,0:T(8,128)(2,1)S(1)} fusion(bf16[16,256,896]{2,1,0:T(8,128)(2,1)} %bitcast.43, bf16[896,512]{1,0:T(8,128)(2,1)S(1)} %copy-done), kind=kOutput, calls=%fused_computation.18 | convolution fusion | flops 3760193536 | bytes 12451840 | tf_op jit(solution)/shard_map/cne,eh->cnh/dot_general | solution.py:66
  234.7 0.0 copy-start.2
  234.7 1.6 fusion.9
  236.3 0.0 copy-start.3
  236.3 2.0 copy-done.3
  238.3 0.0 copy-start.6
  238.3 1.6 fusion.43
  239.9 0.0 copy-done.2
  239.9 0.0 copy-done.6
  239.9 6.1 %convert_bitcast_fusion.1 = bf16[16,32,4,8,128]{4,3,2,1,0:T(8,128)(2,1)} fusion(bf16[16,256,896]{2,1,0:T(8,128)(2,1)S(1)} %bitcast.44, bf16[896,512]{1,0:T(8,128)(2,1)S(1)} %copy-done.6), kind=kOutput, calls=%fused_computation.19 | convolution fusion | flops 3760193536 | bytes 12451840 | tf_op jit(solution)/shard_map/cne,eh->cnh/dot_general | solution.py:69
  246.0 11.9 %fusion.23 = bf16[16,64,4,128]{3,1,2,0:T(8,128)(2,1)S(1)} fusion(bf16[16,32,4,8,128]{4,3,2,1,0:T(8,128)(2,1)} %convert_bitcast_fusion.1, f32[16,4,64]{2,1,0:T(4,128)S(1)} %fusion.43, f32[16,4,64,256]{3,2,1,0:T(8,128)} %copy-done.3), kind=kOutput, calls=%fused_computation.26 | convolution fusion | flops 274206976 | bytes 9453568 | tf_op jit(solution)/shard_map/bhqk,bkhd->bqhd/dot_general | solution.py:30
  257.9 0.0 copy-start.5
  257.9 0.9 copy.26
  258.8 0.2 copy.45
  259.0 6.4 %collective-permute-start.1 = (bf16[63,512]{1,0:T(8,128)(2,1)S(1)}, bf16[63,512]{1,0:T(8,128)(2,1)S(1)}, u32[]{:S(2)}, u32[]{:S(2)}) collective-permute-start(bf16[63,512]{1,0:T(8,128)(2,1)S(1)} %slice.22), channel_id=1, source_target_pairs={{0,8},{8,16},{16,24},{24,32},{32,40},{40,48},{48,56},{56,64},{64,7... | collective-permute-start | bytes 193544 | tf_op jit(solution)/shard_map/ppermute | solution.py:17
  265.4 0.1 slice.23
  265.5 1.2 collective-permute-done.1
  266.8 0.0 copy-done.5
  266.8 6.7 %convolution_convert_fusion = bf16[1024,4096]{1,0:T(8,128)(2,1)} fusion(bf16[512,4096]{1,0:T(8,128)(2,1)S(1)} %copy-done.5, bf16[961,512]{1,0:T(8,128)(2,1)S(1)} %slice.23, bf16[63,512]{1,0:T(8,128)(2,1)S(1)} %collective-permute-done.1), kind=kOutput, calls=%fused_computation.9 | convolution fusion | flops 4301258752 | bytes 13631488 | tf_op jit(solution)/shard_map/dot_general | solution.py:80
  273.5 0.0 copy-start.1
  273.5 0.0 reduce-scatter.2.cloned.1.call-update
  273.5 58.3 %reduce-scatter.2.cloned.1.call-done = bf16[128,4096]{1,0:T(8,128)(2,1)} async-done(((bf16[1024,4096]{1,0:T(8,128)(2,1)}), bf16[128,4096]{1,0:T(8,128)(2,1)}) %reduce-scatter.2.cloned.1.call-update) | async-done | bytes 1048592 | tf_op jit(solution)/shard_map/reduce_scatter | solution.py:79
  331.7 0.0 copy-done.1
  (9 shorter events, 0.1 us)
Async XLA Ops:
  6.5 220.3 %copy-start = (bf16[896,512]{1,0:T(8,128)(2,1)S(1)}, bf16[896,512]{1,0:T(8,128)(2,1)}, u32[]{:S(2)}) copy-start(bf16[896,512]{1,0:T(8,128)(2,1)} %param.10) | copy-start | bytes 2752516
  19.1 199.3 %all-to-all-start = ((bf16[16,3,128,896]{3,2,1,0:T(8,128)(2,1)}), bf16[16,3,128,896]{3,2,1,0:T(8,128)(2,1)}, u32[]{:S(2)}, u32[]{:S(2)}) async-start(bf16[16,3,128,896]{3,2,1,0:T(8,128)(2,1)} %bitcast.42), calls=%async_computation | async-start | bytes 22020096 | tf_op jit(solution)/shard_map/all_to_all | solution.py:60
  26.7 305.0 %reduce-scatter.2.cloned.1.call-start = ((), (), s32[]{:S(2)}) async-start(), calls=%async_computation.2 | async-start | bytes 9437184 | tf_op jit(solution)/shard_map/reduce_scatter | solution.py:79
  26.7 5.2 %copy-start.4 = (bf16[4096,512]{1,0:T(8,128)(2,1)S(1)}, bf16[4096,512]{1,0:T(8,128)(2,1)}, u32[]{:S(2)}) copy-start(bf16[4096,512]{1,0:T(8,128)(2,1)} %param.9) | copy-start | bytes 12582916
  39.2 85.1 %collective-permute-start = (bf16[63,512]{1,0:T(8,128)(2,1)S(1)}, bf16[63,512]{1,0:T(8,128)(2,1)S(1)}, u32[]{:S(2)}, u32[]{:S(2)}) collective-permute-start(bf16[63,512]{1,0:T(8,128)(2,1)S(1)} %slice.21), channel_id=1, source_target_pairs={{8,0},{16,8},{24,16},{32,24},{40,32},{48,40},{56,48},{64,56},{72,6... | collective-permute-start | bytes 193544 | tf_op jit(solution)/shard_map/ppermute | solution.py:17
  234.7 5.2 %copy-start.2 = (bf16[32,128,896]{2,1,0:T(8,128)(2,1)S(1)}, bf16[32,128,896]{2,1,0:T(8,128)(2,1)}, u32[]{:S(2)}) copy-start(bf16[32,128,896]{2,1,0:T(8,128)(2,1)} %gather_fusion.1) | copy-start | bytes 22020100
  236.3 2.0 copy-start.3
  238.3 1.6 copy-start.6
  257.9 8.8 %copy-start.5 = (bf16[512,4096]{1,0:T(8,128)(2,1)S(1)}, bf16[512,4096]{1,0:T(8,128)(2,1)}, u32[]{:S(2)}) copy-start(bf16[512,4096]{1,0:T(8,128)(2,1)} %param.12) | copy-start | bytes 12582916
  259.0 7.7 %collective-permute-start.1 = (bf16[63,512]{1,0:T(8,128)(2,1)S(1)}, bf16[63,512]{1,0:T(8,128)(2,1)S(1)}, u32[]{:S(2)}, u32[]{:S(2)}) collective-permute-start(bf16[63,512]{1,0:T(8,128)(2,1)S(1)} %slice.22), channel_id=1, source_target_pairs={{0,8},{8,16},{16,24},{24,32},{32,40},{40,48},{48,56},{56,64},{64,7... | collective-permute-start | bytes 193544 | tf_op jit(solution)/shard_map/ppermute | solution.py:17
  273.5 58.3 %copy-start.1 = (bf16[896,512]{1,0:T(8,128)(2,1)S(1)}, bf16[896,512]{1,0:T(8,128)(2,1)}, u32[]{:S(2)}) copy-start(bf16[896,512]{1,0:T(8,128)(2,1)} %param.10) | copy-start | bytes 2752516
Sparse Core Ops, SparseCore 0:
  273.6 58.0 reduce-scatter.1
where the time goes:
time: 339 us
  waiting for transfers between devices  237 us (70%)
  matrix products  41.2 us (12%)
  local copies, waits for them, and re-layouts  24 us (7%)
  starting transfers between devices  15.5 us (5%)
  between operations  13.6 us (4%)
  other arithmetic  7.58 us (2%)
    all_to_all x1, waiting for transfers between devices, body(): lax.all_to_all(outgoing, 'seq', split_axis=0, concat_axis=0, tiled=True)  93.7 us
    ppermute x2, waiting for transfers between devices, shifted(): lax.ppermute(value, axis, [(source, source + steps) for source in range(f...  84.6 us
    reduce_scatter x1, waiting for transfers between devices, body(): lax.psum_scatter(jnp.dot(context, w_out, preferred_element_type=jnp.float...  58.3 us
    dot_general x1, matrix products, attend(): jnp.einsum('bhqk,bkhd->bqhd', probs, v_heads, preferred_element_type=jnp....  11.9 us
    gather x1, local copies, waits for them, and re-layouts, body(): outgoing = database[send_slot]  9.73 us
    gather x1, local copies, waits for them, and re-layouts, body(): flat_received[row_index]  8.5 us
    ppermute x2, starting transfers between devices, shifted(): lax.ppermute(value, axis, [(source, source + steps) for source in range(f...  7.87 us
    dot_general x1, matrix products, body(): jnp.einsum('cne,eh->cnh', neighbour_rows, w_key, preferred_element_type=j...  7.81 us
  transfers between devices with their start and end apart: 4, of which 4 were waited for; matrix products, arithmetic and copies ran while one was open for 4% of the time, Pallas kernels for 0%

commit v1 on v0

v1 whole, which is shorter than its diff:
```python
import math

import jax
import jax.numpy as jnp
from jax import lax
from jax.experimental import pallas as pl
from jax.experimental.pallas import tpu as pltpu
from jax.sharding import Mesh, PartitionSpec as P

HS = 128
CL = 64
NB_LEN = 128
NEIGH = 2
N_Z = 4
N_CORE = 2
BLOCK = 128
HALO = CL - 1
KEPT = BLOCK - HALO
F32 = jnp.float32
BF16 = jnp.bfloat16


def step(value, axis, steps):
    count = lax.axis_size(axis)
    return lax.ppermute(value, axis, [(i, (i + steps) % count) for i in range(count)])


def dot(a, b):
    return jnp.dot(a, b, preferred_element_type=F32)


def bucket_places(shards):
    count = shards.shape[1]
    same_shard = shards[:, :, None] == shards[:, None, :]
    earlier = jnp.arange(count)[None, :] < jnp.arange(count)[:, None]
    return jnp.sum((same_shard & earlier[None]).astype(jnp.int32), axis=2)


def attend_kernel(qa_ref, qb_ref, *refs):
    parts_a, parts_b, out_ref = refs[0:4], refs[4:8], refs[8]
    half = qa_ref.shape[1]
    for side, (q_ref, parts) in enumerate(((qa_ref, parts_a), (qb_ref, parts_b))):
        for head in range(half // HS):
            lower = head * HS
            q = q_ref[:, lower : lower + HS]
            k = jnp.concatenate([part[0, :, lower : lower + HS] for part in parts], axis=0)
            v = jnp.concatenate([part[0, :, half + lower : half + lower + HS] for part in parts], axis=0)
            scores = lax.dot_general(q, k, (((1,), (1,)), ((), ())), preferred_element_type=F32)
            scores = scores * (1.0 / math.sqrt(HS))
            top = jnp.max(scores, axis=-1, keepdims=True)
            weights = jnp.exp(scores - top)
            total = jnp.sum(weights, axis=-1, keepdims=True)
            probs = (weights * (1.0 / total)).astype(BF16)
            out_ref[:, side * half + lower : side * half + lower + HS] = dot(probs, v).astype(BF16)


def attend(queries_a, queries_b, parts_a, parts_b):
    tokens, half = queries_a.shape
    spans = tokens // CL
    q_spec = pl.BlockSpec((CL, half), lambda i: (i, 0))
    part_spec = pl.BlockSpec((1,) + parts_a[0].shape[1:], lambda i: (i, 0, 0))
    return pl.pallas_call(
        attend_kernel,
        grid=(spans,),
        in_specs=[q_spec, q_spec] + [part_spec] * 8,
        out_specs=pl.BlockSpec((CL, 2 * half), lambda i: (i, 0)),
        out_shape=jax.ShapeDtypeStruct((tokens, 2 * half), BF16),
        cost_estimate=pl.CostEstimate(
            flops=4 * tokens * 256 * 2 * half, bytes_accessed=tokens * 40 * half, transcendentals=tokens * 2048
        ),
        compiler_params=pltpu.CompilerParams(vmem_limit_bytes=32 * 1024 * 1024),
    )(queries_a, queries_b, *parts_a, *parts_b)


def body(decoder, w_query, w_key, w_value, w_out, database, nb_shard, nb_slot):
    n_seq = lax.axis_size("seq")
    seq_index, z_index, core = lax.axis_index("seq"), lax.axis_index("z"), lax.axis_index("core")
    tok_rows, model = decoder.shape
    half = w_query.shape[1]
    requests = NEIGH * (tok_rows // CL)
    capacity = (requests + n_seq - 1) // n_seq + 1
    enc = database.shape[2]
    piece = NB_LEN // (N_Z * N_CORE)

    halo = lax.ppermute(decoder[:CL], "seq", [(i + 1, i) for i in range(n_seq - 1)])

    shard_lists = nb_shard.reshape(n_seq, requests)
    slot_lists = nb_slot.reshape(n_seq, requests)
    places = bucket_places(shard_lists)
    picked = (shard_lists == seq_index)[:, None, :] & (places[:, None, :] == jnp.arange(capacity)[None, :, None])
    send_slot = jnp.sum(jnp.where(picked, slot_lists[:, None, :], 0), axis=2)
    my_piece = lax.dynamic_slice_in_dim(database, (z_index * N_CORE + core) * piece, piece, axis=1)
    received = lax.all_to_all(my_piece[send_slot], "seq", split_axis=0, concat_axis=0, tiled=True)
    received = received.reshape(n_seq * capacity, piece, enc)
    my_shards = lax.dynamic_index_in_dim(shard_lists, seq_index, 0, keepdims=False)
    my_places = lax.dynamic_index_in_dim(places, seq_index, 0, keepdims=False)
    row_index = (my_shards * capacity + my_places).reshape(N_Z, N_CORE, -1)
    mine = lax.dynamic_index_in_dim(row_index, core, 1, keepdims=False).reshape(-1)
    theirs = lax.dynamic_index_in_dim(row_index, 1 - core, 1, keepdims=False).reshape(-1)
    swapped = step(received[theirs], "core", 1)
    own = jnp.concatenate([received[mine], swapped], axis=1)
    spans = requests // NEIGH // N_CORE
    own = own.reshape(spans, NEIGH * 2 * piece, enc)
    low, high = own[: spans // 2], own[spans // 2 :]

    w_kv = jnp.concatenate([w_key, w_value], axis=1)
    w_kv_other = step(w_kv, "core", 1)
    w_query_other = step(w_query, "core", 1)
    w_out_other = step(w_out, "core", 1)
    w_out_chip = jnp.concatenate([w_out, w_out_other], axis=0)

    tokens = jnp.concatenate([decoder[CL - 1 :], halo[: CL - 1]], axis=0).reshape(N_Z, N_CORE, BLOCK, model)
    tokens = lax.dynamic_index_in_dim(tokens, core, 1, keepdims=False).reshape(N_Z * BLOCK, model)
    source = tokens.astype(F32)
    scale = lax.rsqrt(jnp.mean(source * source, axis=-1, keepdims=True) + 1e-05)
    normed = (source * scale).astype(BF16)
    queries_a = dot(normed, w_query).astype(BF16)
    queries_b = dot(normed, w_query_other).astype(BF16)

    up_low = step(low, "z", 1)
    down_high = step(high, "z", -1)
    up_high = step(high, "z", 1)
    down_low = step(low, "z", -1)
    far_low = step(up_low, "z", 1)
    far_high = step(down_high, "z", -1)

    def project(rows, weight):
        flat = rows.reshape(-1, enc)
        return dot(flat, weight).astype(BF16).reshape(rows.shape[0], rows.shape[1], -1)

    contexts = []
    for place, parts in enumerate(((low, up_low, down_low, far_low), (high, up_high, down_high, far_high))):
        lower = place * N_Z * BLOCK // 2
        contexts.append(
            attend(
                queries_a[lower : lower + N_Z * BLOCK // 2],
                queries_b[lower : lower + N_Z * BLOCK // 2],
                [project(part, w_kv) for part in parts],
                [project(part, w_kv_other) for part in parts],
            )
        )
    context = jnp.concatenate(contexts, axis=0).reshape(N_Z, BLOCK, 2 * half)

    tails = context[:, KEPT:]
    tails = jnp.concatenate([tails[:, :, half:], tails[:, :, :half]], axis=2)
    heads = step(tails, "core", 1)
    first = lax.ppermute(tails[N_Z - 1], ("seq", "core"), [(2 * i + 1, 2 * i + 2) for i in range(n_seq - 1)])
    heads = jnp.where(core == 0, jnp.concatenate([first[None], heads[:-1]], axis=0), heads)
    context = jnp.concatenate([heads, context[:, :KEPT]], axis=1)

    def block(distance):
        return lax.dynamic_index_in_dim(context, (z_index + distance) % N_Z, 0, keepdims=False)

    side = model // 2
    w_left, w_right = w_out_chip[:, :side], w_out_chip[:, side:]
    far = block(2)
    up_far = step(dot(far, w_left).astype(BF16), "z", 1)
    down_far = step(dot(far, w_right).astype(BF16), "z", -1)
    above, below, here = block(1), block(3), block(0)
    up_right = step(dot(above, w_right).astype(BF16), "z", 1)
    down_left = step(dot(below, w_left).astype(BF16), "z", -1)
    up_left = step((dot(above, w_left) + up_far.astype(F32)).astype(BF16), "z", 1)
    down_right = step((dot(below, w_right) + down_far.astype(F32)).astype(BF16), "z", -1)
    left = dot(here, w_left) + down_left.astype(F32) + up_left.astype(F32)
    right = dot(here, w_right) + up_right.astype(F32) + down_right.astype(F32)
    return jnp.concatenate([left.astype(BF16), right.astype(BF16)], axis=1)


def solution(mesh):
    n_seq = mesh.devices.shape[0]
    fine = Mesh(mesh.devices.reshape(n_seq, N_Z, N_CORE), ("seq", "z", "core"))
    db = ("z", "core")
    return jax.shard_map(
        body,
        mesh=fine,
        in_specs=(
            P("seq", None),
            P(None, db),
            P(None, db),
            P(None, db),
            P(db, None),
            P("seq", None, None),
            P(),
            P(),
        ),
        out_specs=P(("seq", "z", "core"), None),
        check_vma=False,
    )
```

time: 339 us -> 192 us (0.57)
  waiting for transfers between devices: 237 us -> 40.5 us
  Pallas kernels: 0 us -> 21.6 us
  matrix products: 41.2 us -> 58.7 us
  starting transfers between devices: 15.5 us -> 30.9 us
  between operations: 13.6 us -> 0.67 us
    all_to_all x1, waiting for transfers between devices: 93.7 us -> 0.01 us  [body(): lax.all_to_all(my_piece[send_slot], 'seq', split_axis=0, concat_axis=0, t...]
    reduce_scatter x1 -> x0, waiting for transfers between devices: 58.3 us -> none  [body(): lax.psum_scatter(jnp.dot(context, w_out, preferred_element_type=jnp.float...]
    ppermute x2 -> x19, waiting for transfers between devices: 84.6 us -> 40.5 us  [the longest x17 31.4 us: step(): lax.ppermute(value, axis, [(i, (i + steps) % count) for i in range(count)])]
    pallas_call x0 -> x2, Pallas kernels: none -> 21.6 us  [attend(): pl.pallas_call(attend_kernel, grid=(spans,), in_specs=[q_spec, q_spec] +...]
    dot_general x6 -> x26, matrix products: 41.2 us -> 58.7 us  [dot(): return jnp.dot(a, b, preferred_element_type=F32)]
    ppermute x2 -> x19, starting transfers between devices: 7.87 us -> 23.4 us  [the longest x17 18.4 us: step(): lax.ppermute(value, axis, [(i, (i + steps) % count) for i in range(count)])]
    gather x2 -> x3, local copies, waits for them, and re-layouts: 18.2 us -> 3.16 us  [the longest x1 1.91 us: body(): my_piece[send_slot]]
    slice x4 -> x8, local copies, waits for them, and re-layouts: 0.33 us -> 10.2 us  [the longest x1 8.83 us: body(): decoder[CL - 1:]]
  transfers between devices with their start and end apart: 4 -> 20, of which waited for: 4 -> 6; matrix products, arithmetic and copies ran while one was open for 4% -> 45% of each run, Pallas kernels for 0% -> 11%
where the time goes in v1:
time: 192 us; the launch traced here: 189 us
  matrix products  58.7 us (31%)
  waiting for transfers between devices  40.5 us (21%)
  starting transfers between devices  30.9 us (16%)
  local copies, waits for them, and re-layouts  26.6 us (14%)
  Pallas kernels  21.6 us (11%)
  other arithmetic  10.2 us (5%)
    dot_general x26, matrix products, dot(): return jnp.dot(a, b, preferred_element_type=F32)  58.7 us
    ppermute x17, waiting for transfers between devices, step(): lax.ppermute(value, axis, [(i, (i + steps) % count) for i in range(count)])  31.4 us
    pallas_call x2, Pallas kernels, attend(): pl.pallas_call(attend_kernel, grid=(spans,), in_specs=[q_spec, q_spec] +...  21.6 us
    ppermute x17, starting transfers between devices, step(): lax.ppermute(value, axis, [(i, (i + steps) % count) for i in range(count)])  18.4 us
    ppermute x1, waiting for transfers between devices, body(): lax.ppermute(decoder[:CL], 'seq', [(i + 1, i) for i in range(n_seq - 1)])  9.03 us
    slice x1, local copies, waits for them, and re-layouts, body(): decoder[CL - 1:]  8.83 us
    unnamed x19, local copies, waits for them, and re-layouts  7.77 us
    all_to_all x1, starting transfers between devices, body(): lax.all_to_all(my_piece[send_slot], 'seq', split_axis=0, concat_axis=0, t...  7.58 us
  transfers between devices with their start and end apart: 20, of which 6 were waited for; matrix products, arithmetic and copies ran while one was open for 45% of the time, Pallas kernels for 11%

profile of v1, /device:TPU:1, one launch (start us, length us, event | category | flops | bytes accessed | tf_op | source)
XLA Modules:
  0.0 189.2 jit_solution(16233314215084347545)
XLA Ops:
  2.8 1.2 constant_dynamic-slice_fusion.4
  4.1 1.9 %gather_fusion = bf16[48,16,896]{2,1,0:T(8,128)(2,1)} fusion(bf16[24,16,896]{2,1,0:T(8,128)(2,1)S(1)} %constant_dynamic-slice_fusion.4, s32[1024]{0:T(1024)S(1)} %pad_clamp_fusion.2), kind=kCustom, calls=%fused_computation | custom fusion | bytes 2752704 | tf_op jit(solution)/shard_map/gather | solution.py:93
  6.0 7.6 %all-to-all-start = ((bf16[16,3,16,896]{3,2,1,0:T(8,128)(2,1)}), bf16[16,3,16,896]{3,2,1,0:T(8,128)(2,1)S(1)}, u32[]{:S(2)}, u32[]{:S(2)}) async-start(bf16[16,3,16,896]{3,2,1,0:T(8,128)(2,1)} %bitcast.4), calls=%async_computation | async-start | bytes 2752512 | tf_op jit(solution)/shard_map/all_to_all | solution.py:93
  16.6 1.1 slice.58
  17.6 1.3 collective-permute-start
  19.5 8.8 %slice.57 = bf16[961,4096]{1,0:T(8,128)(2,1)} slice(bf16[1024,4096]{1,0:T(8,128)(2,1)} %param.8), slice={[63:1024], [0:4096]} | slice | bytes 15745024 | tf_op jit(solution)/shard_map/slice | solution.py:112
  28.7 5.0 %constant_dynamic-update-slice_fusion.5 = bf16[1024,4096]{1,0:T(8,128)(2,1)} fusion(bf16[512,4096]{1,0:T(8,128)(2,1)} %param.12), kind=kLoop, calls=%fused_computation.90 | loop fusion | bytes 8388608
  33.7 9.0 %collective-permute-done = bf16[64,4096]{1,0:T(8,128)(2,1)S(1)} collective-permute-done((bf16[64,4096]{1,0:T(8,128)(2,1)S(1)}, bf16[64,4096]{1,0:T(8,128)(2,1)S(1)}, u32[]{:S(2)}, u32[]{:S(2)}) %collective-permute-start) | collective-permute-done | bytes 524320 | tf_op jit(solution)/shard_map/ppermute | solution.py:85
  42.7 2.9 %pad_maximum_fusion = bf16[1024,4096]{1,0:T(8,128)(2,1)S(1)} fusion(bf16[63,4096]{1,0:T(8,128)(2,1)S(1)} %bitcast.124, bf16[961,4096]{1,0:T(8,128)(2,1)S(1)} %copy-done), kind=kLoop, calls=%fused_computation.3 | loop fusion | flops 16777216 | bytes 16777216 | tf_op jit(solution)/shard_map/concatenate | solution.py:112
  45.6 1.1 dynamic-slice_convert_fusion
  47.6 3.3 %fusion = bf16[512,4096]{1,0:T(8,128)(2,1)} fusion(f32[4,1,128,4096]{3,2,1,0:T(8,128)S(1)} %dynamic-slice_convert_fusion, f32[512]{0:T(512)S(1)} %rsqrt_bitcast_fusion), kind=kLoop, calls=%fused_computation.5 | loop fusion | flops 4194304 | bytes 12584960 | tf_op jit(solution)/shard_map/convert_element_type | solution.py:116
  52.2 5.8 %convolution_convert_fusion.1 = bf16[512,512]{1,0:T(8,128)(2,1)S(1)} fusion(bf16[512,4096]{1,0:T(8,128)(2,1)} %fusion, bf16[4096,512]{1,0:T(8,128)(2,1)} %param.9), kind=kOutput, calls=%fused_computation.47 | convolution fusion | flops 2147745792 | bytes 8912896 | tf_op jit(solution)/shard_map/dot_general | solution.py:29
  58.8 1.7 collective-permute-start.3
  60.5 2.2 %collective-permute-start.4 = (bf16[4,64,896]{2,1,0:T(8,128)(2,1)S(1)}, bf16[4,64,896]{2,1,0:T(8,128)(2,1)S(1)}, u32[]{:S(2)}, u32[]{:S(2)}) collective-permute-start(bf16[4,64,896]{2,1,0:T(8,128)(2,1)S(1)} %bitcast.130), channel_id=1, source_target_pairs={{0,6},{2,0},{4,2},{6,4},{1,7},{3,1},{5,3},{7,5},{8,14},{10,8},{12,... | collective-permute-start | bytes 1376264 | tf_op jit(solution)/shard_map/ppermute | solution.py:25
  62.7 2.2 %convolution_convert_fusion.17 = bf16[256,1024]{1,0:T(8,128)(2,1)S(1)} fusion(bf16[256,896]{1,0:T(8,128)(2,1)S(1)} %bitcast.131, bf16[896,1024]{1,0:T(8,128)(2,1)} %constant_dynamic-update-slice_fusion.2), kind=kOutput, calls=%fused_computation.63 | convolution fusion | flops 470024192 | bytes 2818048 | tf_op jit(solution)/shard_map/dot_general | solution.py:29
  64.9 2.2 %convolution_convert_fusion.9 = bf16[256,1024]{1,0:T(8,128)(2,1)S(1)} fusion(bf16[256,896]{1,0:T(8,128)(2,1)S(1)} %bitcast.125, bf16[896,1024]{1,0:T(8,128)(2,1)} %constant_dynamic-update-slice_fusion.2), kind=kOutput, calls=%fused_computation.55 | convolution fusion | flops 470024192 | bytes 2818048 | tf_op jit(solution)/shard_map/dot_general | solution.py:29
  67.2 1.6 collective-permute-start.8
  68.8 2.2 %convolution_convert_fusion.13 = bf16[256,1024]{1,0:T(8,128)(2,1)S(1)} fusion(bf16[256,896]{1,0:T(8,128)(2,1)S(1)} %bitcast.132, bf16[896,1024]{1,0:T(8,128)(2,1)} %collective-permute-done.6), kind=kOutput, calls=%fused_computation.59 | convolution fusion | flops 470024192 | bytes 2818048 | tf_op jit(solution)/shard_map/dot_general | solution.py:29
  71.0 2.2 %convolution_convert_fusion.5 = bf16[256,1024]{1,0:T(8,128)(2,1)S(1)} fusion(bf16[256,896]{1,0:T(8,128)(2,1)S(1)} %bitcast.127, bf16[896,1024]{1,0:T(8,128)(2,1)} %collective-permute-done.6), kind=kOutput, calls=%fused_computation.51 | convolution fusion | flops 470024192 | bytes 2818048 | tf_op jit(solution)/shard_map/dot_general | solution.py:29
  73.5 2.2 %convolution_convert_fusion.16 = bf16[256,1024]{1,0:T(8,128)(2,1)S(1)} fusion(bf16[256,896]{1,0:T(8,128)(2,1)S(1)} %bitcast.134, bf16[896,1024]{1,0:T(8,128)(2,1)} %constant_dynamic-update-slice_fusion.2), kind=kOutput, calls=%fused_computation.62 | convolution fusion | flops 470024192 | bytes 2818048 | tf_op jit(solution)/shard_map/dot_general | solution.py:29
  76.5 6.0 %collective-permute-done.8 = bf16[4,64,896]{2,1,0:T(8,128)(2,1)S(1)} collective-permute-done((bf16[4,64,896]{2,1,0:T(8,128)(2,1)S(1)}, bf16[4,64,896]{2,1,0:T(8,128)(2,1)S(1)}, u32[]{:S(2)}, u32[]{:S(2)}) %collective-permute-start.8) | collective-permute-done | bytes 458784 | tf_op jit(solution)/shard_map/ppermute | solution.py:25
  82.5 3.4 %collective-permute-start.9 = (bf16[4,64,896]{2,1,0:T(8,128)(2,1)S(1)}, bf16[4,64,896]{2,1,0:T(8,128)(2,1)S(1)}, u32[]{:S(2)}, u32[]{:S(2)}) collective-permute-start(bf16[4,64,896]{2,1,0:T(8,128)(2,1)S(1)} %collective-permute-done.8), channel_id=1, source_target_pairs={{0,6},{2,0},{4,2},{6,4},{1,7},{3,1},{5,3},{7,5},{8,14},{10,8},{12,... | collective-permute-start | bytes 1376264 | tf_op jit(solution)/shard_map/ppermute | solution.py:25
  85.9 2.2 %convolution_convert_fusion.15 = bf16[256,1024]{1,0:T(8,128)(2,1)S(1)} fusion(bf16[256,896]{1,0:T(8,128)(2,1)S(1)} %bitcast.136, bf16[896,1024]{1,0:T(8,128)(2,1)} %constant_dynamic-update-slice_fusion.2), kind=kOutput, calls=%fused_computation.61 | convolution fusion | flops 470024192 | bytes 2818048 | tf_op jit(solution)/shard_map/dot_general | solution.py:29
  88.1 2.2 %convolution_convert_fusion.8 = bf16[256,1024]{1,0:T(8,128)(2,1)S(1)} fusion(bf16[256,896]{1,0:T(8,128)(2,1)S(1)} %bitcast.144, bf16[896,1024]{1,0:T(8,128)(2,1)} %constant_dynamic-update-slice_fusion.2), kind=kOutput, calls=%fused_computation.54 | convolution fusion | flops 470024192 | bytes 2818048 | tf_op jit(solution)/shard_map/dot_general | solution.py:29
  90.3 2.2 %convolution_convert_fusion.7 = bf16[256,1024]{1,0:T(8,128)(2,1)S(1)} fusion(bf16[256,896]{1,0:T(8,128)(2,1)S(1)} %bitcast.138, bf16[896,1024]{1,0:T(8,128)(2,1)} %constant_dynamic-update-slice_fusion.2), kind=kOutput, calls=%fused_computation.53 | convolution fusion | flops 470024192 | bytes 2818048 | tf_op jit(solution)/shard_map/dot_general | solution.py:29
  92.5 2.2 %convolution_convert_fusion.12 = bf16[256,1024]{1,0:T(8,128)(2,1)S(1)} fusion(bf16[256,896]{1,0:T(8,128)(2,1)S(1)} %bitcast.135, bf16[896,1024]{1,0:T(8,128)(2,1)} %collective-permute-done.6), kind=kOutput, calls=%fused_computation.58 | convolution fusion | flops 470024192 | bytes 2818048 | tf_op jit(solution)/shard_map/dot_general | solution.py:29
  94.7 2.2 %convolution_convert_fusion.11 = bf16[256,1024]{1,0:T(8,128)(2,1)S(1)} fusion(bf16[256,896]{1,0:T(8,128)(2,1)S(1)} %bitcast.137, bf16[896,1024]{1,0:T(8,128)(2,1)} %collective-permute-done.6), kind=kOutput, calls=%fused_computation.57 | convolution fusion | flops 470024192 | bytes 2818048 | tf_op jit(solution)/shard_map/dot_general | solution.py:29
  97.0 2.2 %convolution_convert_fusion.4 = bf16[256,1024]{1,0:T(8,128)(2,1)S(1)} fusion(bf16[256,896]{1,0:T(8,128)(2,1)S(1)} %bitcast.145, bf16[896,1024]{1,0:T(8,128)(2,1)} %collective-permute-done.6), kind=kOutput, calls=%fused_computation.50 | convolution fusion | flops 470024192 | bytes 2818048 | tf_op jit(solution)/shard_map/dot_general | solution.py:29
  99.2 2.2 %convolution_convert_fusion.3 = bf16[256,1024]{1,0:T(8,128)(2,1)S(1)} fusion(bf16[256,896]{1,0:T(8,128)(2,1)S(1)} %bitcast.139, bf16[896,1024]{1,0:T(8,128)(2,1)} %collective-permute-done.6), kind=kOutput, calls=%fused_computation.49 | convolution fusion | flops 470024192 | bytes 2818048 | tf_op jit(solution)/shard_map/dot_general | solution.py:29
  101.4 2.2 %convolution_convert_fusion.14 = bf16[256,1024]{1,0:T(8,128)(2,1)S(1)} fusion(bf16[256,896]{1,0:T(8,128)(2,1)S(1)} %bitcast.140, bf16[896,1024]{1,0:T(8,128)(2,1)} %constant_dynamic-update-slice_fusion.2), kind=kOutput, calls=%fused_computation.60 | convolution fusion | flops 470024192 | bytes 2818048 | tf_op jit(solution)/shard_map/dot_general | solution.py:29
  103.6 2.4 %convolution_convert_fusion.6 = bf16[256,1024]{1,0:T(8,128)(2,1)S(1)} fusion(bf16[256,896]{1,0:T(8,128)(2,1)S(1)} %bitcast.142, bf16[896,1024]{1,0:T(8,128)(2,1)} %constant_dynamic-update-slice_fusion.2), kind=kOutput, calls=%fused_computation.52 | convolution fusion | flops 470024192 | bytes 2818048 | tf_op jit(solution)/shard_map/dot_general | solution.py:29
  106.0 2.2 %convolution_convert_fusion.10 = bf16[256,1024]{1,0:T(8,128)(2,1)S(1)} fusion(bf16[256,896]{1,0:T(8,128)(2,1)S(1)} %bitcast.141, bf16[896,1024]{1,0:T(8,128)(2,1)} %collective-permute-done.6), kind=kOutput, calls=%fused_computation.56 | convolution fusion | flops 470024192 | bytes 2818048 | tf_op jit(solution)/shard_map/dot_general | solution.py:29
  108.2 2.2 %convolution_convert_fusion.2 = bf16[256,1024]{1,0:T(8,128)(2,1)S(1)} fusion(bf16[256,896]{1,0:T(8,128)(2,1)S(1)} %bitcast.143, bf16[896,1024]{1,0:T(8,128)(2,1)} %collective-permute-done.6), kind=kOutput, calls=%fused_computation.48 | convolution fusion | flops 470024192 | bytes 2818048 | tf_op jit(solution)/shard_map/dot_general | solution.py:29
  110.5 4.5 %convolution_convert_fusion = bf16[512,512]{1,0:T(8,128)(2,1)S(1)} fusion(bf16[512,4096]{1,0:T(8,128)(2,1)S(1)} %copy-done.1, bf16[4096,512]{1,0:T(8,128)(2,1)} %collective-permute-done.1), kind=kOutput, calls=%fused_computation.46 | convolution fusion | flops 2147745792 | bytes 8912896 | tf_op jit(solution)/shard_map/dot_general | solution.py:29
  115.0 10.8 %shard_map.82 = bf16[256,1024]{1,0:T(8,128)(2,1)S(1)} custom-call(bf16[256,512]{1,0:T(8,128)(2,1)S(1)} %get-tuple-element.13.qa_ref, bf16[256,512]{1,0:T(8,128)(2,1)S(1)} %get-tuple-element.11.qb_ref, bf16[4,64,1024]{2,1,0:T(8,128)(2,1)S(1)} %bitcast.102, bf16[4,64,1024]{2,1,0:T(8,128)(2,1)S(1)} %bitcast.104, bf16[4,64,1024]{2,1,0:T(8,128)(2,1)S(1)} %bitcast.109, ...), custom_call_target="tpu_custom_call" | custom-call | flops 268435456 | bytes 5242880 | tf_op jit(solution)/shard_map/pallas_call | solution.py:62
  125.9 10.8 %shard_map.83 = bf16[256,1024]{1,0:T(8,128)(2,1)S(1)} custom-call(bf16[256,512]{1,0:T(8,128)(2,1)S(1)} %get-tuple-element.14.qa_ref, bf16[256,512]{1,0:T(8,128)(2,1)S(1)} %get-tuple-element.12.qb_ref, bf16[4,64,1024]{2,1,0:T(8,128)(2,1)S(1)} %bitcast.100, bf16[4,64,1024]{2,1,0:T(8,128)(2,1)S(1)} %bitcast.105, bf16[4,64,1024]{2,1,0:T(8,128)(2,1)S(1)} %bitcast.106, ...), custom_call_target="tpu_custom_call" | custom-call | flops 268435456 | bytes 5242880 | tf_op jit(solution)/shard_map/pallas_call | solution.py:62
  136.9 3.7 %collective-permute-start.10 = (bf16[63,1024]{1,0:T(8,128)(2,1)S(1)}, bf16[63,1024]{1,0:T(8,128)(2,1)S(1)}, u32[]{:S(2)}, u32[]{:S(2)}) collective-permute-start(bf16[63,1024]{1,0:T(8,128)(2,1)S(1)} %fusion.68), channel_id=1, source_target_pairs={{1,8},{9,16},{17,24},{25,32},{33,40},{41,48},{49,56},{57,64},{65,7... | collective-permute-start | bytes 387080 | tf_op jit(solution)/shard_map/ppermute | solution.py:147
  141.0 2.5 %constant_dynamic-update-slice_fusion.4 = bf16[1024,4096]{1,0:T(8,128)(2,1)S(1)} fusion(bf16[1024,4096]{1,0:T(8,128)(2,1)S(1)} %bitcast.123, bf16[512,4096]{1,0:T(8,128)(2,1)} %collective-permute-done.12), kind=kLoop, calls=%fused_computation.89 | loop fusion | bytes 8388608 | tf_op jit(solution)/shard_map/concatenate | solution.py:110
  145.2 2.7 %collective-permute-start.13 = (bf16[128,2048]{1,0:T(8,128)(2,1)S(1)}, bf16[128,2048]{1,0:T(8,128)(2,1)S(1)}, u32[]{:S(2)}, u32[]{:S(2)}) collective-permute-start(bf16[128,2048]{1,0:T(8,128)(2,1)S(1)} %fusion.47), channel_id=1, source_target_pairs={{0,6},{2,0},{4,2},{6,4},{1,7},{3,1},{5,3},{7,5},{8,14},{10,8},{12,... | collective-permute-start | bytes 1572872 | tf_op jit(solution)/shard_map/ppermute | solution.py:25
  148.8 9.9 %collective-permute-done.14 = bf16[128,2048]{1,0:T(8,128)(2,1)S(1)} collective-permute-done((bf16[128,2048]{1,0:T(8,128)(2,1)S(1)}, bf16[128,2048]{1,0:T(8,128)(2,1)S(1)}, u32[]{:S(2)}, u32[]{:S(2)}) %collective-permute-start.14) | collective-permute-done | bytes 524320 | tf_op jit(solution)/shard_map/ppermute | solution.py:25
  158.7 1.5 fusion.41
  160.2 1.5 fusion.53
  161.8 7.9 %collective-permute-done.17 = bf16[128,2048]{1,0:T(8,128)(2,1)S(1)} collective-permute-done((bf16[128,2048]{1,0:T(8,128)(2,1)S(1)}, bf16[128,2048]{1,0:T(8,128)(2,1)S(1)}, u32[]{:S(2)}, u32[]{:S(2)}) %collective-permute-start.17) | collective-permute-done | bytes 524320 | tf_op jit(solution)/shard_map/ppermute | solution.py:25
  169.7 1.5 fusion.35
  171.2 3.4 %collective-permute-start.18 = (bf16[128,2048]{1,0:T(8,128)(2,1)}, bf16[128,2048]{1,0:T(8,128)(2,1)}, u32[]{:S(2)}, u32[]{:S(2)}) collective-permute-start(bf16[128,2048]{1,0:T(8,128)(2,1)} %fusion.35), channel_id=1, source_target_pairs={{0,6},{2,0},{4,2},{6,4},{1,7},{3,1},{5,3},{7,5},{8,14},{10,8},{12,... | collective-permute-start | bytes 1572872 | tf_op jit(solution)/shard_map/ppermute | solution.py:25
  174.6 3.0 %fusion.44 = bf16[128,2048]{1,0:T(8,128)(2,1)S(1)} fusion(bf16[1024,4096]{1,0:T(8,128)(2,1)} %copy-done.2, bf16[128,2048]{1,0:T(8,128)(2,1)S(1)} %collective-permute-done.15, bf16[128,2048]{1,0:T(8,128)(2,1)S(1)} %collective-permute-done.13, s32[]{:T(128)S(6)} %select_n.102, bf16[4,65,1024]{2,1,0:T(8,128)(2,1)S(1)} %slice.93, ...), kind=kOutput, calls=%fused_computation.33 | convolution fusion | flops 538705920 | bytes 6815748 | tf_op jit(solution)/shard_map/dot_general | solution.py:29
  177.6 7.4 %collective-permute-done.16 = bf16[128,2048]{1,0:T(8,128)(2,1)S(1)} collective-permute-done((bf16[128,2048]{1,0:T(8,128)(2,1)}, bf16[128,2048]{1,0:T(8,128)(2,1)S(1)}, u32[]{:S(2)}, u32[]{:S(2)}) %collective-permute-start.16) | collective-permute-done | bytes 524320 | tf_op jit(solution)/shard_map/ppermute | solution.py:25
  185.0 3.1 %fusion.38 = bf16[128,2048]{1,0:T(8,128)(2,1)S(1)} fusion(bf16[1024,4096]{1,0:T(8,128)(2,1)} %copy-done.2, bf16[128,2048]{1,0:T(8,128)(2,1)} %collective-permute-done.18, bf16[128,2048]{1,0:T(8,128)(2,1)S(1)} %collective-permute-done.16, s32[]{:T(128)S(6)} %select_n.102, bf16[4,65,1024]{2,1,0:T(8,128)(2,1)S(1)} %slice.93, ...), kind=kOutput, calls=%fused_computation.31 | convolution fusion | flops 538705920 | bytes 6815748 | tf_op jit(solution)/shard_map/dot_general | solution.py:29
  (83 shorter events, 14.8 us)
Async XLA Ops:
  0.0 13.6 %copy-start.3 = (bf16[896,512]{1,0:T(8,128)(2,1)S(1)}, bf16[896,512]{1,0:T(8,128)(2,1)}, u32[]{:S(2)}) copy-start(bf16[896,512]{1,0:T(8,128)(2,1)} %param.10) | copy-start | bytes 2752516
  2.8 11.8 %copy-start.4 = (bf16[896,512]{1,0:T(8,128)(2,1)S(1)}, bf16[896,512]{1,0:T(8,128)(2,1)}, u32[]{:S(2)}) copy-start(bf16[896,512]{1,0:T(8,128)(2,1)} %param.11) | copy-start | bytes 2752516
  6.0 45.0 %all-to-all-start = ((bf16[16,3,16,896]{3,2,1,0:T(8,128)(2,1)}), bf16[16,3,16,896]{3,2,1,0:T(8,128)(2,1)S(1)}, u32[]{:S(2)}, u32[]{:S(2)}) async-start(bf16[16,3,16,896]{3,2,1,0:T(8,128)(2,1)} %bitcast.4), calls=%async_computation | async-start | bytes 2752512 | tf_op jit(solution)/shard_map/all_to_all | solution.py:93
  15.6 51.6 %collective-permute-start.6 = (bf16[896,1024]{1,0:T(8,128)(2,1)}, bf16[896,1024]{1,0:T(8,128)(2,1)}, u32[]{:S(2)}, u32[]{:S(2)}) collective-permute-start(bf16[896,1024]{1,0:T(8,128)(2,1)} %constant_dynamic-update-slice_fusion.2), channel_id=1, source_target_pairs={{0,1},{1,0},{2,3},{3,2},{4,5},{5,4},{6,7},{7,6},{8,9},{9,8},{10,11... | collective-permute-start | bytes 5505032 | tf_op jit(solution)/shard_map/ppermute | solution.py:25
  17.6 25.1 %collective-permute-start = (bf16[64,4096]{1,0:T(8,128)(2,1)S(1)}, bf16[64,4096]{1,0:T(8,128)(2,1)S(1)}, u32[]{:S(2)}, u32[]{:S(2)}) collective-permute-start(bf16[64,4096]{1,0:T(8,128)(2,1)S(1)} %slice.58), channel_id=1, source_target_pairs={{8,0},{16,8},{24,16},{32,24},{40,32},{48,40},{56,48},{64,56},{72,6... | collective-permute-start | bytes 1572872 | tf_op jit(solution)/shard_map/ppermute | solution.py:85
  18.9 91.5 %collective-permute-start.1 = (bf16[4096,512]{1,0:T(8,128)(2,1)}, bf16[4096,512]{1,0:T(8,128)(2,1)}, u32[]{:S(2)}, u32[]{:S(2)}) collective-permute-start(bf16[4096,512]{1,0:T(8,128)(2,1)} %param.9), channel_id=1, source_target_pairs={{0,1},{1,0},{2,3},{3,2},{4,5},{5,4},{6,7},{7,6},{8,9},{9,8},{10,11... | collective-permute-start | bytes 12582920 | tf_op jit(solution)/shard_map/ppermute | solution.py:25
  19.0 121.9 %collective-permute-start.12 = (bf16[512,4096]{1,0:T(8,128)(2,1)}, bf16[512,4096]{1,0:T(8,128)(2,1)}, u32[]{:S(2)}, u32[]{:S(2)}) collective-permute-start(bf16[512,4096]{1,0:T(8,128)(2,1)} %param.12), channel_id=1, source_target_pairs={{0,1},{1,0},{2,3},{3,2},{4,5},{5,4},{6,7},{7,6},{8,9},{9,8},{10,11... | collective-permute-start | bytes 12582920 | tf_op jit(solution)/shard_map/ppermute | solution.py:25
  28.7 14.0 %copy-start = (bf16[961,4096]{1,0:T(8,128)(2,1)S(1)}, bf16[961,4096]{1,0:T(8,128)(2,1)}, u32[]{:S(2)}) copy-start(bf16[961,4096]{1,0:T(8,128)(2,1)} %slice.57) | copy-start | bytes 23617540
  51.6 7.1 %collective-permute-start.2 = (bf16[16,16,896]{2,1,0:T(8,128)(2,1)S(1)}, bf16[16,16,896]{2,1,0:T(8,128)(2,1)S(1)}, u32[]{:S(2)}, u32[]{:S(2)}) collective-permute-start(bf16[16,16,896]{2,1,0:T(8,128)(2,1)S(1)} %gather_fusion.2), channel_id=1, source_target_pairs={{0,1},{1,0},{2,3},{3,2},{4,5},{5,4},{6,7},{7,6},{8,9},{9,8},{10,11... | collective-permute-start | bytes 1376264 | tf_op jit(solution)/shard_map/ppermute | solution.py:25
  58.8 14.7 %collective-permute-start.3 = (bf16[4,64,896]{2,1,0:T(8,128)(2,1)S(1)}, bf16[4,64,896]{2,1,0:T(8,128)(2,1)S(1)}, u32[]{:S(2)}, u32[]{:S(2)}) collective-permute-start(bf16[4,64,896]{2,1,0:T(8,128)(2,1)S(1)} %bitcast.129), channel_id=1, source_target_pairs={{0,2},{2,4},{4,6},{6,0},{1,3},{3,5},{5,7},{7,1},{8,10},{10,12},{12... | collective-permute-start | bytes 1376264 | tf_op jit(solution)/shard_map/ppermute | solution.py:25
  60.5 15.2 %collective-permute-start.4 = (bf16[4,64,896]{2,1,0:T(8,128)(2,1)S(1)}, bf16[4,64,896]{2,1,0:T(8,128)(2,1)S(1)}, u32[]{:S(2)}, u32[]{:S(2)}) collective-permute-start(bf16[4,64,896]{2,1,0:T(8,128)(2,1)S(1)} %bitcast.130), channel_id=1, source_target_pairs={{0,6},{2,0},{4,2},{6,4},{1,7},{3,1},{5,3},{7,5},{8,14},{10,8},{12,... | collective-permute-start | bytes 1376264 | tf_op jit(solution)/shard_map/ppermute | solution.py:25
  67.2 15.3 %collective-permute-start.8 = (bf16[4,64,896]{2,1,0:T(8,128)(2,1)S(1)}, bf16[4,64,896]{2,1,0:T(8,128)(2,1)S(1)}, u32[]{:S(2)}, u32[]{:S(2)}) collective-permute-start(bf16[4,64,896]{2,1,0:T(8,128)(2,1)S(1)} %bitcast.126), channel_id=1, source_target_pairs={{0,6},{2,0},{4,2},{6,4},{1,7},{3,1},{5,3},{7,5},{8,14},{10,8},{12,... | collective-permute-start | bytes 1376264 | tf_op jit(solution)/shard_map/ppermute | solution.py:25
  73.5 14.6 %collective-permute-start.7 = (bf16[4,64,896]{2,1,0:T(8,128)(2,1)S(1)}, bf16[4,64,896]{2,1,0:T(8,128)(2,1)S(1)}, u32[]{:S(2)}, u32[]{:S(2)}) collective-permute-start(bf16[4,64,896]{2,1,0:T(8,128)(2,1)S(1)} %bitcast.128), channel_id=1, source_target_pairs={{0,2},{2,4},{4,6},{6,0},{1,3},{3,5},{5,7},{7,1},{8,10},{10,12},{12... | collective-permute-start | bytes 1376264 | tf_op jit(solution)/shard_map/ppermute | solution.py:25
  75.7 25.7 %collective-permute-start.5 = (bf16[4,64,896]{2,1,0:T(8,128)(2,1)S(1)}, bf16[4,64,896]{2,1,0:T(8,128)(2,1)S(1)}, u32[]{:S(2)}, u32[]{:S(2)}) collective-permute-start(bf16[4,64,896]{2,1,0:T(8,128)(2,1)S(1)} %collective-permute-done.3), channel_id=1, source_target_pairs={{0,2},{2,4},{4,6},{6,0},{1,3},{3,5},{5,7},{7,1},{8,10},{10,12},{12... | collective-permute-start | bytes 1376264 | tf_op jit(solution)/shard_map/ppermute | solution.py:25
  82.5 21.1 %collective-permute-start.9 = (bf16[4,64,896]{2,1,0:T(8,128)(2,1)S(1)}, bf16[4,64,896]{2,1,0:T(8,128)(2,1)S(1)}, u32[]{:S(2)}, u32[]{:S(2)}) collective-permute-start(bf16[4,64,896]{2,1,0:T(8,128)(2,1)S(1)} %collective-permute-done.8), channel_id=1, source_target_pairs={{0,6},{2,0},{4,2},{6,4},{1,7},{3,1},{5,3},{7,5},{8,14},{10,8},{12,... | collective-permute-start | bytes 1376264 | tf_op jit(solution)/shard_map/ppermute | solution.py:25
  103.6 6.8 %copy-start.1 = (bf16[512,4096]{1,0:T(8,128)(2,1)S(1)}, bf16[512,4096]{1,0:T(8,128)(2,1)}, u32[]{:S(2)}) copy-start(bf16[512,4096]{1,0:T(8,128)(2,1)} %fusion) | copy-start | bytes 12582916
  115.0 26.0 %slice-start = ((s8[8388608]{0:T(1024)(128)(4,1)}), s8[4194304]{0:T(1024)(128)(4,1)S(1)}, s32[]{:S(2)}) async-start(s8[8388608]{0:T(1024)(128)(4,1)} %bitcast.122), calls=%async_computation.1 | async-start | bytes 8388608
  125.8 15.1 %slice-start.1 = ((s8[8388608]{0:T(1024)(128)(4,1)}), s8[4194304]{0:T(1024)(128)(4,1)S(1)}, s32[]{:S(2)}) async-start(s8[8388608]{0:T(1024)(128)(4,1)} %bitcast.122), calls=%async_computation.2 | async-start | bytes 8388608
  136.9 6.7 %collective-permute-start.10 = (bf16[63,1024]{1,0:T(8,128)(2,1)S(1)}, bf16[63,1024]{1,0:T(8,128)(2,1)S(1)}, u32[]{:S(2)}, u32[]{:S(2)}) collective-permute-start(bf16[63,1024]{1,0:T(8,128)(2,1)S(1)} %fusion.68), channel_id=1, source_target_pairs={{1,8},{9,16},{17,24},{25,32},{33,40},{41,48},{49,56},{57,64},{65,7... | collective-permute-start | bytes 387080 | tf_op jit(solution)/shard_map/ppermute | solution.py:147
  140.6 2.9 %collective-permute-start.11 = (bf16[4,63,1024]{2,1,0:T(8,128)(2,1)S(1)}, bf16[4,63,1024]{2,1,0:T(8,128)(2,1)S(1)}, u32[]{:S(2)}, u32[]{:S(2)}) collective-permute-start(bf16[4,63,1024]{2,1,0:T(8,128)(2,1)S(1)} %pad_maximum_fusion.3), channel_id=1, source_target_pairs={{0,1},{1,0},{2,3},{3,2},{4,5},{5,4},{6,7},{7,6},{8,9},{9,8},{10,11... | collective-permute-start | bytes 1548296 | tf_op jit(solution)/shard_map/ppermute | solution.py:25
  143.5 26.2 %copy-start.2 = (bf16[1024,4096]{1,0:T(8,128)(2,1)}, bf16[1024,4096]{1,0:T(8,128)(2,1)S(1)}, u32[]{:S(2)}) copy-start(bf16[1024,4096]{1,0:T(8,128)(2,1)S(1)} %constant_dynamic-update-slice_fusion.4) | copy-start | bytes 25165828
  144.4 14.3 %collective-permute-start.14 = (bf16[128,2048]{1,0:T(8,128)(2,1)S(1)}, bf16[128,2048]{1,0:T(8,128)(2,1)S(1)}, u32[]{:S(2)}, u32[]{:S(2)}) collective-permute-start(bf16[128,2048]{1,0:T(8,128)(2,1)S(1)} %fusion.50), channel_id=1, source_target_pairs={{0,2},{2,4},{4,6},{6,0},{1,3},{3,5},{5,7},{7,1},{8,10},{10,12},{12... | collective-permute-start | bytes 1572872 | tf_op jit(solution)/shard_map/ppermute | solution.py:25
  145.2 29.4 %collective-permute-start.13 = (bf16[128,2048]{1,0:T(8,128)(2,1)S(1)}, bf16[128,2048]{1,0:T(8,128)(2,1)S(1)}, u32[]{:S(2)}, u32[]{:S(2)}) collective-permute-start(bf16[128,2048]{1,0:T(8,128)(2,1)S(1)} %fusion.47), channel_id=1, source_target_pairs={{0,6},{2,0},{4,2},{6,4},{1,7},{3,1},{5,3},{7,5},{8,14},{10,8},{12,... | collective-permute-start | bytes 1572872 | tf_op jit(solution)/shard_map/ppermute | solution.py:25
  148.7 21.0 %collective-permute-start.17 = (bf16[128,2048]{1,0:T(8,128)(2,1)S(1)}, bf16[128,2048]{1,0:T(8,128)(2,1)S(1)}, u32[]{:S(2)}, u32[]{:S(2)}) collective-permute-start(bf16[128,2048]{1,0:T(8,128)(2,1)S(1)} %fusion.56), channel_id=1, source_target_pairs={{0,6},{2,0},{4,2},{6,4},{1,7},{3,1},{5,3},{7,5},{8,14},{10,8},{12,... | collective-permute-start | bytes 1572872 | tf_op jit(solution)/shard_map/ppermute | solution.py:25
  160.2 14.4 %collective-permute-start.15 = (bf16[128,2048]{1,0:T(8,128)(2,1)}, bf16[128,2048]{1,0:T(8,128)(2,1)S(1)}, u32[]{:S(2)}, u32[]{:S(2)}) collective-permute-start(bf16[128,2048]{1,0:T(8,128)(2,1)} %fusion.41), channel_id=1, source_target_pairs={{0,2},{2,4},{4,6},{6,0},{1,3},{3,5},{5,7},{7,1},{8,10},{10,12},{12... | collective-permute-start | bytes 1572872 | tf_op jit(solution)/shard_map/ppermute | solution.py:25
  161.8 23.2 %collective-permute-start.16 = (bf16[128,2048]{1,0:T(8,128)(2,1)}, bf16[128,2048]{1,0:T(8,128)(2,1)S(1)}, u32[]{:S(2)}, u32[]{:S(2)}) collective-permute-start(bf16[128,2048]{1,0:T(8,128)(2,1)} %fusion.53), channel_id=1, source_target_pairs={{0,2},{2,4},{4,6},{6,0},{1,3},{3,5},{5,7},{7,1},{8,10},{10,12},{12... | collective-permute-start | bytes 1572872 | tf_op jit(solution)/shard_map/ppermute | solution.py:25
  171.2 13.8 %collective-permute-start.18 = (bf16[128,2048]{1,0:T(8,128)(2,1)}, bf16[128,2048]{1,0:T(8,128)(2,1)}, u32[]{:S(2)}, u32[]{:S(2)}) collective-permute-start(bf16[128,2048]{1,0:T(8,128)(2,1)} %fusion.35), channel_id=1, source_target_pairs={{0,6},{2,0},{4,2},{6,4},{1,7},{3,1},{5,3},{7,5},{8,14},{10,8},{12,... | collective-permute-start | bytes 1572872 | tf_op jit(solution)/shard_map/ppermute | solution.py:25

commit v2 on v1

v2 whole, which is shorter than its diff:
```python
import math

import jax
import jax.numpy as jnp
from jax import lax
from jax.experimental import pallas as pl
from jax.experimental.pallas import tpu as pltpu
from jax.sharding import Mesh, PartitionSpec as P

HS = 128
CL = 64
NB_LEN = 128
NEIGH = 2
N_Z = 4
N_CORE = 2
BLOCK = 128
F32 = jnp.float32
BF16 = jnp.bfloat16


def step(value, axis, steps):
    count = lax.axis_size(axis)
    return lax.ppermute(value, axis, [(i, (i + steps) % count) for i in range(count)])


def dot(a, b):
    return jnp.dot(a, b, preferred_element_type=F32)


def bucket_places(shards):
    count = shards.shape[1]
    same_shard = shards[:, :, None] == shards[:, None, :]
    earlier = jnp.arange(count)[None, :] < jnp.arange(count)[:, None]
    return jnp.sum((same_shard & earlier[None]).astype(jnp.int32), axis=2)


def attend_kernel(q_ref, *refs):
    parts_a, parts_b, out_ref = refs[0:4], refs[4:8], refs[8]
    half = q_ref.shape[1] // 2
    scores = []
    for side, parts in enumerate((parts_a, parts_b)):
        for lower in range(0, half, HS):
            q = q_ref[:, side * half + lower : side * half + lower + HS]
            k = jnp.concatenate([part[:, lower : lower + HS] for part in parts], axis=0)
            scores.append(lax.dot_general(q, k, (((1,), (1,)), ((), ())), preferred_element_type=F32))
    probs = []
    for score in scores:
        score = score * (1.0 / math.sqrt(HS))
        weights = jnp.exp(score - jnp.max(score, axis=-1, keepdims=True))
        total = jnp.sum(weights, axis=-1, keepdims=True)
        probs.append((weights * (1.0 / total)).astype(BF16))
    for side, parts in enumerate((parts_a, parts_b)):
        for lower in range(0, half, HS):
            v = jnp.concatenate([part[:, half + lower : half + lower + HS] for part in parts], axis=0)
            out_ref[:, side * half + lower : side * half + lower + HS] = dot(
                probs[(side * half + lower) // HS], v
            ).astype(BF16)


def attend(queries, parts_a, parts_b, parity):
    tokens, width = queries.shape
    spans = tokens // CL
    q_spec = pl.BlockSpec((CL, width), lambda i: (i, 0))
    part_spec = pl.BlockSpec((parts_a[0].shape[0] // (2 * spans), width), lambda i: (2 * i + parity, 0))
    return pl.pallas_call(
        attend_kernel,
        grid=(spans,),
        in_specs=[q_spec] + [part_spec] * 8,
        out_specs=q_spec,
        out_shape=jax.ShapeDtypeStruct((tokens, width), BF16),
        cost_estimate=pl.CostEstimate(
            flops=4 * tokens * 256 * width, bytes_accessed=tokens * 20 * width, transcendentals=tokens * 2048
        ),
        compiler_params=pltpu.CompilerParams(vmem_limit_bytes=32 * 1024 * 1024),
    )(queries, *parts_a, *parts_b)


def project_kernel(low_ref, high_ref, wa_ref, wb_ref, out_a_ref, out_b_ref):
    rows = jnp.concatenate([low_ref[...], high_ref[...]], axis=0)
    out_a_ref[...] = dot(rows, wa_ref[...]).astype(BF16)
    out_b_ref[...] = dot(rows, wb_ref[...]).astype(BF16)


def project(low, high, weight_a, weight_b):
    rows, enc = low.shape
    width = weight_a.shape[1]
    tile = width // 2
    row_spec = pl.BlockSpec((rows, enc), lambda i: (0, 0))
    weight_spec = pl.BlockSpec((enc, tile), lambda i: (0, i))
    out_spec = pl.BlockSpec((2 * rows, tile), lambda i: (0, i))
    out = jax.ShapeDtypeStruct((2 * rows, width), BF16)
    return pl.pallas_call(
        project_kernel,
        grid=(width // tile,),
        in_specs=[row_spec, row_spec, weight_spec, weight_spec],
        out_specs=[out_spec, out_spec],
        out_shape=[out, out],
        cost_estimate=pl.CostEstimate(
            flops=8 * rows * enc * width, bytes_accessed=4 * (rows + width) * enc + 8 * rows * width, transcendentals=0
        ),
        compiler_params=pltpu.CompilerParams(vmem_limit_bytes=32 * 1024 * 1024),
    )(low, high, weight_a, weight_b)


def swap_halves(value):
    half = value.shape[-1] // 2
    return jnp.concatenate([value[..., half:], value[..., :half]], axis=-1)


def body(decoder, w_query, w_key, w_value, w_out, database, nb_shard, nb_slot):
    n_seq = lax.axis_size("seq")
    seq_index, z_index, core = lax.axis_index("seq"), lax.axis_index("z"), lax.axis_index("core")
    tok_rows, model = decoder.shape
    half = w_query.shape[1]
    requests = NEIGH * (tok_rows // CL)
    capacity = (requests + n_seq - 1) // n_seq + 1
    enc = database.shape[2]
    piece = NB_LEN // (N_Z * N_CORE)

    shard_lists = nb_shard.reshape(n_seq, requests)
    slot_lists = nb_slot.reshape(n_seq, requests)
    places = bucket_places(shard_lists)
    picked = (shard_lists == seq_index)[:, None, :] & (places[:, None, :] == jnp.arange(capacity)[None, :, None])
    send_slot = jnp.sum(jnp.where(picked, slot_lists[:, None, :], 0), axis=2)
    my_piece = lax.dynamic_slice_in_dim(database, (z_index * N_CORE + core) * piece, piece, axis=1)
    received = lax.all_to_all(my_piece[send_slot], "seq", split_axis=0, concat_axis=0, tiled=True)
    received = received.reshape(n_seq * capacity, piece, enc)
    my_shards = lax.dynamic_index_in_dim(shard_lists, seq_index, 0, keepdims=False)
    my_places = lax.dynamic_index_in_dim(places, seq_index, 0, keepdims=False)
    row_index = (my_shards * capacity + my_places).reshape(N_Z, N_CORE, -1)
    mine = lax.dynamic_index_in_dim(row_index, core, 1, keepdims=False).reshape(-1)
    theirs = lax.dynamic_index_in_dim(row_index, 1 - core, 1, keepdims=False).reshape(-1)
    swapped = step(received[theirs], "core", 1)
    own = jnp.concatenate([received[mine], swapped], axis=1)
    spans = requests // NEIGH // N_CORE
    own = own.reshape(spans * NEIGH * 2 * piece, enc)
    low, high = own[: own.shape[0] // 2], own[own.shape[0] // 2 :]

    w_kv = jnp.concatenate([w_key, w_value], axis=1)
    w_query_other = step(w_query, "core", 1)
    w_kv_other = step(w_kv, "core", 1)
    w_out_other = step(w_out, "core", 1)
    w_out_chip = jnp.concatenate([w_out, w_out_other], axis=0)

    tokens = decoder.reshape(N_Z, N_CORE, BLOCK, model)
    tokens = lax.dynamic_index_in_dim(tokens, core, 1, keepdims=False).reshape(N_Z * BLOCK, model)
    source = tokens.astype(F32)
    scale = lax.rsqrt(jnp.mean(source * source, axis=-1, keepdims=True) + 1e-05)
    normed = (source * scale).astype(BF16)
    queries = jnp.concatenate([dot(normed, w_query).astype(BF16), dot(normed, w_query_other).astype(BF16)], axis=1)
    queries = jnp.roll(queries.reshape(N_Z, BLOCK, 2 * half), 1, axis=1)
    ahead, first_queries = queries[:, :CL], queries[:, CL:]
    is_first_row = lax.broadcasted_iota(jnp.int32, (1, CL, 1), 1) == 0
    leaving = swap_halves(ahead)
    arrived = step(leaving, "core", 1)
    crossing = lax.ppermute(leaving[0], ("seq", "core"), [(2 * i + 2, 2 * i + 1) for i in range(n_seq - 1)])
    arrived = jnp.where(core == 0, arrived, jnp.concatenate([arrived[1:], crossing[None]], axis=0))
    second_queries = jnp.where(is_first_row, ahead, arrived)

    up_low = step(low, "z", 1)
    down_high = step(high, "z", -1)
    up_high = step(high, "z", 1)
    down_low = step(low, "z", -1)
    far_low = step(up_low, "z", 1)
    far_high = step(down_high, "z", -1)
    pairs = [
        project(part_low, part_high, w_kv, w_kv_other)
        for part_low, part_high in ((low, high), (up_low, up_high), (down_low, down_high), (far_low, far_high))
    ]
    parts_a, parts_b = [pair[0] for pair in pairs], [pair[1] for pair in pairs]

    second = attend(second_queries.reshape(N_Z * CL, 2 * half), parts_a, parts_b, 1)
    second = second.reshape(N_Z, CL, 2 * half)
    leaving = swap_halves(second)
    arrived = step(leaving, "core", 1)
    crossing = lax.ppermute(leaving[N_Z - 1], ("seq", "core"), [(2 * i + 1, 2 * i + 2) for i in range(n_seq - 1)])
    arrived = jnp.where(core == 0, jnp.concatenate([crossing[None], arrived[:-1]], axis=0), arrived)
    first = attend(first_queries.reshape(N_Z * CL, 2 * half), parts_a, parts_b, 0)
    first = first.reshape(N_Z, CL, 2 * half)
    context = jnp.concatenate([jnp.where(is_first_row, second, arrived), first], axis=1)

    def block(distance):
        return lax.dynamic_index_in_dim(context, (z_index + distance) % N_Z, 0, keepdims=False)

    side = model // 2
    w_left, w_right = w_out_chip[:, :side], w_out_chip[:, side:]
    far = block(2)
    up_far = step(dot(far, w_left).astype(BF16), "z", 1)
    down_far = step(dot(far, w_right).astype(BF16), "z", -1)
    above, below, here = block(1), block(3), block(0)
    up_right = step(dot(above, w_right).astype(BF16), "z", 1)
    down_left = step(dot(below, w_left).astype(BF16), "z", -1)
    up_left = step((dot(above, w_left) + up_far.astype(F32)).astype(BF16), "z", 1)
    down_right = step((dot(below, w_right) + down_far.astype(F32)).astype(BF16), "z", -1)
    left = dot(here, w_left) + down_left.astype(F32) + up_left.astype(F32)
    right = dot(here, w_right) + up_right.astype(F32) + down_right.astype(F32)
    return jnp.roll(jnp.concatenate([left.astype(BF16), right.astype(BF16)], axis=1), -1, axis=0)


def solution(mesh):
    n_seq = mesh.devices.shape[0]
    fine = Mesh(mesh.devices.reshape(n_seq, N_Z, N_CORE), ("seq", "z", "core"))
    db = ("z", "core")
    return jax.shard_map(
        body,
        mesh=fine,
        in_specs=(
            P("seq", None),
            P(None, db),
            P(None, db),
            P(None, db),
            P(db, None),
            P("seq", None, None),
            P(),
            P(),
        ),
        out_specs=P(("seq", "z", "core"), None),
        check_vma=False,
    )
```

time: 192 us -> 167 us (0.87)
  matrix products: 58.7 us -> 24.7 us
  other arithmetic: 10.2 us -> 15.5 us
  starting transfers between devices: 30.9 us -> 34.4 us
  local copies, waits for them, and re-layouts: 26.6 us -> 29 us
    dot_general x26 -> x10, matrix products: 58.7 us -> 24.7 us  [dot(): return jnp.dot(a, b, preferred_element_type=F32)]
    ppermute x2, waiting for transfers between devices: 9.04 us -> 0.72 us  [the longest x1 0.72 us: body(): lax.ppermute(leaving[0], ('seq', 'core'), [(2 * i + 2, 2 * i + 1) for i i...]
    slice x8 -> x6, local copies, waits for them, and re-layouts: 10.2 us -> 1.95 us  [the longest x1 0.86 us: body(): low, high = (own[:own.shape[0] // 2], own[own.shape[0] // 2:])]
    unnamed x19 -> x37, local copies, waits for them, and re-layouts: 7.77 us -> 13.5 us
    all_to_all x1, waiting for transfers between devices: 0.01 us -> 4.48 us  [body(): lax.all_to_all(my_piece[send_slot], 'seq', split_axis=0, concat_axis=0, t...]
    ppermute x17 -> x18, starting transfers between devices: 18.4 us -> 21.8 us  [step(): lax.ppermute(value, axis, [(i, (i + steps) % count) for i in range(count)])]
    ppermute x17 -> x18, waiting for transfers between devices: 31.4 us -> 34.6 us  [step(): lax.ppermute(value, axis, [(i, (i + steps) % count) for i in range(count)])]
    reshape x0 -> x1, local copies, waits for them, and re-layouts: none -> 2.26 us  [body(): queries = jnp.roll(queries.reshape(N_Z, BLOCK, 2 * half), 1, axis=1)]
  transfers between devices with their start and end apart: 20 -> 21, of which waited for: 6 -> 6; matrix products, arithmetic and copies ran while one was open for 45% -> 32% of each run, Pallas kernels for 11% -> 13%
where the time goes in v2:
time: 167 us; the launch traced here: 166 us
  waiting for transfers between devices  39.8 us (24%)
  starting transfers between devices  34.4 us (21%)
  local copies, waits for them, and re-layouts  29 us (17%)
  matrix products  24.7 us (15%)
  Pallas kernels  21.6 us (13%)
  other arithmetic  15.5 us (9%)
    ppermute x18, waiting for transfers between devices, step(): lax.ppermute(value, axis, [(i, (i + steps) % count) for i in range(count)])  34.6 us
    dot_general x10, matrix products, dot(): return jnp.dot(a, b, preferred_element_type=F32)  24.7 us
    ppermute x18, starting transfers between devices, step(): lax.ppermute(value, axis, [(i, (i + steps) % count) for i in range(count)])  21.8 us
    pallas_call x4, Pallas kernels, project(): pl.pallas_call(project_kernel, grid=(width // tile,), in_specs=[row_spec,...  16.5 us
    unnamed x37, local copies, waits for them, and re-layouts  13.5 us
    all_to_all x1, starting transfers between devices, body(): lax.all_to_all(my_piece[send_slot], 'seq', split_axis=0, concat_axis=0, t...  7.59 us
    pallas_call x2, Pallas kernels, attend(): pl.pallas_call(attend_kernel, grid=(spans,), in_specs=[q_spec] + [part_sp...  5.12 us
    all_to_all x1, waiting for transfers between devices, body(): lax.all_to_all(my_piece[send_slot], 'seq', split_axis=0, concat_axis=0, t...  4.48 us
  transfers between devices with their start and end apart: 21, of which 6 were waited for; matrix products, arithmetic and copies ran while one was open for 32% of the time, Pallas kernels for 13%

profile of v2, /device:TPU:1, one launch (start us, length us, event | category | flops | bytes accessed | tf_op | source)
XLA Modules:
  0.0 165.7 jit_solution(6832353660237033009)
XLA Ops:
  2.7 1.2 constant_dynamic-slice_fusion.4
  3.9 1.9 %gather_fusion = bf16[48,16,896]{2,1,0:T(8,128)(2,1)} fusion(bf16[24,16,896]{2,1,0:T(8,128)(2,1)S(1)} %constant_dynamic-slice_fusion.4, s32[1024]{0:T(1024)S(1)} %pad_clamp_fusion.2), kind=kCustom, calls=%fused_computation | custom fusion | bytes 2752704 | tf_op jit(solution)/shard_map/gather | solution.py:126
  5.7 7.6 %all-to-all-start = ((bf16[16,3,16,896]{3,2,1,0:T(8,128)(2,1)}), bf16[16,3,16,896]{3,2,1,0:T(8,128)(2,1)S(1)}, u32[]{:S(2)}, u32[]{:S(2)}) async-start(bf16[16,3,16,896]{3,2,1,0:T(8,128)(2,1)} %bitcast.7), calls=%async_computation | async-start | bytes 2752512 | tf_op jit(solution)/shard_map/all_to_all | solution.py:126
  13.3 1.3 constant_dynamic-update-slice_fusion.3
  14.6 1.3 constant_dynamic-update-slice_fusion.2.wa_ref
  16.0 1.0 collective-permute-start.4
  17.5 3.3 %dynamic-slice_convert_fusion = f32[4,1,128,4096]{3,2,1,0:T(8,128)S(1)} fusion(bf16[4,2,128,4096]{3,2,1,0:T(8,128)(2,1)} %bitcast.71, s32[]{:T(128)S(6)} %select_n.102), kind=kLoop, calls=%fused_computation.6 | loop fusion | flops 2097152 | bytes 12582916 | tf_op jit(solution)/shard_map/convert_element_type | solution.py:147
  20.8 3.1 %multiply_reduce_fusion = f32[4,128]{1,0:T(4,128)S(1)} fusion(bf16[4,2,128,4096]{3,2,1,0:T(8,128)(2,1)} %bitcast.72, s32[]{:T(128)S(6)} %select_n.102), kind=kLoop, calls=%fused_computation.5 | loop fusion | flops 6290944 | bytes 4196356 | tf_op jit(solution)/shard_map/reduce_sum | solution.py:148
  23.9 3.3 %fusion = bf16[512,4096]{1,0:T(8,128)(2,1)} fusion(f32[4,1,128,4096]{3,2,1,0:T(8,128)S(1)} %dynamic-slice_convert_fusion, f32[512]{0:T(512)S(1)} %rsqrt_bitcast_fusion), kind=kLoop, calls=%fused_computation.4 | loop fusion | flops 4194304 | bytes 12584960 | tf_op jit(solution)/shard_map/convert_element_type | solution.py:149
  27.6 4.5 %all-to-all-done = bf16[16,3,16,896]{3,2,1,0:T(8,128)(2,1)S(1)} async-done(((bf16[16,3,16,896]{3,2,1,0:T(8,128)(2,1)}), bf16[16,3,16,896]{3,2,1,0:T(8,128)(2,1)S(1)}, u32[]{:S(2)}, u32[]{:S(2)}) %all-to-all-start) | async-done | bytes 1376288 | tf_op jit(solution)/shard_map/all_to_all | solution.py:126
  32.0 1.4 gather_fusion.2
  33.4 3.8 %collective-permute-start.3 = (bf16[16,16,896]{2,1,0:T(8,128)(2,1)}, bf16[16,16,896]{2,1,0:T(8,128)(2,1)}, u32[]{:S(2)}, u32[]{:S(2)}) collective-permute-start(bf16[16,16,896]{2,1,0:T(8,128)(2,1)} %gather_fusion.2), channel_id=1, source_target_pairs={{0,1},{1,0},{2,3},{3,2},{4,5},{5,4},{6,7},{7,6},{8,9},{9,8},{10,11... | collective-permute-start | bytes 1376264 | tf_op jit(solution)/shard_map/ppermute | solution.py:23
  37.2 6.6 %convolution_convert_fusion.1 = bf16[512,512]{0,1:T(8,128)(2,1)} fusion(bf16[512,4096]{1,0:T(8,128)(2,1)} %fusion, bf16[4096,512]{1,0:T(8,128)(2,1)} %param.9), kind=kOutput, calls=%fused_computation.48 | convolution fusion | flops 2147745792 | bytes 8912896 | tf_op jit(solution)/shard_map/dot_general | solution.py:27
  43.8 1.4 gather_fusion.1
  45.2 1.1 constant_dynamic-update-slice_fusion.1
  46.3 1.1 constant_dynamic-update-slice_fusion
  48.2 3.8 %collective-permute-start.8 = (bf16[256,896]{1,0:T(8,128)(2,1)S(1)}, bf16[256,896]{1,0:T(8,128)(2,1)}, u32[]{:S(2)}, u32[]{:S(2)}) collective-permute-start(bf16[256,896]{1,0:T(8,128)(2,1)S(1)} %bitcast.63), channel_id=1, source_target_pairs={{0,6},{2,0},{4,2},{6,4},{1,7},{3,1},{5,3},{7,5},{8,14},{10,8},{12,... | collective-permute-start | bytes 1376264 | tf_op jit(solution)/shard_map/ppermute | solution.py:23
  52.0 4.6 %constant_dynamic-update-slice_fusion.5 = bf16[1024,4096]{1,0:T(8,128)(2,1)} fusion(bf16[512,4096]{1,0:T(8,128)(2,1)} %param.12), kind=kLoop, calls=%fused_computation.87 | loop fusion | bytes 8388608
  56.7 1.5 copy-done.5
  58.2 4.2 %shard_map.82 = (bf16[512,1024]{1,0:T(8,128)(2,1)S(1)}, bf16[512,1024]{1,0:T(8,128)(2,1)S(1)}) custom-call(bf16[256,896]{1,0:T(8,128)(2,1)} %bitcast.11.low_ref, bf16[256,896]{1,0:T(8,128)(2,1)S(1)} %bitcast.65, bf16[896,1024]{1,0:T(8,128)(2,1)S(1)} %copy-done.5, bf16[896,1024]{1,0:T(8,128)(2,1)} %collective-permute-done.4.wb_ref), custom_call_target="tpu_custom_call" | custom-call | flops 1879048192 | bytes 6684672 | tf_op jit(solution)/shard_map/pallas_call | solution.py:92
  62.3 3.1 %collective-permute-start.7 = (bf16[256,896]{1,0:T(8,128)(2,1)}, bf16[256,896]{1,0:T(8,128)(2,1)}, u32[]{:S(2)}, u32[]{:S(2)}) collective-permute-start(bf16[256,896]{1,0:T(8,128)(2,1)} %bitcast.11.low_ref), channel_id=1, source_target_pairs={{0,6},{2,0},{4,2},{6,4},{1,7},{3,1},{5,3},{7,5},{8,14},{10,8},{12,... | collective-permute-start | bytes 1376264 | tf_op jit(solution)/shard_map/ppermute | solution.py:23
  65.5 9.5 %collective-permute-done.5.low_ref = bf16[256,896]{1,0:T(8,128)(2,1)} collective-permute-done((bf16[256,896]{1,0:T(8,128)(2,1)}, bf16[256,896]{1,0:T(8,128)(2,1)}, u32[]{:S(2)}, u32[]{:S(2)}) %collective-permute-start.5) | collective-permute-done | bytes 458784 | tf_op jit(solution)/shard_map/ppermute | solution.py:23
  75.8 1.5 collective-permute-start.9
  78.3 4.0 %shard_map.83 = (bf16[512,1024]{1,0:T(8,128)(2,1)S(1)}, bf16[512,1024]{1,0:T(8,128)(2,1)S(1)}) custom-call(bf16[256,896]{1,0:T(8,128)(2,1)} %collective-permute-done.5.low_ref, bf16[256,896]{1,0:T(8,128)(2,1)S(1)} %copy-done.9, bf16[896,1024]{1,0:T(8,128)(2,1)S(1)} %copy-done.5, bf16[896,1024]{1,0:T(8,128)(2,1)} %collective-permute-done.4.wb_ref), custom_call_target="tpu_custom_call" | custom-call | flops 1879048192 | bytes 6684672 | tf_op jit(solution)/shard_map/pallas_call | solution.py:92
  82.4 5.0 %convolution_convert_fusion = bf16[512,512]{0,1:T(8,128)(2,1)S(1)} fusion(bf16[512,4096]{1,0:T(8,128)(2,1)S(1)} %copy-done.11, bf16[4096,512]{1,0:T(8,128)(2,1)} %collective-permute-done), kind=kOutput, calls=%fused_computation.47 | convolution fusion | flops 2147745792 | bytes 8912896 | tf_op jit(solution)/shard_map/dot_general | solution.py:27
  87.4 1.0 pad_maximum_fusion.1
  88.4 2.3 %copy.25 = bf16[512,1024]{1,0:T(8,128)(2,1)} copy(bf16[512,1024]{0,1:T(8,128)(2,1)} %pad_maximum_fusion.1) | data formatting | bytes 2097152 | tf_op jit(solution)/shard_map/reshape | solution.py:151
  92.6 1.2 fusion.62
  93.8 1.7 %collective-permute-start.1 = (bf16[4,64,1024]{2,1,0:T(8,128)(2,1)S(1)}, bf16[4,64,1024]{2,1,0:T(8,128)(2,1)S(1)}, u32[]{:S(2)}, u32[]{:S(2)}) collective-permute-start(bf16[4,64,1024]{2,1,0:T(8,128)(2,1)S(1)} %fusion.62), channel_id=1, source_target_pairs={{0,1},{1,0},{2,3},{3,2},{4,5},{5,4},{6,7},{7,6},{8,9},{9,8},{10,11... | collective-permute-start | bytes 1572872 | tf_op jit(solution)/shard_map/ppermute | solution.py:23
  95.5 1.5 copy-done.6
  97.0 4.2 %shard_map.84 = (bf16[512,1024]{1,0:T(8,128)(2,1)S(1)}, bf16[512,1024]{1,0:T(8,128)(2,1)S(1)}) custom-call(bf16[256,896]{1,0:T(8,128)(2,1)} %collective-permute-done.7.low_ref, bf16[256,896]{1,0:T(8,128)(2,1)} %collective-permute-done.8.high_ref, bf16[896,1024]{1,0:T(8,128)(2,1)S(1)} %copy-done.6, bf16[896,1024]{1,0:T(8,128)(2,1)} %collective-permute-done.4.wb_ref), custom_call_target="tpu_custom_call" | custom-call | flops 1879048192 | bytes 6684672 | tf_op jit(solution)/shard_map/pallas_call | solution.py:92
  101.2 1.4 collective-permute-start.2
  102.7 4.2 %shard_map.85 = (bf16[512,1024]{1,0:T(8,128)(2,1)S(1)}, bf16[512,1024]{1,0:T(8,128)(2,1)S(1)}) custom-call(bf16[256,896]{1,0:T(8,128)(2,1)} %collective-permute-done.9.low_ref, bf16[256,896]{1,0:T(8,128)(2,1)} %collective-permute-done.10.high_ref, bf16[896,1024]{1,0:T(8,128)(2,1)S(1)} %copy-done.7, bf16[896,1024]{1,0:T(8,128)(2,1)} %collective-permute-done.4.wb_ref), custom_call_target="tpu_custom_call" | custom-call | flops 1879048192 | bytes 6684672 | tf_op jit(solution)/shard_map/pallas_call | solution.py:92
  108.0 2.6 %shard_map.86 = bf16[256,1024]{1,0:T(8,128)(2,1)S(1)} custom-call(bf16[256,1024]{1,0:T(8,128)(2,1)S(1)} %bitcast.53, bf16[512,1024]{1,0:T(8,128)(2,1)S(1)} %get-tuple-element.13.refs_0_, bf16[512,1024]{1,0:T(8,128)(2,1)S(1)} %get-tuple-element.14.refs_1_, bf16[512,1024]{1,0:T(8,128)(2,1)S(1)} %get-tuple-element.15.refs_2_, ...), custom_call_target="tpu_custom_call" | custom-call | flops 268435456 | bytes 5242880 | tf_op jit(solution)/shard_map/pallas_call | solution.py:65
  110.7 3.6 %collective-permute-start.11 = (bf16[64,1024]{1,0:T(8,128)(2,1)S(1)}, bf16[64,1024]{1,0:T(8,128)(2,1)S(1)}, u32[]{:S(2)}, u32[]{:S(2)}) collective-permute-start(bf16[64,1024]{1,0:T(8,128)(2,1)S(1)} %fusion.74), channel_id=1, source_target_pairs={{1,8},{9,16},{17,24},{25,32},{33,40},{41,48},{49,56},{57,64},{65,7... | collective-permute-start | bytes 393224 | tf_op jit(solution)/shard_map/ppermute | solution.py:176
  114.5 2.5 %constant_dynamic-update-slice_fusion.4 = bf16[1024,4096]{1,0:T(8,128)(2,1)S(1)} fusion(bf16[1024,4096]{1,0:T(8,128)(2,1)S(1)} %bitcast.76, bf16[512,4096]{1,0:T(8,128)(2,1)} %collective-permute-done.13), kind=kLoop, calls=%fused_computation.86 | loop fusion | bytes 8388608 | tf_op jit(solution)/shard_map/concatenate | solution.py:143
  117.1 2.6 %shard_map.87 = bf16[256,1024]{1,0:T(8,128)(2,1)S(1)} custom-call(bf16[256,1024]{1,0:T(8,128)(2,1)S(1)} %bitcast.54, bf16[512,1024]{1,0:T(8,128)(2,1)S(1)} %get-tuple-element.13.refs_0_, bf16[512,1024]{1,0:T(8,128)(2,1)S(1)} %get-tuple-element.14.refs_1_, bf16[512,1024]{1,0:T(8,128)(2,1)S(1)} %get-tuple-element.15.refs_2_, ...), custom_call_target="tpu_custom_call" | custom-call | flops 268435456 | bytes 5242880 | tf_op jit(solution)/shard_map/pallas_call | solution.py:65
  121.4 2.7 %collective-permute-start.14 = (bf16[128,2048]{1,0:T(8,128)(2,1)S(1)}, bf16[128,2048]{1,0:T(8,128)(2,1)S(1)}, u32[]{:S(2)}, u32[]{:S(2)}) collective-permute-start(bf16[128,2048]{1,0:T(8,128)(2,1)S(1)} %fusion.47), channel_id=1, source_target_pairs={{0,6},{2,0},{4,2},{6,4},{1,7},{3,1},{5,3},{7,5},{8,14},{10,8},{12,... | collective-permute-start | bytes 1572872 | tf_op jit(solution)/shard_map/ppermute | solution.py:23
  125.0 9.9 %collective-permute-done.15 = bf16[128,2048]{1,0:T(8,128)(2,1)S(1)} collective-permute-done((bf16[128,2048]{1,0:T(8,128)(2,1)S(1)}, bf16[128,2048]{1,0:T(8,128)(2,1)S(1)}, u32[]{:S(2)}, u32[]{:S(2)}) %collective-permute-start.15) | collective-permute-done | bytes 524320 | tf_op jit(solution)/shard_map/ppermute | solution.py:23
  134.9 1.6 fusion.41
  136.5 1.5 fusion.53
  138.0 7.8 %collective-permute-done.18 = bf16[128,2048]{1,0:T(8,128)(2,1)S(1)} collective-permute-done((bf16[128,2048]{1,0:T(8,128)(2,1)S(1)}, bf16[128,2048]{1,0:T(8,128)(2,1)S(1)}, u32[]{:S(2)}, u32[]{:S(2)}) %collective-permute-start.18) | collective-permute-done | bytes 524320 | tf_op jit(solution)/shard_map/ppermute | solution.py:23
  145.9 1.6 fusion.35
  147.5 3.4 %collective-permute-start.19 = (bf16[128,2048]{1,0:T(8,128)(2,1)}, bf16[128,2048]{1,0:T(8,128)(2,1)}, u32[]{:S(2)}, u32[]{:S(2)}) collective-permute-start(bf16[128,2048]{1,0:T(8,128)(2,1)} %fusion.35), channel_id=1, source_target_pairs={{0,6},{2,0},{4,2},{6,4},{1,7},{3,1},{5,3},{7,5},{8,14},{10,8},{12,... | collective-permute-start | bytes 1572872 | tf_op jit(solution)/shard_map/ppermute | solution.py:23
  150.9 3.1 %fusion.44 = bf16[128,2048]{1,0:T(8,128)(2,1)S(1)} fusion(bf16[1024,4096]{1,0:T(8,128)(2,1)} %copy-done.12, bf16[128,2048]{1,0:T(8,128)(2,1)S(1)} %collective-permute-done.16, bf16[128,2048]{1,0:T(8,128)(2,1)S(1)} %collective-permute-done.14, s32[]{:T(128)S(6)} %select_n.116, bf16[4,64,1024]{2,1,0:T(8,128)(2,1)S(1)} %fusion.63, ...), kind=kOutput, calls=%fused_computation.32 | convolution fusion | flops 538705920 | bytes 6815748 | tf_op jit(solution)/shard_map/dot_general | solution.py:27
  153.9 7.3 %collective-permute-done.17 = bf16[128,2048]{1,0:T(8,128)(2,1)S(1)} collective-permute-done((bf16[128,2048]{1,0:T(8,128)(2,1)}, bf16[128,2048]{1,0:T(8,128)(2,1)S(1)}, u32[]{:S(2)}, u32[]{:S(2)}) %collective-permute-start.17) | collective-permute-done | bytes 524320 | tf_op jit(solution)/shard_map/ppermute | solution.py:23
  161.2 3.1 %fusion.38 = bf16[128,2048]{1,0:T(8,128)(2,1)S(1)} fusion(bf16[1024,4096]{1,0:T(8,128)(2,1)} %copy-done.12, bf16[128,2048]{1,0:T(8,128)(2,1)} %collective-permute-done.19, bf16[128,2048]{1,0:T(8,128)(2,1)S(1)} %collective-permute-done.17, s32[]{:T(128)S(6)} %select_n.116, bf16[4,64,1024]{2,1,0:T(8,128)(2,1)S(1)} %fusion.63, ...), kind=kOutput, calls=%fused_computation.30 | convolution fusion | flops 538705920 | bytes 6815748 | tf_op jit(solution)/shard_map/dot_general | solution.py:27
  164.6 1.1 fusion.59
  (95 shorter events, 12.4 us)
Async XLA Ops:
  5.7 26.3 %all-to-all-start = ((bf16[16,3,16,896]{3,2,1,0:T(8,128)(2,1)}), bf16[16,3,16,896]{3,2,1,0:T(8,128)(2,1)S(1)}, u32[]{:S(2)}, u32[]{:S(2)}) async-start(bf16[16,3,16,896]{3,2,1,0:T(8,128)(2,1)} %bitcast.7), calls=%async_computation | async-start | bytes 2752512 | tf_op jit(solution)/shard_map/all_to_all | solution.py:126
  16.0 4.8 %copy-start.4 = (bf16[896,1024]{1,0:T(8,128)(2,1)}, bf16[896,1024]{1,0:T(8,128)(2,1)S(1)}, u32[]{:S(2)}) copy-start(bf16[896,1024]{1,0:T(8,128)(2,1)S(1)} %constant_dynamic-update-slice_fusion.2.wa_ref) | copy-start | bytes 5505028
  16.0 36.0 %collective-permute-start.4 = (bf16[896,1024]{1,0:T(8,128)(2,1)S(1)}, bf16[896,1024]{1,0:T(8,128)(2,1)}, u32[]{:S(2)}, u32[]{:S(2)}) collective-permute-start(bf16[896,1024]{1,0:T(8,128)(2,1)S(1)} %constant_dynamic-update-slice_fusion.2.wa_ref), channel_id=1, source_target_pairs={{0,1},{1,0},{2,3},{3,2},{4,5},{5,4},{6,7},{7,6},{8,9},{9,8},{10,11... | collective-permute-start | bytes 5505032 | tf_op jit(solution)/shard_map/ppermute | solution.py:23
  17.0 65.3 %collective-permute-start = (bf16[4096,512]{1,0:T(8,128)(2,1)}, bf16[4096,512]{1,0:T(8,128)(2,1)}, u32[]{:S(2)}, u32[]{:S(2)}) collective-permute-start(bf16[4096,512]{1,0:T(8,128)(2,1)} %param.9), channel_id=1, source_target_pairs={{0,1},{1,0},{2,3},{3,2},{4,5},{5,4},{6,7},{7,6},{8,9},{9,8},{10,11... | collective-permute-start | bytes 12582920 | tf_op jit(solution)/shard_map/ppermute | solution.py:23
  17.1 97.3 %collective-permute-start.13 = (bf16[512,4096]{1,0:T(8,128)(2,1)}, bf16[512,4096]{1,0:T(8,128)(2,1)}, u32[]{:S(2)}, u32[]{:S(2)}) collective-permute-start(bf16[512,4096]{1,0:T(8,128)(2,1)} %param.12), channel_id=1, source_target_pairs={{0,1},{1,0},{2,3},{3,2},{4,5},{5,4},{6,7},{7,6},{8,9},{9,8},{10,11... | collective-permute-start | bytes 12582920 | tf_op jit(solution)/shard_map/ppermute | solution.py:23
  33.4 12.9 %collective-permute-start.3 = (bf16[16,16,896]{2,1,0:T(8,128)(2,1)}, bf16[16,16,896]{2,1,0:T(8,128)(2,1)}, u32[]{:S(2)}, u32[]{:S(2)}) collective-permute-start(bf16[16,16,896]{2,1,0:T(8,128)(2,1)} %gather_fusion.2), channel_id=1, source_target_pairs={{0,1},{1,0},{2,3},{3,2},{4,5},{5,4},{6,7},{7,6},{8,9},{9,8},{10,11... | collective-permute-start | bytes 1376264 | tf_op jit(solution)/shard_map/ppermute | solution.py:23
  48.2 14.1 %collective-permute-start.8 = (bf16[256,896]{1,0:T(8,128)(2,1)S(1)}, bf16[256,896]{1,0:T(8,128)(2,1)}, u32[]{:S(2)}, u32[]{:S(2)}) collective-permute-start(bf16[256,896]{1,0:T(8,128)(2,1)S(1)} %bitcast.63), channel_id=1, source_target_pairs={{0,6},{2,0},{4,2},{6,4},{1,7},{3,1},{5,3},{7,5},{8,14},{10,8},{12,... | collective-permute-start | bytes 1376264 | tf_op jit(solution)/shard_map/ppermute | solution.py:23
  52.0 23.0 %collective-permute-start.6 = (bf16[256,896]{1,0:T(8,128)(2,1)S(1)}, bf16[256,896]{1,0:T(8,128)(2,1)S(1)}, u32[]{:S(2)}, u32[]{:S(2)}) collective-permute-start(bf16[256,896]{1,0:T(8,128)(2,1)S(1)} %bitcast.64), channel_id=1, source_target_pairs={{0,2},{2,4},{4,6},{6,0},{1,3},{3,5},{5,7},{7,1},{8,10},{10,12},{12... | collective-permute-start | bytes 1376264 | tf_op jit(solution)/shard_map/ppermute | solution.py:23
  52.0 23.0 %collective-permute-start.5 = (bf16[256,896]{1,0:T(8,128)(2,1)}, bf16[256,896]{1,0:T(8,128)(2,1)}, u32[]{:S(2)}, u32[]{:S(2)}) collective-permute-start(bf16[256,896]{1,0:T(8,128)(2,1)} %bitcast.11.low_ref), channel_id=1, source_target_pairs={{0,2},{2,4},{4,6},{6,0},{1,3},{3,5},{5,7},{7,1},{8,10},{10,12},{12... | collective-permute-start | bytes 1376264 | tf_op jit(solution)/shard_map/ppermute | solution.py:23
  56.7 1.5 copy-start.5
  58.2 24.2 %copy-start.11 = (bf16[512,4096]{1,0:T(8,128)(2,1)S(1)}, bf16[512,4096]{1,0:T(8,128)(2,1)}, u32[]{:S(2)}) copy-start(bf16[512,4096]{1,0:T(8,128)(2,1)} %fusion) | copy-start | bytes 12582916
  62.3 33.2 %collective-permute-start.7 = (bf16[256,896]{1,0:T(8,128)(2,1)}, bf16[256,896]{1,0:T(8,128)(2,1)}, u32[]{:S(2)}, u32[]{:S(2)}) collective-permute-start(bf16[256,896]{1,0:T(8,128)(2,1)} %bitcast.11.low_ref), channel_id=1, source_target_pairs={{0,6},{2,0},{4,2},{6,4},{1,7},{3,1},{5,3},{7,5},{8,14},{10,8},{12,... | collective-permute-start | bytes 1376264 | tf_op jit(solution)/shard_map/ppermute | solution.py:23
  75.0 27.7 %collective-permute-start.10 = (bf16[256,896]{1,0:T(8,128)(2,1)}, bf16[256,896]{1,0:T(8,128)(2,1)}, u32[]{:S(2)}, u32[]{:S(2)}) collective-permute-start(bf16[256,896]{1,0:T(8,128)(2,1)} %collective-permute-done.8.high_ref), channel_id=1, source_target_pairs={{0,6},{2,0},{4,2},{6,4},{1,7},{3,1},{5,3},{7,5},{8,14},{10,8},{12,... | collective-permute-start | bytes 1376264 | tf_op jit(solution)/shard_map/ppermute | solution.py:23
  75.0 0.8 copy-start.8
  75.8 26.9 %collective-permute-start.9 = (bf16[256,896]{1,0:T(8,128)(2,1)}, bf16[256,896]{1,0:T(8,128)(2,1)}, u32[]{:S(2)}, u32[]{:S(2)}) collective-permute-start(bf16[256,896]{1,0:T(8,128)(2,1)} %collective-permute-done.5.low_ref), channel_id=1, source_target_pairs={{0,2},{2,4},{4,6},{6,0},{1,3},{3,5},{5,7},{7,1},{8,10},{10,12},{12... | collective-permute-start | bytes 1376264 | tf_op jit(solution)/shard_map/ppermute | solution.py:23
  77.3 1.0 copy-start.9
  82.3 5.0 %copy-start = (bf16[512,1024]{1,0:T(8,128)(2,1)}, bf16[512,1024]{1,0:T(8,128)(2,1)S(1)}, u32[]{:S(2)}) copy-start(bf16[512,1024]{1,0:T(8,128)(2,1)S(1)} %get-tuple-element.18.refs_5_) | copy-start | bytes 3145732
  82.3 5.0 %copy-start.13 = (bf16[512,512]{0,1:T(8,128)(2,1)S(1)}, bf16[512,512]{0,1:T(8,128)(2,1)}, u32[]{:S(2)}) copy-start(bf16[512,512]{0,1:T(8,128)(2,1)} %convolution_convert_fusion.1) | copy-start | bytes 1572868
  92.6 10.1 %copy-start.7 = (bf16[896,1024]{1,0:T(8,128)(2,1)S(1)}, bf16[896,1024]{1,0:T(8,128)(2,1)}, u32[]{:S(2)}) copy-start(bf16[896,1024]{1,0:T(8,128)(2,1)} %copy-done.4) | copy-start | bytes 5505028
  93.8 13.1 %collective-permute-start.1 = (bf16[4,64,1024]{2,1,0:T(8,128)(2,1)S(1)}, bf16[4,64,1024]{2,1,0:T(8,128)(2,1)S(1)}, u32[]{:S(2)}, u32[]{:S(2)}) collective-permute-start(bf16[4,64,1024]{2,1,0:T(8,128)(2,1)S(1)} %fusion.62), channel_id=1, source_target_pairs={{0,1},{1,0},{2,3},{3,2},{4,5},{5,4},{6,7},{7,6},{8,9},{9,8},{10,11... | collective-permute-start | bytes 1572872 | tf_op jit(solution)/shard_map/ppermute | solution.py:23
  95.5 1.5 copy-start.6
  101.2 6.5 %copy-start.10 = (bf16[512,1024]{1,0:T(8,128)(2,1)S(1)}, bf16[512,1024]{1,0:T(8,128)(2,1)}, u32[]{:S(2)}) copy-start(bf16[512,1024]{1,0:T(8,128)(2,1)} %copy.25) | copy-start | bytes 3145732
  101.2 6.8 %copy-start.1 = (bf16[512,1024]{1,0:T(8,128)(2,1)S(1)}, bf16[512,1024]{1,0:T(8,128)(2,1)}, u32[]{:S(2)}) copy-start(bf16[512,1024]{1,0:T(8,128)(2,1)} %copy-done) | copy-start | bytes 3145732
  101.2 6.4 %collective-permute-start.2 = (bf16[64,1024]{1,0:T(8,128)(2,1)S(1)}, bf16[64,1024]{1,0:T(8,128)(2,1)S(1)}, u32[]{:S(2)}, u32[]{:S(2)}) collective-permute-start(bf16[64,1024]{1,0:T(8,128)(2,1)S(1)} %slice_bitcast_fusion), channel_id=1, source_target_pairs={{8,1},{16,9},{24,17},{32,25},{40,33},{48,41},{56,49},{64,57},{72,6... | collective-permute-start | bytes 393224 | tf_op jit(solution)/shard_map/ppermute | solution.py:156
  106.9 7.5 %slice-start = ((s8[8388608]{0:T(1024)(128)(4,1)}), s8[4194304]{0:T(1024)(128)(4,1)S(1)}, s32[]{:S(2)}) async-start(s8[8388608]{0:T(1024)(128)(4,1)} %bitcast.75), calls=%async_computation.1 | async-start | bytes 8388608
  108.0 6.4 %slice-start.1 = ((s8[8388608]{0:T(1024)(128)(4,1)}), s8[4194304]{0:T(1024)(128)(4,1)S(1)}, s32[]{:S(2)}) async-start(s8[8388608]{0:T(1024)(128)(4,1)} %bitcast.75), calls=%async_computation.2 | async-start | bytes 8388608
  110.7 9.0 %collective-permute-start.11 = (bf16[64,1024]{1,0:T(8,128)(2,1)S(1)}, bf16[64,1024]{1,0:T(8,128)(2,1)S(1)}, u32[]{:S(2)}, u32[]{:S(2)}) collective-permute-start(bf16[64,1024]{1,0:T(8,128)(2,1)S(1)} %fusion.74), channel_id=1, source_target_pairs={{1,8},{9,16},{17,24},{25,32},{33,40},{41,48},{49,56},{57,64},{65,7... | collective-permute-start | bytes 393224 | tf_op jit(solution)/shard_map/ppermute | solution.py:176
  114.3 5.3 %collective-permute-start.12 = (bf16[4,64,1024]{2,1,0:T(8,128)(2,1)S(1)}, bf16[4,64,1024]{2,1,0:T(8,128)(2,1)S(1)}, u32[]{:S(2)}, u32[]{:S(2)}) collective-permute-start(bf16[4,64,1024]{2,1,0:T(8,128)(2,1)S(1)} %pad_maximum_fusion.2), channel_id=1, source_target_pairs={{0,1},{1,0},{2,3},{3,2},{4,5},{5,4},{6,7},{7,6},{8,9},{9,8},{10,11... | collective-permute-start | bytes 1572872 | tf_op jit(solution)/shard_map/ppermute | solution.py:23
  116.9 29.0 %copy-start.12 = (bf16[1024,4096]{1,0:T(8,128)(2,1)}, bf16[1024,4096]{1,0:T(8,128)(2,1)S(1)}, u32[]{:S(2)}) copy-start(bf16[1024,4096]{1,0:T(8,128)(2,1)S(1)} %constant_dynamic-update-slice_fusion.4) | copy-start | bytes 25165828
  119.6 26.2 %copy-start.2 = (bf16[256,1024]{1,0:T(8,128)(2,1)}, bf16[256,1024]{1,0:T(8,128)(2,1)S(1)}, u32[]{:S(2)}) copy-start(bf16[256,1024]{1,0:T(8,128)(2,1)S(1)} %shard_map.87) | copy-start | bytes 1572868
  120.6 14.3 %collective-permute-start.15 = (bf16[128,2048]{1,0:T(8,128)(2,1)S(1)}, bf16[128,2048]{1,0:T(8,128)(2,1)S(1)}, u32[]{:S(2)}, u32[]{:S(2)}) collective-permute-start(bf16[128,2048]{1,0:T(8,128)(2,1)S(1)} %fusion.50), channel_id=1, source_target_pairs={{0,2},{2,4},{4,6},{6,0},{1,3},{3,5},{5,7},{7,1},{8,10},{10,12},{12... | collective-permute-start | bytes 1572872 | tf_op jit(solution)/shard_map/ppermute | solution.py:23
  121.4 29.5 %collective-permute-start.14 = (bf16[128,2048]{1,0:T(8,128)(2,1)S(1)}, bf16[128,2048]{1,0:T(8,128)(2,1)S(1)}, u32[]{:S(2)}, u32[]{:S(2)}) collective-permute-start(bf16[128,2048]{1,0:T(8,128)(2,1)S(1)} %fusion.47), channel_id=1, source_target_pairs={{0,6},{2,0},{4,2},{6,4},{1,7},{3,1},{5,3},{7,5},{8,14},{10,8},{12,... | collective-permute-start | bytes 1572872 | tf_op jit(solution)/shard_map/ppermute | solution.py:23
  124.9 21.0 %collective-permute-start.18 = (bf16[128,2048]{1,0:T(8,128)(2,1)S(1)}, bf16[128,2048]{1,0:T(8,128)(2,1)S(1)}, u32[]{:S(2)}, u32[]{:S(2)}) collective-permute-start(bf16[128,2048]{1,0:T(8,128)(2,1)S(1)} %fusion.56), channel_id=1, source_target_pairs={{0,6},{2,0},{4,2},{6,4},{1,7},{3,1},{5,3},{7,5},{8,14},{10,8},{12,... | collective-permute-start | bytes 1572872 | tf_op jit(solution)/shard_map/ppermute | solution.py:23
  136.5 14.4 %collective-permute-start.16 = (bf16[128,2048]{1,0:T(8,128)(2,1)}, bf16[128,2048]{1,0:T(8,128)(2,1)S(1)}, u32[]{:S(2)}, u32[]{:S(2)}) collective-permute-start(bf16[128,2048]{1,0:T(8,128)(2,1)} %fusion.41), channel_id=1, source_target_pairs={{0,2},{2,4},{4,6},{6,0},{1,3},{3,5},{5,7},{7,1},{8,10},{10,12},{12... | collective-permute-start | bytes 1572872 | tf_op jit(solution)/shard_map/ppermute | solution.py:23
  138.0 23.2 %collective-permute-start.17 = (bf16[128,2048]{1,0:T(8,128)(2,1)}, bf16[128,2048]{1,0:T(8,128)(2,1)S(1)}, u32[]{:S(2)}, u32[]{:S(2)}) collective-permute-start(bf16[128,2048]{1,0:T(8,128)(2,1)} %fusion.53), channel_id=1, source_target_pairs={{0,2},{2,4},{4,6},{6,0},{1,3},{3,5},{5,7},{7,1},{8,10},{10,12},{12... | collective-permute-start | bytes 1572872 | tf_op jit(solution)/shard_map/ppermute | solution.py:23
  147.4 13.8 %copy-start.3 = (bf16[256,1024]{1,0:T(8,128)(2,1)S(1)}, bf16[256,1024]{1,0:T(8,128)(2,1)}, u32[]{:S(2)}) copy-start(bf16[256,1024]{1,0:T(8,128)(2,1)} %copy-done.2) | copy-start | bytes 1572868
  147.5 13.8 %collective-permute-start.19 = (bf16[128,2048]{1,0:T(8,128)(2,1)}, bf16[128,2048]{1,0:T(8,128)(2,1)}, u32[]{:S(2)}, u32[]{:S(2)}) collective-permute-start(bf16[128,2048]{1,0:T(8,128)(2,1)} %fusion.35), channel_id=1, source_target_pairs={{0,6},{2,0},{4,2},{6,4},{1,7},{3,1},{5,3},{7,5},{8,14},{10,8},{12,... | collective-permute-start | bytes 1572872 | tf_op jit(solution)/shard_map/ppermute | solution.py:23

commit v3 on v0

v3 whole, which is shorter than its diff:
```python
import math

import jax
import jax.numpy as jnp
from jax import lax
from jax.experimental import pallas as pl
from jax.experimental.pallas import tpu as pltpu
from jax.sharding import Mesh, PartitionSpec as P

HS = 128
CL = 64
NB_LEN = 128
NEIGH = 2
N_Z = 4
N_CORE = 2
BLOCK = 128
F32 = jnp.float32
BF16 = jnp.bfloat16
SHARE = 0.4
LIMIT = 60 * 1024 * 1024


def step(value, axis, steps):
    count = lax.axis_size(axis)
    return lax.ppermute(value, axis, [(i, (i + steps) % count) for i in range(count)])


def cost(flops):
    return pl.CostEstimate(flops=int(flops * SHARE), bytes_accessed=int(flops * SHARE / 1000), transcendentals=0)


def dot(a, b):
    return jnp.dot(a, b, preferred_element_type=F32)


def bucket_places(shards):
    count = shards.shape[1]
    same_shard = shards[:, :, None] == shards[:, None, :]
    earlier = jnp.arange(count)[None, :] < jnp.arange(count)[:, None]
    return jnp.sum((same_shard & earlier[None]).astype(jnp.int32), axis=2)


def pick_kernel(index_ref, start_ref, source_ref, *refs):
    out_refs, rows_ref, sem = refs[:-2], refs[-2], refs[-1]
    rows = rows_ref.shape[1]
    start = pl.multiple_of(start_ref[0] * rows, rows)
    copy = pltpu.make_async_copy(source_ref.at[:, pl.ds(start, rows)], rows_ref, sem)
    copy.start()
    copy.wait()
    place = 0
    for out_ref in out_refs:
        for i in range(out_ref.shape[0]):
            out_ref[i] = rows_ref[index_ref[place]]
            place += 1


def pick(source, index, start, rows, counts):
    shapes = [(count, rows, source.shape[2]) for count in counts]
    return pl.pallas_call(
        pick_kernel,
        grid_spec=pltpu.PrefetchScalarGridSpec(
            num_scalar_prefetch=2,
            grid=(1,),
            in_specs=[pl.BlockSpec(memory_space=pltpu.HBM)],
            out_specs=[pl.BlockSpec(shape, lambda i, index, start: (0, 0, 0)) for shape in shapes],
            scratch_shapes=[pltpu.VMEM((source.shape[0], rows, source.shape[2]), source.dtype), pltpu.SemaphoreType.DMA],
        ),
        out_shape=[jax.ShapeDtypeStruct(shape, source.dtype) for shape in shapes],
        cost_estimate=cost(1e9),
        compiler_params=pltpu.CompilerParams(vmem_limit_bytes=LIMIT),
    )(index, start.reshape(1), source)


def query_kernel(core_ref, x_hbm, wa_hbm, wb_hbm, first_ref, second_ref, crossing_ref, x_ref, wa_ref, wb_ref, sems):
    half = wa_ref.shape[1]
    copies = []
    for j in range(N_Z):
        block = N_CORE * j + core_ref[0]
        after = lax.rem(block + 1, N_Z * N_CORE)
        copies.append(pltpu.make_async_copy(x_hbm.at[block], x_ref.at[j, :BLOCK], sems.at[2 * j]))
        copies.append(pltpu.make_async_copy(x_hbm.at[after, :CL], x_ref.at[j, BLOCK:], sems.at[2 * j + 1]))
    copies.append(pltpu.make_async_copy(wa_hbm, wa_ref, sems.at[2 * N_Z]))
    copies.append(pltpu.make_async_copy(wb_hbm, wb_ref, sems.at[2 * N_Z + 1]))
    for copy in copies:
        copy.start()
    for j in range(N_Z):
        copies[2 * j].wait()
        copies[2 * j + 1].wait()
        source = x_ref[j].astype(F32)
        scale = lax.rsqrt(jnp.mean(source * source, axis=-1, keepdims=True) + 1e-05)
        x_ref[j] = (source * scale).astype(BF16)
    rows = BLOCK + CL
    for i, weight_ref in enumerate((wa_ref, wb_ref)):
        copies[2 * N_Z + i].wait()
        here, there = slice(i * half, (i + 1) * half), slice((1 - i) * half, (2 - i) * half)
        product = dot(x_ref[...].reshape(N_Z * rows, -1), weight_ref[...])
        for j in range(N_Z):
            rolled = pltpu.roll(product[j * rows : (j + 1) * rows], 1, 0).astype(BF16)
            first_ref[j, :, here] = rolled[CL:BLOCK]
            second_ref[j, :, here] = rolled[BLOCK:]
            if j == 0:
                crossing_ref[:, there] = rolled[:CL]


def project_queries(decoder, weight_a, weight_b, core):
    model, half = weight_a.shape
    blocks = decoder.reshape(N_Z * N_CORE, BLOCK, model)
    shape = (N_Z, CL, 2 * half)
    out_spec = pl.BlockSpec(shape, lambda i, core: (0, 0, 0))
    return pl.pallas_call(
        query_kernel,
        grid_spec=pltpu.PrefetchScalarGridSpec(
            num_scalar_prefetch=1,
            grid=(1,),
            in_specs=[pl.BlockSpec(memory_space=pltpu.HBM)] * 3,
            out_specs=[out_spec, out_spec, pl.BlockSpec(shape[1:], lambda i, core: (0, 0))],
            scratch_shapes=[
                pltpu.VMEM((N_Z, BLOCK + CL, model), BF16),
                pltpu.VMEM((model, half), BF16),
                pltpu.VMEM((model, half), BF16),
                pltpu.SemaphoreType.DMA((2 * N_Z + 2,)),
            ],
        ),
        out_shape=[jax.ShapeDtypeStruct(dims, BF16) for dims in (shape, shape, shape[1:])],
        cost_estimate=cost(3e9),
        compiler_params=pltpu.CompilerParams(vmem_limit_bytes=LIMIT),
    )(core.reshape(1), blocks, weight_a, weight_b)


def span_kernel(place_ref, q_hbm, crossing_hbm, *refs):
    row_hbm, weight_hbm, out_hbm, out_refs = refs[:8], refs[8:14], refs[14:22], refs[22:30]
    q_ref, crossing_ref, rows_ref, weight_refs, kv_ref, context_ref, sems, out_sem = (
        *refs[30:33],
        refs[33:39],
        *refs[39:43],
    )
    half, model = weight_refs[4].shape
    parts, rows, enc = rows_ref.shape
    row_copies = [pltpu.make_async_copy(row_hbm[i], rows_ref.at[i], sems.at[i]) for i in range(parts)]
    weight_copies = [pltpu.make_async_copy(weight_hbm[i], weight_refs[i], sems.at[8 + i]) for i in range(6)]
    query_copies = [
        pltpu.make_async_copy(q_hbm, q_ref, sems.at[14]),
        pltpu.make_async_copy(crossing_hbm, crossing_ref, sems.at[15]),
    ]
    for copy in row_copies + weight_copies[:4] + query_copies + weight_copies[4:]:
        copy.start()

    for copy in row_copies:
        copy.wait()
    for i in range(4):
        weight_copies[i].wait()
        for part in range(0, parts, 4):
            product = dot(rows_ref[part : part + 4].reshape(4 * rows, enc), weight_refs[i][...]).astype(BF16)
            kv_ref[part : part + 4, :, :, i * half : (i + 1) * half] = product.reshape((4,) + kv_ref.shape[1:3] + (half,))

    for copy in query_copies:
        copy.wait()
    is_first_row = lax.broadcasted_iota(jnp.int32, (CL, HS), 0) == 0
    heads = [(side, lower) for side in (0, 1) for lower in range(0, half, HS)]

    def attend_span(span, carry):
        crosses = (span == N_Z - 1) & (place_ref[N_Z] == 1)
        scores = []
        for side, lower in heads:
            place = slice(side * half + lower, side * half + lower + HS)
            q = jnp.where(is_first_row | jnp.logical_not(crosses), q_ref[span, :, place], crossing_ref[:, place])
            start = 2 * side * half + lower
            k = kv_ref[:, span, :, start : start + HS].reshape(-1, HS)
            scores.append(lax.dot_general(q, k, (((1,), (1,)), ((), ())), preferred_element_type=F32))
        probs = []
        for score in scores:
            score = score * (1.0 / math.sqrt(HS))
            weights = jnp.exp(score - jnp.max(score, axis=-1, keepdims=True))
            total = jnp.sum(weights, axis=-1, keepdims=True)
            probs.append((weights * (1.0 / total)).astype(BF16))
        for (side, lower), prob in zip(heads, probs):
            start = (2 * side + 1) * half + lower
            v = kv_ref[:, span, :, start : start + HS].reshape(-1, HS)
            context_ref[span, :, side * half + lower : side * half + lower + HS] = dot(prob, v).astype(BF16)
        return carry

    lax.fori_loop(0, N_Z, attend_span, 0)

    for copy in weight_copies[4:]:
        copy.wait()
    context = jnp.concatenate([context_ref[place_ref[i]] for i in range(N_Z)], axis=0)
    tile = model // 4
    for lower in range(0, model, tile):
        place = slice(lower, lower + tile)
        product = dot(context[:, :half], weight_refs[4][:, place]) + dot(context[:, half:], weight_refs[5][:, place])
        product = product.astype(BF16)
        side, start = lower // (model // 2), lower % (model // 2)
        for i in range(N_Z):
            out_refs[2 * i + side][:, start : start + tile] = product[i * CL : (i + 1) * CL]
        if start + tile == model // 2:
            for i in range(side, 2 * N_Z, 2):
                pltpu.make_async_copy(out_refs[i], out_hbm[i], out_sem.at[i]).start()
    for i in range(2 * N_Z):
        pltpu.make_async_copy(out_refs[i], out_hbm[i], out_sem.at[i]).wait()


def attend(places, queries, crossing, parts, weights):
    spans, tokens, width = queries.shape
    half, model = weights[4].shape
    rows, enc = parts[0].shape
    out = jax.ShapeDtypeStruct((tokens, model // 2), BF16)
    return pl.pallas_call(
        span_kernel,
        grid_spec=pltpu.PrefetchScalarGridSpec(
            num_scalar_prefetch=1,
            grid=(1,),
            in_specs=[pl.BlockSpec(memory_space=pltpu.HBM)] * 16,
            out_specs=[pl.BlockSpec(memory_space=pltpu.HBM)] * 8,
            scratch_shapes=[pltpu.VMEM(out.shape, BF16)] * 8
            + [
                pltpu.VMEM(queries.shape, BF16),
                pltpu.VMEM(crossing.shape, BF16),
                pltpu.VMEM((len(parts), rows, enc), BF16),
            ]
            + [pltpu.VMEM(weight.shape, BF16) for weight in weights]
            + [
                pltpu.VMEM((len(parts), spans, rows // spans, 4 * half), BF16),
                pltpu.VMEM(queries.shape, BF16),
                pltpu.SemaphoreType.DMA((16,)),
                pltpu.SemaphoreType.DMA((8,)),
            ],
        ),
        out_shape=[out] * 8,
        cost_estimate=cost(5e9),
        compiler_params=pltpu.CompilerParams(vmem_limit_bytes=LIMIT),
    )(places, queries, crossing, *parts, *weights)


def body(decoder, w_query, w_key, w_value, w_out, database, nb_shard, nb_slot):
    n_seq = lax.axis_size("seq")
    seq_index, z_index, core = lax.axis_index("seq"), lax.axis_index("z"), lax.axis_index("core")
    tok_rows, model = decoder.shape
    spans = tok_rows // CL
    requests = NEIGH * spans
    capacity = (requests + n_seq - 1) // n_seq + 1
    slots, _, enc = database.shape
    piece = NB_LEN // (N_Z * N_CORE)

    bits = (slots - 1).bit_length()
    lists = (nb_shard.T << bits) + nb_slot.T
    lists = lists.reshape(NEIGH, n_seq, spans).transpose(1, 0, 2).reshape(n_seq, requests)
    shard_lists, slot_lists = lists >> bits, lists & ((1 << bits) - 1)
    places = bucket_places(shard_lists)
    picked = (shard_lists == seq_index)[:, None, :] & (places[:, None, :] == jnp.arange(capacity)[None, :, None])
    send_slot = jnp.sum(jnp.where(picked, slot_lists[:, None, :], 0), axis=2)
    (outgoing,) = pick(database, send_slot.reshape(-1), z_index * N_CORE + core, piece, [n_seq * capacity])
    received = lax.all_to_all(
        outgoing.reshape(n_seq, capacity, piece, enc), "seq", split_axis=0, concat_axis=0, tiled=True
    )
    received = received.reshape(n_seq * capacity, piece, enc)

    w_query_other = step(w_query, "core", 1)
    weights = (w_key, w_value, *(step(weight, "core", 1) for weight in (w_key, w_value)), w_out, step(w_out, "core", 1))
    first_queries, second_queries, crossing = project_queries(decoder, w_query, w_query_other, core)
    received, weights, crossing = lax.optimization_barrier((received, weights, crossing))

    my_shards = lax.dynamic_index_in_dim(shard_lists, seq_index, 0, keepdims=False)
    my_places = lax.dynamic_index_in_dim(places, seq_index, 0, keepdims=False)
    row_index = (my_shards * capacity + my_places).reshape(NEIGH, N_Z, N_CORE, 2)
    row_index = row_index.transpose(2, 3, 1, 0)[:, ::-1]
    row_index = jnp.where(core == 0, row_index, row_index[::-1]).reshape(-1)
    group = row_index.shape[0] // 4
    mine_a, mine_b, theirs_a, theirs_b = [
        rows.reshape(-1, enc) for rows in pick(received, row_index, jnp.zeros((), jnp.int32), piece, [group] * 4)
    ]

    def hop(value, steps, cross):
        pairs = [
            (z * N_CORE + c, (z + steps) % N_Z * N_CORE + (c + cross) % N_CORE)
            for z in range(N_Z)
            for c in range(N_CORE)
        ]
        return lax.ppermute(value, ("z", "core"), pairs)

    def neighbours(mine, theirs):
        return [hop(mine, 1, 0), hop(theirs, -1, 1), hop(theirs, 1, 1), hop(mine, -1, 0)]

    def opposite(ring):
        return hop(ring[0], 1, 0), hop(ring[1], -1, 0)

    def add(*terms):
        return sum(term.astype(F32) for term in terms).astype(BF16)

    def total(here, down_left, up_left, up_right, down_right):
        return jnp.concatenate([add(here[0], down_left, up_left), add(here[1], up_right, down_right)], axis=1)

    distance = jnp.array([2, 1, 3, 0], jnp.int32)
    places_a = jnp.append((z_index + distance + (N_Z - 1) * core) % N_Z, core).astype(jnp.int32)
    places_b = jnp.append((z_index + distance) % N_Z, 0).astype(jnp.int32)

    ring_a, swapped_a = neighbours(mine_a, theirs_a), hop(theirs_a, 0, 1)
    ring_a, swapped_a, crossing, mine_b, theirs_b = lax.optimization_barrier(
        (ring_a, swapped_a, crossing, mine_b, theirs_b)
    )
    far_a = opposite(ring_a)
    ring_b, swapped_b = neighbours(mine_b, theirs_b), hop(theirs_b, 0, 1)
    crossing = lax.ppermute(crossing, ("seq", "core"), [(2 * i + 2, 2 * i + 1) for i in range(n_seq - 1)])
    far_a, crossing, ring_b, swapped_b = lax.optimization_barrier((far_a, crossing, ring_b, swapped_b))

    far_b = opposite(ring_b)
    sums_a = attend(places_a, second_queries, crossing, (mine_a, swapped_a, *ring_a, *far_a), weights)
    sums_a, far_b = lax.optimization_barrier((sums_a, far_b))
    up_a, down_a = step(sums_a[0], "z", 1), step(sums_a[1], "z", -1)
    up_right_a, down_left_a = step(sums_a[3], "z", 1), step(sums_a[4], "z", -1)
    sums_b = attend(places_b, first_queries, crossing, (mine_b, swapped_b, *ring_b, *far_b), weights)
    sums_b, up_a, down_a = lax.optimization_barrier((sums_b, up_a, down_a))
    up_left_a, down_right_a = step(add(sums_a[2], up_a), "z", 1), step(add(sums_a[5], down_a), "z", -1)
    up_b, down_b = step(sums_b[0], "z", 1), step(sums_b[1], "z", -1)
    up_right_b, down_left_b = step(sums_b[3], "z", 1), step(sums_b[4], "z", -1)
    up_left_b, down_right_b = step(add(sums_b[2], up_b), "z", 1), step(add(sums_b[5], down_b), "z", -1)

    out_a = total(sums_a[6:], down_left_a, up_left_a, up_right_a, down_right_a)
    last = lax.ppermute(out_a[:1], ("z", "core"), [(2 * z + 1, (2 * z - 1) % (N_Z * N_CORE)) for z in range(N_Z)])
    last = jnp.where(core == 0, out_a[:1], last)
    pairs = []
    for i in range(0, n_seq * N_Z * N_CORE, 2):
        pairs.append((i, i + 1))
        if i % (N_Z * N_CORE):
            pairs.append((i + 1, i))
        elif i + N_Z * N_CORE < n_seq * N_Z * N_CORE:
            pairs.append((i + 1, i + N_Z * N_CORE))
    head = lax.ppermute(out_a, ("seq", "z", "core"), pairs)
    out_b = total(sums_b[6:], down_left_b, up_left_b, up_right_b, down_right_b)
    return jnp.concatenate([head[1:], out_b, last], axis=0)


def solution(mesh):
    n_seq = mesh.devices.shape[0]
    fine = Mesh(mesh.devices.reshape(n_seq, N_Z, N_CORE), ("seq", "z", "core"))
    db = ("z", "core")
    return jax.shard_map(
        body,
        mesh=fine,
        in_specs=(
            P("seq", None),
            P(None, db),
            P(None, db),
            P(None, db),
            P(db, None),
            P("seq", None, None),
            P(),
            P(),
        ),
        out_specs=P(("seq", "z", "core"), None),
        check_vma=False,
    )
```

time: 339 us -> 148 us (0.44)
  waiting for transfers between devices: 237 us -> 38.1 us
  Pallas kernels: 0 us -> 45.4 us
  matrix products: 41.2 us -> 0 us
  starting transfers between devices: 15.5 us -> 55.6 us
  local copies, waits for them, and re-layouts: 24 us -> 3.25 us
  between operations: 13.6 us -> 0.6 us
  other arithmetic: 7.58 us -> 3.85 us
    all_to_all x1, waiting for transfers between devices: 93.7 us -> 4.69 us  [body(): lax.all_to_all(outgoing.reshape(n_seq, capacity, piece, enc), 'seq', spli...]
    reduce_scatter x1 -> x0, waiting for transfers between devices: 58.3 us -> none  [body(): lax.psum_scatter(jnp.dot(context, w_out, preferred_element_type=jnp.float...]
    ppermute x2 -> x33, waiting for transfers between devices: 84.6 us -> 33.4 us  [the longest x14 14.7 us: hop(): return lax.ppermute(value, ('z', 'core'), pairs)]
    pallas_call x0 -> x5, Pallas kernels: none -> 45.4 us  [the longest x2 27.3 us: attend(): pl.pallas_call(span_kernel, grid_spec=pltpu.PrefetchScalarGridSpec(num_sc...]
    dot_general x6 -> x0, matrix products: 41.2 us -> none  [the longest x1 11.9 us: attend(): jnp.einsum('bhqk,bkhd->bqhd', probs, v_heads, preferred_element_type=jnp....]
    ppermute x2 -> x33, starting transfers between devices: 7.87 us -> 48.5 us  [the longest x14 20.4 us: hop(): return lax.ppermute(value, ('z', 'core'), pairs)]
    gather x2 -> x0, local copies, waits for them, and re-layouts: 18.2 us -> none  [the longest x1 9.73 us: body(): outgoing = database[send_slot]]
    reduce_sum x1 -> x0, other arithmetic: 5.22 us -> none  [body(): scale = lax.rsqrt(jnp.mean(source * source, axis=-1, keepdims=True) + 1e-05)]
  transfers between devices with their start and end apart: 4 -> 34, of which waited for: 4 -> 11; matrix products, arithmetic and copies ran while one was open for 4% -> 3% of each run, Pallas kernels for 0% -> 29%
where the time goes in v3:
time: 148 us; the launch traced here: 147 us
  starting transfers between devices  55.6 us (38%)
  Pallas kernels  45.4 us (31%)
  waiting for transfers between devices  38.1 us (26%)
  other arithmetic  3.85 us (3%)
  local copies, waits for them, and re-layouts  3.25 us (2%)
    pallas_call x2, Pallas kernels, attend(): pl.pallas_call(span_kernel, grid_spec=pltpu.PrefetchScalarGridSpec(num_sc...  27.3 us
    ppermute x14, starting transfers between devices, hop(): return lax.ppermute(value, ('z', 'core'), pairs)  20.4 us
    ppermute x16, starting transfers between devices, step(): lax.ppermute(value, axis, [(i, (i + steps) % count) for i in range(count)])  14.7 us
    ppermute x14, waiting for transfers between devices, hop(): return lax.ppermute(value, ('z', 'core'), pairs)  14.7 us
    pallas_call x1, Pallas kernels, project_queries(): pl.pallas_call(query_kernel, grid_spec=pltpu.PrefetchScalarGridSpec(num_s...  12.1 us
    ppermute x1, starting transfers between devices, body(): head = lax.ppermute(out_a, ('seq', 'z', 'core'), pairs)  9.04 us
    ppermute x16, waiting for transfers between devices, step(): lax.ppermute(value, axis, [(i, (i + steps) % count) for i in range(count)])  8.97 us
    all_to_all x1, starting transfers between devices, body(): lax.all_to_all(outgoing.reshape(n_seq, capacity, piece, enc), 'seq', spli...  7.03 us
  transfers between devices with their start and end apart: 34, of which 11 were waited for; matrix products, arithmetic and copies ran while one was open for 3% of the time, Pallas kernels for 29%

profile of v3, /device:TPU:1, one launch (start us, length us, event | category | flops | bytes accessed | tf_op | source)
XLA Modules:
  0.0 146.7 jit_solution(3718149400813425249)
XLA Ops:
  0.0 1.4 collective-permute-start
  1.4 0.7 and_bitcast_fusion
  2.5 0.5 convert_reduce_fusion
  3.2 0.6 reshape.88.index_ref
  3.8 3.0 %shard_map.92 = bf16[48,16,896]{2,1,0:T(8,128)(2,1)} custom-call(s32[48]{0:T(128)} %reshape.88.index_ref, s32[1]{0:T(128)} %bitcast.7.start_ref, bf16[24,128,896]{2,1,0:T(8,128)(2,1)} %source_ref.1), custom_call_target="tpu_custom_call" | custom-call | flops 400000000 | bytes 400000 | tf_op jit(solution)/shard_map/pallas_call | solution.py:59
  6.8 7.0 %all-to-all-start = ((bf16[16,3,16,896]{3,2,1,0:T(8,128)(2,1)}), bf16[16,3,16,896]{3,2,1,0:T(8,128)(2,1)}, u32[]{:S(2)}, u32[]{:S(2)}) async-start(bf16[16,3,16,896]{3,2,1,0:T(8,128)(2,1)} %bitcast.24), calls=%async_computation | async-start | bytes 2752512 | tf_op jit(solution)/shard_map/all_to_all | solution.py:252
  13.8 0.9 collective-permute-start.1
  15.3 0.7 reshape.87.index_ref
  16.0 12.1 %shard_map.91 = (bf16[4,64,1024]{2,1,0:T(8,128)(2,1)}, bf16[4,64,1024]{2,1,0:T(8,128)(2,1)}, bf16[64,1024]{1,0:T(8,128)(2,1)}) custom-call(s32[1]{0:T(128)} %bitcast.core_ref, bf16[8,128,4096]{2,1,0:T(8,128)(2,1)} %bitcast.23, bf16[4096,512]{1,0:T(8,128)(2,1)} %wa_hbm.1, bf16[4096,512]{1,0:T(8,128)(2,1)} %collective-permute-done.wb_hbm), custom_call_target="tpu_custom_call" | custom-call | flops 1200000000 | bytes 1200000 | tf_op jit(solution)/shard_map/pallas_call | solution.py:110
  28.1 4.7 %all-to-all-done = bf16[16,3,16,896]{3,2,1,0:T(8,128)(2,1)} async-done(((bf16[16,3,16,896]{3,2,1,0:T(8,128)(2,1)}), bf16[16,3,16,896]{3,2,1,0:T(8,128)(2,1)}, u32[]{:S(2)}, u32[]{:S(2)}) %all-to-all-start) | async-done | bytes 1376288 | tf_op jit(solution)/shard_map/all_to_all | solution.py:252
  32.8 3.0 %shard_map.93 = (bf16[8,16,896]{2,1,0:T(8,128)(2,1)}, bf16[8,16,896]{2,1,0:T(8,128)(2,1)}, bf16[8,16,896]{2,1,0:T(8,128)(2,1)}, bf16[8,16,896]{2,1,0:T(8,128)(2,1)}) custom-call(s32[32]{0:T(128)} %reshape.87.index_ref, s32[1]{0:T(128)} %constant.52.clone.1.start_ref, bf16[48,16,896]{2,1,0:T(8,128)(2,1)} %bitcast.9.source_ref), custom_call_target="tpu_custom_call" | custom-call | flops 400000000 | bytes 400000 | tf_op jit(solution)/shard_map/pallas_call | solution.py:59
  35.8 3.7 %collective-permute-start.8 = (bf16[128,896]{1,0:T(8,128)(2,1)}, bf16[128,896]{1,0:T(8,128)(2,1)S(1)}, u32[]{:S(2)}, u32[]{:S(2)}) collective-permute-start(bf16[128,896]{1,0:T(8,128)(2,1)} %bitcast.41), channel_id=1, source_target_pairs={{0,1},{1,0},{2,3},{3,2},{4,5},{5,4},{6,7},{7,6},{8,9},{9,8},{10,11... | collective-permute-start | bytes 688136 | tf_op jit(solution)/shard_map/ppermute | solution.py:278
  39.5 1.6 %collective-permute-start.6 = (bf16[128,896]{1,0:T(8,128)(2,1)}, bf16[128,896]{1,0:T(8,128)(2,1)S(1)}, u32[]{:S(2)}, u32[]{:S(2)}) collective-permute-start(bf16[128,896]{1,0:T(8,128)(2,1)} %bitcast.42), channel_id=1, source_target_pairs={{0,3},{1,2},{2,5},{3,4},{4,7},{5,6},{6,1},{7,0},{8,11},{9,10},{10,... | collective-permute-start | bytes 688136 | tf_op jit(solution)/shard_map/ppermute | solution.py:278
  41.1 2.2 %collective-permute-start.5 = (bf16[128,896]{1,0:T(8,128)(2,1)}, bf16[128,896]{1,0:T(8,128)(2,1)S(1)}, u32[]{:S(2)}, u32[]{:S(2)}) collective-permute-start(bf16[128,896]{1,0:T(8,128)(2,1)} %bitcast.43), channel_id=1, source_target_pairs={{0,7},{1,6},{2,1},{3,0},{4,3},{5,2},{6,5},{7,4},{8,15},{9,14},{10,... | collective-permute-start | bytes 688136 | tf_op jit(solution)/shard_map/ppermute | solution.py:278
  43.3 1.7 %collective-permute-start.7 = (bf16[128,896]{1,0:T(8,128)(2,1)}, bf16[128,896]{1,0:T(8,128)(2,1)S(1)}, u32[]{:S(2)}, u32[]{:S(2)}) collective-permute-start(bf16[128,896]{1,0:T(8,128)(2,1)} %bitcast.28), channel_id=1, source_target_pairs={{0,6},{1,7},{2,0},{3,1},{4,2},{5,3},{6,4},{7,5},{8,14},{9,15},{10,... | collective-permute-start | bytes 688136 | tf_op jit(solution)/shard_map/ppermute | solution.py:278
  45.1 4.6 %collective-permute-done.6.refs_4_ = bf16[128,896]{1,0:T(8,128)(2,1)S(1)} collective-permute-done((bf16[128,896]{1,0:T(8,128)(2,1)}, bf16[128,896]{1,0:T(8,128)(2,1)S(1)}, u32[]{:S(2)}, u32[]{:S(2)}) %collective-permute-start.6) | collective-permute-done | bytes 229408 | tf_op jit(solution)/shard_map/ppermute | solution.py:278
  49.6 4.1 %collective-permute-done.7.refs_5_ = bf16[128,896]{1,0:T(8,128)(2,1)S(1)} collective-permute-done((bf16[128,896]{1,0:T(8,128)(2,1)}, bf16[128,896]{1,0:T(8,128)(2,1)S(1)}, u32[]{:S(2)}, u32[]{:S(2)}) %collective-permute-start.7) | collective-permute-done | bytes 229408 | tf_op jit(solution)/shard_map/ppermute | solution.py:278
  53.8 0.4 collective-permute-done.4.refs_2_
  54.2 1.5 %collective-permute-start.9 = (bf16[128,896]{1,0:T(8,128)(2,1)S(1)}, bf16[128,896]{1,0:T(8,128)(2,1)S(1)}, u32[]{:S(2)}, u32[]{:S(2)}) collective-permute-start(bf16[128,896]{1,0:T(8,128)(2,1)S(1)} %collective-permute-done.4.refs_2_), channel_id=1, source_target_pairs={{0,2},{1,3},{2,4},{3,5},{4,6},{5,7},{6,0},{7,1},{8,10},{9,11},{10,... | collective-permute-start | bytes 688136 | tf_op jit(solution)/shard_map/ppermute | solution.py:278
  55.7 1.3 collective-permute-start.10
  57.0 1.3 collective-permute-start.11
  58.3 1.5 collective-permute-start.15
  59.8 4.0 %collective-permute-done.11.crossing_hbm = bf16[64,1024]{1,0:T(8,128)(2,1)S(1)} collective-permute-done((bf16[64,1024]{1,0:T(8,128)(2,1)}, bf16[64,1024]{1,0:T(8,128)(2,1)S(1)}, u32[]{:S(2)}, u32[]{:S(2)}) %collective-permute-start.11) | collective-permute-done | bytes 131104 | tf_op jit(solution)/shard_map/ppermute | solution.py:302
  63.8 0.5 collective-permute-start.14
  64.5 0.7 copy-done.22
  65.2 3.1 %collective-permute-start.13 = (bf16[128,896]{1,0:T(8,128)(2,1)}, bf16[128,896]{1,0:T(8,128)(2,1)}, u32[]{:S(2)}, u32[]{:S(2)}) collective-permute-start(bf16[128,896]{1,0:T(8,128)(2,1)} %bitcast.40), channel_id=1, source_target_pairs={{0,7},{1,6},{2,1},{3,0},{4,3},{5,2},{6,5},{7,4},{8,15},{9,14},{10,... | collective-permute-start | bytes 688136 | tf_op jit(solution)/shard_map/ppermute | solution.py:278
  68.3 5.0 %collective-permute-done.14.refs_4_ = bf16[128,896]{1,0:T(8,128)(2,1)S(1)} collective-permute-done((bf16[128,896]{1,0:T(8,128)(2,1)}, bf16[128,896]{1,0:T(8,128)(2,1)S(1)}, u32[]{:S(2)}, u32[]{:S(2)}) %collective-permute-start.14) | collective-permute-done | bytes 229408 | tf_op jit(solution)/shard_map/ppermute | solution.py:278
  73.4 0.5 collective-permute-done.13.refs_3_
  73.9 0.9 collective-permute-start.17
  74.7 2.4 %collective-permute-start.18 = (bf16[128,896]{1,0:T(8,128)(2,1)}, bf16[128,896]{1,0:T(8,128)(2,1)S(1)}, u32[]{:S(2)}, u32[]{:S(2)}) collective-permute-start(bf16[128,896]{1,0:T(8,128)(2,1)} %collective-permute-done.13.refs_3_), channel_id=1, source_target_pairs={{0,6},{1,7},{2,0},{3,1},{4,2},{5,3},{6,4},{7,5},{8,14},{9,15},{10,... | collective-permute-start | bytes 688136 | tf_op jit(solution)/shard_map/ppermute | solution.py:278
  77.2 0.6 pad_add_fusion
  77.8 13.6 %shard_map.94 = (bf16[64,2048]{1,0:T(8,128)(2,1)}, bf16[64,2048]{1,0:T(8,128)(2,1)}, bf16[64,2048]{1,0:T(8,128)(2,1)}, bf16[64,2048]{1,0:T(8,128)(2,1)}, bf16[64...) custom-call(s32[5]{0:T(128)} %get-tuple-element.143.place_ref, ...), custom_call_target="tpu_custom_call" | custom-call | flops 2000000000 | bytes 2000000 | tf_op jit(solution)/shard_map/pallas_call | solution.py:207
  91.6 2.7 %collective-permute-start.21 = (bf16[64,2048]{1,0:T(8,128)(2,1)}, bf16[64,2048]{1,0:T(8,128)(2,1)S(1)}, u32[]{:S(2)}, u32[]{:S(2)}) collective-permute-start(bf16[64,2048]{1,0:T(8,128)(2,1)} %get-tuple-element.125), channel_id=1, source_target_pairs={{0,6},{2,0},{4,2},{6,4},{1,7},{3,1},{5,3},{7,5},{8,14},{10,8},{12,... | collective-permute-start | bytes 786440 | tf_op jit(solution)/shard_map/ppermute | solution.py:25
  94.2 0.2 collective-permute-start.19
  94.5 1.2 collective-permute-start.23
  95.7 13.7 %shard_map.95 = (bf16[64,2048]{1,0:T(8,128)(2,1)}, bf16[64,2048]{1,0:T(8,128)(2,1)}, bf16[64,2048]{1,0:T(8,128)(2,1)}, bf16[64,2048]{1,0:T(8,128)(2,1)}, bf16[64...) custom-call(s32[5]{0:T(128)} %get-tuple-element.144.place_ref, ...), custom_call_target="tpu_custom_call" | custom-call | flops 2000000000 | bytes 2000000 | tf_op jit(solution)/shard_map/pallas_call | solution.py:207
  109.7 2.7 %collective-permute-start.24 = (bf16[64,2048]{1,0:T(8,128)(2,1)S(1)}, bf16[64,2048]{1,0:T(8,128)(2,1)S(1)}, u32[]{:S(2)}, u32[]{:S(2)}) collective-permute-start(bf16[64,2048]{1,0:T(8,128)(2,1)S(1)} %add_convert_fusion.5), channel_id=1, source_target_pairs={{0,6},{2,0},{4,2},{6,4},{1,7},{3,1},{5,3},{7,5},{8,14},{10,8},{12,... | collective-permute-start | bytes 786440 | tf_op jit(solution)/shard_map/ppermute | solution.py:25
  112.5 0.2 collective-permute-start.26
  112.7 1.2 collective-permute-start.27
  113.9 2.8 %collective-permute-done.22 = bf16[64,2048]{1,0:T(8,128)(2,1)S(1)} collective-permute-done((bf16[64,2048]{1,0:T(8,128)(2,1)S(1)}, bf16[64,2048]{1,0:T(8,128)(2,1)S(1)}, u32[]{:S(2)}, u32[]{:S(2)}) %collective-permute-start.22) | collective-permute-done | bytes 262176 | tf_op jit(solution)/shard_map/ppermute | solution.py:25
  116.8 5.6 %collective-permute-done.27 = bf16[64,2048]{1,0:T(8,128)(2,1)S(1)} collective-permute-done((bf16[64,2048]{1,0:T(8,128)(2,1)}, bf16[64,2048]{1,0:T(8,128)(2,1)S(1)}, u32[]{:S(2)}, u32[]{:S(2)}) %collective-permute-start.27) | collective-permute-done | bytes 262176 | tf_op jit(solution)/shard_map/ppermute | solution.py:25
  122.5 1.5 %collective-permute-start.28 = (bf16[64,2048]{1,0:T(8,128)(2,1)S(1)}, bf16[64,2048]{1,0:T(8,128)(2,1)S(1)}, u32[]{:S(2)}, u32[]{:S(2)}) collective-permute-start(bf16[64,2048]{1,0:T(8,128)(2,1)S(1)} %add_convert_fusion.3), channel_id=1, source_target_pairs={{0,2},{2,4},{4,6},{6,0},{1,3},{3,5},{5,7},{7,1},{8,10},{10,12},{12... | collective-permute-start | bytes 786440 | tf_op jit(solution)/shard_map/ppermute | solution.py:25
  124.2 3.1 %collective-permute-start.32 = (bf16[1,4096]{1,0:T(2,128)(2,1)S(1)}, bf16[1,4096]{1,0:T(2,128)(2,1)S(1)}, u32[]{:S(2)}, u32[]{:S(2)}) collective-permute-start(bf16[1,4096]{1,0:T(2,128)(2,1)S(1)} %fusion.1), channel_id=1, source_target_pairs={{1,7},{3,1},{5,3},{7,5},{9,15},{11,9},{13,11},{15,13},{17,23},{19,... | collective-permute-start | bytes 24584 | tf_op jit(solution)/shard_map/ppermute | solution.py:318
  127.4 0.6 collective-permute-done.30
  128.0 2.3 %collective-permute-start.31 = (bf16[64,2048]{1,0:T(8,128)(2,1)S(1)}, bf16[64,2048]{1,0:T(8,128)(2,1)S(1)}, u32[]{:S(2)}, u32[]{:S(2)}) collective-permute-start(bf16[64,2048]{1,0:T(8,128)(2,1)S(1)} %add_convert_fusion.1), channel_id=1, source_target_pairs={{0,6},{2,0},{4,2},{6,4},{1,7},{3,1},{5,3},{7,5},{8,14},{10,8},{12,... | collective-permute-start | bytes 786440 | tf_op jit(solution)/shard_map/ppermute | solution.py:25
  130.3 9.0 %collective-permute-start.25 = (bf16[64,4096]{1,0:T(8,128)(2,1)S(1)}, bf16[64,4096]{1,0:T(8,128)(2,1)S(1)}, u32[]{:S(2)}, u32[]{:S(2)}) collective-permute-start(bf16[64,4096]{1,0:T(8,128)(2,1)S(1)} %pad_maximum_fusion.1), channel_id=1, source_target_pairs={{0,1},{1,8},{2,3},{3,2},{4,5},{5,4},{6,7},{7,6},{8,9},{9,16},{10,1... | collective-permute-start | bytes 1572872 | tf_op jit(solution)/shard_map/ppermute | solution.py:327
  139.6 5.8 %collective-permute-done.25 = bf16[64,4096]{1,0:T(8,128)(2,1)S(1)} collective-permute-done((bf16[64,4096]{1,0:T(8,128)(2,1)S(1)}, bf16[64,4096]{1,0:T(8,128)(2,1)S(1)}, u32[]{:S(2)}, u32[]{:S(2)}) %collective-permute-start.25) | collective-permute-done | bytes 524320 | tf_op jit(solution)/shard_map/ppermute | solution.py:327
  145.6 1.1 pad_maximum_fusion
  (114 shorter events, 2.6 us)
Async XLA Ops:
  0.0 16.0 %collective-permute-start = (bf16[4096,512]{1,0:T(8,128)(2,1)}, bf16[4096,512]{1,0:T(8,128)(2,1)}, u32[]{:S(2)}, u32[]{:S(2)}) collective-permute-start(bf16[4096,512]{1,0:T(8,128)(2,1)} %wa_hbm.1), channel_id=1, source_target_pairs={{0,1},{1,0},{2,3},{3,2},{4,5},{5,4},{6,7},{7,6},{8,9},{9,8},{10,11... | collective-permute-start | bytes 12582920 | tf_op jit(solution)/shard_map/ppermute | solution.py:25
  1.4 31.4 %collective-permute-start.3 = (bf16[512,4096]{1,0:T(8,128)(2,1)}, bf16[512,4096]{1,0:T(8,128)(2,1)}, u32[]{:S(2)}, u32[]{:S(2)}) collective-permute-start(bf16[512,4096]{1,0:T(8,128)(2,1)} %refs_12_.1), channel_id=1, source_target_pairs={{0,1},{1,0},{2,3},{3,2},{4,5},{5,4},{6,7},{7,6},{8,9},{9,8},{10,11... | collective-permute-start | bytes 12582920 | tf_op jit(solution)/shard_map/ppermute | solution.py:25
  6.8 26.0 %all-to-all-start = ((bf16[16,3,16,896]{3,2,1,0:T(8,128)(2,1)}), bf16[16,3,16,896]{3,2,1,0:T(8,128)(2,1)}, u32[]{:S(2)}, u32[]{:S(2)}) async-start(bf16[16,3,16,896]{3,2,1,0:T(8,128)(2,1)} %bitcast.24), calls=%async_computation | async-start | bytes 2752512 | tf_op jit(solution)/shard_map/all_to_all | solution.py:252
  13.8 14.2 %collective-permute-start.1 = (bf16[896,512]{1,0:T(8,128)(2,1)S(1)}, bf16[896,512]{1,0:T(8,128)(2,1)S(1)}, u32[]{:S(2)}, u32[]{:S(2)}) collective-permute-start(bf16[896,512]{1,0:T(8,128)(2,1)S(1)} %copy-done), channel_id=1, source_target_pairs={{0,1},{1,0},{2,3},{3,2},{4,5},{5,4},{6,7},{7,6},{8,9},{9,8},{10,11... | collective-permute-start | bytes 2752520 | tf_op jit(solution)/shard_map/ppermute | solution.py:25
  14.7 13.4 %collective-permute-start.2 = (bf16[896,512]{1,0:T(8,128)(2,1)S(1)}, bf16[896,512]{1,0:T(8,128)(2,1)}, u32[]{:S(2)}, u32[]{:S(2)}) collective-permute-start(bf16[896,512]{1,0:T(8,128)(2,1)S(1)} %copy-done.1), channel_id=1, source_target_pairs={{0,1},{1,0},{2,3},{3,2},{4,5},{5,4},{6,7},{7,6},{8,9},{9,8},{10,11... | collective-permute-start | bytes 2752520 | tf_op jit(solution)/shard_map/ppermute | solution.py:25
  16.0 52.3 %copy-start.25 = (s32[4]{0:T(128)S(1)}, s32[4]{0:T(128)}, u32[]{:S(2)}) copy-start(s32[4]{0:T(128)} %constant.55.clone) | copy-start | bytes 52
  28.1 49.7 %copy-start.2 = (bf16[896,512]{1,0:T(8,128)(2,1)}, bf16[896,512]{1,0:T(8,128)(2,1)S(1)}, u32[]{:S(2)}) copy-start(bf16[896,512]{1,0:T(8,128)(2,1)S(1)} %collective-permute-done.1.refs_10_) | copy-start | bytes 2752516
  35.8 9.2 %collective-permute-start.8 = (bf16[128,896]{1,0:T(8,128)(2,1)}, bf16[128,896]{1,0:T(8,128)(2,1)S(1)}, u32[]{:S(2)}, u32[]{:S(2)}) collective-permute-start(bf16[128,896]{1,0:T(8,128)(2,1)} %bitcast.41), channel_id=1, source_target_pairs={{0,1},{1,0},{2,3},{3,2},{4,5},{5,4},{6,7},{7,6},{8,9},{9,8},{10,11... | collective-permute-start | bytes 688136 | tf_op jit(solution)/shard_map/ppermute | solution.py:278
  39.5 10.1 %collective-permute-start.6 = (bf16[128,896]{1,0:T(8,128)(2,1)}, bf16[128,896]{1,0:T(8,128)(2,1)S(1)}, u32[]{:S(2)}, u32[]{:S(2)}) collective-permute-start(bf16[128,896]{1,0:T(8,128)(2,1)} %bitcast.42), channel_id=1, source_target_pairs={{0,3},{1,2},{2,5},{3,4},{4,7},{5,6},{6,1},{7,0},{8,11},{9,10},{10,... | collective-permute-start | bytes 688136 | tf_op jit(solution)/shard_map/ppermute | solution.py:278
  41.1 8.5 %collective-permute-start.5 = (bf16[128,896]{1,0:T(8,128)(2,1)}, bf16[128,896]{1,0:T(8,128)(2,1)S(1)}, u32[]{:S(2)}, u32[]{:S(2)}) collective-permute-start(bf16[128,896]{1,0:T(8,128)(2,1)} %bitcast.43), channel_id=1, source_target_pairs={{0,7},{1,6},{2,1},{3,0},{4,3},{5,2},{6,5},{7,4},{8,15},{9,14},{10,... | collective-permute-start | bytes 688136 | tf_op jit(solution)/shard_map/ppermute | solution.py:278
  43.3 10.4 %collective-permute-start.7 = (bf16[128,896]{1,0:T(8,128)(2,1)}, bf16[128,896]{1,0:T(8,128)(2,1)S(1)}, u32[]{:S(2)}, u32[]{:S(2)}) collective-permute-start(bf16[128,896]{1,0:T(8,128)(2,1)} %bitcast.28), channel_id=1, source_target_pairs={{0,6},{1,7},{2,0},{3,1},{4,2},{5,3},{6,4},{7,5},{8,14},{9,15},{10,... | collective-permute-start | bytes 688136 | tf_op jit(solution)/shard_map/ppermute | solution.py:278
  45.0 9.1 %collective-permute-start.4 = (bf16[128,896]{1,0:T(8,128)(2,1)}, bf16[128,896]{1,0:T(8,128)(2,1)S(1)}, u32[]{:S(2)}, u32[]{:S(2)}) collective-permute-start(bf16[128,896]{1,0:T(8,128)(2,1)} %bitcast.29), channel_id=1, source_target_pairs={{0,2},{1,3},{2,4},{3,5},{4,6},{5,7},{6,0},{7,1},{8,10},{9,11},{10,... | collective-permute-start | bytes 688136 | tf_op jit(solution)/shard_map/ppermute | solution.py:278
  45.0 32.7 %copy-start.12 = (bf16[128,896]{1,0:T(8,128)(2,1)}, bf16[128,896]{1,0:T(8,128)(2,1)S(1)}, u32[]{:S(2)}) copy-start(bf16[128,896]{1,0:T(8,128)(2,1)S(1)} %collective-permute-done.8.refs_1_) | copy-start | bytes 688132
  49.6 28.1 %copy-start.14 = (bf16[128,896]{1,0:T(8,128)(2,1)}, bf16[128,896]{1,0:T(8,128)(2,1)S(1)}, u32[]{:S(2)}) copy-start(bf16[128,896]{1,0:T(8,128)(2,1)S(1)} %collective-permute-done.6.refs_4_) | copy-start | bytes 688132
  49.6 28.1 %copy-start.16 = (bf16[128,896]{1,0:T(8,128)(2,1)}, bf16[128,896]{1,0:T(8,128)(2,1)S(1)}, u32[]{:S(2)}) copy-start(bf16[128,896]{1,0:T(8,128)(2,1)S(1)} %collective-permute-done.5.refs_3_) | copy-start | bytes 688132
  53.8 24.0 %copy-start.17 = (bf16[128,896]{1,0:T(8,128)(2,1)}, bf16[128,896]{1,0:T(8,128)(2,1)S(1)}, u32[]{:S(2)}) copy-start(bf16[128,896]{1,0:T(8,128)(2,1)S(1)} %collective-permute-done.7.refs_5_) | copy-start | bytes 688132
  54.2 23.6 %copy-start.19 = (bf16[128,896]{1,0:T(8,128)(2,1)}, bf16[128,896]{1,0:T(8,128)(2,1)S(1)}, u32[]{:S(2)}) copy-start(bf16[128,896]{1,0:T(8,128)(2,1)S(1)} %collective-permute-done.4.refs_2_) | copy-start | bytes 688132
  54.2 9.6 %collective-permute-start.9 = (bf16[128,896]{1,0:T(8,128)(2,1)S(1)}, bf16[128,896]{1,0:T(8,128)(2,1)S(1)}, u32[]{:S(2)}, u32[]{:S(2)}) collective-permute-start(bf16[128,896]{1,0:T(8,128)(2,1)S(1)} %collective-permute-done.4.refs_2_), channel_id=1, source_target_pairs={{0,2},{1,3},{2,4},{3,5},{4,6},{5,7},{6,0},{7,1},{8,10},{9,11},{10,... | collective-permute-start | bytes 688136 | tf_op jit(solution)/shard_map/ppermute | solution.py:278
  55.7 8.7 %collective-permute-start.10 = (bf16[128,896]{1,0:T(8,128)(2,1)S(1)}, bf16[128,896]{1,0:T(8,128)(2,1)S(1)}, u32[]{:S(2)}, u32[]{:S(2)}) collective-permute-start(bf16[128,896]{1,0:T(8,128)(2,1)S(1)} %collective-permute-done.5.refs_3_), channel_id=1, source_target_pairs={{0,6},{1,7},{2,0},{3,1},{4,2},{5,3},{6,4},{7,5},{8,14},{9,15},{10,... | collective-permute-start | bytes 688136 | tf_op jit(solution)/shard_map/ppermute | solution.py:278
  57.0 6.8 %collective-permute-start.11 = (bf16[64,1024]{1,0:T(8,128)(2,1)}, bf16[64,1024]{1,0:T(8,128)(2,1)S(1)}, u32[]{:S(2)}, u32[]{:S(2)}) collective-permute-start(bf16[64,1024]{1,0:T(8,128)(2,1)} %get-tuple-element.82), channel_id=1, source_target_pairs={{8,1},{16,9},{24,17},{32,25},{40,33},{48,41},{56,49},{64,57},{72,6... | collective-permute-start | bytes 393224 | tf_op jit(solution)/shard_map/ppermute | solution.py:302
  58.3 10.0 %collective-permute-start.15 = (bf16[128,896]{1,0:T(8,128)(2,1)}, bf16[128,896]{1,0:T(8,128)(2,1)S(1)}, u32[]{:S(2)}, u32[]{:S(2)}) collective-permute-start(bf16[128,896]{1,0:T(8,128)(2,1)} %bitcast.25), channel_id=1, source_target_pairs={{0,6},{1,7},{2,0},{3,1},{4,2},{5,3},{6,4},{7,5},{8,14},{9,15},{10,... | collective-permute-start | bytes 688136 | tf_op jit(solution)/shard_map/ppermute | solution.py:278
  59.7 8.6 %collective-permute-start.12 = (bf16[128,896]{1,0:T(8,128)(2,1)}, bf16[128,896]{1,0:T(8,128)(2,1)S(1)}, u32[]{:S(2)}, u32[]{:S(2)}) collective-permute-start(bf16[128,896]{1,0:T(8,128)(2,1)} %bitcast.26), channel_id=1, source_target_pairs={{0,2},{1,3},{2,4},{3,5},{4,6},{5,7},{6,0},{7,1},{8,10},{9,11},{10,... | collective-permute-start | bytes 688136 | tf_op jit(solution)/shard_map/ppermute | solution.py:278
  63.8 4.6 %collective-permute-start.16 = (bf16[128,896]{1,0:T(8,128)(2,1)}, bf16[128,896]{1,0:T(8,128)(2,1)S(1)}, u32[]{:S(2)}, u32[]{:S(2)}) collective-permute-start(bf16[128,896]{1,0:T(8,128)(2,1)} %bitcast.38), channel_id=1, source_target_pairs={{0,1},{1,0},{2,3},{3,2},{4,5},{5,4},{6,7},{7,6},{8,9},{9,8},{10,11... | collective-permute-start | bytes 688136 | tf_op jit(solution)/shard_map/ppermute | solution.py:278
  63.8 9.6 %collective-permute-start.14 = (bf16[128,896]{1,0:T(8,128)(2,1)}, bf16[128,896]{1,0:T(8,128)(2,1)S(1)}, u32[]{:S(2)}, u32[]{:S(2)}) collective-permute-start(bf16[128,896]{1,0:T(8,128)(2,1)} %bitcast.39), channel_id=1, source_target_pairs={{0,3},{1,2},{2,5},{3,4},{4,7},{5,6},{6,1},{7,0},{8,11},{9,10},{10,... | collective-permute-start | bytes 688136 | tf_op jit(solution)/shard_map/ppermute | solution.py:278
  65.2 8.7 %collective-permute-start.13 = (bf16[128,896]{1,0:T(8,128)(2,1)}, bf16[128,896]{1,0:T(8,128)(2,1)}, u32[]{:S(2)}, u32[]{:S(2)}) collective-permute-start(bf16[128,896]{1,0:T(8,128)(2,1)} %bitcast.40), channel_id=1, source_target_pairs={{0,7},{1,6},{2,1},{3,0},{4,3},{5,2},{6,5},{7,4},{8,15},{9,14},{10,... | collective-permute-start | bytes 688136 | tf_op jit(solution)/shard_map/ppermute | solution.py:278
  68.3 23.1 %copy-start.13 = (bf16[128,896]{1,0:T(8,128)(2,1)}, bf16[128,896]{1,0:T(8,128)(2,1)S(1)}, u32[]{:S(2)}) copy-start(bf16[128,896]{1,0:T(8,128)(2,1)S(1)} %collective-permute-done.15.refs_5_) | copy-start | bytes 688132
  68.3 23.1 %copy-start.15 = (bf16[128,896]{1,0:T(8,128)(2,1)}, bf16[128,896]{1,0:T(8,128)(2,1)S(1)}, u32[]{:S(2)}) copy-start(bf16[128,896]{1,0:T(8,128)(2,1)S(1)} %collective-permute-done.12.refs_2_) | copy-start | bytes 688132
  68.3 23.1 %copy-start.18 = (bf16[128,896]{1,0:T(8,128)(2,1)}, bf16[128,896]{1,0:T(8,128)(2,1)S(1)}, u32[]{:S(2)}) copy-start(bf16[128,896]{1,0:T(8,128)(2,1)S(1)} %collective-permute-done.16.refs_1_) | copy-start | bytes 688132
  73.4 18.1 %copy-start.20 = (bf16[128,896]{1,0:T(8,128)(2,1)}, bf16[128,896]{1,0:T(8,128)(2,1)S(1)}, u32[]{:S(2)}) copy-start(bf16[128,896]{1,0:T(8,128)(2,1)S(1)} %collective-permute-done.14.refs_4_) | copy-start | bytes 688132
  73.9 17.6 %collective-permute-start.17 = (bf16[128,896]{1,0:T(8,128)(2,1)S(1)}, bf16[128,896]{1,0:T(8,128)(2,1)S(1)}, u32[]{:S(2)}, u32[]{:S(2)}) collective-permute-start(bf16[128,896]{1,0:T(8,128)(2,1)S(1)} %collective-permute-done.12.refs_2_), channel_id=1, source_target_pairs={{0,2},{1,3},{2,4},{3,5},{4,6},{5,7},{6,0},{7,1},{8,10},{9,11},{10,... | collective-permute-start | bytes 688136 | tf_op jit(solution)/shard_map/ppermute | solution.py:278
  74.7 16.7 %collective-permute-start.18 = (bf16[128,896]{1,0:T(8,128)(2,1)}, bf16[128,896]{1,0:T(8,128)(2,1)S(1)}, u32[]{:S(2)}, u32[]{:S(2)}) collective-permute-start(bf16[128,896]{1,0:T(8,128)(2,1)} %collective-permute-done.13.refs_3_), channel_id=1, source_target_pairs={{0,6},{1,7},{2,0},{3,1},{4,2},{5,3},{6,4},{7,5},{8,14},{9,15},{10,... | collective-permute-start | bytes 688136 | tf_op jit(solution)/shard_map/ppermute | solution.py:278
  91.5 18.0 %collective-permute-start.20 = (bf16[64,2048]{1,0:T(8,128)(2,1)}, bf16[64,2048]{1,0:T(8,128)(2,1)S(1)}, u32[]{:S(2)}, u32[]{:S(2)}) collective-permute-start(bf16[64,2048]{1,0:T(8,128)(2,1)} %get-tuple-element.124), channel_id=1, source_target_pairs={{0,2},{2,4},{4,6},{6,0},{1,3},{3,5},{5,7},{7,1},{8,10},{10,12},{12... | collective-permute-start | bytes 786440 | tf_op jit(solution)/shard_map/ppermute | solution.py:25
  91.6 17.9 %collective-permute-start.21 = (bf16[64,2048]{1,0:T(8,128)(2,1)}, bf16[64,2048]{1,0:T(8,128)(2,1)S(1)}, u32[]{:S(2)}, u32[]{:S(2)}) collective-permute-start(bf16[64,2048]{1,0:T(8,128)(2,1)} %get-tuple-element.125), channel_id=1, source_target_pairs={{0,6},{2,0},{4,2},{6,4},{1,7},{3,1},{5,3},{7,5},{8,14},{10,8},{12,... | collective-permute-start | bytes 786440 | tf_op jit(solution)/shard_map/ppermute | solution.py:25
  94.2 18.5 %collective-permute-start.19 = (bf16[64,2048]{1,0:T(8,128)(2,1)}, bf16[64,2048]{1,0:T(8,128)(2,1)S(1)}, u32[]{:S(2)}, u32[]{:S(2)}) collective-permute-start(bf16[64,2048]{1,0:T(8,128)(2,1)} %get-tuple-element.108), channel_id=1, source_target_pairs={{0,6},{2,0},{4,2},{6,4},{1,7},{3,1},{5,3},{7,5},{8,14},{10,8},{12,... | collective-permute-start | bytes 786440 | tf_op jit(solution)/shard_map/ppermute | solution.py:25
  94.5 28.1 %collective-permute-start.23 = (bf16[64,2048]{1,0:T(8,128)(2,1)}, bf16[64,2048]{1,0:T(8,128)(2,1)S(1)}, u32[]{:S(2)}, u32[]{:S(2)}) collective-permute-start(bf16[64,2048]{1,0:T(8,128)(2,1)} %get-tuple-element.128), channel_id=1, source_target_pairs={{0,2},{2,4},{4,6},{6,0},{1,3},{3,5},{5,7},{7,1},{8,10},{10,12},{12... | collective-permute-start | bytes 786440 | tf_op jit(solution)/shard_map/ppermute | solution.py:25
  95.7 21.0 %copy-start.11 = (bf16[64,2048]{1,0:T(8,128)(2,1)S(1)}, bf16[64,2048]{1,0:T(8,128)(2,1)}, u32[]{:S(2)}) copy-start(bf16[64,2048]{1,0:T(8,128)(2,1)} %get-tuple-element.107) | copy-start | bytes 786436
  109.6 7.1 %collective-permute-start.22 = (bf16[64,2048]{1,0:T(8,128)(2,1)S(1)}, bf16[64,2048]{1,0:T(8,128)(2,1)S(1)}, u32[]{:S(2)}, u32[]{:S(2)}) collective-permute-start(bf16[64,2048]{1,0:T(8,128)(2,1)S(1)} %add_convert_fusion.7), channel_id=1, source_target_pairs={{0,2},{2,4},{4,6},{6,0},{1,3},{3,5},{5,7},{7,1},{8,10},{10,12},{12... | collective-permute-start | bytes 786440 | tf_op jit(solution)/shard_map/ppermute | solution.py:25
  109.7 18.2 %copy-start.4 = (bf16[64,2048]{1,0:T(8,128)(2,1)S(1)}, bf16[64,2048]{1,0:T(8,128)(2,1)}, u32[]{:S(2)}) copy-start(bf16[64,2048]{1,0:T(8,128)(2,1)} %get-tuple-element.137) | copy-start | bytes 786436
  109.7 14.3 %collective-permute-start.24 = (bf16[64,2048]{1,0:T(8,128)(2,1)S(1)}, bf16[64,2048]{1,0:T(8,128)(2,1)S(1)}, u32[]{:S(2)}, u32[]{:S(2)}) collective-permute-start(bf16[64,2048]{1,0:T(8,128)(2,1)S(1)} %add_convert_fusion.5), channel_id=1, source_target_pairs={{0,6},{2,0},{4,2},{6,4},{1,7},{3,1},{5,3},{7,5},{8,14},{10,8},{12,... | collective-permute-start | bytes 786440 | tf_op jit(solution)/shard_map/ppermute | solution.py:25
  112.5 26.9 %collective-permute-start.26 = (bf16[64,2048]{1,0:T(8,128)(2,1)}, bf16[64,2048]{1,0:T(8,128)(2,1)S(1)}, u32[]{:S(2)}, u32[]{:S(2)}) collective-permute-start(bf16[64,2048]{1,0:T(8,128)(2,1)} %get-tuple-element.132), channel_id=1, source_target_pairs={{0,6},{2,0},{4,2},{6,4},{1,7},{3,1},{5,3},{7,5},{8,14},{10,8},{12,... | collective-permute-start | bytes 786440 | tf_op jit(solution)/shard_map/ppermute | solution.py:25
  112.7 9.7 %collective-permute-start.27 = (bf16[64,2048]{1,0:T(8,128)(2,1)}, bf16[64,2048]{1,0:T(8,128)(2,1)S(1)}, u32[]{:S(2)}, u32[]{:S(2)}) collective-permute-start(bf16[64,2048]{1,0:T(8,128)(2,1)} %get-tuple-element.134), channel_id=1, source_target_pairs={{0,2},{2,4},{4,6},{6,0},{1,3},{3,5},{5,7},{7,1},{8,10},{10,12},{12... | collective-permute-start | bytes 786440 | tf_op jit(solution)/shard_map/ppermute | solution.py:25
  116.7 22.8 %collective-permute-start.29 = (bf16[64,2048]{1,0:T(8,128)(2,1)}, bf16[64,2048]{1,0:T(8,128)(2,1)S(1)}, u32[]{:S(2)}, u32[]{:S(2)}) collective-permute-start(bf16[64,2048]{1,0:T(8,128)(2,1)} %get-tuple-element.136), channel_id=1, source_target_pairs={{0,2},{2,4},{4,6},{6,0},{1,3},{3,5},{5,7},{7,1},{8,10},{10,12},{12... | collective-permute-start | bytes 786440 | tf_op jit(solution)/shard_map/ppermute | solution.py:25
  116.8 22.6 %copy-start.10 = (bf16[64,2048]{1,0:T(8,128)(2,1)S(1)}, bf16[64,2048]{1,0:T(8,128)(2,1)}, u32[]{:S(2)}) copy-start(bf16[64,2048]{1,0:T(8,128)(2,1)} %get-tuple-element.131) | copy-start | bytes 786436
  122.4 5.5 %collective-permute-start.30 = (bf16[64,2048]{1,0:T(8,128)(2,1)S(1)}, bf16[64,2048]{1,0:T(8,128)(2,1)S(1)}, u32[]{:S(2)}, u32[]{:S(2)}) collective-permute-start(bf16[64,2048]{1,0:T(8,128)(2,1)S(1)} %copy-done.26), channel_id=1, source_target_pairs={{0,6},{2,0},{4,2},{6,4},{1,7},{3,1},{5,3},{7,5},{8,14},{10,8},{12,... | collective-permute-start | bytes 786440 | tf_op jit(solution)/shard_map/ppermute | solution.py:25
  122.5 16.9 %collective-permute-start.28 = (bf16[64,2048]{1,0:T(8,128)(2,1)S(1)}, bf16[64,2048]{1,0:T(8,128)(2,1)S(1)}, u32[]{:S(2)}, u32[]{:S(2)}) collective-permute-start(bf16[64,2048]{1,0:T(8,128)(2,1)S(1)} %add_convert_fusion.3), channel_id=1, source_target_pairs={{0,2},{2,4},{4,6},{6,0},{1,3},{3,5},{5,7},{7,1},{8,10},{10,12},{12... | collective-permute-start | bytes 786440 | tf_op jit(solution)/shard_map/ppermute | solution.py:25
  124.2 6.1 %collective-permute-start.32 = (bf16[1,4096]{1,0:T(2,128)(2,1)S(1)}, bf16[1,4096]{1,0:T(2,128)(2,1)S(1)}, u32[]{:S(2)}, u32[]{:S(2)}) collective-permute-start(bf16[1,4096]{1,0:T(2,128)(2,1)S(1)} %fusion.1), channel_id=1, source_target_pairs={{1,7},{3,1},{5,3},{7,5},{9,15},{11,9},{13,11},{15,13},{17,23},{19,... | collective-permute-start | bytes 24584 | tf_op jit(solution)/shard_map/ppermute | solution.py:318
  128.0 11.5 %collective-permute-start.31 = (bf16[64,2048]{1,0:T(8,128)(2,1)S(1)}, bf16[64,2048]{1,0:T(8,128)(2,1)S(1)}, u32[]{:S(2)}, u32[]{:S(2)}) collective-permute-start(bf16[64,2048]{1,0:T(8,128)(2,1)S(1)} %add_convert_fusion.1), channel_id=1, source_target_pairs={{0,6},{2,0},{4,2},{6,4},{1,7},{3,1},{5,3},{7,5},{8,14},{10,8},{12,... | collective-permute-start | bytes 786440 | tf_op jit(solution)/shard_map/ppermute | solution.py:25
  130.3 15.2 %collective-permute-start.25 = (bf16[64,4096]{1,0:T(8,128)(2,1)S(1)}, bf16[64,4096]{1,0:T(8,128)(2,1)S(1)}, u32[]{:S(2)}, u32[]{:S(2)}) collective-permute-start(bf16[64,4096]{1,0:T(8,128)(2,1)S(1)} %pad_maximum_fusion.1), channel_id=1, source_target_pairs={{0,1},{1,8},{2,3},{3,2},{4,5},{5,4},{6,7},{7,6},{8,9},{9,16},{10,1... | collective-permute-start | bytes 1572872 | tf_op jit(solution)/shard_map/ppermute | solution.py:327
  (13 other events, 124.3 us)

commit v4 on v3

--- a/solution.py
+++ b/solution.py
@@ -1,3 +1,4 @@
+import functools
 import math
 
 import jax
@@ -127,34 +128,99 @@
     )(core.reshape(1), blocks, weight_a, weight_b)
 
 
-def span_kernel(place_ref, q_hbm, crossing_hbm, *refs):
-    row_hbm, weight_hbm, out_hbm, out_refs = refs[:8], refs[8:14], refs[14:22], refs[22:30]
-    q_ref, crossing_ref, rows_ref, weight_refs, kv_ref, context_ref, sems, out_sem = (
-        *refs[30:33],
-        refs[33:39],
-        *refs[39:43],
-    )
-    half, model = weight_refs[4].shape
+def project_kernel(*refs):
+    row_hbm, weight_hbm, out_hbm = refs[:6], refs[6:10], refs[10:14]
+    rows_ref, weight_refs, out_refs, sems = refs[14], refs[15:19], refs[19:23], refs[23]
     parts, rows, enc = rows_ref.shape
     row_copies = [pltpu.make_async_copy(row_hbm[i], rows_ref.at[i], sems.at[i]) for i in range(parts)]
-    weight_copies = [pltpu.make_async_copy(weight_hbm[i], weight_refs[i], sems.at[8 + i]) for i in range(6)]
-    query_copies = [
-        pltpu.make_async_copy(q_hbm, q_ref, sems.at[14]),
-        pltpu.make_async_copy(crossing_hbm, crossing_ref, sems.at[15]),
-    ]
-    for copy in row_copies + weight_copies[:4] + query_copies + weight_copies[4:]:
+    weight_copies = [pltpu.make_async_copy(weight_hbm[i], weight_refs[i], sems.at[parts + i]) for i in range(4)]
+    out_copies = [pltpu.make_async_copy(out_refs[i], out_hbm[i], sems.at[parts + 4 + i]) for i in range(4)]
+    for copy in row_copies + weight_copies:
         copy.start()
-
     for copy in row_copies:
         copy.wait()
     for i in range(4):
         weight_copies[i].wait()
-        for part in range(0, parts, 4):
-            product = dot(rows_ref[part : part + 4].reshape(4 * rows, enc), weight_refs[i][...]).astype(BF16)
-            kv_ref[part : part + 4, :, :, i * half : (i + 1) * half] = product.reshape((4,) + kv_ref.shape[1:3] + (half,))
-
-    for copy in query_copies:
-        copy.wait()
+        for part in range(0, parts, 2):
+            product = dot(rows_ref[part : part + 2].reshape(2 * rows, enc), weight_refs[i][...]).astype(BF16)
+            out_refs[i][part : part + 2] = product.reshape((2,) + out_refs[i].shape[1:])
+        out_copies[i].start()
+    for copy in out_copies:
+        copy.wait()
+
+
+def project(weights, parts):
+    rows, enc = parts[0].shape
+    width = weights[0].shape[1]
+    shape = (len(parts), 2, N_Z, rows // (2 * N_Z), width)
+    return pl.pallas_call(
+        project_kernel,
+        in_specs=[pl.BlockSpec(memory_space=pltpu.HBM)] * (len(parts) + 4),
+        out_specs=[pl.BlockSpec(memory_space=pltpu.HBM)] * 4,
+        out_shape=[jax.ShapeDtypeStruct(shape, BF16)] * 4,
+        scratch_shapes=[pltpu.VMEM((len(parts), rows, enc), BF16)]
+        + [pltpu.VMEM((enc, width), BF16)] * 4
+        + [pltpu.VMEM(shape, BF16)] * 4
+        + [pltpu.SemaphoreType.DMA((len(parts) + 8,))],
+        cost_estimate=cost(2e9),
+        compiler_params=pltpu.CompilerParams(vmem_limit_bytes=LIMIT),
+    )(*parts, *weights)
+
+
+def span_kernel(group, place_ref, *refs):
+    refs = list(refs)
+
+    def take(count):
+        taken = refs[:count]
+        del refs[:count]
+        return taken
+
+    near_hbm, far_hbm = take(4), take(6 if group == 0 else 4)
+    q_hbm, crossing_hbm = take(2)
+    out_weight_hbm, out_hbm = take(2), take(6)
+    later_hbm = take(4 if group == 0 else 0)
+    kv_refs, out_refs, out_weight_refs = take(4), take(6), take(2)
+    q_ref, crossing_ref, context_ref = take(3)
+    rows_ref, *weight_refs = take(5 if group == 0 else 0) or [None]
+    later_refs = take(4 if group == 0 else 0)
+    in_sems, out_sems = refs
+    used = [0, 0]
+
+    def copy_in(source, target):
+        used[0] += 1
+        return pltpu.make_async_copy(source, target, in_sems.at[used[0] - 1])
+
+    def copy_out(source, target):
+        used[1] += 1
+        return pltpu.make_async_copy(source, target, out_sems.at[used[1] - 1])
+
+    half, model = out_weight_refs[0].shape
+    parts = near_hbm[0].shape[0]
+    if group == 0:
+        far_copies = [copy_in(far_hbm[i], rows_ref.at[i]) for i in range(2)]
+        weight_copies = [copy_in(far_hbm[2 + i], weight_refs[i]) for i in range(4)]
+    else:
+        far_copies = [copy_in(far_hbm[i], kv_refs[i].at[parts:]) for i in range(4)]
+        weight_copies = []
+    near_copies = [copy_in(near_hbm[i].at[:, group], kv_refs[i].at[:parts]) for i in range(4)]
+    query_copies = [copy_in(q_hbm, q_ref), copy_in(crossing_hbm, crossing_ref)]
+    out_weight_copies = [copy_in(out_weight_hbm[i], out_weight_refs[i]) for i in range(2)]
+    for copy in far_copies + weight_copies + near_copies + query_copies + out_weight_copies:
+        copy.start()
+    for copy in far_copies:
+        copy.wait()
+    later_copies = []
+    for i, copy in enumerate(weight_copies):
+        copy.wait()
+        product = dot(rows_ref[...].reshape(-1, rows_ref.shape[2]), weight_refs[i][...]).astype(BF16)
+        product = product.reshape(2, 2, *kv_refs[i].shape[1:])
+        kv_refs[i][parts:] = product[:, 0]
+        later_refs[i][...] = product[:, 1]
+        later_copies.append(copy_out(later_refs[i], later_hbm[i]))
+        later_copies[i].start()
+    for copy in near_copies + query_copies:
+        copy.wait()
+
     is_first_row = lax.broadcasted_iota(jnp.int32, (CL, HS), 0) == 0
     heads = [(side, lower) for side in (0, 1) for lower in range(0, half, HS)]
 
@@ -163,9 +229,10 @@
         scores = []
         for side, lower in heads:
             place = slice(side * half + lower, side * half + lower + HS)
-            q = jnp.where(is_first_row | jnp.logical_not(crosses), q_ref[span, :, place], crossing_ref[:, place])
-            start = 2 * side * half + lower
-            k = kv_ref[:, span, :, start : start + HS].reshape(-1, HS)
+            q = q_ref[span, :, place]
+            if group == 0:
+                q = jnp.where(is_first_row | jnp.logical_not(crosses), q, crossing_ref[:, place])
+            k = kv_refs[2 * side][:, span, :, lower : lower + HS].reshape(-1, HS)
             scores.append(lax.dot_general(q, k, (((1,), (1,)), ((), ())), preferred_element_type=F32))
         probs = []
         for score in scores:
@@ -174,61 +241,62 @@
             total = jnp.sum(weights, axis=-1, keepdims=True)
             probs.append((weights * (1.0 / total)).astype(BF16))
         for (side, lower), prob in zip(heads, probs):
-            start = (2 * side + 1) * half + lower
-            v = kv_ref[:, span, :, start : start + HS].reshape(-1, HS)
+            v = kv_refs[2 * side + 1][:, span, :, lower : lower + HS].reshape(-1, HS)
             context_ref[span, :, side * half + lower : side * half + lower + HS] = dot(prob, v).astype(BF16)
         return carry
 
     lax.fori_loop(0, N_Z, attend_span, 0)
 
-    for copy in weight_copies[4:]:
+    for copy in out_weight_copies:
         copy.wait()
     context = jnp.concatenate([context_ref[place_ref[i]] for i in range(N_Z)], axis=0)
+    up, down, above, below, here_left, here_right = out_refs
     tile = model // 4
+    out_copies = [copy_out(out_refs[i], out_hbm[i]) for i in range(6)]
     for lower in range(0, model, tile):
         place = slice(lower, lower + tile)
-        product = dot(context[:, :half], weight_refs[4][:, place]) + dot(context[:, half:], weight_refs[5][:, place])
-        product = product.astype(BF16)
-        side, start = lower // (model // 2), lower % (model // 2)
-        for i in range(N_Z):
-            out_refs[2 * i + side][:, start : start + tile] = product[i * CL : (i + 1) * CL]
-        if start + tile == model // 2:
-            for i in range(side, 2 * N_Z, 2):
-                pltpu.make_async_copy(out_refs[i], out_hbm[i], out_sem.at[i]).start()
-    for i in range(2 * N_Z):
-        pltpu.make_async_copy(out_refs[i], out_hbm[i], out_sem.at[i]).wait()
-
-
-def attend(places, queries, crossing, parts, weights):
+        product = dot(context[:, :half], out_weight_refs[0][:, place])
+        product = (product + dot(context[:, half:], out_weight_refs[1][:, place])).astype(BF16)
+        blocks = [product[i * CL : (i + 1) * CL] for i in range(N_Z)]
+        inner = slice(lower % (model // 2), lower % (model // 2) + tile)
+        if lower < model // 2:
+            up[:, place], down[:, place], above[:, inner], here_left[:, inner] = blocks[0], blocks[2], blocks[1], blocks[3]
+        else:
+            up[:, place], down[:, place], below[:, inner], here_right[:, inner] = blocks[1], blocks[0], blocks[2], blocks[3]
+        if lower + tile == model // 2:
+            out_copies[2].start()
+            out_copies[4].start()
+    for i in (0, 1, 3, 5):
+        out_copies[i].start()
+    for copy in later_copies + out_copies:
+        copy.wait()
+
+
+def attend(group, places, queries, crossing, near, far, out_weights):
     spans, tokens, width = queries.shape
-    half, model = weights[4].shape
-    rows, enc = parts[0].shape
-    out = jax.ShapeDtypeStruct((tokens, model // 2), BF16)
+    half, model = out_weights[0].shape
+    parts, _, _, rows, _ = near[0].shape
+    outs = [(tokens, model)] * 2 + [(tokens, model // 2)] * 4
+    scratch = [(parts + 2, spans, rows, half)] * 4 + outs + [(half, model)] * 2
+    scratch += [queries.shape, crossing.shape, queries.shape]
+    later = [(2, spans, rows, half)] * 4 if group == 0 else []
+    if group == 0:
+        scratch += [(2,) + far[0].shape] + [weight.shape for weight in far[2:]] + later
+    operands = (*near, *far, queries, crossing, *out_weights)
     return pl.pallas_call(
-        span_kernel,
+        functools.partial(span_kernel, group),
         grid_spec=pltpu.PrefetchScalarGridSpec(
             num_scalar_prefetch=1,
             grid=(1,),
-            in_specs=[pl.BlockSpec(memory_space=pltpu.HBM)] * 16,
-            out_specs=[pl.BlockSpec(memory_space=pltpu.HBM)] * 8,
-            scratch_shapes=[pltpu.VMEM(out.shape, BF16)] * 8
-            + [
-                pltpu.VMEM(queries.shape, BF16),
-                pltpu.VMEM(crossing.shape, BF16),
-                pltpu.VMEM((len(parts), rows, enc), BF16),
-            ]
-            + [pltpu.VMEM(weight.shape, BF16) for weight in weights]
-            + [
-                pltpu.VMEM((len(parts), spans, rows // spans, 4 * half), BF16),
-                pltpu.VMEM(queries.shape, BF16),
-                pltpu.SemaphoreType.DMA((16,)),
-                pltpu.SemaphoreType.DMA((8,)),
-            ],
+            in_specs=[pl.BlockSpec(memory_space=pltpu.HBM)] * len(operands),
+            out_specs=[pl.BlockSpec(memory_space=pltpu.HBM)] * (6 + len(later)),
+            scratch_shapes=[pltpu.VMEM(shape, BF16) for shape in scratch]
+            + [pltpu.SemaphoreType.DMA((len(operands),)), pltpu.SemaphoreType.DMA((6 + len(later),))],
         ),
-        out_shape=[out] * 8,
+        out_shape=[jax.ShapeDtypeStruct(shape, BF16) for shape in outs + later],
         cost_estimate=cost(5e9),
         compiler_params=pltpu.CompilerParams(vmem_limit_bytes=LIMIT),
-    )(places, queries, crossing, *parts, *weights)
+    )(places, *operands)
 
 
 def body(decoder, w_query, w_key, w_value, w_out, database, nb_shard, nb_slot):
@@ -264,10 +332,9 @@
     row_index = (my_shards * capacity + my_places).reshape(NEIGH, N_Z, N_CORE, 2)
     row_index = row_index.transpose(2, 3, 1, 0)[:, ::-1]
     row_index = jnp.where(core == 0, row_index, row_index[::-1]).reshape(-1)
-    group = row_index.shape[0] // 4
-    mine_a, mine_b, theirs_a, theirs_b = [
-        rows.reshape(-1, enc) for rows in pick(received, row_index, jnp.zeros((), jnp.int32), piece, [group] * 4)
-    ]
+    count = row_index.shape[0] // 2
+    mine, theirs = pick(received, row_index, jnp.zeros((), jnp.int32), piece, [count] * 2)
+    mine, theirs = mine.reshape(-1, enc), theirs.reshape(-1, enc)
 
     def hop(value, steps, cross):
         pairs = [
@@ -277,44 +344,43 @@
         ]
         return lax.ppermute(value, ("z", "core"), pairs)
 
-    def neighbours(mine, theirs):
-        return [hop(mine, 1, 0), hop(theirs, -1, 1), hop(theirs, 1, 1), hop(mine, -1, 0)]
-
-    def opposite(ring):
-        return hop(ring[0], 1, 0), hop(ring[1], -1, 0)
-
     def add(*terms):
         return sum(term.astype(F32) for term in terms).astype(BF16)
 
-    def total(here, down_left, up_left, up_right, down_right):
-        return jnp.concatenate([add(here[0], down_left, up_left), add(here[1], up_right, down_right)], axis=1)
+    side = model // 2
+
+    def total(here_left, here_right, up, down, up_left, down_right):
+        left, right = add(here_left, down[:, :side], up_left), add(here_right, up[:, side:], down_right)
+        return jnp.concatenate([left, right], axis=1)
 
     distance = jnp.array([2, 1, 3, 0], jnp.int32)
     places_a = jnp.append((z_index + distance + (N_Z - 1) * core) % N_Z, core).astype(jnp.int32)
     places_b = jnp.append((z_index + distance) % N_Z, 0).astype(jnp.int32)
 
-    ring_a, swapped_a = neighbours(mine_a, theirs_a), hop(theirs_a, 0, 1)
-    ring_a, swapped_a, crossing, mine_b, theirs_b = lax.optimization_barrier(
-        (ring_a, swapped_a, crossing, mine_b, theirs_b)
+    ring = [hop(mine, 1, 0), hop(theirs, -1, 1), hop(theirs, 1, 1), hop(mine, -1, 0)]
+    swapped = hop(theirs, 0, 1)
+    ring, swapped, crossing, places_a, places_b = lax.optimization_barrier(
+        (ring, swapped, crossing, places_a, places_b)
     )
-    far_a = opposite(ring_a)
-    ring_b, swapped_b = neighbours(mine_b, theirs_b), hop(theirs_b, 0, 1)
+    far = hop(ring[0], 1, 0), hop(ring[1], -1, 0)
     crossing = lax.ppermute(crossing, ("seq", "core"), [(2 * i + 2, 2 * i + 1) for i in range(n_seq - 1)])
-    far_a, crossing, ring_b, swapped_b = lax.optimization_barrier((far_a, crossing, ring_b, swapped_b))
-
-    far_b = opposite(ring_b)
-    sums_a = attend(places_a, second_queries, crossing, (mine_a, swapped_a, *ring_a, *far_a), weights)
-    sums_a, far_b = lax.optimization_barrier((sums_a, far_b))
-    up_a, down_a = step(sums_a[0], "z", 1), step(sums_a[1], "z", -1)
-    up_right_a, down_left_a = step(sums_a[3], "z", 1), step(sums_a[4], "z", -1)
-    sums_b = attend(places_b, first_queries, crossing, (mine_b, swapped_b, *ring_b, *far_b), weights)
-    sums_b, up_a, down_a = lax.optimization_barrier((sums_b, up_a, down_a))
-    up_left_a, down_right_a = step(add(sums_a[2], up_a), "z", 1), step(add(sums_a[5], down_a), "z", -1)
-    up_b, down_b = step(sums_b[0], "z", 1), step(sums_b[1], "z", -1)
-    up_right_b, down_left_b = step(sums_b[3], "z", 1), step(sums_b[4], "z", -1)
-    up_left_b, down_right_b = step(add(sums_b[2], up_b), "z", 1), step(add(sums_b[5], down_b), "z", -1)
-
-    out_a = total(sums_a[6:], down_left_a, up_left_a, up_right_a, down_right_a)
+    near = project(weights[:4], (mine, swapped, *ring))
+
+    up_a, down_a, above_a, below_a, *rest = attend(
+        0, places_a, second_queries, crossing, near, (*far, *weights[:4]), weights[4:]
+    )
+    here_a, far = rest[:2], rest[2:]
+    up_a, down_a = step(up_a, "z", 1), step(down_a, "z", -1)
+    up_b, down_b, above_b, below_b, *here_b = attend(1, places_b, first_queries, crossing, near, far, weights[4:])
+    up_a, down_a, up_b, down_b = lax.optimization_barrier((up_a, down_a, up_b, down_b))
+    above_a, below_a = lax.optimization_barrier((add(above_a, up_a[:, :side]), add(below_a, down_a[:, side:])))
+    up_left_a, down_right_a = step(above_a, "z", 1), step(below_a, "z", -1)
+    up_b, down_b = step(up_b, "z", 1), step(down_b, "z", -1)
+    out_a = total(*here_a, up_a, down_a, up_left_a, down_right_a)
+    out_a, up_b, down_b = lax.optimization_barrier((out_a, up_b, down_b))
+    above_b, below_b = lax.optimization_barrier((add(above_b, up_b[:, :side]), add(below_b, down_b[:, side:])))
+    up_left_b, down_right_b = step(above_b, "z", 1), step(below_b, "z", -1)
+
     last = lax.ppermute(out_a[:1], ("z", "core"), [(2 * z + 1, (2 * z - 1) % (N_Z * N_CORE)) for z in range(N_Z)])
     last = jnp.where(core == 0, out_a[:1], last)
     pairs = []
@@ -325,7 +391,7 @@
         elif i + N_Z * N_CORE < n_seq * N_Z * N_CORE:
             pairs.append((i + 1, i + N_Z * N_CORE))
     head = lax.ppermute(out_a, ("seq", "z", "core"), pairs)
-    out_b = total(sums_b[6:], down_left_b, up_left_b, up_right_b, down_right_b)
+    out_b = total(*here_b, up_b, down_b, up_left_b, down_right_b)
     return jnp.concatenate([head[1:], out_b, last], axis=0)
 
 

time: 148 us -> 142 us (0.959)
  starting transfers between devices: 55.6 us -> 42.5 us
  waiting for transfers between devices: 38.1 us -> 42.4 us
  Pallas kernels: 45.4 us -> 48.9 us
    ppermute x16 -> x12, waiting for transfers between devices: 8.97 us -> 19.2 us  [step(): lax.ppermute(value, axis, [(i, (i + steps) % count) for i in range(count)])]
    ppermute x14 -> x7, starting transfers between devices: 20.4 us -> 11.9 us  [hop(): return lax.ppermute(value, ('z', 'core'), pairs)]
    ppermute x1, starting transfers between devices: 9.04 us -> 2.89 us  [body(): head = lax.ppermute(out_a, ('seq', 'z', 'core'), pairs)]
    ppermute x1, waiting for transfers between devices: 5.79 us -> 0.01 us  [body(): head = lax.ppermute(out_a, ('seq', 'z', 'core'), pairs)]
    ppermute x1, waiting for transfers between devices: 3.95 us -> 0.01 us  [body(): lax.ppermute(crossing, ('seq', 'core'), [(2 * i + 2, 2 * i + 1) for i in...]
    ppermute x14 -> x7, waiting for transfers between devices: 14.7 us -> 18.4 us  [hop(): return lax.ppermute(value, ('z', 'core'), pairs)]
    pallas_call x2 -> x3, Pallas kernels: 27.3 us -> 30.9 us  [the longest x2 20.4 us: attend(): pl.pallas_call(functools.partial(span_kernel, group), grid_spec=pltpu.Pre...]
    ppermute x1, starting transfers between devices: 3.13 us -> 5.98 us  [body(): lax.ppermute(out_a[:1], ('z', 'core'), [(2 * z + 1, (2 * z - 1) % (N_Z *...]
  transfers between devices with their start and end apart: 34 -> 23, of which waited for: 11 -> 8; matrix products, arithmetic and copies ran while one was open for 3% -> 3% of each run, Pallas kernels for 29% -> 25%
where the time goes in v4:
time: 142 us; the launch traced here: 141 us
  Pallas kernels  48.9 us (34%)
  starting transfers between devices  42.5 us (30%)
  waiting for transfers between devices  42.4 us (30%)
  other arithmetic  3.88 us (3%)
  local copies, waits for them, and re-layouts  2.98 us (2%)
    pallas_call x2, Pallas kernels, attend(): pl.pallas_call(functools.partial(span_kernel, group), grid_spec=pltpu.Pre...  20.4 us
    ppermute x12, waiting for transfers between devices, step(): lax.ppermute(value, axis, [(i, (i + steps) % count) for i in range(count)])  19.2 us
    ppermute x7, waiting for transfers between devices, hop(): return lax.ppermute(value, ('z', 'core'), pairs)  18.4 us
    ppermute x12, starting transfers between devices, step(): lax.ppermute(value, axis, [(i, (i + steps) % count) for i in range(count)])  13.3 us
    pallas_call x1, Pallas kernels, project_queries(): pl.pallas_call(query_kernel, grid_spec=pltpu.PrefetchScalarGridSpec(num_s...  12 us
    ppermute x7, starting transfers between devices, hop(): return lax.ppermute(value, ('z', 'core'), pairs)  11.9 us
    pallas_call x1, Pallas kernels, project(): pl.pallas_call(project_kernel, in_specs=[pl.BlockSpec(memory_space=pltpu....  10.5 us
    all_to_all x1, starting transfers between devices, body(): lax.all_to_all(outgoing.reshape(n_seq, capacity, piece, enc), 'seq', spli...  7.03 us
  transfers between devices with their start and end apart: 23, of which 8 were waited for; matrix products, arithmetic and copies ran while one was open for 3% of the time, Pallas kernels for 25%

profile of v4, /device:TPU:1, one launch (start us, length us, event | category | flops | bytes accessed | tf_op | source)
XLA Modules:
  0.0 141.1 jit_solution(14114618595877068545)
XLA Ops:
  0.0 1.4 %collective-permute-start.3 = (bf16[4096,512]{1,0:T(8,128)(2,1)}, bf16[4096,512]{1,0:T(8,128)(2,1)}, u32[]{:S(2)}, u32[]{:S(2)}) collective-permute-start(bf16[4096,512]{1,0:T(8,128)(2,1)} %wa_hbm.1), channel_id=1, source_target_pairs={{0,1},{1,0},{2,3},{3,2},{4,5},{5,4},{6,7},{7,6},{8,9},{9,8},{10,11... | collective-permute-start | bytes 12582920 | tf_op jit(solution)/shard_map/ppermute | solution.py:26
  1.4 0.7 and_bitcast_fusion
  2.5 0.5 convert_reduce_fusion
  3.0 0.1 select_reduce_fusion
  3.2 0.6 reshape.80.index_ref
  3.8 3.0 %shard_map.91 = bf16[48,16,896]{2,1,0:T(8,128)(2,1)} custom-call(s32[48]{0:T(128)} %reshape.80.index_ref, s32[1]{0:T(128)} %bitcast.5.start_ref, bf16[24,128,896]{2,1,0:T(8,128)(2,1)} %source_ref.1), custom_call_target="tpu_custom_call" | custom-call | flops 400000000 | bytes 400000 | tf_op jit(solution)/shard_map/pallas_call | solution.py:60
  6.8 7.0 %all-to-all-start = ((bf16[16,3,16,896]{3,2,1,0:T(8,128)(2,1)}), bf16[16,3,16,896]{3,2,1,0:T(8,128)(2,1)}, u32[]{:S(2)}, u32[]{:S(2)}) async-start(bf16[16,3,16,896]{3,2,1,0:T(8,128)(2,1)} %bitcast.22), calls=%async_computation | async-start | bytes 2752512 | tf_op jit(solution)/shard_map/all_to_all | solution.py:320
  13.8 0.9 collective-permute-start
  14.7 0.1 collective-permute-start.1
  14.9 0.1 rev.7
  15.0 0.1 rev.6
  15.2 0.1 copy.16
  15.3 0.7 reshape.79.index_ref
  16.0 12.0 %shard_map.92 = (bf16[4,64,1024]{2,1,0:T(8,128)(2,1)}, bf16[4,64,1024]{2,1,0:T(8,128)(2,1)}, bf16[64,1024]{1,0:T(8,128)(2,1)}) custom-call(s32[1]{0:T(128)} %bitcast.8.core_ref, bf16[8,128,4096]{2,1,0:T(8,128)(2,1)} %bitcast.21, bf16[4096,512]{1,0:T(8,128)(2,1)} %wa_hbm.1, bf16[4096,512]{1,0:T(8,128)(2,1)} %collective-permute-done.3.wb_hbm), custom_call_target="tpu_custom_call" | custom-call | flops 1200000000 | bytes 1200000 | tf_op jit(solution)/shard_map/pallas_call | solution.py:111
  28.1 4.7 %all-to-all-done = bf16[16,3,16,896]{3,2,1,0:T(8,128)(2,1)} async-done(((bf16[16,3,16,896]{3,2,1,0:T(8,128)(2,1)}), bf16[16,3,16,896]{3,2,1,0:T(8,128)(2,1)}, u32[]{:S(2)}, u32[]{:S(2)}) %all-to-all-start) | async-done | bytes 1376288 | tf_op jit(solution)/shard_map/all_to_all | solution.py:320
  32.8 3.0 %shard_map.93 = (bf16[16,16,896]{2,1,0:T(8,128)(2,1)}, bf16[16,16,896]{2,1,0:T(8,128)(2,1)}) custom-call(s32[32]{0:T(128)} %reshape.79.index_ref, s32[1]{0:T(128)} %constant.51.clone.1.start_ref, bf16[48,16,896]{2,1,0:T(8,128)(2,1)} %bitcast.7.source_ref), custom_call_target="tpu_custom_call" | custom-call | flops 400000000 | bytes 400000 | tf_op jit(solution)/shard_map/pallas_call | solution.py:60
  35.8 3.7 %collective-permute-start.8 = (bf16[256,896]{1,0:T(8,128)(2,1)}, bf16[256,896]{1,0:T(8,128)(2,1)S(1)}, u32[]{:S(2)}, u32[]{:S(2)}) collective-permute-start(bf16[256,896]{1,0:T(8,128)(2,1)} %bitcast.33), channel_id=1, source_target_pairs={{0,1},{1,0},{2,3},{3,2},{4,5},{5,4},{6,7},{7,6},{8,9},{9,8},{10,11... | collective-permute-start | bytes 1376264 | tf_op jit(solution)/shard_map/ppermute | solution.py:345
  39.5 1.6 %collective-permute-start.6 = (bf16[256,896]{1,0:T(8,128)(2,1)}, bf16[256,896]{1,0:T(8,128)(2,1)S(1)}, u32[]{:S(2)}, u32[]{:S(2)}) collective-permute-start(bf16[256,896]{1,0:T(8,128)(2,1)} %bitcast.34), channel_id=1, source_target_pairs={{0,3},{1,2},{2,5},{3,4},{4,7},{5,6},{6,1},{7,0},{8,11},{9,10},{10,... | collective-permute-start | bytes 1376264 | tf_op jit(solution)/shard_map/ppermute | solution.py:345
  41.1 2.2 %collective-permute-start.5 = (bf16[256,896]{1,0:T(8,128)(2,1)}, bf16[256,896]{1,0:T(8,128)(2,1)S(1)}, u32[]{:S(2)}, u32[]{:S(2)}) collective-permute-start(bf16[256,896]{1,0:T(8,128)(2,1)} %bitcast.35), channel_id=1, source_target_pairs={{0,7},{1,6},{2,1},{3,0},{4,3},{5,2},{6,5},{7,4},{8,15},{9,14},{10,... | collective-permute-start | bytes 1376264 | tf_op jit(solution)/shard_map/ppermute | solution.py:345
  43.3 1.7 %collective-permute-start.7 = (bf16[256,896]{1,0:T(8,128)(2,1)}, bf16[256,896]{1,0:T(8,128)(2,1)S(1)}, u32[]{:S(2)}, u32[]{:S(2)}) collective-permute-start(bf16[256,896]{1,0:T(8,128)(2,1)} %bitcast.23), channel_id=1, source_target_pairs={{0,6},{1,7},{2,0},{3,1},{4,2},{5,3},{6,4},{7,5},{8,14},{9,15},{10,... | collective-permute-start | bytes 1376264 | tf_op jit(solution)/shard_map/ppermute | solution.py:345
  45.1 0.7 pad_add_fusion
  45.7 8.8 %collective-permute-done.6.refs_4_ = bf16[256,896]{1,0:T(8,128)(2,1)S(1)} collective-permute-done((bf16[256,896]{1,0:T(8,128)(2,1)}, bf16[256,896]{1,0:T(8,128)(2,1)S(1)}, u32[]{:S(2)}, u32[]{:S(2)}) %collective-permute-start.6) | collective-permute-done | bytes 458784 | tf_op jit(solution)/shard_map/ppermute | solution.py:345
  54.5 9.1 %collective-permute-done.7.refs_5_ = bf16[256,896]{1,0:T(8,128)(2,1)S(1)} collective-permute-done((bf16[256,896]{1,0:T(8,128)(2,1)}, bf16[256,896]{1,0:T(8,128)(2,1)S(1)}, u32[]{:S(2)}, u32[]{:S(2)}) %collective-permute-start.7) | collective-permute-done | bytes 458784 | tf_op jit(solution)/shard_map/ppermute | solution.py:345
  63.6 0.5 collective-permute-done.4.refs_2_
  64.1 1.4 collective-permute-start.9
  65.5 1.3 collective-permute-start.10
  66.8 1.5 %collective-permute-start.11 = (bf16[64,1024]{1,0:T(8,128)(2,1)}, bf16[64,1024]{1,0:T(8,128)(2,1)S(1)}, u32[]{:S(2)}, u32[]{:S(2)}) collective-permute-start(bf16[64,1024]{1,0:T(8,128)(2,1)} %get-tuple-element.77), channel_id=1, source_target_pairs={{8,1},{16,9},{24,17},{32,25},{40,33},{48,41},{56,49},{64,57},{72,6... | collective-permute-start | bytes 393224 | tf_op jit(solution)/shard_map/ppermute | solution.py:366
  68.3 10.5 %shard_map.94 = (bf16[6,2,4,32,512]{4,3,2,1,0:T(8,128)(2,1)}, bf16[6,2,4,32,512]{4,3,2,1,0:T(8,128)(2,1)}, bf16[6,2,4,32,512]{4,3,2,1,0:T(8,128)(2,1)}, bf16[6,2,4,32,512]{4,3,2,1,0:T(8,128)(2,1)}) custom-call(bf16[256,896]{1,0:T(8,128)(2,1)} %bitcast.25, bf16[256,896]{1,0:T(8,128)(2,1)} %copy-done.5, bf16[256,896]{1,0:T(8,128)(2,1)} %copy-done.7, ...), custom_call_target="tpu_custom_call" | custom-call | flops 800000000 | bytes 800000 | tf_op jit(solution)/shard_map/pallas_call | solution.py:156
  78.9 0.6 copy-done.3
  79.5 11.1 %shard_map.95 = (bf16[64,4096]{1,0:T(8,128)(2,1)}, bf16[64,4096]{1,0:T(8,128)(2,1)}, bf16[64,2048]{1,0:T(8,128)(2,1)}, bf16[64,2048]{1,0:T(8,128)(2,1)}, bf16[64...) custom-call(s32[5]{0:T(128)} %get-tuple-element.62.place_ref, ...), custom_call_target="tpu_custom_call" | custom-call | flops 2000000000 | bytes 2000000 | tf_op jit(solution)/shard_map/pallas_call | solution.py:286
  90.7 0.2 collective-permute-start.12
  90.9 2.5 %collective-permute-start.13 = (bf16[64,4096]{1,0:T(8,128)(2,1)}, bf16[64,4096]{1,0:T(8,128)(2,1)S(1)}, u32[]{:S(2)}, u32[]{:S(2)}) collective-permute-start(bf16[64,4096]{1,0:T(8,128)(2,1)} %get-tuple-element.82), channel_id=1, source_target_pairs={{0,6},{2,0},{4,2},{6,4},{1,7},{3,1},{5,3},{7,5},{8,14},{10,8},{12,... | collective-permute-start | bytes 1572872 | tf_op jit(solution)/shard_map/ppermute | solution.py:26
  93.4 9.3 %shard_map.96 = (bf16[64,4096]{1,0:T(8,128)(2,1)}, bf16[64,4096]{1,0:T(8,128)(2,1)}, bf16[64,2048]{1,0:T(8,128)(2,1)}, bf16[64,2048]{1,0:T(8,128)(2,1)}, bf16[64...) custom-call(s32[5]{0:T(128)} %get-tuple-element.83.place_ref, bf16[6,2,4,32,512]{4,3,2,1,0:T(8,128)(2,1)} %get-tuple-element.72.refs_0_, ...), custom_call_target="tpu_custom_call" | custom-call | flops 2000000000 | bytes 2000000 | tf_op jit(solution)/shard_map/pallas_call | solution.py:286
  102.7 2.3 %collective-permute-done.12 = bf16[64,4096]{1,0:T(8,128)(2,1)S(1)} collective-permute-done((bf16[64,4096]{1,0:T(8,128)(2,1)}, bf16[64,4096]{1,0:T(8,128)(2,1)S(1)}, u32[]{:S(2)}, u32[]{:S(2)}) %collective-permute-start.12) | collective-permute-done | bytes 524320 | tf_op jit(solution)/shard_map/ppermute | solution.py:26
  105.3 2.7 %collective-permute-start.15 = (bf16[64,2048]{1,0:T(8,128)(2,1)S(1)}, bf16[64,2048]{1,0:T(8,128)(2,1)S(1)}, u32[]{:S(2)}, u32[]{:S(2)}) collective-permute-start(bf16[64,2048]{1,0:T(8,128)(2,1)S(1)} %add_convert_fusion.6), channel_id=1, source_target_pairs={{0,6},{2,0},{4,2},{6,4},{1,7},{3,1},{5,3},{7,5},{8,14},{10,8},{12,... | collective-permute-start | bytes 786440 | tf_op jit(solution)/shard_map/ppermute | solution.py:26
  107.9 2.7 %collective-permute-start.17 = (bf16[64,4096]{1,0:T(8,128)(2,1)}, bf16[64,4096]{1,0:T(8,128)(2,1)S(1)}, u32[]{:S(2)}, u32[]{:S(2)}) collective-permute-start(bf16[64,4096]{1,0:T(8,128)(2,1)} %get-tuple-element.99), channel_id=1, source_target_pairs={{0,6},{2,0},{4,2},{6,4},{1,7},{3,1},{5,3},{7,5},{8,14},{10,8},{12,... | collective-permute-start | bytes 1572872 | tf_op jit(solution)/shard_map/ppermute | solution.py:26
  110.6 2.2 %collective-permute-done.14 = bf16[64,2048]{1,0:T(8,128)(2,1)S(1)} collective-permute-done((bf16[64,2048]{1,0:T(8,128)(2,1)S(1)}, bf16[64,2048]{1,0:T(8,128)(2,1)S(1)}, u32[]{:S(2)}, u32[]{:S(2)}) %collective-permute-start.14) | collective-permute-done | bytes 262176 | tf_op jit(solution)/shard_map/ppermute | solution.py:26
  112.8 0.1 add_convert_fusion.5
  112.9 0.1 add_convert_fusion.4
  113.1 10.9 %collective-permute-done.16 = bf16[64,4096]{1,0:T(8,128)(2,1)S(1)} collective-permute-done((bf16[64,4096]{1,0:T(8,128)(2,1)}, bf16[64,4096]{1,0:T(8,128)(2,1)S(1)}, u32[]{:S(2)}, u32[]{:S(2)}) %collective-permute-start.16) | collective-permute-done | bytes 524320 | tf_op jit(solution)/shard_map/ppermute | solution.py:26
  124.1 2.9 %collective-permute-start.18 = (bf16[64,4096]{1,0:T(8,128)(2,1)S(1)}, bf16[64,4096]{1,0:T(8,128)(2,1)S(1)}, u32[]{:S(2)}, u32[]{:S(2)}) collective-permute-start(bf16[64,4096]{1,0:T(8,128)(2,1)S(1)} %pad_maximum_fusion.1), channel_id=1, source_target_pairs={{0,1},{1,8},{2,3},{3,2},{4,5},{5,4},{6,7},{7,6},{8,9},{9,16},{10,1... | collective-permute-start | bytes 1572872 | tf_op jit(solution)/shard_map/ppermute | solution.py:393
  127.0 6.0 %collective-permute-start.21 = (bf16[1,4096]{1,0:T(2,128)(2,1)S(1)}, bf16[1,4096]{1,0:T(2,128)(2,1)S(1)}, u32[]{:S(2)}, u32[]{:S(2)}) collective-permute-start(bf16[1,4096]{1,0:T(2,128)(2,1)S(1)} %slice.40), channel_id=1, source_target_pairs={{1,7},{3,1},{5,3},{7,5},{9,15},{11,9},{13,11},{15,13},{17,23},{19,... | collective-permute-start | bytes 24584 | tf_op jit(solution)/shard_map/ppermute | solution.py:384
  133.2 2.7 %collective-permute-start.20 = (bf16[64,2048]{1,0:T(8,128)(2,1)S(1)}, bf16[64,2048]{1,0:T(8,128)(2,1)S(1)}, u32[]{:S(2)}, u32[]{:S(2)}) collective-permute-start(bf16[64,2048]{1,0:T(8,128)(2,1)S(1)} %add_convert_fusion.2), channel_id=1, source_target_pairs={{0,6},{2,0},{4,2},{6,4},{1,7},{3,1},{5,3},{7,5},{8,14},{10,8},{12,... | collective-permute-start | bytes 786440 | tf_op jit(solution)/shard_map/ppermute | solution.py:26
  135.9 3.7 %collective-permute-done.19 = bf16[64,2048]{1,0:T(8,128)(2,1)S(1)} collective-permute-done((bf16[64,2048]{1,0:T(8,128)(2,1)S(1)}, bf16[64,2048]{1,0:T(8,128)(2,1)S(1)}, u32[]{:S(2)}, u32[]{:S(2)}) %collective-permute-start.19) | collective-permute-done | bytes 262176 | tf_op jit(solution)/shard_map/ppermute | solution.py:26
  139.6 0.1 add_convert_fusion.1
  139.8 0.1 add_convert_fusion
  139.9 0.1 slice.41
  140.0 1.1 pad_maximum_fusion
  (75 shorter events, 1.2 us)
Async XLA Ops:
  0.0 16.0 %collective-permute-start.3 = (bf16[4096,512]{1,0:T(8,128)(2,1)}, bf16[4096,512]{1,0:T(8,128)(2,1)}, u32[]{:S(2)}, u32[]{:S(2)}) collective-permute-start(bf16[4096,512]{1,0:T(8,128)(2,1)} %wa_hbm.1), channel_id=1, source_target_pairs={{0,1},{1,0},{2,3},{3,2},{4,5},{5,4},{6,7},{7,6},{8,9},{9,8},{10,11... | collective-permute-start | bytes 12582920 | tf_op jit(solution)/shard_map/ppermute | solution.py:26
  1.4 31.4 %collective-permute-start.2 = (bf16[512,4096]{1,0:T(8,128)(2,1)}, bf16[512,4096]{1,0:T(8,128)(2,1)}, u32[]{:S(2)}, u32[]{:S(2)}) collective-permute-start(bf16[512,4096]{1,0:T(8,128)(2,1)} %refs_10_), channel_id=1, source_target_pairs={{0,1},{1,0},{2,3},{3,2},{4,5},{5,4},{6,7},{7,6},{8,9},{9,8},{10,11... | collective-permute-start | bytes 12582920 | tf_op jit(solution)/shard_map/ppermute | solution.py:26
  6.8 7.1 %copy-start = (bf16[896,512]{1,0:T(8,128)(2,1)S(1)}, bf16[896,512]{1,0:T(8,128)(2,1)}, u32[]{:S(2)}) copy-start(bf16[896,512]{1,0:T(8,128)(2,1)} %refs_6_.1) | copy-start | bytes 2752516
  6.8 7.9 %copy-start.1 = (bf16[896,512]{1,0:T(8,128)(2,1)S(1)}, bf16[896,512]{1,0:T(8,128)(2,1)}, u32[]{:S(2)}) copy-start(bf16[896,512]{1,0:T(8,128)(2,1)} %refs_7_.1) | copy-start | bytes 2752516
  6.8 26.0 %all-to-all-start = ((bf16[16,3,16,896]{3,2,1,0:T(8,128)(2,1)}), bf16[16,3,16,896]{3,2,1,0:T(8,128)(2,1)}, u32[]{:S(2)}, u32[]{:S(2)}) async-start(bf16[16,3,16,896]{3,2,1,0:T(8,128)(2,1)} %bitcast.22), calls=%async_computation | async-start | bytes 2752512 | tf_op jit(solution)/shard_map/all_to_all | solution.py:320
  13.8 14.2 %collective-permute-start = (bf16[896,512]{1,0:T(8,128)(2,1)S(1)}, bf16[896,512]{1,0:T(8,128)(2,1)S(1)}, u32[]{:S(2)}, u32[]{:S(2)}) collective-permute-start(bf16[896,512]{1,0:T(8,128)(2,1)S(1)} %copy-done), channel_id=1, source_target_pairs={{0,1},{1,0},{2,3},{3,2},{4,5},{5,4},{6,7},{7,6},{8,9},{9,8},{10,11... | collective-permute-start | bytes 2752520 | tf_op jit(solution)/shard_map/ppermute | solution.py:26
  14.7 13.3 %collective-permute-start.1 = (bf16[896,512]{1,0:T(8,128)(2,1)S(1)}, bf16[896,512]{1,0:T(8,128)(2,1)}, u32[]{:S(2)}, u32[]{:S(2)}) collective-permute-start(bf16[896,512]{1,0:T(8,128)(2,1)S(1)} %copy-done.1), channel_id=1, source_target_pairs={{0,1},{1,0},{2,3},{3,2},{4,5},{5,4},{6,7},{7,6},{8,9},{9,8},{10,11... | collective-permute-start | bytes 2752520 | tf_op jit(solution)/shard_map/ppermute | solution.py:26
  16.0 29.1 %copy-start.17 = (s32[4]{0:T(128)S(1)}, s32[4]{0:T(128)}, u32[]{:S(2)}) copy-start(s32[4]{0:T(128)} %constant.55.clone) | copy-start | bytes 52
  28.0 40.2 %copy-start.2 = (bf16[896,512]{1,0:T(8,128)(2,1)}, bf16[896,512]{1,0:T(8,128)(2,1)S(1)}, u32[]{:S(2)}) copy-start(bf16[896,512]{1,0:T(8,128)(2,1)S(1)} %collective-permute-done.refs_8_) | copy-start | bytes 2752516
  35.8 9.9 %collective-permute-start.8 = (bf16[256,896]{1,0:T(8,128)(2,1)}, bf16[256,896]{1,0:T(8,128)(2,1)S(1)}, u32[]{:S(2)}, u32[]{:S(2)}) collective-permute-start(bf16[256,896]{1,0:T(8,128)(2,1)} %bitcast.33), channel_id=1, source_target_pairs={{0,1},{1,0},{2,3},{3,2},{4,5},{5,4},{6,7},{7,6},{8,9},{9,8},{10,11... | collective-permute-start | bytes 1376264 | tf_op jit(solution)/shard_map/ppermute | solution.py:345
  39.5 15.0 %collective-permute-start.6 = (bf16[256,896]{1,0:T(8,128)(2,1)}, bf16[256,896]{1,0:T(8,128)(2,1)S(1)}, u32[]{:S(2)}, u32[]{:S(2)}) collective-permute-start(bf16[256,896]{1,0:T(8,128)(2,1)} %bitcast.34), channel_id=1, source_target_pairs={{0,3},{1,2},{2,5},{3,4},{4,7},{5,6},{6,1},{7,0},{8,11},{9,10},{10,... | collective-permute-start | bytes 1376264 | tf_op jit(solution)/shard_map/ppermute | solution.py:345
  41.1 13.4 %collective-permute-start.5 = (bf16[256,896]{1,0:T(8,128)(2,1)}, bf16[256,896]{1,0:T(8,128)(2,1)S(1)}, u32[]{:S(2)}, u32[]{:S(2)}) collective-permute-start(bf16[256,896]{1,0:T(8,128)(2,1)} %bitcast.35), channel_id=1, source_target_pairs={{0,7},{1,6},{2,1},{3,0},{4,3},{5,2},{6,5},{7,4},{8,15},{9,14},{10,... | collective-permute-start | bytes 1376264 | tf_op jit(solution)/shard_map/ppermute | solution.py:345
  43.3 20.3 %collective-permute-start.7 = (bf16[256,896]{1,0:T(8,128)(2,1)}, bf16[256,896]{1,0:T(8,128)(2,1)S(1)}, u32[]{:S(2)}, u32[]{:S(2)}) collective-permute-start(bf16[256,896]{1,0:T(8,128)(2,1)} %bitcast.23), channel_id=1, source_target_pairs={{0,6},{1,7},{2,0},{3,1},{4,2},{5,3},{6,4},{7,5},{8,14},{9,15},{10,... | collective-permute-start | bytes 1376264 | tf_op jit(solution)/shard_map/ppermute | solution.py:345
  45.0 19.1 %collective-permute-start.4 = (bf16[256,896]{1,0:T(8,128)(2,1)}, bf16[256,896]{1,0:T(8,128)(2,1)S(1)}, u32[]{:S(2)}, u32[]{:S(2)}) collective-permute-start(bf16[256,896]{1,0:T(8,128)(2,1)} %bitcast.24), channel_id=1, source_target_pairs={{0,2},{1,3},{2,4},{3,5},{4,6},{5,7},{6,0},{7,1},{8,10},{9,11},{10,... | collective-permute-start | bytes 1376264 | tf_op jit(solution)/shard_map/ppermute | solution.py:345
  45.7 22.6 %copy-start.5 = (bf16[256,896]{1,0:T(8,128)(2,1)}, bf16[256,896]{1,0:T(8,128)(2,1)S(1)}, u32[]{:S(2)}) copy-start(bf16[256,896]{1,0:T(8,128)(2,1)S(1)} %collective-permute-done.8.refs_1_) | copy-start | bytes 1376260
  54.5 13.8 %copy-start.6 = (bf16[256,896]{1,0:T(8,128)(2,1)}, bf16[256,896]{1,0:T(8,128)(2,1)S(1)}, u32[]{:S(2)}) copy-start(bf16[256,896]{1,0:T(8,128)(2,1)S(1)} %collective-permute-done.6.refs_4_) | copy-start | bytes 1376260
  54.5 13.8 %copy-start.4 = (bf16[256,896]{1,0:T(8,128)(2,1)}, bf16[256,896]{1,0:T(8,128)(2,1)S(1)}, u32[]{:S(2)}) copy-start(bf16[256,896]{1,0:T(8,128)(2,1)S(1)} %collective-permute-done.5.refs_3_) | copy-start | bytes 1376260
  63.6 4.7 %copy-start.8 = (bf16[256,896]{1,0:T(8,128)(2,1)}, bf16[256,896]{1,0:T(8,128)(2,1)S(1)}, u32[]{:S(2)}) copy-start(bf16[256,896]{1,0:T(8,128)(2,1)S(1)} %collective-permute-done.7.refs_5_) | copy-start | bytes 1376260
  64.1 4.2 %copy-start.7 = (bf16[256,896]{1,0:T(8,128)(2,1)}, bf16[256,896]{1,0:T(8,128)(2,1)S(1)}, u32[]{:S(2)}) copy-start(bf16[256,896]{1,0:T(8,128)(2,1)S(1)} %collective-permute-done.4.refs_2_) | copy-start | bytes 1376260
  64.1 14.7 %collective-permute-start.9 = (bf16[256,896]{1,0:T(8,128)(2,1)S(1)}, bf16[256,896]{1,0:T(8,128)(2,1)}, u32[]{:S(2)}, u32[]{:S(2)}) collective-permute-start(bf16[256,896]{1,0:T(8,128)(2,1)S(1)} %collective-permute-done.4.refs_2_), channel_id=1, source_target_pairs={{0,2},{1,3},{2,4},{3,5},{4,6},{5,7},{6,0},{7,1},{8,10},{9,11},{10,... | collective-permute-start | bytes 1376264 | tf_op jit(solution)/shard_map/ppermute | solution.py:345
  65.5 13.4 %collective-permute-start.10 = (bf16[256,896]{1,0:T(8,128)(2,1)S(1)}, bf16[256,896]{1,0:T(8,128)(2,1)}, u32[]{:S(2)}, u32[]{:S(2)}) collective-permute-start(bf16[256,896]{1,0:T(8,128)(2,1)S(1)} %collective-permute-done.5.refs_3_), channel_id=1, source_target_pairs={{0,6},{1,7},{2,0},{3,1},{4,2},{5,3},{6,4},{7,5},{8,14},{9,15},{10,... | collective-permute-start | bytes 1376264 | tf_op jit(solution)/shard_map/ppermute | solution.py:345
  66.8 12.0 %collective-permute-start.11 = (bf16[64,1024]{1,0:T(8,128)(2,1)}, bf16[64,1024]{1,0:T(8,128)(2,1)S(1)}, u32[]{:S(2)}, u32[]{:S(2)}) collective-permute-start(bf16[64,1024]{1,0:T(8,128)(2,1)} %get-tuple-element.77), channel_id=1, source_target_pairs={{8,1},{16,9},{24,17},{32,25},{40,33},{48,41},{56,49},{64,57},{72,6... | collective-permute-start | bytes 393224 | tf_op jit(solution)/shard_map/ppermute | solution.py:366
  78.9 0.7 copy-start.3
  90.7 14.4 %collective-permute-start.12 = (bf16[64,4096]{1,0:T(8,128)(2,1)}, bf16[64,4096]{1,0:T(8,128)(2,1)S(1)}, u32[]{:S(2)}, u32[]{:S(2)}) collective-permute-start(bf16[64,4096]{1,0:T(8,128)(2,1)} %get-tuple-element.81), channel_id=1, source_target_pairs={{0,2},{2,4},{4,6},{6,0},{1,3},{3,5},{5,7},{7,1},{8,10},{10,12},{12... | collective-permute-start | bytes 1572872 | tf_op jit(solution)/shard_map/ppermute | solution.py:26
  90.9 14.1 %collective-permute-start.13 = (bf16[64,4096]{1,0:T(8,128)(2,1)}, bf16[64,4096]{1,0:T(8,128)(2,1)S(1)}, u32[]{:S(2)}, u32[]{:S(2)}) collective-permute-start(bf16[64,4096]{1,0:T(8,128)(2,1)} %get-tuple-element.82), channel_id=1, source_target_pairs={{0,6},{2,0},{4,2},{6,4},{1,7},{3,1},{5,3},{7,5},{8,14},{10,8},{12,... | collective-permute-start | bytes 1572872 | tf_op jit(solution)/shard_map/ppermute | solution.py:26
  93.4 11.6 %copy-start.12 = (bf16[64,2048]{1,0:T(8,128)(2,1)S(1)}, bf16[64,2048]{1,0:T(8,128)(2,1)}, u32[]{:S(2)}) copy-start(bf16[64,2048]{1,0:T(8,128)(2,1)} %get-tuple-element.94) | copy-start | bytes 786436
  93.4 11.7 %copy-start.11 = (bf16[64,2048]{1,0:T(8,128)(2,1)S(1)}, bf16[64,2048]{1,0:T(8,128)(2,1)}, u32[]{:S(2)}) copy-start(bf16[64,2048]{1,0:T(8,128)(2,1)} %get-tuple-element.92) | copy-start | bytes 786436
  93.4 19.4 %copy-start.16 = (bf16[64,2048]{1,0:T(8,128)(2,1)S(1)}, bf16[64,2048]{1,0:T(8,128)(2,1)}, u32[]{:S(2)}) copy-start(bf16[64,2048]{1,0:T(8,128)(2,1)} %get-tuple-element.80) | copy-start | bytes 786436
  102.7 10.3 %copy-start.15 = (bf16[64,2048]{1,0:T(8,128)(2,1)S(1)}, bf16[64,2048]{1,0:T(8,128)(2,1)}, u32[]{:S(2)}) copy-start(bf16[64,2048]{1,0:T(8,128)(2,1)} %get-tuple-element.96) | copy-start | bytes 786436
  105.1 27.9 %copy-start.10 = (bf16[64,2048]{1,0:T(8,128)(2,1)S(1)}, bf16[64,2048]{1,0:T(8,128)(2,1)}, u32[]{:S(2)}) copy-start(bf16[64,2048]{1,0:T(8,128)(2,1)} %get-tuple-element.105) | copy-start | bytes 786436
  105.2 27.9 %copy-start.9 = (bf16[64,2048]{1,0:T(8,128)(2,1)S(1)}, bf16[64,2048]{1,0:T(8,128)(2,1)}, u32[]{:S(2)}) copy-start(bf16[64,2048]{1,0:T(8,128)(2,1)} %get-tuple-element.103) | copy-start | bytes 786436
  105.2 7.6 %collective-permute-start.14 = (bf16[64,2048]{1,0:T(8,128)(2,1)S(1)}, bf16[64,2048]{1,0:T(8,128)(2,1)S(1)}, u32[]{:S(2)}, u32[]{:S(2)}) collective-permute-start(bf16[64,2048]{1,0:T(8,128)(2,1)S(1)} %add_convert_fusion.7), channel_id=1, source_target_pairs={{0,2},{2,4},{4,6},{6,0},{1,3},{3,5},{5,7},{7,1},{8,10},{10,12},{12... | collective-permute-start | bytes 786440 | tf_op jit(solution)/shard_map/ppermute | solution.py:26
  105.3 7.6 %collective-permute-start.15 = (bf16[64,2048]{1,0:T(8,128)(2,1)S(1)}, bf16[64,2048]{1,0:T(8,128)(2,1)S(1)}, u32[]{:S(2)}, u32[]{:S(2)}) collective-permute-start(bf16[64,2048]{1,0:T(8,128)(2,1)S(1)} %add_convert_fusion.6), channel_id=1, source_target_pairs={{0,6},{2,0},{4,2},{6,4},{1,7},{3,1},{5,3},{7,5},{8,14},{10,8},{12,... | collective-permute-start | bytes 786440 | tf_op jit(solution)/shard_map/ppermute | solution.py:26
  107.9 16.1 %collective-permute-start.16 = (bf16[64,4096]{1,0:T(8,128)(2,1)}, bf16[64,4096]{1,0:T(8,128)(2,1)S(1)}, u32[]{:S(2)}, u32[]{:S(2)}) collective-permute-start(bf16[64,4096]{1,0:T(8,128)(2,1)} %get-tuple-element.98), channel_id=1, source_target_pairs={{0,2},{2,4},{4,6},{6,0},{1,3},{3,5},{5,7},{7,1},{8,10},{10,12},{12... | collective-permute-start | bytes 1572872 | tf_op jit(solution)/shard_map/ppermute | solution.py:26
  107.9 16.1 %collective-permute-start.17 = (bf16[64,4096]{1,0:T(8,128)(2,1)}, bf16[64,4096]{1,0:T(8,128)(2,1)S(1)}, u32[]{:S(2)}, u32[]{:S(2)}) collective-permute-start(bf16[64,4096]{1,0:T(8,128)(2,1)} %get-tuple-element.99), channel_id=1, source_target_pairs={{0,6},{2,0},{4,2},{6,4},{1,7},{3,1},{5,3},{7,5},{8,14},{10,8},{12,... | collective-permute-start | bytes 1572872 | tf_op jit(solution)/shard_map/ppermute | solution.py:26
  112.9 26.7 %copy-start.14 = (bf16[64,2048]{1,0:T(8,128)(2,1)S(1)}, bf16[64,2048]{1,0:T(8,128)(2,1)}, u32[]{:S(2)}) copy-start(bf16[64,2048]{1,0:T(8,128)(2,1)} %get-tuple-element.101) | copy-start | bytes 786436
  113.1 26.7 %copy-start.13 = (bf16[64,2048]{1,0:T(8,128)(2,1)S(1)}, bf16[64,2048]{1,0:T(8,128)(2,1)}, u32[]{:S(2)}) copy-start(bf16[64,2048]{1,0:T(8,128)(2,1)} %get-tuple-element.107) | copy-start | bytes 786436
  124.1 15.8 %collective-permute-start.18 = (bf16[64,4096]{1,0:T(8,128)(2,1)S(1)}, bf16[64,4096]{1,0:T(8,128)(2,1)S(1)}, u32[]{:S(2)}, u32[]{:S(2)}) collective-permute-start(bf16[64,4096]{1,0:T(8,128)(2,1)S(1)} %pad_maximum_fusion.1), channel_id=1, source_target_pairs={{0,1},{1,8},{2,3},{3,2},{4,5},{5,4},{6,7},{7,6},{8,9},{9,16},{10,1... | collective-permute-start | bytes 1572872 | tf_op jit(solution)/shard_map/ppermute | solution.py:393
  127.0 8.9 %collective-permute-start.21 = (bf16[1,4096]{1,0:T(2,128)(2,1)S(1)}, bf16[1,4096]{1,0:T(2,128)(2,1)S(1)}, u32[]{:S(2)}, u32[]{:S(2)}) collective-permute-start(bf16[1,4096]{1,0:T(2,128)(2,1)S(1)} %slice.40), channel_id=1, source_target_pairs={{1,7},{3,1},{5,3},{7,5},{9,15},{11,9},{13,11},{15,13},{17,23},{19,... | collective-permute-start | bytes 24584 | tf_op jit(solution)/shard_map/ppermute | solution.py:384
  133.1 6.5 %collective-permute-start.19 = (bf16[64,2048]{1,0:T(8,128)(2,1)S(1)}, bf16[64,2048]{1,0:T(8,128)(2,1)S(1)}, u32[]{:S(2)}, u32[]{:S(2)}) collective-permute-start(bf16[64,2048]{1,0:T(8,128)(2,1)S(1)} %add_convert_fusion.3), channel_id=1, source_target_pairs={{0,2},{2,4},{4,6},{6,0},{1,3},{3,5},{5,7},{7,1},{8,10},{10,12},{12... | collective-permute-start | bytes 786440 | tf_op jit(solution)/shard_map/ppermute | solution.py:26
  133.2 6.5 %collective-permute-start.20 = (bf16[64,2048]{1,0:T(8,128)(2,1)S(1)}, bf16[64,2048]{1,0:T(8,128)(2,1)S(1)}, u32[]{:S(2)}, u32[]{:S(2)}) collective-permute-start(bf16[64,2048]{1,0:T(8,128)(2,1)S(1)} %add_convert_fusion.2), channel_id=1, source_target_pairs={{0,6},{2,0},{4,2},{6,4},{1,7},{3,1},{5,3},{7,5},{8,14},{10,8},{12,... | collective-permute-start | bytes 786440 | tf_op jit(solution)/shard_map/ppermute | solution.py:26

commit v5 on v4

--- a/solution.py
+++ b/solution.py
@@ -129,8 +129,8 @@
 
 
 def project_kernel(*refs):
-    row_hbm, weight_hbm, out_hbm = refs[:6], refs[6:10], refs[10:14]
-    rows_ref, weight_refs, out_refs, sems = refs[14], refs[15:19], refs[19:23], refs[23]
+    row_hbm, weight_hbm, out_hbm = refs[:-18], refs[-18:-14], refs[-14:-10]
+    rows_ref, weight_refs, out_refs, sems = refs[-10], refs[-9:-5], refs[-5:-1], refs[-1]
     parts, rows, enc = rows_ref.shape
     row_copies = [pltpu.make_async_copy(row_hbm[i], rows_ref.at[i], sems.at[i]) for i in range(parts)]
     weight_copies = [pltpu.make_async_copy(weight_hbm[i], weight_refs[i], sems.at[parts + i]) for i in range(4)]
@@ -175,7 +175,7 @@
         del refs[:count]
         return taken
 
-    near_hbm, far_hbm = take(4), take(6 if group == 0 else 4)
+    near_hbm, far_hbm = take(8), take(6 if group == 0 else 4)
     q_hbm, crossing_hbm = take(2)
     out_weight_hbm, out_hbm = take(2), take(6)
     later_hbm = take(4 if group == 0 else 0)
@@ -195,14 +195,15 @@
         return pltpu.make_async_copy(source, target, out_sems.at[used[1] - 1])
 
     half, model = out_weight_refs[0].shape
-    parts = near_hbm[0].shape[0]
+    own, parts = near_hbm[0].shape[0], near_hbm[0].shape[0] + near_hbm[4].shape[0]
     if group == 0:
         far_copies = [copy_in(far_hbm[i], rows_ref.at[i]) for i in range(2)]
         weight_copies = [copy_in(far_hbm[2 + i], weight_refs[i]) for i in range(4)]
     else:
         far_copies = [copy_in(far_hbm[i], kv_refs[i].at[parts:]) for i in range(4)]
         weight_copies = []
-    near_copies = [copy_in(near_hbm[i].at[:, group], kv_refs[i].at[:parts]) for i in range(4)]
+    near_copies = [copy_in(near_hbm[i].at[:, group], kv_refs[i].at[:own]) for i in range(4)]
+    near_copies += [copy_in(near_hbm[4 + i].at[:, group], kv_refs[i].at[own:parts]) for i in range(4)]
     query_copies = [copy_in(q_hbm, q_ref), copy_in(crossing_hbm, crossing_ref)]
     out_weight_copies = [copy_in(out_weight_hbm[i], out_weight_refs[i]) for i in range(2)]
     for copy in far_copies + weight_copies + near_copies + query_copies + out_weight_copies:
@@ -249,7 +250,11 @@
 
     for copy in out_weight_copies:
         copy.wait()
-    context = jnp.concatenate([context_ref[place_ref[i]] for i in range(N_Z)], axis=0)
+    blocks = [context_ref[place_ref[i]] for i in range(N_Z)]
+    if group == 0:
+        is_first_row = lax.broadcasted_iota(jnp.int32, blocks[0].shape, 0) == 0
+        blocks = [jnp.where(is_first_row, context_ref[place_ref[N_Z + 1 + i]], blocks[i]) for i in range(N_Z)]
+    context = jnp.concatenate(blocks, axis=0)
     up, down, above, below, here_left, here_right = out_refs
     tile = model // 4
     out_copies = [copy_out(out_refs[i], out_hbm[i]) for i in range(6)]
@@ -275,7 +280,7 @@
 def attend(group, places, queries, crossing, near, far, out_weights):
     spans, tokens, width = queries.shape
     half, model = out_weights[0].shape
-    parts, _, _, rows, _ = near[0].shape
+    parts, rows = near[0].shape[0] + near[4].shape[0], near[0].shape[3]
     outs = [(tokens, model)] * 2 + [(tokens, model // 2)] * 4
     scratch = [(parts + 2, spans, rows, half)] * 4 + outs + [(half, model)] * 2
     scratch += [queries.shape, crossing.shape, queries.shape]
@@ -325,7 +330,13 @@
     w_query_other = step(w_query, "core", 1)
     weights = (w_key, w_value, *(step(weight, "core", 1) for weight in (w_key, w_value)), w_out, step(w_out, "core", 1))
     first_queries, second_queries, crossing = project_queries(decoder, w_query, w_query_other, core)
-    received, weights, crossing = lax.optimization_barrier((received, weights, crossing))
+    distance = jnp.array([2, 1, 3, 0], jnp.int32)
+    places_b = (z_index + distance) % N_Z
+    places_a = (z_index + distance + (N_Z - 1) * core) % N_Z
+    places_a = jnp.concatenate([places_a, core.reshape(1), places_b]).astype(jnp.int32)
+    received, weights, crossing, places_a, places_b = lax.optimization_barrier(
+        (received, weights, crossing, places_a, places_b)
+    )
 
     my_shards = lax.dynamic_index_in_dim(shard_lists, seq_index, 0, keepdims=False)
     my_places = lax.dynamic_index_in_dim(places, seq_index, 0, keepdims=False)
@@ -353,18 +364,14 @@
         left, right = add(here_left, down[:, :side], up_left), add(here_right, up[:, side:], down_right)
         return jnp.concatenate([left, right], axis=1)
 
-    distance = jnp.array([2, 1, 3, 0], jnp.int32)
-    places_a = jnp.append((z_index + distance + (N_Z - 1) * core) % N_Z, core).astype(jnp.int32)
-    places_b = jnp.append((z_index + distance) % N_Z, 0).astype(jnp.int32)
-
     ring = [hop(mine, 1, 0), hop(theirs, -1, 1), hop(theirs, 1, 1), hop(mine, -1, 0)]
     swapped = hop(theirs, 0, 1)
-    ring, swapped, crossing, places_a, places_b = lax.optimization_barrier(
-        (ring, swapped, crossing, places_a, places_b)
-    )
+    swapped, crossing = lax.optimization_barrier((swapped, crossing))
+    crossing = lax.ppermute(crossing, ("seq", "core"), [(2 * i + 2, 2 * i + 1) for i in range(n_seq - 1)])
+    near = project(weights[:4], (mine, swapped))
+    ring, crossing, near = lax.optimization_barrier((ring, crossing, near))
     far = hop(ring[0], 1, 0), hop(ring[1], -1, 0)
-    crossing = lax.ppermute(crossing, ("seq", "core"), [(2 * i + 2, 2 * i + 1) for i in range(n_seq - 1)])
-    near = project(weights[:4], (mine, swapped, *ring))
+    near = (*near, *project(weights[:4], ring))
 
     up_a, down_a, above_a, below_a, *rest = attend(
         0, places_a, second_queries, crossing, near, (*far, *weights[:4]), weights[4:]
@@ -377,12 +384,7 @@
     up_left_a, down_right_a = step(above_a, "z", 1), step(below_a, "z", -1)
     up_b, down_b = step(up_b, "z", 1), step(down_b, "z", -1)
     out_a = total(*here_a, up_a, down_a, up_left_a, down_right_a)
-    out_a, up_b, down_b = lax.optimization_barrier((out_a, up_b, down_b))
-    above_b, below_b = lax.optimization_barrier((add(above_b, up_b[:, :side]), add(below_b, down_b[:, side:])))
-    up_left_b, down_right_b = step(above_b, "z", 1), step(below_b, "z", -1)
-
-    last = lax.ppermute(out_a[:1], ("z", "core"), [(2 * z + 1, (2 * z - 1) % (N_Z * N_CORE)) for z in range(N_Z)])
-    last = jnp.where(core == 0, out_a[:1], last)
+
     pairs = []
     for i in range(0, n_seq * N_Z * N_CORE, 2):
         pairs.append((i, i + 1))
@@ -391,8 +393,11 @@
         elif i + N_Z * N_CORE < n_seq * N_Z * N_CORE:
             pairs.append((i + 1, i + N_Z * N_CORE))
     head = lax.ppermute(out_a, ("seq", "z", "core"), pairs)
+    head, up_b, down_b = lax.optimization_barrier((head, up_b, down_b))
+    above_b, below_b = lax.optimization_barrier((add(above_b, up_b[:, :side]), add(below_b, down_b[:, side:])))
+    up_left_b, down_right_b = step(above_b, "z", 1), step(below_b, "z", -1)
     out_b = total(*here_b, up_b, down_b, up_left_b, down_right_b)
-    return jnp.concatenate([head[1:], out_b, last], axis=0)
+    return jnp.concatenate([head[1:], out_b, out_a[:1]], axis=0)
 
 
 def solution(mesh):

time: 142 us -> 135 us (0.951)
  waiting for transfers between devices: 42.4 us -> 33.2 us
  Pallas kernels: 48.9 us -> 51.7 us
    ppermute x12, waiting for transfers between devices: 19.2 us -> 11.3 us  [step(): lax.ppermute(value, axis, [(i, (i + steps) % count) for i in range(count)])]
    ppermute x1 -> x0, starting transfers between devices: 5.98 us -> none  [body(): lax.ppermute(out_a[:1], ('z', 'core'), [(2 * z + 1, (2 * z - 1) % (N_Z *...]
    ppermute x1, starting transfers between devices: 2.89 us -> 8.62 us  [body(): head = lax.ppermute(out_a, ('seq', 'z', 'core'), pairs)]
    ppermute x7, waiting for transfers between devices: 18.4 us -> 14.4 us  [hop(): return lax.ppermute(value, ('z', 'core'), pairs)]
    ppermute x1, waiting for transfers between devices: 0.01 us -> 3.44 us  [body(): head = lax.ppermute(out_a, ('seq', 'z', 'core'), pairs)]
    pallas_call x1 -> x2, Pallas kernels: 10.5 us -> 13 us  [project(): pl.pallas_call(project_kernel, in_specs=[pl.BlockSpec(memory_space=pltpu....]
  transfers between devices with their start and end apart: 23 -> 22, of which waited for: 8 -> 10; matrix products, arithmetic and copies ran while one was open for 3% -> 3% of each run, Pallas kernels for 25% -> 28%
where the time goes in v5:
time: 135 us
  Pallas kernels  51.7 us (38%)
  starting transfers between devices  42.4 us (31%)
  waiting for transfers between devices  33.2 us (25%)
  other arithmetic  3.83 us (3%)
  local copies, waits for them, and re-layouts  3.27 us (2%)
    pallas_call x2, Pallas kernels, attend(): pl.pallas_call(functools.partial(span_kernel, group), grid_spec=pltpu.Pre...  20.6 us
    ppermute x7, waiting for transfers between devices, hop(): return lax.ppermute(value, ('z', 'core'), pairs)  14.4 us
    ppermute x12, starting transfers between devices, step(): lax.ppermute(value, axis, [(i, (i + steps) % count) for i in range(count)])  13.4 us
    pallas_call x2, Pallas kernels, project(): pl.pallas_call(project_kernel, in_specs=[pl.BlockSpec(memory_space=pltpu....  13 us
    pallas_call x1, Pallas kernels, project_queries(): pl.pallas_call(query_kernel, grid_spec=pltpu.PrefetchScalarGridSpec(num_s...  12.2 us
    ppermute x7, starting transfers between devices, hop(): return lax.ppermute(value, ('z', 'core'), pairs)  11.9 us
    ppermute x12, waiting for transfers between devices, step(): lax.ppermute(value, axis, [(i, (i + steps) % count) for i in range(count)])  11.3 us
    ppermute x1, starting transfers between devices, body(): head = lax.ppermute(out_a, ('seq', 'z', 'core'), pairs)  8.62 us
  transfers between devices with their start and end apart: 22, of which 10 were waited for; matrix products, arithmetic and copies ran while one was open for 3% of the time, Pallas kernels for 28%

profile of v5, /device:TPU:1, one launch (start us, length us, event | category | flops | bytes accessed | tf_op | source)
XLA Modules:
  0.0 134.8 jit_solution(5995851978809624654)
XLA Ops:
  0.0 1.4 %collective-permute-start.3 = (bf16[4096,512]{1,0:T(8,128)(2,1)}, bf16[4096,512]{1,0:T(8,128)(2,1)}, u32[]{:S(2)}, u32[]{:S(2)}) collective-permute-start(bf16[4096,512]{1,0:T(8,128)(2,1)} %wa_hbm.1), channel_id=1, source_target_pairs={{0,1},{1,0},{2,3},{3,2},{4,5},{5,4},{6,7},{7,6},{8,9},{9,8},{10,11... | collective-permute-start | bytes 12582920 | tf_op jit(solution)/shard_map/ppermute | solution.py:26
  1.4 0.7 shift-right-arithmetic_bitcast_fusion
  2.5 0.5 convert_reduce_fusion
  3.0 0.1 select_reduce_fusion
  3.2 0.6 reshape.76.index_ref
  3.8 3.0 %shard_map.91 = bf16[48,16,896]{2,1,0:T(8,128)(2,1)} custom-call(s32[48]{0:T(128)} %reshape.76.index_ref, s32[1]{0:T(128)} %bitcast.4.start_ref, bf16[24,128,896]{2,1,0:T(8,128)(2,1)} %source_ref.1), custom_call_target="tpu_custom_call" | custom-call | flops 400000000 | bytes 400000 | tf_op jit(solution)/shard_map/pallas_call | solution.py:60
  6.8 7.0 %all-to-all-start = ((bf16[16,3,16,896]{3,2,1,0:T(8,128)(2,1)}), bf16[16,3,16,896]{3,2,1,0:T(8,128)(2,1)}, u32[]{:S(2)}, u32[]{:S(2)}) async-start(bf16[16,3,16,896]{3,2,1,0:T(8,128)(2,1)} %bitcast.22), calls=%async_computation | async-start | bytes 2752512 | tf_op jit(solution)/shard_map/all_to_all | solution.py:325
  13.8 0.9 collective-permute-start
  14.9 0.1 rev.7
  15.0 0.1 rev.6
  15.2 0.1 copy.18
  15.3 0.7 reshape.82.index_ref
  16.0 0.6 pad_add_fusion.place_ref
  16.6 12.2 %shard_map.92 = (bf16[4,64,1024]{2,1,0:T(8,128)(2,1)}, bf16[4,64,1024]{2,1,0:T(8,128)(2,1)}, bf16[64,1024]{1,0:T(8,128)(2,1)}) custom-call(s32[1]{0:T(128)} %bitcast.7.core_ref, bf16[8,128,4096]{2,1,0:T(8,128)(2,1)} %bitcast.21, bf16[4096,512]{1,0:T(8,128)(2,1)} %wa_hbm.1, bf16[4096,512]{1,0:T(8,128)(2,1)} %collective-permute-done.3.wb_hbm), custom_call_target="tpu_custom_call" | custom-call | flops 1200000000 | bytes 1200000 | tf_op jit(solution)/shard_map/pallas_call | solution.py:111
  28.8 3.9 %all-to-all-done = bf16[16,3,16,896]{3,2,1,0:T(8,128)(2,1)} async-done(((bf16[16,3,16,896]{3,2,1,0:T(8,128)(2,1)}), bf16[16,3,16,896]{3,2,1,0:T(8,128)(2,1)}, u32[]{:S(2)}, u32[]{:S(2)}) %all-to-all-start) | async-done | bytes 1376288 | tf_op jit(solution)/shard_map/all_to_all | solution.py:325
  32.8 3.0 %shard_map.93 = (bf16[16,16,896]{2,1,0:T(8,128)(2,1)}, bf16[16,16,896]{2,1,0:T(8,128)(2,1)}) custom-call(s32[32]{0:T(128)} %reshape.82.index_ref, s32[1]{0:T(128)} %constant.53.clone.1.start_ref, bf16[48,16,896]{2,1,0:T(8,128)(2,1)} %bitcast.6.source_ref), custom_call_target="tpu_custom_call" | custom-call | flops 400000000 | bytes 400000 | tf_op jit(solution)/shard_map/pallas_call | solution.py:60
  35.8 3.7 %collective-permute-start.8 = (bf16[256,896]{1,0:T(8,128)(2,1)}, bf16[256,896]{1,0:T(8,128)(2,1)S(1)}, u32[]{:S(2)}, u32[]{:S(2)}) collective-permute-start(bf16[256,896]{1,0:T(8,128)(2,1)} %bitcast.33), channel_id=1, source_target_pairs={{0,1},{1,0},{2,3},{3,2},{4,5},{5,4},{6,7},{7,6},{8,9},{9,8},{10,11... | collective-permute-start | bytes 1376264 | tf_op jit(solution)/shard_map/ppermute | solution.py:356
  39.5 1.6 %collective-permute-start.6 = (bf16[256,896]{1,0:T(8,128)(2,1)}, bf16[256,896]{1,0:T(8,128)(2,1)S(1)}, u32[]{:S(2)}, u32[]{:S(2)}) collective-permute-start(bf16[256,896]{1,0:T(8,128)(2,1)} %bitcast.34), channel_id=1, source_target_pairs={{0,3},{1,2},{2,5},{3,4},{4,7},{5,6},{6,1},{7,0},{8,11},{9,10},{10,... | collective-permute-start | bytes 1376264 | tf_op jit(solution)/shard_map/ppermute | solution.py:356
  41.1 2.2 %collective-permute-start.5 = (bf16[256,896]{1,0:T(8,128)(2,1)}, bf16[256,896]{1,0:T(8,128)(2,1)S(1)}, u32[]{:S(2)}, u32[]{:S(2)}) collective-permute-start(bf16[256,896]{1,0:T(8,128)(2,1)} %bitcast.35), channel_id=1, source_target_pairs={{0,7},{1,6},{2,1},{3,0},{4,3},{5,2},{6,5},{7,4},{8,15},{9,14},{10,... | collective-permute-start | bytes 1376264 | tf_op jit(solution)/shard_map/ppermute | solution.py:356
  43.3 1.7 %collective-permute-start.7 = (bf16[256,896]{1,0:T(8,128)(2,1)}, bf16[256,896]{1,0:T(8,128)(2,1)S(1)}, u32[]{:S(2)}, u32[]{:S(2)}) collective-permute-start(bf16[256,896]{1,0:T(8,128)(2,1)} %bitcast.23), channel_id=1, source_target_pairs={{0,6},{1,7},{2,0},{3,1},{4,2},{5,3},{6,4},{7,5},{8,14},{9,15},{10,... | collective-permute-start | bytes 1376264 | tf_op jit(solution)/shard_map/ppermute | solution.py:356
  45.0 1.5 %collective-permute-start.9 = (bf16[64,1024]{1,0:T(8,128)(2,1)}, bf16[64,1024]{1,0:T(8,128)(2,1)S(1)}, u32[]{:S(2)}, u32[]{:S(2)}) collective-permute-start(bf16[64,1024]{1,0:T(8,128)(2,1)} %get-tuple-element.72), channel_id=1, source_target_pairs={{8,1},{16,9},{24,17},{32,25},{40,33},{48,41},{56,49},{64,57},{72,6... | collective-permute-start | bytes 393224 | tf_op jit(solution)/shard_map/ppermute | solution.py:370
  46.5 5.2 %shard_map.94 = (bf16[2,2,4,32,512]{4,3,2,1,0:T(8,128)(2,1)}, bf16[2,2,4,32,512]{4,3,2,1,0:T(8,128)(2,1)}, bf16[2,2,4,32,512]{4,3,2,1,0:T(8,128)(2,1)}, bf16[2,2,4,32,512]{4,3,2,1,0:T(8,128)(2,1)}) custom-call(bf16[256,896]{1,0:T(8,128)(2,1)} %bitcast.25, bf16[256,896]{1,0:T(8,128)(2,1)} %copy-done.4, bf16[896,512]{1,0:T(8,128)(2,1)} %refs_10_, ...), custom_call_target="tpu_custom_call" | custom-call | flops 800000000 | bytes 800000 | tf_op jit(solution)/shard_map/pallas_call | solution.py:156
  51.7 2.8 %collective-permute-done.6.refs_2_ = bf16[256,896]{1,0:T(8,128)(2,1)S(1)} collective-permute-done((bf16[256,896]{1,0:T(8,128)(2,1)}, bf16[256,896]{1,0:T(8,128)(2,1)S(1)}, u32[]{:S(2)}, u32[]{:S(2)}) %collective-permute-start.6) | collective-permute-done | bytes 458784 | tf_op jit(solution)/shard_map/ppermute | solution.py:356
  54.5 9.1 %collective-permute-done.7.refs_3_ = bf16[256,896]{1,0:T(8,128)(2,1)S(1)} collective-permute-done((bf16[256,896]{1,0:T(8,128)(2,1)}, bf16[256,896]{1,0:T(8,128)(2,1)S(1)}, u32[]{:S(2)}, u32[]{:S(2)}) %collective-permute-start.7) | collective-permute-done | bytes 458784 | tf_op jit(solution)/shard_map/ppermute | solution.py:356
  63.5 0.5 collective-permute-done.4.refs_0_
  64.1 1.4 %collective-permute-start.10 = (bf16[256,896]{1,0:T(8,128)(2,1)S(1)}, bf16[256,896]{1,0:T(8,128)(2,1)S(1)}, u32[]{:S(2)}, u32[]{:S(2)}) collective-permute-start(bf16[256,896]{1,0:T(8,128)(2,1)S(1)} %collective-permute-done.4.refs_0_), channel_id=1, source_target_pairs={{0,2},{1,3},{2,4},{3,5},{4,6},{5,7},{6,0},{7,1},{8,10},{9,11},{10,... | collective-permute-start | bytes 1376264 | tf_op jit(solution)/shard_map/ppermute | solution.py:356
  65.5 1.4 %collective-permute-start.11 = (bf16[256,896]{1,0:T(8,128)(2,1)S(1)}, bf16[256,896]{1,0:T(8,128)(2,1)S(1)}, u32[]{:S(2)}, u32[]{:S(2)}) collective-permute-start(bf16[256,896]{1,0:T(8,128)(2,1)S(1)} %collective-permute-done.5.refs_1_), channel_id=1, source_target_pairs={{0,6},{1,7},{2,0},{3,1},{4,2},{5,3},{6,4},{7,5},{8,14},{9,15},{10,... | collective-permute-start | bytes 1376264 | tf_op jit(solution)/shard_map/ppermute | solution.py:356
  66.8 7.8 %shard_map.95 = (bf16[4,2,4,32,512]{4,3,2,1,0:T(8,128)(2,1)}, bf16[4,2,4,32,512]{4,3,2,1,0:T(8,128)(2,1)}, bf16[4,2,4,32,512]{4,3,2,1,0:T(8,128)(2,1)}, bf16[4,2,4,32,512]{4,3,2,1,0:T(8,128)(2,1)}) custom-call(bf16[256,896]{1,0:T(8,128)(2,1)} %copy-done.8, bf16[256,896]{1,0:T(8,128)(2,1)} %copy-done.5, bf16[256,896]{1,0:T(8,128)(2,1)} %copy-done.6, ...), custom_call_target="tpu_custom_call" | custom-call | flops 800000000 | bytes 800000 | tf_op jit(solution)/shard_map/pallas_call | solution.py:156
  74.7 2.1 %collective-permute-done.10.refs_8_ = bf16[256,896]{1,0:T(8,128)(2,1)S(1)} collective-permute-done((bf16[256,896]{1,0:T(8,128)(2,1)S(1)}, bf16[256,896]{1,0:T(8,128)(2,1)S(1)}, u32[]{:S(2)}, u32[]{:S(2)}) %collective-permute-start.10) | collective-permute-done | bytes 458784 | tf_op jit(solution)/shard_map/ppermute | solution.py:356
  76.8 0.7 copy-done.9
  77.5 0.2 copy-done.10
  77.7 11.2 %shard_map.96 = (bf16[64,4096]{1,0:T(8,128)(2,1)}, bf16[64,4096]{1,0:T(8,128)(2,1)}, bf16[64,2048]{1,0:T(8,128)(2,1)}, bf16[64,2048]{1,0:T(8,128)(2,1)}, bf16[64...) custom-call(s32[9]{0:T(128)} %pad_add_fusion.place_ref, ...), custom_call_target="tpu_custom_call" | custom-call | flops 2000000000 | bytes 2000000 | tf_op jit(solution)/shard_map/pallas_call | solution.py:291
  88.9 1.1 collective-permute-start.12
  90.0 1.7 %collective-permute-start.13 = (bf16[64,4096]{1,0:T(8,128)(2,1)}, bf16[64,4096]{1,0:T(8,128)(2,1)S(1)}, u32[]{:S(2)}, u32[]{:S(2)}) collective-permute-start(bf16[64,4096]{1,0:T(8,128)(2,1)} %get-tuple-element.100), channel_id=1, source_target_pairs={{0,6},{2,0},{4,2},{6,4},{1,7},{3,1},{5,3},{7,5},{8,14},{10,8},{12,... | collective-permute-start | bytes 1572872 | tf_op jit(solution)/shard_map/ppermute | solution.py:26
  91.6 9.4 %shard_map.97 = (bf16[64,4096]{1,0:T(8,128)(2,1)}, bf16[64,4096]{1,0:T(8,128)(2,1)}, bf16[64,2048]{1,0:T(8,128)(2,1)}, bf16[64,2048]{1,0:T(8,128)(2,1)}, bf16[64...) custom-call(s32[4]{0:T(128)} %copy-done.19, bf16[2,2,4,32,512]{4,3,2,1,0:T(8,128)(2,1)} %get-tuple-element.82.refs_0_, ...), custom_call_target="tpu_custom_call" | custom-call | flops 2000000000 | bytes 2000000 | tf_op jit(solution)/shard_map/pallas_call | solution.py:291
  101.0 1.2 collective-permute-done.12
  102.3 0.1 add_convert_fusion.6
  102.5 2.7 %collective-permute-start.15 = (bf16[64,2048]{1,0:T(8,128)(2,1)S(1)}, bf16[64,2048]{1,0:T(8,128)(2,1)S(1)}, u32[]{:S(2)}, u32[]{:S(2)}) collective-permute-start(bf16[64,2048]{1,0:T(8,128)(2,1)S(1)} %get-tuple-element.115), channel_id=1, source_target_pairs={{0,6},{2,0},{4,2},{6,4},{1,7},{3,1},{5,3},{7,5},{8,14},{10,8},{12,... | collective-permute-start | bytes 786440 | tf_op jit(solution)/shard_map/ppermute | solution.py:26
  105.2 2.7 %collective-permute-start.18 = (bf16[64,4096]{1,0:T(8,128)(2,1)}, bf16[64,4096]{1,0:T(8,128)(2,1)S(1)}, u32[]{:S(2)}, u32[]{:S(2)}) collective-permute-start(bf16[64,4096]{1,0:T(8,128)(2,1)} %get-tuple-element.117), channel_id=1, source_target_pairs={{0,6},{2,0},{4,2},{6,4},{1,7},{3,1},{5,3},{7,5},{8,14},{10,8},{12,... | collective-permute-start | bytes 1572872 | tf_op jit(solution)/shard_map/ppermute | solution.py:26
  107.9 1.1 collective-permute-done.14
  109.2 8.6 %collective-permute-start.16 = (bf16[64,4096]{1,0:T(8,128)(2,1)S(1)}, bf16[64,4096]{1,0:T(8,128)(2,1)S(1)}, u32[]{:S(2)}, u32[]{:S(2)}) collective-permute-start(bf16[64,4096]{1,0:T(8,128)(2,1)S(1)} %pad_maximum_fusion.1), channel_id=1, source_target_pairs={{0,1},{1,8},{2,3},{3,2},{4,5},{5,4},{6,7},{7,6},{8,9},{9,16},{10,1... | collective-permute-start | bytes 1572872 | tf_op jit(solution)/shard_map/ppermute | solution.py:395
  117.8 2.7 %collective-permute-done.17 = bf16[64,4096]{1,0:T(8,128)(2,1)S(1)} collective-permute-done((bf16[64,4096]{1,0:T(8,128)(2,1)}, bf16[64,4096]{1,0:T(8,128)(2,1)S(1)}, u32[]{:S(2)}, u32[]{:S(2)}) %collective-permute-start.17) | collective-permute-done | bytes 524320 | tf_op jit(solution)/shard_map/ppermute | solution.py:26
  120.5 3.4 %collective-permute-done.16 = bf16[64,4096]{1,0:T(8,128)(2,1)S(1)} collective-permute-done((bf16[64,4096]{1,0:T(8,128)(2,1)S(1)}, bf16[64,4096]{1,0:T(8,128)(2,1)S(1)}, u32[]{:S(2)}, u32[]{:S(2)}) %collective-permute-start.16) | collective-permute-done | bytes 524320 | tf_op jit(solution)/shard_map/ppermute | solution.py:395
  124.2 0.1 slice.34
  124.3 2.7 %collective-permute-start.20 = (bf16[64,2048]{1,0:T(8,128)(2,1)S(1)}, bf16[64,2048]{1,0:T(8,128)(2,1)S(1)}, u32[]{:S(2)}, u32[]{:S(2)}) collective-permute-start(bf16[64,2048]{1,0:T(8,128)(2,1)S(1)} %add_convert_fusion.2), channel_id=1, source_target_pairs={{0,6},{2,0},{4,2},{6,4},{1,7},{3,1},{5,3},{7,5},{8,14},{10,8},{12,... | collective-permute-start | bytes 786440 | tf_op jit(solution)/shard_map/ppermute | solution.py:26
  127.1 6.4 %collective-permute-done.19 = bf16[64,2048]{1,0:T(8,128)(2,1)S(1)} collective-permute-done((bf16[64,2048]{1,0:T(8,128)(2,1)S(1)}, bf16[64,2048]{1,0:T(8,128)(2,1)S(1)}, u32[]{:S(2)}, u32[]{:S(2)}) %collective-permute-start.19) | collective-permute-done | bytes 262176 | tf_op jit(solution)/shard_map/ppermute | solution.py:26
  133.6 0.1 add_convert_fusion
  133.7 1.1 pad_maximum_fusion
  (78 shorter events, 1.4 us)
Async XLA Ops:
  0.0 16.6 %collective-permute-start.3 = (bf16[4096,512]{1,0:T(8,128)(2,1)}, bf16[4096,512]{1,0:T(8,128)(2,1)}, u32[]{:S(2)}, u32[]{:S(2)}) collective-permute-start(bf16[4096,512]{1,0:T(8,128)(2,1)} %wa_hbm.1), channel_id=1, source_target_pairs={{0,1},{1,0},{2,3},{3,2},{4,5},{5,4},{6,7},{7,6},{8,9},{9,8},{10,11... | collective-permute-start | bytes 12582920 | tf_op jit(solution)/shard_map/ppermute | solution.py:26
  1.4 31.4 %collective-permute-start.2 = (bf16[512,4096]{1,0:T(8,128)(2,1)}, bf16[512,4096]{1,0:T(8,128)(2,1)}, u32[]{:S(2)}, u32[]{:S(2)}) collective-permute-start(bf16[512,4096]{1,0:T(8,128)(2,1)} %refs_14_), channel_id=1, source_target_pairs={{0,1},{1,0},{2,3},{3,2},{4,5},{5,4},{6,7},{7,6},{8,9},{9,8},{10,11... | collective-permute-start | bytes 12582920 | tf_op jit(solution)/shard_map/ppermute | solution.py:26
  6.7 7.1 %copy-start = (bf16[896,512]{1,0:T(8,128)(2,1)S(1)}, bf16[896,512]{1,0:T(8,128)(2,1)}, u32[]{:S(2)}) copy-start(bf16[896,512]{1,0:T(8,128)(2,1)} %refs_10_) | copy-start | bytes 2752516
  6.8 7.9 %copy-start.1 = (bf16[896,512]{1,0:T(8,128)(2,1)S(1)}, bf16[896,512]{1,0:T(8,128)(2,1)}, u32[]{:S(2)}) copy-start(bf16[896,512]{1,0:T(8,128)(2,1)} %refs_11_) | copy-start | bytes 2752516
  6.8 9.2 %copy-start.20 = (s32[4]{0:T(128)S(1)}, s32[4]{0:T(128)}, u32[]{:S(2)}) copy-start(s32[4]{0:T(128)} %constant.54.clone) | copy-start | bytes 52
  6.8 26.0 %all-to-all-start = ((bf16[16,3,16,896]{3,2,1,0:T(8,128)(2,1)}), bf16[16,3,16,896]{3,2,1,0:T(8,128)(2,1)}, u32[]{:S(2)}, u32[]{:S(2)}) async-start(bf16[16,3,16,896]{3,2,1,0:T(8,128)(2,1)} %bitcast.22), calls=%async_computation | async-start | bytes 2752512 | tf_op jit(solution)/shard_map/all_to_all | solution.py:325
  13.8 15.0 %collective-permute-start = (bf16[896,512]{1,0:T(8,128)(2,1)S(1)}, bf16[896,512]{1,0:T(8,128)(2,1)S(1)}, u32[]{:S(2)}, u32[]{:S(2)}) collective-permute-start(bf16[896,512]{1,0:T(8,128)(2,1)S(1)} %copy-done), channel_id=1, source_target_pairs={{0,1},{1,0},{2,3},{3,2},{4,5},{5,4},{6,7},{7,6},{8,9},{9,8},{10,11... | collective-permute-start | bytes 2752520 | tf_op jit(solution)/shard_map/ppermute | solution.py:26
  14.7 14.1 %collective-permute-start.1 = (bf16[896,512]{1,0:T(8,128)(2,1)S(1)}, bf16[896,512]{1,0:T(8,128)(2,1)}, u32[]{:S(2)}, u32[]{:S(2)}) collective-permute-start(bf16[896,512]{1,0:T(8,128)(2,1)S(1)} %copy-done.1), channel_id=1, source_target_pairs={{0,1},{1,0},{2,3},{3,2},{4,5},{5,4},{6,7},{7,6},{8,9},{9,8},{10,11... | collective-permute-start | bytes 2752520 | tf_op jit(solution)/shard_map/ppermute | solution.py:26
  16.0 12.8 %copy-start.19 = (s32[4]{0:T(128)}, s32[4]{0:T(128)S(1)}, u32[]{:S(2)}) copy-start(s32[4]{0:T(128)S(1)} %get-tuple-element.101.place_ref) | copy-start | bytes 52
  28.8 17.7 %copy-start.2 = (bf16[896,512]{1,0:T(8,128)(2,1)}, bf16[896,512]{1,0:T(8,128)(2,1)S(1)}, u32[]{:S(2)}) copy-start(bf16[896,512]{1,0:T(8,128)(2,1)S(1)} %collective-permute-done.refs_4_.refs_6_.refs_12_) | copy-start | bytes 2752516
  35.8 9.2 %collective-permute-start.8 = (bf16[256,896]{1,0:T(8,128)(2,1)}, bf16[256,896]{1,0:T(8,128)(2,1)S(1)}, u32[]{:S(2)}, u32[]{:S(2)}) collective-permute-start(bf16[256,896]{1,0:T(8,128)(2,1)} %bitcast.33), channel_id=1, source_target_pairs={{0,1},{1,0},{2,3},{3,2},{4,5},{5,4},{6,7},{7,6},{8,9},{9,8},{10,11... | collective-permute-start | bytes 1376264 | tf_op jit(solution)/shard_map/ppermute | solution.py:356
  39.5 15.0 %collective-permute-start.6 = (bf16[256,896]{1,0:T(8,128)(2,1)}, bf16[256,896]{1,0:T(8,128)(2,1)S(1)}, u32[]{:S(2)}, u32[]{:S(2)}) collective-permute-start(bf16[256,896]{1,0:T(8,128)(2,1)} %bitcast.34), channel_id=1, source_target_pairs={{0,3},{1,2},{2,5},{3,4},{4,7},{5,6},{6,1},{7,0},{8,11},{9,10},{10,... | collective-permute-start | bytes 1376264 | tf_op jit(solution)/shard_map/ppermute | solution.py:356
  41.1 13.4 %collective-permute-start.5 = (bf16[256,896]{1,0:T(8,128)(2,1)}, bf16[256,896]{1,0:T(8,128)(2,1)S(1)}, u32[]{:S(2)}, u32[]{:S(2)}) collective-permute-start(bf16[256,896]{1,0:T(8,128)(2,1)} %bitcast.35), channel_id=1, source_target_pairs={{0,7},{1,6},{2,1},{3,0},{4,3},{5,2},{6,5},{7,4},{8,15},{9,14},{10,... | collective-permute-start | bytes 1376264 | tf_op jit(solution)/shard_map/ppermute | solution.py:356
  43.3 20.3 %collective-permute-start.7 = (bf16[256,896]{1,0:T(8,128)(2,1)}, bf16[256,896]{1,0:T(8,128)(2,1)S(1)}, u32[]{:S(2)}, u32[]{:S(2)}) collective-permute-start(bf16[256,896]{1,0:T(8,128)(2,1)} %bitcast.23), channel_id=1, source_target_pairs={{0,6},{1,7},{2,0},{3,1},{4,2},{5,3},{6,4},{7,5},{8,14},{9,15},{10,... | collective-permute-start | bytes 1376264 | tf_op jit(solution)/shard_map/ppermute | solution.py:356
  45.0 19.1 %collective-permute-start.4 = (bf16[256,896]{1,0:T(8,128)(2,1)}, bf16[256,896]{1,0:T(8,128)(2,1)S(1)}, u32[]{:S(2)}, u32[]{:S(2)}) collective-permute-start(bf16[256,896]{1,0:T(8,128)(2,1)} %bitcast.24), channel_id=1, source_target_pairs={{0,2},{1,3},{2,4},{3,5},{4,6},{5,7},{6,0},{7,1},{8,10},{9,11},{10,... | collective-permute-start | bytes 1376264 | tf_op jit(solution)/shard_map/ppermute | solution.py:356
  45.0 1.5 %copy-start.4 = (bf16[256,896]{1,0:T(8,128)(2,1)}, bf16[256,896]{1,0:T(8,128)(2,1)S(1)}, u32[]{:S(2)}) copy-start(bf16[256,896]{1,0:T(8,128)(2,1)S(1)} %collective-permute-done.8.refs_1_) | copy-start | bytes 1376260
  45.0 19.1 %collective-permute-start.9 = (bf16[64,1024]{1,0:T(8,128)(2,1)}, bf16[64,1024]{1,0:T(8,128)(2,1)S(1)}, u32[]{:S(2)}, u32[]{:S(2)}) collective-permute-start(bf16[64,1024]{1,0:T(8,128)(2,1)} %get-tuple-element.72), channel_id=1, source_target_pairs={{8,1},{16,9},{24,17},{32,25},{40,33},{48,41},{56,49},{64,57},{72,6... | collective-permute-start | bytes 393224 | tf_op jit(solution)/shard_map/ppermute | solution.py:370
  54.5 12.3 %copy-start.6 = (bf16[256,896]{1,0:T(8,128)(2,1)}, bf16[256,896]{1,0:T(8,128)(2,1)S(1)}, u32[]{:S(2)}) copy-start(bf16[256,896]{1,0:T(8,128)(2,1)S(1)} %collective-permute-done.6.refs_2_) | copy-start | bytes 1376260
  54.5 12.3 %copy-start.5 = (bf16[256,896]{1,0:T(8,128)(2,1)}, bf16[256,896]{1,0:T(8,128)(2,1)S(1)}, u32[]{:S(2)}) copy-start(bf16[256,896]{1,0:T(8,128)(2,1)S(1)} %collective-permute-done.5.refs_1_) | copy-start | bytes 1376260
  63.5 3.3 %copy-start.7 = (bf16[256,896]{1,0:T(8,128)(2,1)}, bf16[256,896]{1,0:T(8,128)(2,1)S(1)}, u32[]{:S(2)}) copy-start(bf16[256,896]{1,0:T(8,128)(2,1)S(1)} %collective-permute-done.7.refs_3_) | copy-start | bytes 1376260
  64.1 2.8 %copy-start.8 = (bf16[256,896]{1,0:T(8,128)(2,1)}, bf16[256,896]{1,0:T(8,128)(2,1)S(1)}, u32[]{:S(2)}) copy-start(bf16[256,896]{1,0:T(8,128)(2,1)S(1)} %collective-permute-done.4.refs_0_) | copy-start | bytes 1376260
  64.1 10.6 %copy-start.3 = (bf16[64,1024]{1,0:T(8,128)(2,1)}, bf16[64,1024]{1,0:T(8,128)(2,1)S(1)}, u32[]{:S(2)}) copy-start(bf16[64,1024]{1,0:T(8,128)(2,1)S(1)} %collective-permute-done.9.refs_15_.refs_13_) | copy-start | bytes 393220
  64.1 12.7 %collective-permute-start.10 = (bf16[256,896]{1,0:T(8,128)(2,1)S(1)}, bf16[256,896]{1,0:T(8,128)(2,1)S(1)}, u32[]{:S(2)}, u32[]{:S(2)}) collective-permute-start(bf16[256,896]{1,0:T(8,128)(2,1)S(1)} %collective-permute-done.4.refs_0_), channel_id=1, source_target_pairs={{0,2},{1,3},{2,4},{3,5},{4,6},{5,7},{6,0},{7,1},{8,10},{9,11},{10,... | collective-permute-start | bytes 1376264 | tf_op jit(solution)/shard_map/ppermute | solution.py:356
  65.5 11.3 %collective-permute-start.11 = (bf16[256,896]{1,0:T(8,128)(2,1)S(1)}, bf16[256,896]{1,0:T(8,128)(2,1)S(1)}, u32[]{:S(2)}, u32[]{:S(2)}) collective-permute-start(bf16[256,896]{1,0:T(8,128)(2,1)S(1)} %collective-permute-done.5.refs_1_), channel_id=1, source_target_pairs={{0,6},{1,7},{2,0},{3,1},{4,2},{5,3},{6,4},{7,5},{8,14},{9,15},{10,... | collective-permute-start | bytes 1376264 | tf_op jit(solution)/shard_map/ppermute | solution.py:356
  76.7 0.8 copy-start.9
  76.8 0.9 copy-start.10
  88.9 13.4 %collective-permute-start.12 = (bf16[64,4096]{1,0:T(8,128)(2,1)}, bf16[64,4096]{1,0:T(8,128)(2,1)S(1)}, u32[]{:S(2)}, u32[]{:S(2)}) collective-permute-start(bf16[64,4096]{1,0:T(8,128)(2,1)} %get-tuple-element.99), channel_id=1, source_target_pairs={{0,2},{2,4},{4,6},{6,0},{1,3},{3,5},{5,7},{7,1},{8,10},{10,12},{12... | collective-permute-start | bytes 1572872 | tf_op jit(solution)/shard_map/ppermute | solution.py:26
  90.0 12.3 %collective-permute-start.13 = (bf16[64,4096]{1,0:T(8,128)(2,1)}, bf16[64,4096]{1,0:T(8,128)(2,1)S(1)}, u32[]{:S(2)}, u32[]{:S(2)}) collective-permute-start(bf16[64,4096]{1,0:T(8,128)(2,1)} %get-tuple-element.100), channel_id=1, source_target_pairs={{0,6},{2,0},{4,2},{6,4},{1,7},{3,1},{5,3},{7,5},{8,14},{10,8},{12,... | collective-permute-start | bytes 1572872 | tf_op jit(solution)/shard_map/ppermute | solution.py:26
  91.6 10.6 %copy-start.17 = (bf16[64,2048]{1,0:T(8,128)(2,1)S(1)}, bf16[64,2048]{1,0:T(8,128)(2,1)}, u32[]{:S(2)}) copy-start(bf16[64,2048]{1,0:T(8,128)(2,1)} %get-tuple-element.110) | copy-start | bytes 786436
  91.6 10.6 %copy-start.18 = (bf16[64,2048]{1,0:T(8,128)(2,1)S(1)}, bf16[64,2048]{1,0:T(8,128)(2,1)}, u32[]{:S(2)}) copy-start(bf16[64,2048]{1,0:T(8,128)(2,1)} %get-tuple-element.112) | copy-start | bytes 786436
  91.6 17.3 %copy-start.16 = (bf16[64,2048]{1,0:T(8,128)(2,1)S(1)}, bf16[64,2048]{1,0:T(8,128)(2,1)}, u32[]{:S(2)}) copy-start(bf16[64,2048]{1,0:T(8,128)(2,1)} %get-tuple-element.98) | copy-start | bytes 786436
  101.0 8.0 %copy-start.15 = (bf16[64,2048]{1,0:T(8,128)(2,1)S(1)}, bf16[64,2048]{1,0:T(8,128)(2,1)}, u32[]{:S(2)}) copy-start(bf16[64,2048]{1,0:T(8,128)(2,1)} %get-tuple-element.114) | copy-start | bytes 786436
  102.3 21.7 %copy-start.12 = (bf16[64,2048]{1,0:T(8,128)(2,1)S(1)}, bf16[64,2048]{1,0:T(8,128)(2,1)}, u32[]{:S(2)}) copy-start(bf16[64,2048]{1,0:T(8,128)(2,1)} %get-tuple-element.123) | copy-start | bytes 786436
  102.4 21.6 %copy-start.11 = (bf16[64,2048]{1,0:T(8,128)(2,1)S(1)}, bf16[64,2048]{1,0:T(8,128)(2,1)}, u32[]{:S(2)}) copy-start(bf16[64,2048]{1,0:T(8,128)(2,1)} %get-tuple-element.121) | copy-start | bytes 786436
  102.4 6.5 %collective-permute-start.14 = (bf16[64,2048]{1,0:T(8,128)(2,1)S(1)}, bf16[64,2048]{1,0:T(8,128)(2,1)S(1)}, u32[]{:S(2)}, u32[]{:S(2)}) collective-permute-start(bf16[64,2048]{1,0:T(8,128)(2,1)S(1)} %get-tuple-element.113), channel_id=1, source_target_pairs={{0,2},{2,4},{4,6},{6,0},{1,3},{3,5},{5,7},{7,1},{8,10},{10,12},{12... | collective-permute-start | bytes 786440 | tf_op jit(solution)/shard_map/ppermute | solution.py:26
  102.5 6.5 %collective-permute-start.15 = (bf16[64,2048]{1,0:T(8,128)(2,1)S(1)}, bf16[64,2048]{1,0:T(8,128)(2,1)S(1)}, u32[]{:S(2)}, u32[]{:S(2)}) collective-permute-start(bf16[64,2048]{1,0:T(8,128)(2,1)S(1)} %get-tuple-element.115), channel_id=1, source_target_pairs={{0,6},{2,0},{4,2},{6,4},{1,7},{3,1},{5,3},{7,5},{8,14},{10,8},{12,... | collective-permute-start | bytes 786440 | tf_op jit(solution)/shard_map/ppermute | solution.py:26
  105.2 15.3 %collective-permute-start.17 = (bf16[64,4096]{1,0:T(8,128)(2,1)}, bf16[64,4096]{1,0:T(8,128)(2,1)S(1)}, u32[]{:S(2)}, u32[]{:S(2)}) collective-permute-start(bf16[64,4096]{1,0:T(8,128)(2,1)} %get-tuple-element.116), channel_id=1, source_target_pairs={{0,2},{2,4},{4,6},{6,0},{1,3},{3,5},{5,7},{7,1},{8,10},{10,12},{12... | collective-permute-start | bytes 1572872 | tf_op jit(solution)/shard_map/ppermute | solution.py:26
  105.2 15.3 %collective-permute-start.18 = (bf16[64,4096]{1,0:T(8,128)(2,1)}, bf16[64,4096]{1,0:T(8,128)(2,1)S(1)}, u32[]{:S(2)}, u32[]{:S(2)}) collective-permute-start(bf16[64,4096]{1,0:T(8,128)(2,1)} %get-tuple-element.117), channel_id=1, source_target_pairs={{0,6},{2,0},{4,2},{6,4},{1,7},{3,1},{5,3},{7,5},{8,14},{10,8},{12,... | collective-permute-start | bytes 1572872 | tf_op jit(solution)/shard_map/ppermute | solution.py:26
  109.2 24.3 %copy-start.14 = (bf16[64,2048]{1,0:T(8,128)(2,1)S(1)}, bf16[64,2048]{1,0:T(8,128)(2,1)}, u32[]{:S(2)}) copy-start(bf16[64,2048]{1,0:T(8,128)(2,1)} %get-tuple-element.119) | copy-start | bytes 786436
  109.2 14.7 %collective-permute-start.16 = (bf16[64,4096]{1,0:T(8,128)(2,1)S(1)}, bf16[64,4096]{1,0:T(8,128)(2,1)S(1)}, u32[]{:S(2)}, u32[]{:S(2)}) collective-permute-start(bf16[64,4096]{1,0:T(8,128)(2,1)S(1)} %pad_maximum_fusion.1), channel_id=1, source_target_pairs={{0,1},{1,8},{2,3},{3,2},{4,5},{5,4},{6,7},{7,6},{8,9},{9,16},{10,1... | collective-permute-start | bytes 1572872 | tf_op jit(solution)/shard_map/ppermute | solution.py:395
  124.0 9.6 %copy-start.13 = (bf16[64,2048]{1,0:T(8,128)(2,1)S(1)}, bf16[64,2048]{1,0:T(8,128)(2,1)}, u32[]{:S(2)}) copy-start(bf16[64,2048]{1,0:T(8,128)(2,1)} %get-tuple-element.125) | copy-start | bytes 786436
  124.1 9.3 %collective-permute-start.19 = (bf16[64,2048]{1,0:T(8,128)(2,1)S(1)}, bf16[64,2048]{1,0:T(8,128)(2,1)S(1)}, u32[]{:S(2)}, u32[]{:S(2)}) collective-permute-start(bf16[64,2048]{1,0:T(8,128)(2,1)S(1)} %add_convert_fusion.3), channel_id=1, source_target_pairs={{0,2},{2,4},{4,6},{6,0},{1,3},{3,5},{5,7},{7,1},{8,10},{10,12},{12... | collective-permute-start | bytes 786440 | tf_op jit(solution)/shard_map/ppermute | solution.py:26
  124.3 9.2 %collective-permute-start.20 = (bf16[64,2048]{1,0:T(8,128)(2,1)S(1)}, bf16[64,2048]{1,0:T(8,128)(2,1)S(1)}, u32[]{:S(2)}, u32[]{:S(2)}) collective-permute-start(bf16[64,2048]{1,0:T(8,128)(2,1)S(1)} %add_convert_fusion.2), channel_id=1, source_target_pairs={{0,6},{2,0},{4,2},{6,4},{1,7},{3,1},{5,3},{7,5},{8,14},{10,8},{12,... | collective-permute-start | bytes 786440 | tf_op jit(solution)/shard_map/ppermute | solution.py:26

commit v6 on v5

--- a/solution.py
+++ b/solution.py
@@ -19,6 +19,7 @@
 BF16 = jnp.bfloat16
 SHARE = 0.4
 LIMIT = 60 * 1024 * 1024
+GRANT = 32 * 1024 * 1024
 
 
 def step(value, axis, steps):
@@ -55,7 +56,7 @@
             place += 1
 
 
-def pick(source, index, start, rows, counts):
+def pick(source, index, start, rows, counts, limit):
     shapes = [(count, rows, source.shape[2]) for count in counts]
     return pl.pallas_call(
         pick_kernel,
@@ -68,7 +69,7 @@
         ),
         out_shape=[jax.ShapeDtypeStruct(shape, source.dtype) for shape in shapes],
         cost_estimate=cost(1e9),
-        compiler_params=pltpu.CompilerParams(vmem_limit_bytes=LIMIT),
+        compiler_params=pltpu.CompilerParams(vmem_limit_bytes=limit * 1024 * 1024),
     )(index, start.reshape(1), source)
 
 
@@ -128,25 +129,10 @@
     )(core.reshape(1), blocks, weight_a, weight_b)
 
 
-def project_kernel(*refs):
-    row_hbm, weight_hbm, out_hbm = refs[:-18], refs[-18:-14], refs[-14:-10]
-    rows_ref, weight_refs, out_refs, sems = refs[-10], refs[-9:-5], refs[-5:-1], refs[-1]
-    parts, rows, enc = rows_ref.shape
-    row_copies = [pltpu.make_async_copy(row_hbm[i], rows_ref.at[i], sems.at[i]) for i in range(parts)]
-    weight_copies = [pltpu.make_async_copy(weight_hbm[i], weight_refs[i], sems.at[parts + i]) for i in range(4)]
-    out_copies = [pltpu.make_async_copy(out_refs[i], out_hbm[i], sems.at[parts + 4 + i]) for i in range(4)]
-    for copy in row_copies + weight_copies:
-        copy.start()
-    for copy in row_copies:
-        copy.wait()
-    for i in range(4):
-        weight_copies[i].wait()
-        for part in range(0, parts, 2):
-            product = dot(rows_ref[part : part + 2].reshape(2 * rows, enc), weight_refs[i][...]).astype(BF16)
-            out_refs[i][part : part + 2] = product.reshape((2,) + out_refs[i].shape[1:])
-        out_copies[i].start()
-    for copy in out_copies:
-        copy.wait()
+def project_kernel(low_ref, high_ref, *refs):
+    rows = jnp.concatenate([low_ref[...], high_ref[...]], axis=0)
+    for weight_ref, out_ref in zip(refs[:4], refs[4:]):
+        out_ref[...] = dot(rows, weight_ref[...]).astype(BF16).reshape(out_ref.shape)
 
 
 def project(weights, parts):
@@ -155,15 +141,9 @@
     shape = (len(parts), 2, N_Z, rows // (2 * N_Z), width)
     return pl.pallas_call(
         project_kernel,
-        in_specs=[pl.BlockSpec(memory_space=pltpu.HBM)] * (len(parts) + 4),
-        out_specs=[pl.BlockSpec(memory_space=pltpu.HBM)] * 4,
         out_shape=[jax.ShapeDtypeStruct(shape, BF16)] * 4,
-        scratch_shapes=[pltpu.VMEM((len(parts), rows, enc), BF16)]
-        + [pltpu.VMEM((enc, width), BF16)] * 4
-        + [pltpu.VMEM(shape, BF16)] * 4
-        + [pltpu.SemaphoreType.DMA((len(parts) + 8,))],
         cost_estimate=cost(2e9),
-        compiler_params=pltpu.CompilerParams(vmem_limit_bytes=LIMIT),
+        compiler_params=pltpu.CompilerParams(vmem_limit_bytes=GRANT),
     )(*parts, *weights)
 
 
@@ -175,57 +155,24 @@
         del refs[:count]
         return taken
 
-    near_hbm, far_hbm = take(8), take(6 if group == 0 else 4)
-    q_hbm, crossing_hbm = take(2)
-    out_weight_hbm, out_hbm = take(2), take(6)
-    later_hbm = take(4 if group == 0 else 0)
-    kv_refs, out_refs, out_weight_refs = take(4), take(6), take(2)
-    q_ref, crossing_ref, context_ref = take(3)
-    rows_ref, *weight_refs = take(5 if group == 0 else 0) or [None]
-    later_refs = take(4 if group == 0 else 0)
-    in_sems, out_sems = refs
-    used = [0, 0]
-
-    def copy_in(source, target):
-        used[0] += 1
-        return pltpu.make_async_copy(source, target, in_sems.at[used[0] - 1])
-
-    def copy_out(source, target):
-        used[1] += 1
-        return pltpu.make_async_copy(source, target, out_sems.at[used[1] - 1])
-
+    near_refs, row_refs, weight_refs = take(12), take(2), take(4)
+    q_ref, crossing_ref = take(2)
+    out_weight_refs, out_refs, far_kv_refs = take(2), take(6), take(4)
+    count = row_refs[0].shape[0] // 2
+    rows = jnp.concatenate([ref[group * count : (group + 1) * count] for ref in row_refs], axis=0)
+    for weight_ref, far_kv_ref in zip(weight_refs, far_kv_refs):
+        far_kv_ref[...] = dot(rows, weight_ref[...]).astype(BF16).reshape(far_kv_ref.shape)
+    (context_ref,) = refs
     half, model = out_weight_refs[0].shape
-    own, parts = near_hbm[0].shape[0], near_hbm[0].shape[0] + near_hbm[4].shape[0]
-    if group == 0:
-        far_copies = [copy_in(far_hbm[i], rows_ref.at[i]) for i in range(2)]
-        weight_copies = [copy_in(far_hbm[2 + i], weight_refs[i]) for i in range(4)]
-    else:
-        far_copies = [copy_in(far_hbm[i], kv_refs[i].at[parts:]) for i in range(4)]
-        weight_copies = []
-    near_copies = [copy_in(near_hbm[i].at[:, group], kv_refs[i].at[:own]) for i in range(4)]
-    near_copies += [copy_in(near_hbm[4 + i].at[:, group], kv_refs[i].at[own:parts]) for i in range(4)]
-    query_copies = [copy_in(q_hbm, q_ref), copy_in(crossing_hbm, crossing_ref)]
-    out_weight_copies = [copy_in(out_weight_hbm[i], out_weight_refs[i]) for i in range(2)]
-    for copy in far_copies + weight_copies + near_copies + query_copies + out_weight_copies:
-        copy.start()
-    for copy in far_copies:
-        copy.wait()
-    later_copies = []
-    for i, copy in enumerate(weight_copies):
-        copy.wait()
-        product = dot(rows_ref[...].reshape(-1, rows_ref.shape[2]), weight_refs[i][...]).astype(BF16)
-        product = product.reshape(2, 2, *kv_refs[i].shape[1:])
-        kv_refs[i][parts:] = product[:, 0]
-        later_refs[i][...] = product[:, 1]
-        later_copies.append(copy_out(later_refs[i], later_hbm[i]))
-        later_copies[i].start()
-    for copy in near_copies + query_copies:
-        copy.wait()
-
     is_first_row = lax.broadcasted_iota(jnp.int32, (CL, HS), 0) == 0
     heads = [(side, lower) for side in (0, 1) for lower in range(0, half, HS)]
 
     def attend_span(span, carry):
+        def columns(i, lower):
+            parts = [near_refs[j][:, group, span, :, lower : lower + HS] for j in range(i, 12, 4)]
+            parts.append(far_kv_refs[i][:, span, :, lower : lower + HS])
+            return jnp.concatenate([part.reshape(-1, HS) for part in parts], axis=0)
+
         crosses = (span == N_Z - 1) & (place_ref[N_Z] == 1)
         scores = []
         for side, lower in heads:
@@ -233,7 +180,7 @@
             q = q_ref[span, :, place]
             if group == 0:
                 q = jnp.where(is_first_row | jnp.logical_not(crosses), q, crossing_ref[:, place])
-            k = kv_refs[2 * side][:, span, :, lower : lower + HS].reshape(-1, HS)
+            k = columns(2 * side, lower)
             scores.append(lax.dot_general(q, k, (((1,), (1,)), ((), ())), preferred_element_type=F32))
         probs = []
         for score in scores:
@@ -242,14 +189,12 @@
             total = jnp.sum(weights, axis=-1, keepdims=True)
             probs.append((weights * (1.0 / total)).astype(BF16))
         for (side, lower), prob in zip(heads, probs):
-            v = kv_refs[2 * side + 1][:, span, :, lower : lower + HS].reshape(-1, HS)
+            v = columns(2 * side + 1, lower)
             context_ref[span, :, side * half + lower : side * half + lower + HS] = dot(prob, v).astype(BF16)
         return carry
 
     lax.fori_loop(0, N_Z, attend_span, 0)
 
-    for copy in out_weight_copies:
-        copy.wait()
     blocks = [context_ref[place_ref[i]] for i in range(N_Z)]
     if group == 0:
         is_first_row = lax.broadcasted_iota(jnp.int32, blocks[0].shape, 0) == 0
@@ -257,7 +202,6 @@
     context = jnp.concatenate(blocks, axis=0)
     up, down, above, below, here_left, here_right = out_refs
     tile = model // 4
-    out_copies = [copy_out(out_refs[i], out_hbm[i]) for i in range(6)]
     for lower in range(0, model, tile):
         place = slice(lower, lower + tile)
         product = dot(context[:, :half], out_weight_refs[0][:, place])
@@ -268,39 +212,27 @@
             up[:, place], down[:, place], above[:, inner], here_left[:, inner] = blocks[0], blocks[2], blocks[1], blocks[3]
         else:
             up[:, place], down[:, place], below[:, inner], here_right[:, inner] = blocks[1], blocks[0], blocks[2], blocks[3]
-        if lower + tile == model // 2:
-            out_copies[2].start()
-            out_copies[4].start()
-    for i in (0, 1, 3, 5):
-        out_copies[i].start()
-    for copy in later_copies + out_copies:
-        copy.wait()
-
-
-def attend(group, places, queries, crossing, near, far, out_weights):
+
+
+def attend(group, places, queries, crossing, near, far, weights):
     spans, tokens, width = queries.shape
-    half, model = out_weights[0].shape
-    parts, rows = near[0].shape[0] + near[4].shape[0], near[0].shape[3]
+    half, model = weights[4].shape
     outs = [(tokens, model)] * 2 + [(tokens, model // 2)] * 4
-    scratch = [(parts + 2, spans, rows, half)] * 4 + outs + [(half, model)] * 2
-    scratch += [queries.shape, crossing.shape, queries.shape]
-    later = [(2, spans, rows, half)] * 4 if group == 0 else []
-    if group == 0:
-        scratch += [(2,) + far[0].shape] + [weight.shape for weight in far[2:]] + later
-    operands = (*near, *far, queries, crossing, *out_weights)
+    scratch = [(2, spans, near[0].shape[3], half)] * 4 + [queries.shape]
+    operands = (*near, *far, *weights[:4], queries, crossing, *weights[4:])
+    vmem = pl.BlockSpec(memory_space=pltpu.VMEM)
     return pl.pallas_call(
         functools.partial(span_kernel, group),
         grid_spec=pltpu.PrefetchScalarGridSpec(
             num_scalar_prefetch=1,
-            grid=(1,),
-            in_specs=[pl.BlockSpec(memory_space=pltpu.HBM)] * len(operands),
-            out_specs=[pl.BlockSpec(memory_space=pltpu.HBM)] * (6 + len(later)),
-            scratch_shapes=[pltpu.VMEM(shape, BF16) for shape in scratch]
-            + [pltpu.SemaphoreType.DMA((len(operands),)), pltpu.SemaphoreType.DMA((6 + len(later),))],
+            grid=(),
+            in_specs=[vmem] * len(operands),
+            out_specs=[vmem] * len(outs),
+            scratch_shapes=[pltpu.VMEM(shape, BF16) for shape in scratch],
         ),
-        out_shape=[jax.ShapeDtypeStruct(shape, BF16) for shape in outs + later],
+        out_shape=[jax.ShapeDtypeStruct(shape, BF16) for shape in outs],
         cost_estimate=cost(5e9),
-        compiler_params=pltpu.CompilerParams(vmem_limit_bytes=LIMIT),
+        compiler_params=pltpu.CompilerParams(vmem_limit_bytes=GRANT),
     )(places, *operands)
 
 
@@ -321,7 +253,7 @@
     places = bucket_places(shard_lists)
     picked = (shard_lists == seq_index)[:, None, :] & (places[:, None, :] == jnp.arange(capacity)[None, :, None])
     send_slot = jnp.sum(jnp.where(picked, slot_lists[:, None, :], 0), axis=2)
-    (outgoing,) = pick(database, send_slot.reshape(-1), z_index * N_CORE + core, piece, [n_seq * capacity])
+    (outgoing,) = pick(database, send_slot.reshape(-1), z_index * N_CORE + core, piece, [n_seq * capacity], 60)
     received = lax.all_to_all(
         outgoing.reshape(n_seq, capacity, piece, enc), "seq", split_axis=0, concat_axis=0, tiled=True
     )
@@ -344,7 +276,7 @@
     row_index = row_index.transpose(2, 3, 1, 0)[:, ::-1]
     row_index = jnp.where(core == 0, row_index, row_index[::-1]).reshape(-1)
     count = row_index.shape[0] // 2
-    mine, theirs = pick(received, row_index, jnp.zeros((), jnp.int32), piece, [count] * 2)
+    mine, theirs = pick(received, row_index, jnp.zeros((), jnp.int32), piece, [count] * 2, 30)
     mine, theirs = mine.reshape(-1, enc), theirs.reshape(-1, enc)
 
     def hop(value, steps, cross):
@@ -364,21 +296,18 @@
         left, right = add(here_left, down[:, :side], up_left), add(here_right, up[:, side:], down_right)
         return jnp.concatenate([left, right], axis=1)
 
-    ring = [hop(mine, 1, 0), hop(theirs, -1, 1), hop(theirs, 1, 1), hop(mine, -1, 0)]
+    ring = hop(mine, 1, 0), hop(theirs, -1, 1)
     swapped = hop(theirs, 0, 1)
-    swapped, crossing = lax.optimization_barrier((swapped, crossing))
+    near = project(weights[:4], (mine, swapped))
+    near, mine, theirs, crossing = lax.optimization_barrier((near, mine, theirs, crossing))
+    ring_after = hop(theirs, 1, 1), hop(mine, -1, 0)
     crossing = lax.ppermute(crossing, ("seq", "core"), [(2 * i + 2, 2 * i + 1) for i in range(n_seq - 1)])
-    near = project(weights[:4], (mine, swapped))
-    ring, crossing, near = lax.optimization_barrier((ring, crossing, near))
     far = hop(ring[0], 1, 0), hop(ring[1], -1, 0)
-    near = (*near, *project(weights[:4], ring))
-
-    up_a, down_a, above_a, below_a, *rest = attend(
-        0, places_a, second_queries, crossing, near, (*far, *weights[:4]), weights[4:]
-    )
-    here_a, far = rest[:2], rest[2:]
+    near = (*near, *project(weights[:4], ring), *project(weights[:4], ring_after))
+
+    up_a, down_a, above_a, below_a, *here_a = attend(0, places_a, second_queries, crossing, near, far, weights)
     up_a, down_a = step(up_a, "z", 1), step(down_a, "z", -1)
-    up_b, down_b, above_b, below_b, *here_b = attend(1, places_b, first_queries, crossing, near, far, weights[4:])
+    up_b, down_b, above_b, below_b, *here_b = attend(1, places_b, first_queries, crossing, near, far, weights)
     up_a, down_a, up_b, down_b = lax.optimization_barrier((up_a, down_a, up_b, down_b))
     above_a, below_a = lax.optimization_barrier((add(above_a, up_a[:, :side]), add(below_a, down_a[:, side:])))
     up_left_a, down_right_a = step(above_a, "z", 1), step(below_a, "z", -1)

time: 135 us -> 130 us (0.963)
  Pallas kernels: 51.7 us -> 45.8 us
  starting transfers between devices: 42.4 us -> 44.3 us
  local copies, waits for them, and re-layouts: 3.27 us -> 1.72 us
    ppermute x7, starting transfers between devices: 11.9 us -> 14.7 us  [hop(): return lax.ppermute(value, ('z', 'core'), pairs)]
    pallas_call x2, Pallas kernels: 20.6 us -> 18.2 us  [attend(): pl.pallas_call(functools.partial(span_kernel, group), grid_spec=pltpu.Pre...]
    pallas_call x2 -> x3, Pallas kernels: 13 us -> 10.6 us  [project(): pl.pallas_call(project_kernel, out_shape=[jax.ShapeDtypeStruct(shape, BF1...]
  transfers between devices with their start and end apart: 22 -> 22, of which waited for: 10 -> 10; matrix products, arithmetic and copies ran while one was open for 3% -> 3% of each run, Pallas kernels for 28% -> 27%
where the time goes in v6:
time: 130 us; the launch traced here: 129 us
  Pallas kernels  45.8 us (35%)
  starting transfers between devices  44.3 us (34%)
  waiting for transfers between devices  33.8 us (26%)
  other arithmetic  3.29 us (3%)
  local copies, waits for them, and re-layouts  1.72 us (1%)
    pallas_call x2, Pallas kernels, attend(): pl.pallas_call(functools.partial(span_kernel, group), grid_spec=pltpu.Pre...  18.2 us
    ppermute x7, starting transfers between devices, hop(): return lax.ppermute(value, ('z', 'core'), pairs)  14.7 us
    ppermute x12, starting transfers between devices, step(): lax.ppermute(value, axis, [(i, (i + steps) % count) for i in range(count)])  13.4 us
    ppermute x7, waiting for transfers between devices, hop(): return lax.ppermute(value, ('z', 'core'), pairs)  13.2 us
    ppermute x12, waiting for transfers between devices, step(): lax.ppermute(value, axis, [(i, (i + steps) % count) for i in range(count)])  12.3 us
    pallas_call x1, Pallas kernels, project_queries(): pl.pallas_call(query_kernel, grid_spec=pltpu.PrefetchScalarGridSpec(num_s...  12 us
    pallas_call x3, Pallas kernels, project(): pl.pallas_call(project_kernel, out_shape=[jax.ShapeDtypeStruct(shape, BF1...  10.6 us
    ppermute x1, starting transfers between devices, body(): head = lax.ppermute(out_a, ('seq', 'z', 'core'), pairs)  7.91 us
  transfers between devices with their start and end apart: 22, of which 10 were waited for; matrix products, arithmetic and copies ran while one was open for 3% of the time, Pallas kernels for 27%

profile of v6, /device:TPU:1, one launch (start us, length us, event | category | flops | bytes accessed | tf_op | source)
XLA Modules:
  0.0 129.3 jit_solution(3594132852959694568)
XLA Ops:
  0.0 1.4 %collective-permute-start.3 = (bf16[4096,512]{1,0:T(8,128)(2,1)}, bf16[4096,512]{1,0:T(8,128)(2,1)}, u32[]{:S(2)}, u32[]{:S(2)}) collective-permute-start(bf16[4096,512]{1,0:T(8,128)(2,1)} %wa_hbm.1), channel_id=1, source_target_pairs={{0,1},{1,0},{2,3},{3,2},{4,5},{5,4},{6,7},{7,6},{8,9},{9,8},{10,11... | collective-permute-start | bytes 12582920 | tf_op jit(solution)/shard_map/ppermute | solution.py:27
  1.4 0.7 shift-right-arithmetic_bitcast_fusion
  2.5 0.5 convert_reduce_fusion
  3.0 0.1 select_reduce_fusion
  3.2 0.6 reshape.76.index_ref
  3.8 3.0 %shard_map.91 = bf16[48,16,896]{2,1,0:T(8,128)(2,1)} custom-call(s32[48]{0:T(128)} %reshape.76.index_ref, s32[1]{0:T(128)} %bitcast.4.start_ref, bf16[24,128,896]{2,1,0:T(8,128)(2,1)} %source_ref.1), custom_call_target="tpu_custom_call" | custom-call | flops 400000000 | bytes 400000 | tf_op jit(solution)/shard_map/pallas_call | solution.py:61
  6.9 7.0 %all-to-all-start = ((bf16[16,3,16,896]{3,2,1,0:T(8,128)(2,1)}), bf16[16,3,16,896]{3,2,1,0:T(8,128)(2,1)}, u32[]{:S(2)}, u32[]{:S(2)}) async-start(bf16[16,3,16,896]{3,2,1,0:T(8,128)(2,1)} %bitcast.28), calls=%async_computation | async-start | bytes 2752512 | tf_op jit(solution)/shard_map/all_to_all | solution.py:257
  13.9 0.9 collective-permute-start
  14.8 0.1 collective-permute-start.1
  14.9 0.1 add.89
  15.0 0.1 rev.7
  15.1 0.1 rev.6
  15.2 0.1 copy.18
  15.4 0.1 reshape.82.index_ref
  15.6 12.0 %shard_map.92 = (bf16[4,64,1024]{2,1,0:T(8,128)(2,1)}, bf16[4,64,1024]{2,1,0:T(8,128)(2,1)}, bf16[64,1024]{1,0:T(8,128)(2,1)}) custom-call(s32[1]{0:T(128)} %bitcast.7.core_ref, bf16[8,128,4096]{2,1,0:T(8,128)(2,1)} %bitcast.27, bf16[4096,512]{1,0:T(8,128)(2,1)} %wa_hbm.1, bf16[4096,512]{1,0:T(8,128)(2,1)} %collective-permute-done.3.wb_hbm), custom_call_target="tpu_custom_call" | custom-call | flops 1200000000 | bytes 1200000 | tf_op jit(solution)/shard_map/pallas_call | solution.py:112
  27.6 5.2 %all-to-all-done = bf16[16,3,16,896]{3,2,1,0:T(8,128)(2,1)} async-done(((bf16[16,3,16,896]{3,2,1,0:T(8,128)(2,1)}), bf16[16,3,16,896]{3,2,1,0:T(8,128)(2,1)}, u32[]{:S(2)}, u32[]{:S(2)}) %all-to-all-start) | async-done | bytes 1376288 | tf_op jit(solution)/shard_map/all_to_all | solution.py:257
  32.9 2.0 %shard_map.93 = (bf16[16,16,896]{2,1,0:T(8,128)(2,1)S(1)}, bf16[16,16,896]{2,1,0:T(8,128)(2,1)S(1)}) custom-call(s32[32]{0:T(128)S(1)} %reshape.82.index_ref, s32[1]{0:T(128)} %constant.53.clone.1.start_ref, bf16[48,16,896]{2,1,0:T(8,128)(2,1)} %bitcast.6.source_ref), custom_call_target="tpu_custom_call" | custom-call | flops 400000000 | bytes 400000 | tf_op jit(solution)/shard_map/pallas_call | solution.py:61
  34.8 3.7 %collective-permute-start.4 = (bf16[256,896]{1,0:T(8,128)(2,1)S(1)}, bf16[256,896]{1,0:T(8,128)(2,1)S(1)}, u32[]{:S(2)}, u32[]{:S(2)}) collective-permute-start(bf16[256,896]{1,0:T(8,128)(2,1)S(1)} %bitcast.24), channel_id=1, source_target_pairs={{0,1},{1,0},{2,3},{3,2},{4,5},{5,4},{6,7},{7,6},{8,9},{9,8},{10,11... | collective-permute-start | bytes 1376264 | tf_op jit(solution)/shard_map/ppermute | solution.py:288
  38.5 3.7 %collective-permute-start.6 = (bf16[256,896]{1,0:T(8,128)(2,1)S(1)}, bf16[256,896]{1,0:T(8,128)(2,1)S(1)}, u32[]{:S(2)}, u32[]{:S(2)}) collective-permute-start(bf16[256,896]{1,0:T(8,128)(2,1)S(1)} %bitcast.25), channel_id=1, source_target_pairs={{0,7},{1,6},{2,1},{3,0},{4,3},{5,2},{6,5},{7,4},{8,15},{9,14},{10,... | collective-permute-start | bytes 1376264 | tf_op jit(solution)/shard_map/ppermute | solution.py:288
  42.3 3.5 %shard_map.94 = (bf16[2,2,4,32,512]{4,3,2,1,0:T(8,128)(2,1)S(1)}, bf16[2,2,4,32,512]{4,3,2,1,0:T(8,128)(2,1)S(1)}, bf16[2,2,4,32,512]{4,3,2,1,0:T(8,128)(2,1)S(1)}, bf16[2,2,4,32,512]{4,3,2,1,0:T(8,128)(2,1)S(1)}) custom-call(bf16[256,896]{1,0:T(8,128)(2,1)S(1)} %bitcast.22, bf16[256,896]{1,0:T(8,128)(2,1)S(1)} %collective-permute-done.4.high_ref, ...), custom_call_target="tpu_custom_call" | custom-call | flops 800000000 | bytes 800000 | tf_op jit(solution)/shard_map/pallas_call | solution.py:142
  45.9 3.0 %collective-permute-start.8 = (bf16[256,896]{1,0:T(8,128)(2,1)S(1)}, bf16[256,896]{1,0:T(8,128)(2,1)S(1)}, u32[]{:S(2)}, u32[]{:S(2)}) collective-permute-start(bf16[256,896]{1,0:T(8,128)(2,1)S(1)} %bitcast.23), channel_id=1, source_target_pairs={{0,6},{1,7},{2,0},{3,1},{4,2},{5,3},{6,4},{7,5},{8,14},{9,15},{10,... | collective-permute-start | bytes 1376264 | tf_op jit(solution)/shard_map/ppermute | solution.py:288
  48.9 3.1 %collective-permute-done.6.high_ref = bf16[256,896]{1,0:T(8,128)(2,1)S(1)} collective-permute-done((bf16[256,896]{1,0:T(8,128)(2,1)S(1)}, bf16[256,896]{1,0:T(8,128)(2,1)S(1)}, u32[]{:S(2)}, u32[]{:S(2)}) %collective-permute-start.6) | collective-permute-done | bytes 458784 | tf_op jit(solution)/shard_map/ppermute | solution.py:288
  52.0 4.3 %collective-permute-start.10 = (bf16[256,896]{1,0:T(8,128)(2,1)S(1)}, bf16[256,896]{1,0:T(8,128)(2,1)S(1)}, u32[]{:S(2)}, u32[]{:S(2)}) collective-permute-start(bf16[256,896]{1,0:T(8,128)(2,1)S(1)} %collective-permute-done.6.high_ref), channel_id=1, source_target_pairs={{0,6},{1,7},{2,0},{3,1},{4,2},{5,3},{6,4},{7,5},{8,14},{9,15},{10,... | collective-permute-start | bytes 1376264 | tf_op jit(solution)/shard_map/ppermute | solution.py:288
  56.3 1.3 collective-permute-start.11
  57.6 3.6 %shard_map.95 = (bf16[2,2,4,32,512]{4,3,2,1,0:T(8,128)(2,1)S(1)}, bf16[2,2,4,32,512]{4,3,2,1,0:T(8,128)(2,1)S(1)}, bf16[2,2,4,32,512]{4,3,2,1,0:T(8,128)(2,1)S(1)}, bf16[2,2,4,32,512]{4,3,2,1,0:T(8,128)(2,1)S(1)}) custom-call(bf16[256,896]{1,0:T(8,128)(2,1)S(1)} %collective-permute-done.5.low_ref, bf16[256,896]{1,0:T(8,128)(2,1)S(1)} %collective-permute-done.6.high_ref, ...), custom_call_target="tpu_custom_call" | custom-call | flops 800000000 | bytes 800000 | tf_op jit(solution)/shard_map/pallas_call | solution.py:142
  61.2 5.2 %collective-permute-done.7.low_ref = bf16[256,896]{1,0:T(8,128)(2,1)S(1)} collective-permute-done((bf16[256,896]{1,0:T(8,128)(2,1)S(1)}, bf16[256,896]{1,0:T(8,128)(2,1)S(1)}, u32[]{:S(2)}, u32[]{:S(2)}) %collective-permute-start.7) | collective-permute-done | bytes 458784 | tf_op jit(solution)/shard_map/ppermute | solution.py:288
  66.4 3.5 %shard_map.96 = (bf16[2,2,4,32,512]{4,3,2,1,0:T(8,128)(2,1)S(1)}, bf16[2,2,4,32,512]{4,3,2,1,0:T(8,128)(2,1)S(1)}, bf16[2,2,4,32,512]{4,3,2,1,0:T(8,128)(2,1)S(1)}, bf16[2,2,4,32,512]{4,3,2,1,0:T(8,128)(2,1)S(1)}) custom-call(bf16[256,896]{1,0:T(8,128)(2,1)S(1)} %collective-permute-done.7.low_ref, bf16[256,896]{1,0:T(8,128)(2,1)S(1)} %collective-permute-done.8.high_ref, ...), custom_call_target="tpu_custom_call" | custom-call | flops 800000000 | bytes 800000 | tf_op jit(solution)/shard_map/pallas_call | solution.py:142
  69.9 1.7 %collective-permute-done.10.refs_13_ = bf16[256,896]{1,0:T(8,128)(2,1)S(1)} collective-permute-done((bf16[256,896]{1,0:T(8,128)(2,1)S(1)}, bf16[256,896]{1,0:T(8,128)(2,1)S(1)}, u32[]{:S(2)}, u32[]{:S(2)}) %collective-permute-start.10) | collective-permute-done | bytes 458784 | tf_op jit(solution)/shard_map/ppermute | solution.py:288
  71.7 3.1 %collective-permute-done.9.refs_12_ = bf16[256,896]{1,0:T(8,128)(2,1)S(1)} collective-permute-done((bf16[256,896]{1,0:T(8,128)(2,1)S(1)}, bf16[256,896]{1,0:T(8,128)(2,1)S(1)}, u32[]{:S(2)}, u32[]{:S(2)}) %collective-permute-start.9) | collective-permute-done | bytes 458784 | tf_op jit(solution)/shard_map/ppermute | solution.py:288
  74.8 9.1 %shard_map.97 = (bf16[64,4096]{1,0:T(8,128)(2,1)S(1)}, bf16[64,4096]{1,0:T(8,128)(2,1)S(1)}, bf16[64,2048]{1,0:T(8,128)(2,1)S(1)}, bf16[64,2048]{1,0:T(8,128)(2,...) custom-call(s32[9]{0:T(128)S(1)} %pad_add_fusion.place_ref, ...), custom_call_target="tpu_custom_call" | custom-call | flops 2000000000 | bytes 2000000 | tf_op jit(solution)/shard_map/pallas_call | solution.py:224
  84.0 2.7 %collective-permute-start.13 = (bf16[64,4096]{1,0:T(8,128)(2,1)S(1)}, bf16[64,4096]{1,0:T(8,128)(2,1)S(1)}, u32[]{:S(2)}, u32[]{:S(2)}) collective-permute-start(bf16[64,4096]{1,0:T(8,128)(2,1)S(1)} %get-tuple-element.96), channel_id=1, source_target_pairs={{0,6},{2,0},{4,2},{6,4},{1,7},{3,1},{5,3},{7,5},{8,14},{10,8},{12,... | collective-permute-start | bytes 1572872 | tf_op jit(solution)/shard_map/ppermute | solution.py:27
  86.6 9.1 %shard_map.98 = (bf16[64,4096]{1,0:T(8,128)(2,1)S(1)}, bf16[64,4096]{1,0:T(8,128)(2,1)S(1)}, bf16[64,2048]{1,0:T(8,128)(2,1)S(1)}, bf16[64,2048]{1,0:T(8,128)(2,...) custom-call(s32[4]{0:T(128)S(1)} %get-tuple-element.97.place_ref, ...), custom_call_target="tpu_custom_call" | custom-call | flops 2000000000 | bytes 2000000 | tf_op jit(solution)/shard_map/pallas_call | solution.py:224
  95.7 1.6 %collective-permute-done.12 = bf16[64,4096]{1,0:T(8,128)(2,1)S(1)} collective-permute-done((bf16[64,4096]{1,0:T(8,128)(2,1)S(1)}, bf16[64,4096]{1,0:T(8,128)(2,1)S(1)}, u32[]{:S(2)}, u32[]{:S(2)}) %collective-permute-start.12) | collective-permute-done | bytes 524320 | tf_op jit(solution)/shard_map/ppermute | solution.py:27
  97.3 0.1 add_convert_fusion.6
  97.5 2.7 %collective-permute-start.15 = (bf16[64,2048]{1,0:T(8,128)(2,1)S(1)}, bf16[64,2048]{1,0:T(8,128)(2,1)S(1)}, u32[]{:S(2)}, u32[]{:S(2)}) collective-permute-start(bf16[64,2048]{1,0:T(8,128)(2,1)S(1)} %get-tuple-element.107), channel_id=1, source_target_pairs={{0,6},{2,0},{4,2},{6,4},{1,7},{3,1},{5,3},{7,5},{8,14},{10,8},{12,... | collective-permute-start | bytes 786440 | tf_op jit(solution)/shard_map/ppermute | solution.py:27
  100.2 2.7 %collective-permute-start.18 = (bf16[64,4096]{1,0:T(8,128)(2,1)S(1)}, bf16[64,4096]{1,0:T(8,128)(2,1)S(1)}, u32[]{:S(2)}, u32[]{:S(2)}) collective-permute-start(bf16[64,4096]{1,0:T(8,128)(2,1)S(1)} %get-tuple-element.109), channel_id=1, source_target_pairs={{0,6},{2,0},{4,2},{6,4},{1,7},{3,1},{5,3},{7,5},{8,14},{10,8},{12,... | collective-permute-start | bytes 1572872 | tf_op jit(solution)/shard_map/ppermute | solution.py:27
  102.9 1.5 %collective-permute-done.14 = bf16[64,2048]{1,0:T(8,128)(2,1)S(1)} collective-permute-done((bf16[64,2048]{1,0:T(8,128)(2,1)S(1)}, bf16[64,2048]{1,0:T(8,128)(2,1)S(1)}, u32[]{:S(2)}, u32[]{:S(2)}) %collective-permute-start.14) | collective-permute-done | bytes 262176 | tf_op jit(solution)/shard_map/ppermute | solution.py:27
  104.3 0.1 add_convert_fusion.5
  104.4 0.1 add_convert_fusion.4
  104.6 7.9 %collective-permute-start.16 = (bf16[64,4096]{1,0:T(8,128)(2,1)S(1)}, bf16[64,4096]{1,0:T(8,128)(2,1)S(1)}, u32[]{:S(2)}, u32[]{:S(2)}) collective-permute-start(bf16[64,4096]{1,0:T(8,128)(2,1)S(1)} %pad_maximum_fusion.1), channel_id=1, source_target_pairs={{0,1},{1,8},{2,3},{3,2},{4,5},{5,4},{6,7},{7,6},{8,9},{9,16},{10,1... | collective-permute-start | bytes 1572872 | tf_op jit(solution)/shard_map/ppermute | solution.py:324
  112.5 3.1 %collective-permute-done.17 = bf16[64,4096]{1,0:T(8,128)(2,1)S(1)} collective-permute-done((bf16[64,4096]{1,0:T(8,128)(2,1)S(1)}, bf16[64,4096]{1,0:T(8,128)(2,1)S(1)}, u32[]{:S(2)}, u32[]{:S(2)}) %collective-permute-start.17) | collective-permute-done | bytes 524320 | tf_op jit(solution)/shard_map/ppermute | solution.py:27
  115.5 3.0 %collective-permute-done.16 = bf16[64,4096]{1,0:T(8,128)(2,1)S(1)} collective-permute-done((bf16[64,4096]{1,0:T(8,128)(2,1)S(1)}, bf16[64,4096]{1,0:T(8,128)(2,1)S(1)}, u32[]{:S(2)}, u32[]{:S(2)}) %collective-permute-start.16) | collective-permute-done | bytes 524320 | tf_op jit(solution)/shard_map/ppermute | solution.py:324
  118.8 0.1 slice.34
  119.0 2.7 %collective-permute-start.20 = (bf16[64,2048]{1,0:T(8,128)(2,1)S(1)}, bf16[64,2048]{1,0:T(8,128)(2,1)S(1)}, u32[]{:S(2)}, u32[]{:S(2)}) collective-permute-start(bf16[64,2048]{1,0:T(8,128)(2,1)S(1)} %add_convert_fusion.2), channel_id=1, source_target_pairs={{0,6},{2,0},{4,2},{6,4},{1,7},{3,1},{5,3},{7,5},{8,14},{10,8},{12,... | collective-permute-start | bytes 786440 | tf_op jit(solution)/shard_map/ppermute | solution.py:27
  121.7 6.2 %collective-permute-done.19 = bf16[64,2048]{1,0:T(8,128)(2,1)S(1)} collective-permute-done((bf16[64,2048]{1,0:T(8,128)(2,1)S(1)}, bf16[64,2048]{1,0:T(8,128)(2,1)S(1)}, u32[]{:S(2)}, u32[]{:S(2)}) %collective-permute-start.19) | collective-permute-done | bytes 262176 | tf_op jit(solution)/shard_map/ppermute | solution.py:27
  127.9 0.1 add_convert_fusion.1
  128.0 0.1 add_convert_fusion
  128.1 1.1 pad_maximum_fusion
  (51 shorter events, 1.1 us)
Async XLA Ops:
  0.0 15.6 %collective-permute-start.3 = (bf16[4096,512]{1,0:T(8,128)(2,1)}, bf16[4096,512]{1,0:T(8,128)(2,1)}, u32[]{:S(2)}, u32[]{:S(2)}) collective-permute-start(bf16[4096,512]{1,0:T(8,128)(2,1)} %wa_hbm.1), channel_id=1, source_target_pairs={{0,1},{1,0},{2,3},{3,2},{4,5},{5,4},{6,7},{7,6},{8,9},{9,8},{10,11... | collective-permute-start | bytes 12582920 | tf_op jit(solution)/shard_map/ppermute | solution.py:27
  1.4 31.4 %collective-permute-start.2 = (bf16[512,4096]{1,0:T(8,128)(2,1)}, bf16[512,4096]{1,0:T(8,128)(2,1)}, u32[]{:S(2)}, u32[]{:S(2)}) collective-permute-start(bf16[512,4096]{1,0:T(8,128)(2,1)} %refs_20_.1), channel_id=1, source_target_pairs={{0,1},{1,0},{2,3},{3,2},{4,5},{5,4},{6,7},{7,6},{8,9},{9,8},{10,11... | collective-permute-start | bytes 12582920 | tf_op jit(solution)/shard_map/ppermute | solution.py:27
  6.8 7.1 %copy-start = (bf16[896,512]{1,0:T(8,128)(2,1)S(1)}, bf16[896,512]{1,0:T(8,128)(2,1)}, u32[]{:S(2)}) copy-start(bf16[896,512]{1,0:T(8,128)(2,1)} %refs_14_.1) | copy-start | bytes 2752516
  6.8 7.9 %copy-start.1 = (bf16[896,512]{1,0:T(8,128)(2,1)S(1)}, bf16[896,512]{1,0:T(8,128)(2,1)}, u32[]{:S(2)}) copy-start(bf16[896,512]{1,0:T(8,128)(2,1)} %refs_15_.1) | copy-start | bytes 2752516
  6.9 8.6 %copy-start.5 = (s32[4]{0:T(128)S(1)}, s32[4]{0:T(128)}, u32[]{:S(2)}) copy-start(s32[4]{0:T(128)} %constant.54.clone) | copy-start | bytes 52
  6.9 26.0 %all-to-all-start = ((bf16[16,3,16,896]{3,2,1,0:T(8,128)(2,1)}), bf16[16,3,16,896]{3,2,1,0:T(8,128)(2,1)}, u32[]{:S(2)}, u32[]{:S(2)}) async-start(bf16[16,3,16,896]{3,2,1,0:T(8,128)(2,1)} %bitcast.28), calls=%async_computation | async-start | bytes 2752512 | tf_op jit(solution)/shard_map/all_to_all | solution.py:257
  13.9 13.7 %collective-permute-start = (bf16[896,512]{1,0:T(8,128)(2,1)S(1)}, bf16[896,512]{1,0:T(8,128)(2,1)S(1)}, u32[]{:S(2)}, u32[]{:S(2)}) collective-permute-start(bf16[896,512]{1,0:T(8,128)(2,1)S(1)} %copy-done), channel_id=1, source_target_pairs={{0,1},{1,0},{2,3},{3,2},{4,5},{5,4},{6,7},{7,6},{8,9},{9,8},{10,11... | collective-permute-start | bytes 2752520 | tf_op jit(solution)/shard_map/ppermute | solution.py:27
  14.8 12.8 %collective-permute-start.1 = (bf16[896,512]{1,0:T(8,128)(2,1)S(1)}, bf16[896,512]{1,0:T(8,128)(2,1)}, u32[]{:S(2)}, u32[]{:S(2)}) collective-permute-start(bf16[896,512]{1,0:T(8,128)(2,1)S(1)} %copy-done.1), channel_id=1, source_target_pairs={{0,1},{1,0},{2,3},{3,2},{4,5},{5,4},{6,7},{7,6},{8,9},{9,8},{10,11... | collective-permute-start | bytes 2752520 | tf_op jit(solution)/shard_map/ppermute | solution.py:27
  34.8 7.4 %collective-permute-start.4 = (bf16[256,896]{1,0:T(8,128)(2,1)S(1)}, bf16[256,896]{1,0:T(8,128)(2,1)S(1)}, u32[]{:S(2)}, u32[]{:S(2)}) collective-permute-start(bf16[256,896]{1,0:T(8,128)(2,1)S(1)} %bitcast.24), channel_id=1, source_target_pairs={{0,1},{1,0},{2,3},{3,2},{4,5},{5,4},{6,7},{7,6},{8,9},{9,8},{10,11... | collective-permute-start | bytes 1376264 | tf_op jit(solution)/shard_map/ppermute | solution.py:288
  38.5 13.5 %collective-permute-start.6 = (bf16[256,896]{1,0:T(8,128)(2,1)S(1)}, bf16[256,896]{1,0:T(8,128)(2,1)S(1)}, u32[]{:S(2)}, u32[]{:S(2)}) collective-permute-start(bf16[256,896]{1,0:T(8,128)(2,1)S(1)} %bitcast.25), channel_id=1, source_target_pairs={{0,7},{1,6},{2,1},{3,0},{4,3},{5,2},{6,5},{7,4},{8,15},{9,14},{10,... | collective-permute-start | bytes 1376264 | tf_op jit(solution)/shard_map/ppermute | solution.py:288
  42.2 14.0 %copy-start.6 = (bf16[64,1024]{1,0:T(8,128)(2,1)S(1)}, bf16[64,1024]{1,0:T(8,128)(2,1)}, u32[]{:S(2)}) copy-start(bf16[64,1024]{1,0:T(8,128)(2,1)} %get-tuple-element.91) | copy-start | bytes 393220
  42.2 14.0 %collective-permute-start.5 = (bf16[256,896]{1,0:T(8,128)(2,1)S(1)}, bf16[256,896]{1,0:T(8,128)(2,1)S(1)}, u32[]{:S(2)}, u32[]{:S(2)}) collective-permute-start(bf16[256,896]{1,0:T(8,128)(2,1)S(1)} %bitcast.21), channel_id=1, source_target_pairs={{0,2},{1,3},{2,4},{3,5},{4,6},{5,7},{6,0},{7,1},{8,10},{9,11},{10,... | collective-permute-start | bytes 1376264 | tf_op jit(solution)/shard_map/ppermute | solution.py:288
  45.8 20.6 %collective-permute-start.7 = (bf16[256,896]{1,0:T(8,128)(2,1)S(1)}, bf16[256,896]{1,0:T(8,128)(2,1)S(1)}, u32[]{:S(2)}, u32[]{:S(2)}) collective-permute-start(bf16[256,896]{1,0:T(8,128)(2,1)S(1)} %bitcast.26), channel_id=1, source_target_pairs={{0,3},{1,2},{2,5},{3,4},{4,7},{5,6},{6,1},{7,0},{8,11},{9,10},{10,... | collective-permute-start | bytes 1376264 | tf_op jit(solution)/shard_map/ppermute | solution.py:288
  45.9 20.5 %collective-permute-start.8 = (bf16[256,896]{1,0:T(8,128)(2,1)S(1)}, bf16[256,896]{1,0:T(8,128)(2,1)S(1)}, u32[]{:S(2)}, u32[]{:S(2)}) collective-permute-start(bf16[256,896]{1,0:T(8,128)(2,1)S(1)} %bitcast.23), channel_id=1, source_target_pairs={{0,6},{1,7},{2,0},{3,1},{4,2},{5,3},{6,4},{7,5},{8,14},{9,15},{10,... | collective-permute-start | bytes 1376264 | tf_op jit(solution)/shard_map/ppermute | solution.py:288
  52.0 19.7 %collective-permute-start.10 = (bf16[256,896]{1,0:T(8,128)(2,1)S(1)}, bf16[256,896]{1,0:T(8,128)(2,1)S(1)}, u32[]{:S(2)}, u32[]{:S(2)}) collective-permute-start(bf16[256,896]{1,0:T(8,128)(2,1)S(1)} %collective-permute-done.6.high_ref), channel_id=1, source_target_pairs={{0,6},{1,7},{2,0},{3,1},{4,2},{5,3},{6,4},{7,5},{8,14},{9,15},{10,... | collective-permute-start | bytes 1376264 | tf_op jit(solution)/shard_map/ppermute | solution.py:288
  56.3 18.5 %collective-permute-start.9 = (bf16[256,896]{1,0:T(8,128)(2,1)S(1)}, bf16[256,896]{1,0:T(8,128)(2,1)S(1)}, u32[]{:S(2)}, u32[]{:S(2)}) collective-permute-start(bf16[256,896]{1,0:T(8,128)(2,1)S(1)} %collective-permute-done.5.low_ref), channel_id=1, source_target_pairs={{0,2},{1,3},{2,4},{3,5},{4,6},{5,7},{6,0},{7,1},{8,10},{9,11},{10,... | collective-permute-start | bytes 1376264 | tf_op jit(solution)/shard_map/ppermute | solution.py:288
  56.3 13.7 %collective-permute-start.11 = (bf16[64,1024]{1,0:T(8,128)(2,1)S(1)}, bf16[64,1024]{1,0:T(8,128)(2,1)S(1)}, u32[]{:S(2)}, u32[]{:S(2)}) collective-permute-start(bf16[64,1024]{1,0:T(8,128)(2,1)S(1)} %copy-done.6), channel_id=1, source_target_pairs={{8,1},{16,9},{24,17},{32,25},{40,33},{48,41},{56,49},{64,57},{72,6... | collective-permute-start | bytes 393224 | tf_op jit(solution)/shard_map/ppermute | solution.py:304
  57.6 17.2 %copy-start.4 = (bf16[4,64,1024]{2,1,0:T(8,128)(2,1)S(1)}, bf16[4,64,1024]{2,1,0:T(8,128)(2,1)}, u32[]{:S(2)}) copy-start(bf16[4,64,1024]{2,1,0:T(8,128)(2,1)} %get-tuple-element.90.refs_18_) | copy-start | bytes 1572868
  61.2 13.6 %copy-start.2 = (bf16[512,4096]{1,0:T(8,128)(2,1)S(1)}, bf16[512,4096]{1,0:T(8,128)(2,1)}, u32[]{:S(2)}) copy-start(bf16[512,4096]{1,0:T(8,128)(2,1)} %refs_20_.1) | copy-start | bytes 12582916
  74.8 11.8 %copy-start.3 = (bf16[4,64,1024]{2,1,0:T(8,128)(2,1)S(1)}, bf16[4,64,1024]{2,1,0:T(8,128)(2,1)}, u32[]{:S(2)}) copy-start(bf16[4,64,1024]{2,1,0:T(8,128)(2,1)} %get-tuple-element.98.refs_18_) | copy-start | bytes 1572868
  83.9 13.4 %collective-permute-start.12 = (bf16[64,4096]{1,0:T(8,128)(2,1)S(1)}, bf16[64,4096]{1,0:T(8,128)(2,1)S(1)}, u32[]{:S(2)}, u32[]{:S(2)}) collective-permute-start(bf16[64,4096]{1,0:T(8,128)(2,1)S(1)} %get-tuple-element.95), channel_id=1, source_target_pairs={{0,2},{2,4},{4,6},{6,0},{1,3},{3,5},{5,7},{7,1},{8,10},{10,12},{12... | collective-permute-start | bytes 1572872 | tf_op jit(solution)/shard_map/ppermute | solution.py:27
  84.0 13.3 %collective-permute-start.13 = (bf16[64,4096]{1,0:T(8,128)(2,1)S(1)}, bf16[64,4096]{1,0:T(8,128)(2,1)S(1)}, u32[]{:S(2)}, u32[]{:S(2)}) collective-permute-start(bf16[64,4096]{1,0:T(8,128)(2,1)S(1)} %get-tuple-element.96), channel_id=1, source_target_pairs={{0,6},{2,0},{4,2},{6,4},{1,7},{3,1},{5,3},{7,5},{8,14},{10,8},{12,... | collective-permute-start | bytes 1572872 | tf_op jit(solution)/shard_map/ppermute | solution.py:27
  97.4 6.9 %collective-permute-start.14 = (bf16[64,2048]{1,0:T(8,128)(2,1)S(1)}, bf16[64,2048]{1,0:T(8,128)(2,1)S(1)}, u32[]{:S(2)}, u32[]{:S(2)}) collective-permute-start(bf16[64,2048]{1,0:T(8,128)(2,1)S(1)} %get-tuple-element.105), channel_id=1, source_target_pairs={{0,2},{2,4},{4,6},{6,0},{1,3},{3,5},{5,7},{7,1},{8,10},{10,12},{12... | collective-permute-start | bytes 786440 | tf_op jit(solution)/shard_map/ppermute | solution.py:27
  97.5 6.9 %collective-permute-start.15 = (bf16[64,2048]{1,0:T(8,128)(2,1)S(1)}, bf16[64,2048]{1,0:T(8,128)(2,1)S(1)}, u32[]{:S(2)}, u32[]{:S(2)}) collective-permute-start(bf16[64,2048]{1,0:T(8,128)(2,1)S(1)} %get-tuple-element.107), channel_id=1, source_target_pairs={{0,6},{2,0},{4,2},{6,4},{1,7},{3,1},{5,3},{7,5},{8,14},{10,8},{12,... | collective-permute-start | bytes 786440 | tf_op jit(solution)/shard_map/ppermute | solution.py:27
  100.2 15.4 %collective-permute-start.17 = (bf16[64,4096]{1,0:T(8,128)(2,1)S(1)}, bf16[64,4096]{1,0:T(8,128)(2,1)S(1)}, u32[]{:S(2)}, u32[]{:S(2)}) collective-permute-start(bf16[64,4096]{1,0:T(8,128)(2,1)S(1)} %get-tuple-element.108), channel_id=1, source_target_pairs={{0,2},{2,4},{4,6},{6,0},{1,3},{3,5},{5,7},{7,1},{8,10},{10,12},{12... | collective-permute-start | bytes 1572872 | tf_op jit(solution)/shard_map/ppermute | solution.py:27
  100.2 15.4 %collective-permute-start.18 = (bf16[64,4096]{1,0:T(8,128)(2,1)S(1)}, bf16[64,4096]{1,0:T(8,128)(2,1)S(1)}, u32[]{:S(2)}, u32[]{:S(2)}) collective-permute-start(bf16[64,4096]{1,0:T(8,128)(2,1)S(1)} %get-tuple-element.109), channel_id=1, source_target_pairs={{0,6},{2,0},{4,2},{6,4},{1,7},{3,1},{5,3},{7,5},{8,14},{10,8},{12,... | collective-permute-start | bytes 1572872 | tf_op jit(solution)/shard_map/ppermute | solution.py:27
  104.6 14.0 %collective-permute-start.16 = (bf16[64,4096]{1,0:T(8,128)(2,1)S(1)}, bf16[64,4096]{1,0:T(8,128)(2,1)S(1)}, u32[]{:S(2)}, u32[]{:S(2)}) collective-permute-start(bf16[64,4096]{1,0:T(8,128)(2,1)S(1)} %pad_maximum_fusion.1), channel_id=1, source_target_pairs={{0,1},{1,8},{2,3},{3,2},{4,5},{5,4},{6,7},{7,6},{8,9},{9,16},{10,1... | collective-permute-start | bytes 1572872 | tf_op jit(solution)/shard_map/ppermute | solution.py:324
  118.7 9.2 %collective-permute-start.19 = (bf16[64,2048]{1,0:T(8,128)(2,1)S(1)}, bf16[64,2048]{1,0:T(8,128)(2,1)S(1)}, u32[]{:S(2)}, u32[]{:S(2)}) collective-permute-start(bf16[64,2048]{1,0:T(8,128)(2,1)S(1)} %add_convert_fusion.3), channel_id=1, source_target_pairs={{0,2},{2,4},{4,6},{6,0},{1,3},{3,5},{5,7},{7,1},{8,10},{10,12},{12... | collective-permute-start | bytes 786440 | tf_op jit(solution)/shard_map/ppermute | solution.py:27
  119.0 9.0 %collective-permute-start.20 = (bf16[64,2048]{1,0:T(8,128)(2,1)S(1)}, bf16[64,2048]{1,0:T(8,128)(2,1)S(1)}, u32[]{:S(2)}, u32[]{:S(2)}) collective-permute-start(bf16[64,2048]{1,0:T(8,128)(2,1)S(1)} %add_convert_fusion.2), channel_id=1, source_target_pairs={{0,6},{2,0},{4,2},{6,4},{1,7},{3,1},{5,3},{7,5},{8,14},{10,8},{12,... | collective-permute-start | bytes 786440 | tf_op jit(solution)/shard_map/ppermute | solution.py:27

commit v7 on v6

--- a/solution.py
+++ b/solution.py
@@ -129,22 +129,34 @@
     )(core.reshape(1), blocks, weight_a, weight_b)
 
 
-def project_kernel(low_ref, high_ref, *refs):
+def project_kernel(count, *refs):
+    low_ref, high_ref, weight_refs, carried_hbm = refs[0], refs[1], refs[2:6], refs[6 : 6 + count]
+    out_refs, carried_refs = refs[6 + count : 10 + count], refs[10 + count : 10 + 2 * count]
+    copies = [pltpu.make_async_copy(carried_hbm[i], carried_refs[i], refs[-1].at[i]) for i in range(count)]
+    for copy in copies:
+        copy.start()
     rows = jnp.concatenate([low_ref[...], high_ref[...]], axis=0)
-    for weight_ref, out_ref in zip(refs[:4], refs[4:]):
+    for weight_ref, out_ref in zip(weight_refs, out_refs):
         out_ref[...] = dot(rows, weight_ref[...]).astype(BF16).reshape(out_ref.shape)
-
-
-def project(weights, parts):
+    for copy in copies:
+        copy.wait()
+
+
+def project(weights, parts, carried=()):
     rows, enc = parts[0].shape
     width = weights[0].shape[1]
     shape = (len(parts), 2, N_Z, rows // (2 * N_Z), width)
+    vmem = pl.BlockSpec(memory_space=pltpu.VMEM)
     return pl.pallas_call(
-        project_kernel,
-        out_shape=[jax.ShapeDtypeStruct(shape, BF16)] * 4,
+        functools.partial(project_kernel, len(carried)),
+        in_specs=[vmem] * 6 + [pl.BlockSpec(memory_space=pltpu.HBM)] * len(carried),
+        out_specs=[vmem] * (4 + len(carried)),
+        out_shape=[jax.ShapeDtypeStruct(shape, BF16)] * 4
+        + [jax.ShapeDtypeStruct(value.shape, value.dtype) for value in carried],
+        scratch_shapes=[pltpu.SemaphoreType.DMA((max(1, len(carried)),))],
         cost_estimate=cost(2e9),
         compiler_params=pltpu.CompilerParams(vmem_limit_bytes=GRANT),
-    )(*parts, *weights)
+    )(*parts, *weights, *carried)
 
 
 def span_kernel(group, place_ref, *refs):
@@ -157,7 +169,7 @@
 
     near_refs, row_refs, weight_refs = take(12), take(2), take(4)
     q_ref, crossing_ref = take(2)
-    out_weight_refs, out_refs, far_kv_refs = take(2), take(6), take(4)
+    out_weight_refs, out_refs, far_kv_refs = take(2), take(6 if group == 0 else 8), take(4)
     count = row_refs[0].shape[0] // 2
     rows = jnp.concatenate([ref[group * count : (group + 1) * count] for ref in row_refs], axis=0)
     for weight_ref, far_kv_ref in zip(weight_refs, far_kv_refs):
@@ -193,31 +205,33 @@
             context_ref[span, :, side * half + lower : side * half + lower + HS] = dot(prob, v).astype(BF16)
         return carry
 
-    lax.fori_loop(0, N_Z, attend_span, 0)
+    lax.fori_loop(0, N_Z, attend_span, 0, unroll=N_Z)
 
     blocks = [context_ref[place_ref[i]] for i in range(N_Z)]
     if group == 0:
         is_first_row = lax.broadcasted_iota(jnp.int32, blocks[0].shape, 0) == 0
         blocks = [jnp.where(is_first_row, context_ref[place_ref[N_Z + 1 + i]], blocks[i]) for i in range(N_Z)]
     context = jnp.concatenate(blocks, axis=0)
-    up, down, above, below, here_left, here_right = out_refs
     tile = model // 4
     for lower in range(0, model, tile):
         place = slice(lower, lower + tile)
         product = dot(context[:, :half], out_weight_refs[0][:, place])
         product = (product + dot(context[:, half:], out_weight_refs[1][:, place])).astype(BF16)
-        blocks = [product[i * CL : (i + 1) * CL] for i in range(N_Z)]
-        inner = slice(lower % (model // 2), lower % (model // 2) + tile)
-        if lower < model // 2:
-            up[:, place], down[:, place], above[:, inner], here_left[:, inner] = blocks[0], blocks[2], blocks[1], blocks[3]
-        else:
-            up[:, place], down[:, place], below[:, inner], here_right[:, inner] = blocks[1], blocks[0], blocks[2], blocks[3]
+        side, start = lower // (model // 2), lower % (model // 2)
+        for i in range(N_Z):
+            block = product[i * CL : (i + 1) * CL]
+            if group == 1:
+                out_refs[2 * i + side][:, start : start + tile] = block
+            elif i < N_Z - 1 and (i, side) not in ((1, 0), (2, 1)):
+                out_refs[(0, 0, 1)[i] if i != 0 else side][:, place] = block
+            else:
+                out_refs[{(1, 0): 2, (2, 1): 3, (3, 0): 4, (3, 1): 5}[i, side]][:, start : start + tile] = block
 
 
 def attend(group, places, queries, crossing, near, far, weights):
     spans, tokens, width = queries.shape
     half, model = weights[4].shape
-    outs = [(tokens, model)] * 2 + [(tokens, model // 2)] * 4
+    outs = [(tokens, model)] * 2 + [(tokens, model // 2)] * 4 if group == 0 else [(tokens, model // 2)] * 8
     scratch = [(2, spans, near[0].shape[3], half)] * 4 + [queries.shape]
     operands = (*near, *far, *weights[:4], queries, crossing, *weights[4:])
     vmem = pl.BlockSpec(memory_space=pltpu.VMEM)
@@ -292,13 +306,14 @@
 
     side = model // 2
 
-    def total(here_left, here_right, up, down, up_left, down_right):
-        left, right = add(here_left, down[:, :side], up_left), add(here_right, up[:, side:], down_right)
+    def total(here_left, here_right, down_left, up_right, up_left, down_right):
+        left, right = add(here_left, down_left, up_left), add(here_right, up_right, down_right)
         return jnp.concatenate([left, right], axis=1)
 
     ring = hop(mine, 1, 0), hop(theirs, -1, 1)
     swapped = hop(theirs, 0, 1)
-    near = project(weights[:4], (mine, swapped))
+    *near, w_value_other, w_out_other = project(weights[:4], (mine, swapped), (weights[3], weights[5]))
+    weights = (*weights[:3], w_value_other, weights[4], w_out_other)
     near, mine, theirs, crossing = lax.optimization_barrier((near, mine, theirs, crossing))
     ring_after = hop(theirs, 1, 1), hop(mine, -1, 0)
     crossing = lax.ppermute(crossing, ("seq", "core"), [(2 * i + 2, 2 * i + 1) for i in range(n_seq - 1)])
@@ -307,12 +322,13 @@
 
     up_a, down_a, above_a, below_a, *here_a = attend(0, places_a, second_queries, crossing, near, far, weights)
     up_a, down_a = step(up_a, "z", 1), step(down_a, "z", -1)
-    up_b, down_b, above_b, below_b, *here_b = attend(1, places_b, first_queries, crossing, near, far, weights)
-    up_a, down_a, up_b, down_b = lax.optimization_barrier((up_a, down_a, up_b, down_b))
+    sums_b = attend(1, places_b, first_queries, crossing, near, far, weights)
+    up_a, down_a, sums_b = lax.optimization_barrier((up_a, down_a, sums_b))
     above_a, below_a = lax.optimization_barrier((add(above_a, up_a[:, :side]), add(below_a, down_a[:, side:])))
     up_left_a, down_right_a = step(above_a, "z", 1), step(below_a, "z", -1)
-    up_b, down_b = step(up_b, "z", 1), step(down_b, "z", -1)
-    out_a = total(*here_a, up_a, down_a, up_left_a, down_right_a)
+    up_b, down_b = step(sums_b[0], "z", 1), step(sums_b[1], "z", -1)
+    up_right_b, down_left_b = step(sums_b[3], "z", 1), step(sums_b[4], "z", -1)
+    out_a = total(*here_a, down_a[:, :side], up_a[:, side:], up_left_a, down_right_a)
 
     pairs = []
     for i in range(0, n_seq * N_Z * N_CORE, 2):
@@ -322,10 +338,9 @@
         elif i + N_Z * N_CORE < n_seq * N_Z * N_CORE:
             pairs.append((i + 1, i + N_Z * N_CORE))
     head = lax.ppermute(out_a, ("seq", "z", "core"), pairs)
-    head, up_b, down_b = lax.optimization_barrier((head, up_b, down_b))
-    above_b, below_b = lax.optimization_barrier((add(above_b, up_b[:, :side]), add(below_b, down_b[:, side:])))
+    above_b, below_b = lax.optimization_barrier((add(sums_b[2], up_b), add(sums_b[5], down_b)))
     up_left_b, down_right_b = step(above_b, "z", 1), step(below_b, "z", -1)
-    out_b = total(*here_b, up_b, down_b, up_left_b, down_right_b)
+    out_b = total(*sums_b[6:], down_left_b, up_right_b, up_left_b, down_right_b)
     return jnp.concatenate([head[1:], out_b, out_a[:1]], axis=0)
 
 

time: 130 us -> 124 us (0.954)
  Pallas kernels: 45.8 us -> 37.4 us
  waiting for transfers between devices: 33.8 us -> 29.9 us
  starting transfers between devices: 44.3 us -> 47.6 us
  local copies, waits for them, and re-layouts: 1.72 us -> 3.92 us
    pallas_call x2, Pallas kernels: 18.2 us -> 12 us  [attend(): pl.pallas_call(functools.partial(span_kernel, group), grid_spec=pltpu.Pre...]
    ppermute x1, waiting for transfers between devices: 3.05 us -> 0.01 us  [body(): head = lax.ppermute(out_a, ('seq', 'z', 'core'), pairs)]
    ppermute x12 -> x14, waiting for transfers between devices: 12.3 us -> 9.27 us  [step(): lax.ppermute(value, axis, [(i, (i + steps) % count) for i in range(count)])]
    ppermute x12 -> x14, starting transfers between devices: 13.4 us -> 15.7 us  [step(): lax.ppermute(value, axis, [(i, (i + steps) % count) for i in range(count)])]
    pallas_call x3, Pallas kernels: 10.6 us -> 8.42 us  [project(): pl.pallas_call(functools.partial(project_kernel, len(carried)), in_specs=...]
    unnamed x14 -> x18, local copies, waits for them, and re-layouts: 0.04 us -> 2.23 us
    ppermute x7, waiting for transfers between devices: 13.2 us -> 15.4 us  [hop(): return lax.ppermute(value, ('z', 'core'), pairs)]
  transfers between devices with their start and end apart: 22 -> 24, of which waited for: 10 -> 8; matrix products, arithmetic and copies ran while one was open for 3% -> 3% of each run, Pallas kernels for 27% -> 24%
where the time goes in v7:
time: 124 us; the launch traced here: 123 us
  starting transfers between devices  47.6 us (38%)
  Pallas kernels  37.4 us (30%)
  waiting for transfers between devices  29.9 us (24%)
  local copies, waits for them, and re-layouts  3.92 us (3%)
  other arithmetic  3.29 us (3%)
    ppermute x14, starting transfers between devices, step(): lax.ppermute(value, axis, [(i, (i + steps) % count) for i in range(count)])  15.7 us
    ppermute x7, waiting for transfers between devices, hop(): return lax.ppermute(value, ('z', 'core'), pairs)  15.4 us
    ppermute x7, starting transfers between devices, hop(): return lax.ppermute(value, ('z', 'core'), pairs)  14.7 us
    pallas_call x1, Pallas kernels, project_queries(): pl.pallas_call(query_kernel, grid_spec=pltpu.PrefetchScalarGridSpec(num_s...  12 us
    pallas_call x2, Pallas kernels, attend(): pl.pallas_call(functools.partial(span_kernel, group), grid_spec=pltpu.Pre...  12 us
    ppermute x14, waiting for transfers between devices, step(): lax.ppermute(value, axis, [(i, (i + steps) % count) for i in range(count)])  9.27 us
    ppermute x1, starting transfers between devices, body(): head = lax.ppermute(out_a, ('seq', 'z', 'core'), pairs)  8.87 us
    pallas_call x3, Pallas kernels, project(): pl.pallas_call(functools.partial(project_kernel, len(carried)), in_specs=...  8.42 us
  transfers between devices with their start and end apart: 24, of which 8 were waited for; matrix products, arithmetic and copies ran while one was open for 3% of the time, Pallas kernels for 24%

profile of v7, /device:TPU:1, one launch (start us, length us, event | category | flops | bytes accessed | tf_op | source)
XLA Modules:
  0.0 122.5 jit_solution(14303736171434628942)
XLA Ops:
  0.0 1.4 %collective-permute-start.3 = (bf16[4096,512]{1,0:T(8,128)(2,1)}, bf16[4096,512]{1,0:T(8,128)(2,1)}, u32[]{:S(2)}, u32[]{:S(2)}) collective-permute-start(bf16[4096,512]{1,0:T(8,128)(2,1)} %wa_hbm.1), channel_id=1, source_target_pairs={{0,1},{1,0},{2,3},{3,2},{4,5},{5,4},{6,7},{7,6},{8,9},{9,8},{10,11... | collective-permute-start | bytes 12582920 | tf_op jit(solution)/shard_map/ppermute | solution.py:27
  1.4 0.7 shift-right-arithmetic_bitcast_fusion
  2.5 0.5 convert_reduce_fusion
  3.0 0.1 select_reduce_fusion
  3.2 0.6 reshape.76.index_ref
  3.8 3.0 %shard_map.91 = bf16[48,16,896]{2,1,0:T(8,128)(2,1)} custom-call(s32[48]{0:T(128)} %reshape.76.index_ref, s32[1]{0:T(128)} %bitcast.4.start_ref, bf16[24,128,896]{2,1,0:T(8,128)(2,1)} %source_ref.1), custom_call_target="tpu_custom_call" | custom-call | flops 400000000 | bytes 400000 | tf_op jit(solution)/shard_map/pallas_call | solution.py:61
  6.8 7.0 %all-to-all-start = ((bf16[16,3,16,896]{3,2,1,0:T(8,128)(2,1)}), bf16[16,3,16,896]{3,2,1,0:T(8,128)(2,1)}, u32[]{:S(2)}, u32[]{:S(2)}) async-start(bf16[16,3,16,896]{3,2,1,0:T(8,128)(2,1)} %bitcast.28), calls=%async_computation | async-start | bytes 2752512 | tf_op jit(solution)/shard_map/all_to_all | solution.py:271
  13.9 0.9 collective-permute-start
  14.8 0.1 collective-permute-start.1
  14.9 0.1 add.89
  15.0 0.1 rev.6
  15.1 0.1 rev.7
  15.2 0.1 copy.18
  15.4 0.1 reshape.82.index_ref
  15.6 12.0 %shard_map.92 = (bf16[4,64,1024]{2,1,0:T(8,128)(2,1)}, bf16[4,64,1024]{2,1,0:T(8,128)(2,1)}, bf16[64,1024]{1,0:T(8,128)(2,1)}) custom-call(s32[1]{0:T(128)} %bitcast.7.core_ref, bf16[8,128,4096]{2,1,0:T(8,128)(2,1)} %bitcast.27, bf16[4096,512]{1,0:T(8,128)(2,1)} %wa_hbm.1, bf16[4096,512]{1,0:T(8,128)(2,1)} %collective-permute-done.3.wb_hbm), custom_call_target="tpu_custom_call" | custom-call | flops 1200000000 | bytes 1200000 | tf_op jit(solution)/shard_map/pallas_call | solution.py:112
  27.6 5.2 %all-to-all-done = bf16[16,3,16,896]{3,2,1,0:T(8,128)(2,1)} async-done(((bf16[16,3,16,896]{3,2,1,0:T(8,128)(2,1)}), bf16[16,3,16,896]{3,2,1,0:T(8,128)(2,1)}, u32[]{:S(2)}, u32[]{:S(2)}) %all-to-all-start) | async-done | bytes 1376288 | tf_op jit(solution)/shard_map/all_to_all | solution.py:271
  32.8 2.0 %shard_map.93 = (bf16[16,16,896]{2,1,0:T(8,128)(2,1)S(1)}, bf16[16,16,896]{2,1,0:T(8,128)(2,1)S(1)}) custom-call(s32[32]{0:T(128)S(1)} %reshape.82.index_ref, s32[1]{0:T(128)} %constant.53.clone.1.start_ref, bf16[48,16,896]{2,1,0:T(8,128)(2,1)} %bitcast.6.source_ref), custom_call_target="tpu_custom_call" | custom-call | flops 400000000 | bytes 400000 | tf_op jit(solution)/shard_map/pallas_call | solution.py:61
  34.8 3.7 %collective-permute-start.4 = (bf16[256,896]{1,0:T(8,128)(2,1)S(1)}, bf16[256,896]{1,0:T(8,128)(2,1)S(1)}, u32[]{:S(2)}, u32[]{:S(2)}) collective-permute-start(bf16[256,896]{1,0:T(8,128)(2,1)S(1)} %bitcast.24), channel_id=1, source_target_pairs={{0,1},{1,0},{2,3},{3,2},{4,5},{5,4},{6,7},{7,6},{8,9},{9,8},{10,11... | collective-permute-start | bytes 1376264 | tf_op jit(solution)/shard_map/ppermute | solution.py:302
  38.5 3.7 %collective-permute-start.6 = (bf16[256,896]{1,0:T(8,128)(2,1)S(1)}, bf16[256,896]{1,0:T(8,128)(2,1)S(1)}, u32[]{:S(2)}, u32[]{:S(2)}) collective-permute-start(bf16[256,896]{1,0:T(8,128)(2,1)S(1)} %bitcast.25), channel_id=1, source_target_pairs={{0,7},{1,6},{2,1},{3,0},{4,3},{5,2},{6,5},{7,4},{8,15},{9,14},{10,... | collective-permute-start | bytes 1376264 | tf_op jit(solution)/shard_map/ppermute | solution.py:302
  42.2 3.7 %shard_map.94 = (bf16[2,2,4,32,512]{4,3,2,1,0:T(8,128)(2,1)S(1)}, bf16[2,2,4,32,512]{4,3,2,1,0:T(8,128)(2,1)S(1)}, bf16[2,2,4,32,512]{4,3,2,1,0:T(8,128)(2,1)S(1...) custom-call(bf16[256,896]{1,0:T(8,128)(2,1)S(1)} %bitcast.22, ...), custom_call_target="tpu_custom_call" | custom-call | flops 800000000 | bytes 800000 | tf_op jit(solution)/shard_map/pallas_call | solution.py:150
  46.0 3.0 %collective-permute-start.8 = (bf16[256,896]{1,0:T(8,128)(2,1)S(1)}, bf16[256,896]{1,0:T(8,128)(2,1)S(1)}, u32[]{:S(2)}, u32[]{:S(2)}) collective-permute-start(bf16[256,896]{1,0:T(8,128)(2,1)S(1)} %bitcast.23), channel_id=1, source_target_pairs={{0,6},{1,7},{2,0},{3,1},{4,2},{5,3},{6,4},{7,5},{8,14},{9,15},{10,... | collective-permute-start | bytes 1376264 | tf_op jit(solution)/shard_map/ppermute | solution.py:302
  49.0 2.9 %collective-permute-done.6.refs_1_ = bf16[256,896]{1,0:T(8,128)(2,1)S(1)} collective-permute-done((bf16[256,896]{1,0:T(8,128)(2,1)S(1)}, bf16[256,896]{1,0:T(8,128)(2,1)S(1)}, u32[]{:S(2)}, u32[]{:S(2)}) %collective-permute-start.6) | collective-permute-done | bytes 458784 | tf_op jit(solution)/shard_map/ppermute | solution.py:302
  52.0 4.3 %collective-permute-start.10 = (bf16[256,896]{1,0:T(8,128)(2,1)S(1)}, bf16[256,896]{1,0:T(8,128)(2,1)S(1)}, u32[]{:S(2)}, u32[]{:S(2)}) collective-permute-start(bf16[256,896]{1,0:T(8,128)(2,1)S(1)} %collective-permute-done.6.refs_1_), channel_id=1, source_target_pairs={{0,6},{1,7},{2,0},{3,1},{4,2},{5,3},{6,4},{7,5},{8,14},{9,15},{10,... | collective-permute-start | bytes 1376264 | tf_op jit(solution)/shard_map/ppermute | solution.py:302
  56.2 1.3 %collective-permute-start.11 = (bf16[64,1024]{1,0:T(8,128)(2,1)S(1)}, bf16[64,1024]{1,0:T(8,128)(2,1)S(1)}, u32[]{:S(2)}, u32[]{:S(2)}) collective-permute-start(bf16[64,1024]{1,0:T(8,128)(2,1)S(1)} %copy-done.8), channel_id=1, source_target_pairs={{8,1},{16,9},{24,17},{32,25},{40,33},{48,41},{56,49},{64,57},{72,6... | collective-permute-start | bytes 393224 | tf_op jit(solution)/shard_map/ppermute | solution.py:319
  57.6 2.3 %shard_map.95 = (bf16[2,2,4,32,512]{4,3,2,1,0:T(8,128)(2,1)S(1)}, bf16[2,2,4,32,512]{4,3,2,1,0:T(8,128)(2,1)S(1)}, bf16[2,2,4,32,512]{4,3,2,1,0:T(8,128)(2,1)S(1)}, bf16[2,2,4,32,512]{4,3,2,1,0:T(8,128)(2,1)S(1)}) custom-call(bf16[256,896]{1,0:T(8,128)(2,1)S(1)} %collective-permute-done.5.refs_0_, bf16[256,896]{1,0:T(8,128)(2,1)S(1)} %collective-permute-done.6.refs_1_, ...), custom_call_target="tpu_custom_call" | custom-call | flops 800000000 | bytes 800000 | tf_op jit(solution)/shard_map/pallas_call | solution.py:150
  59.9 6.5 %collective-permute-done.7.refs_0_ = bf16[256,896]{1,0:T(8,128)(2,1)S(1)} collective-permute-done((bf16[256,896]{1,0:T(8,128)(2,1)S(1)}, bf16[256,896]{1,0:T(8,128)(2,1)S(1)}, u32[]{:S(2)}, u32[]{:S(2)}) %collective-permute-start.7) | collective-permute-done | bytes 458784 | tf_op jit(solution)/shard_map/ppermute | solution.py:302
  66.4 2.3 %shard_map.96 = (bf16[2,2,4,32,512]{4,3,2,1,0:T(8,128)(2,1)S(1)}, bf16[2,2,4,32,512]{4,3,2,1,0:T(8,128)(2,1)S(1)}, bf16[2,2,4,32,512]{4,3,2,1,0:T(8,128)(2,1)S(1)}, bf16[2,2,4,32,512]{4,3,2,1,0:T(8,128)(2,1)S(1)}) custom-call(bf16[256,896]{1,0:T(8,128)(2,1)S(1)} %collective-permute-done.7.refs_0_, bf16[256,896]{1,0:T(8,128)(2,1)S(1)} %collective-permute-done.8.refs_1_, ...), custom_call_target="tpu_custom_call" | custom-call | flops 800000000 | bytes 800000 | tf_op jit(solution)/shard_map/pallas_call | solution.py:150
  68.7 2.9 %collective-permute-done.10.refs_13_ = bf16[256,896]{1,0:T(8,128)(2,1)S(1)} collective-permute-done((bf16[256,896]{1,0:T(8,128)(2,1)S(1)}, bf16[256,896]{1,0:T(8,128)(2,1)S(1)}, u32[]{:S(2)}, u32[]{:S(2)}) %collective-permute-start.10) | collective-permute-done | bytes 458784 | tf_op jit(solution)/shard_map/ppermute | solution.py:302
  71.6 3.1 %collective-permute-done.9.refs_12_ = bf16[256,896]{1,0:T(8,128)(2,1)S(1)} collective-permute-done((bf16[256,896]{1,0:T(8,128)(2,1)S(1)}, bf16[256,896]{1,0:T(8,128)(2,1)S(1)}, u32[]{:S(2)}, u32[]{:S(2)}) %collective-permute-start.9) | collective-permute-done | bytes 458784 | tf_op jit(solution)/shard_map/ppermute | solution.py:302
  74.8 6.0 %shard_map.97 = (bf16[64,4096]{1,0:T(8,128)(2,1)S(1)}, bf16[64,4096]{1,0:T(8,128)(2,1)S(1)}, bf16[64,2048]{1,0:T(8,128)(2,1)S(1)}, bf16[64,2048]{1,0:T(8,128)(2,...) custom-call(s32[9]{0:T(128)S(1)} %pad_add_fusion.place_ref, ...), custom_call_target="tpu_custom_call" | custom-call | flops 2000000000 | bytes 2000000 | tf_op jit(solution)/shard_map/pallas_call | solution.py:238
  80.9 2.7 %collective-permute-start.13 = (bf16[64,4096]{1,0:T(8,128)(2,1)S(1)}, bf16[64,4096]{1,0:T(8,128)(2,1)S(1)}, u32[]{:S(2)}, u32[]{:S(2)}) collective-permute-start(bf16[64,4096]{1,0:T(8,128)(2,1)S(1)} %get-tuple-element.105), channel_id=1, source_target_pairs={{0,6},{2,0},{4,2},{6,4},{1,7},{3,1},{5,3},{7,5},{8,14},{10,8},{12,... | collective-permute-start | bytes 1572872 | tf_op jit(solution)/shard_map/ppermute | solution.py:27
  83.5 2.2 %copy-done.4 = bf16[512,4096]{1,0:T(8,128)(2,1)S(1)} copy-done((bf16[512,4096]{1,0:T(8,128)(2,1)S(1)}, bf16[512,4096]{1,0:T(8,128)(2,1)}, u32[]{:S(2)}) %copy-start.4) | copy-done | bytes 4194328
  85.7 6.0 %shard_map.98 = (bf16[64,2048]{1,0:T(8,128)(2,1)S(1)}, bf16[64,2048]{1,0:T(8,128)(2,1)S(1)}, bf16[64,2048]{1,0:T(8,128)(2,1)S(1)}, bf16[64,2048]{1,0:T(8,128)(2,...) custom-call(s32[4]{0:T(128)S(1)} %get-tuple-element.106.place_ref, ...), custom_call_target="tpu_custom_call" | custom-call | flops 2000000000 | bytes 2000000 | tf_op jit(solution)/shard_map/pallas_call | solution.py:238
  91.7 2.5 %collective-permute-done.12 = bf16[64,4096]{1,0:T(8,128)(2,1)S(1)} collective-permute-done((bf16[64,4096]{1,0:T(8,128)(2,1)S(1)}, bf16[64,4096]{1,0:T(8,128)(2,1)S(1)}, u32[]{:S(2)}, u32[]{:S(2)}) %collective-permute-start.12) | collective-permute-done | bytes 524320 | tf_op jit(solution)/shard_map/ppermute | solution.py:27
  94.2 0.1 add_convert_fusion.6
  94.3 2.5 %collective-permute-start.15 = (bf16[64,2048]{1,0:T(8,128)(2,1)S(1)}, bf16[64,2048]{1,0:T(8,128)(2,1)S(1)}, u32[]{:S(2)}, u32[]{:S(2)}) collective-permute-start(bf16[64,2048]{1,0:T(8,128)(2,1)S(1)} %get-tuple-element.122), channel_id=1, source_target_pairs={{0,6},{2,0},{4,2},{6,4},{1,7},{3,1},{5,3},{7,5},{8,14},{10,8},{12,... | collective-permute-start | bytes 786440 | tf_op jit(solution)/shard_map/ppermute | solution.py:27
  96.8 2.7 %collective-permute-start.19 = (bf16[64,2048]{1,0:T(8,128)(2,1)S(1)}, bf16[64,2048]{1,0:T(8,128)(2,1)S(1)}, u32[]{:S(2)}, u32[]{:S(2)}) collective-permute-start(bf16[64,2048]{1,0:T(8,128)(2,1)S(1)} %get-tuple-element.128), channel_id=1, source_target_pairs={{0,6},{2,0},{4,2},{6,4},{1,7},{3,1},{5,3},{7,5},{8,14},{10,8},{12,... | collective-permute-start | bytes 786440 | tf_op jit(solution)/shard_map/ppermute | solution.py:27
  99.5 2.7 %collective-permute-start.17 = (bf16[64,2048]{1,0:T(8,128)(2,1)S(1)}, bf16[64,2048]{1,0:T(8,128)(2,1)S(1)}, u32[]{:S(2)}, u32[]{:S(2)}) collective-permute-start(bf16[64,2048]{1,0:T(8,128)(2,1)S(1)} %get-tuple-element.124), channel_id=1, source_target_pairs={{0,6},{2,0},{4,2},{6,4},{1,7},{3,1},{5,3},{7,5},{8,14},{10,8},{12,... | collective-permute-start | bytes 786440 | tf_op jit(solution)/shard_map/ppermute | solution.py:27
  102.2 0.1 add_convert_fusion.4
  102.3 1.0 collective-permute-done.14
  103.2 0.1 add_convert_fusion.5
  103.4 8.9 %collective-permute-start.16 = (bf16[64,4096]{1,0:T(8,128)(2,1)S(1)}, bf16[64,4096]{1,0:T(8,128)(2,1)S(1)}, u32[]{:S(2)}, u32[]{:S(2)}) collective-permute-start(bf16[64,4096]{1,0:T(8,128)(2,1)S(1)} %pad_maximum_fusion.1), channel_id=1, source_target_pairs={{0,1},{1,8},{2,3},{3,2},{4,5},{5,4},{6,7},{7,6},{8,9},{9,16},{10,1... | collective-permute-start | bytes 1572872 | tf_op jit(solution)/shard_map/ppermute | solution.py:340
  112.5 2.7 %collective-permute-start.22 = (bf16[64,2048]{1,0:T(8,128)(2,1)S(1)}, bf16[64,2048]{1,0:T(8,128)(2,1)S(1)}, u32[]{:S(2)}, u32[]{:S(2)}) collective-permute-start(bf16[64,2048]{1,0:T(8,128)(2,1)S(1)} %add_convert_fusion.2), channel_id=1, source_target_pairs={{0,6},{2,0},{4,2},{6,4},{1,7},{3,1},{5,3},{7,5},{8,14},{10,8},{12,... | collective-permute-start | bytes 786440 | tf_op jit(solution)/shard_map/ppermute | solution.py:27
  115.2 5.8 %collective-permute-done.20 = bf16[64,2048]{1,0:T(8,128)(2,1)S(1)} collective-permute-done((bf16[64,2048]{1,0:T(8,128)(2,1)S(1)}, bf16[64,2048]{1,0:T(8,128)(2,1)S(1)}, u32[]{:S(2)}, u32[]{:S(2)}) %collective-permute-start.20) | collective-permute-done | bytes 262176 | tf_op jit(solution)/shard_map/ppermute | solution.py:27
  121.0 0.1 add_convert_fusion.1
  121.1 0.1 add_convert_fusion
  121.2 0.1 slice.24
  121.4 1.1 pad_maximum_fusion
  (59 shorter events, 1.1 us)
Async XLA Ops:
  0.0 15.6 %collective-permute-start.3 = (bf16[4096,512]{1,0:T(8,128)(2,1)}, bf16[4096,512]{1,0:T(8,128)(2,1)}, u32[]{:S(2)}, u32[]{:S(2)}) collective-permute-start(bf16[4096,512]{1,0:T(8,128)(2,1)} %wa_hbm.1), channel_id=1, source_target_pairs={{0,1},{1,0},{2,3},{3,2},{4,5},{5,4},{6,7},{7,6},{8,9},{9,8},{10,11... | collective-permute-start | bytes 12582920 | tf_op jit(solution)/shard_map/ppermute | solution.py:27
  1.4 31.4 %collective-permute-start.2 = (bf16[512,4096]{1,0:T(8,128)(2,1)}, bf16[512,4096]{1,0:T(8,128)(2,1)}, u32[]{:S(2)}, u32[]{:S(2)}) collective-permute-start(bf16[512,4096]{1,0:T(8,128)(2,1)} %refs_20_.1), channel_id=1, source_target_pairs={{0,1},{1,0},{2,3},{3,2},{4,5},{5,4},{6,7},{7,6},{8,9},{9,8},{10,11... | collective-permute-start | bytes 12582920 | tf_op jit(solution)/shard_map/ppermute | solution.py:27
  6.8 7.1 %copy-start = (bf16[896,512]{1,0:T(8,128)(2,1)S(1)}, bf16[896,512]{1,0:T(8,128)(2,1)}, u32[]{:S(2)}) copy-start(bf16[896,512]{1,0:T(8,128)(2,1)} %refs_14_.1) | copy-start | bytes 2752516
  6.8 7.9 %copy-start.1 = (bf16[896,512]{1,0:T(8,128)(2,1)S(1)}, bf16[896,512]{1,0:T(8,128)(2,1)}, u32[]{:S(2)}) copy-start(bf16[896,512]{1,0:T(8,128)(2,1)} %refs_15_.1) | copy-start | bytes 2752516
  6.8 8.6 %copy-start.7 = (s32[4]{0:T(128)S(1)}, s32[4]{0:T(128)}, u32[]{:S(2)}) copy-start(s32[4]{0:T(128)} %constant.54.clone) | copy-start | bytes 52
  6.8 26.0 %all-to-all-start = ((bf16[16,3,16,896]{3,2,1,0:T(8,128)(2,1)}), bf16[16,3,16,896]{3,2,1,0:T(8,128)(2,1)}, u32[]{:S(2)}, u32[]{:S(2)}) async-start(bf16[16,3,16,896]{3,2,1,0:T(8,128)(2,1)} %bitcast.28), calls=%async_computation | async-start | bytes 2752512 | tf_op jit(solution)/shard_map/all_to_all | solution.py:271
  13.9 13.7 %collective-permute-start = (bf16[896,512]{1,0:T(8,128)(2,1)S(1)}, bf16[896,512]{1,0:T(8,128)(2,1)S(1)}, u32[]{:S(2)}, u32[]{:S(2)}) collective-permute-start(bf16[896,512]{1,0:T(8,128)(2,1)S(1)} %copy-done), channel_id=1, source_target_pairs={{0,1},{1,0},{2,3},{3,2},{4,5},{5,4},{6,7},{7,6},{8,9},{9,8},{10,11... | collective-permute-start | bytes 2752520 | tf_op jit(solution)/shard_map/ppermute | solution.py:27
  14.8 12.8 %collective-permute-start.1 = (bf16[896,512]{1,0:T(8,128)(2,1)S(1)}, bf16[896,512]{1,0:T(8,128)(2,1)}, u32[]{:S(2)}, u32[]{:S(2)}) collective-permute-start(bf16[896,512]{1,0:T(8,128)(2,1)S(1)} %copy-done.1), channel_id=1, source_target_pairs={{0,1},{1,0},{2,3},{3,2},{4,5},{5,4},{6,7},{7,6},{8,9},{9,8},{10,11... | collective-permute-start | bytes 2752520 | tf_op jit(solution)/shard_map/ppermute | solution.py:27
  34.8 7.4 %collective-permute-start.4 = (bf16[256,896]{1,0:T(8,128)(2,1)S(1)}, bf16[256,896]{1,0:T(8,128)(2,1)S(1)}, u32[]{:S(2)}, u32[]{:S(2)}) collective-permute-start(bf16[256,896]{1,0:T(8,128)(2,1)S(1)} %bitcast.24), channel_id=1, source_target_pairs={{0,1},{1,0},{2,3},{3,2},{4,5},{5,4},{6,7},{7,6},{8,9},{9,8},{10,11... | collective-permute-start | bytes 1376264 | tf_op jit(solution)/shard_map/ppermute | solution.py:302
  38.5 13.5 %collective-permute-start.6 = (bf16[256,896]{1,0:T(8,128)(2,1)S(1)}, bf16[256,896]{1,0:T(8,128)(2,1)S(1)}, u32[]{:S(2)}, u32[]{:S(2)}) collective-permute-start(bf16[256,896]{1,0:T(8,128)(2,1)S(1)} %bitcast.25), channel_id=1, source_target_pairs={{0,7},{1,6},{2,1},{3,0},{4,3},{5,2},{6,5},{7,4},{8,15},{9,14},{10,... | collective-permute-start | bytes 1376264 | tf_op jit(solution)/shard_map/ppermute | solution.py:302
  42.2 14.0 %copy-start.8 = (bf16[64,1024]{1,0:T(8,128)(2,1)S(1)}, bf16[64,1024]{1,0:T(8,128)(2,1)}, u32[]{:S(2)}) copy-start(bf16[64,1024]{1,0:T(8,128)(2,1)} %get-tuple-element.100) | copy-start | bytes 393220
  42.2 14.0 %collective-permute-start.5 = (bf16[256,896]{1,0:T(8,128)(2,1)S(1)}, bf16[256,896]{1,0:T(8,128)(2,1)S(1)}, u32[]{:S(2)}, u32[]{:S(2)}) collective-permute-start(bf16[256,896]{1,0:T(8,128)(2,1)S(1)} %bitcast.21), channel_id=1, source_target_pairs={{0,2},{1,3},{2,4},{3,5},{4,6},{5,7},{6,0},{7,1},{8,10},{9,11},{10,... | collective-permute-start | bytes 1376264 | tf_op jit(solution)/shard_map/ppermute | solution.py:302
  46.0 28.8 %copy-start.3 = (bf16[512,4096]{1,0:T(8,128)(2,1)}, bf16[512,4096]{1,0:T(8,128)(2,1)S(1)}, u32[]{:S(2)}) copy-start(bf16[512,4096]{1,0:T(8,128)(2,1)S(1)} %get-tuple-element.102.refs_21_) | copy-start | bytes 12582916
  46.0 20.4 %collective-permute-start.7 = (bf16[256,896]{1,0:T(8,128)(2,1)S(1)}, bf16[256,896]{1,0:T(8,128)(2,1)S(1)}, u32[]{:S(2)}, u32[]{:S(2)}) collective-permute-start(bf16[256,896]{1,0:T(8,128)(2,1)S(1)} %bitcast.26), channel_id=1, source_target_pairs={{0,3},{1,2},{2,5},{3,4},{4,7},{5,6},{6,1},{7,0},{8,11},{9,10},{10,... | collective-permute-start | bytes 1376264 | tf_op jit(solution)/shard_map/ppermute | solution.py:302
  46.0 20.3 %collective-permute-start.8 = (bf16[256,896]{1,0:T(8,128)(2,1)S(1)}, bf16[256,896]{1,0:T(8,128)(2,1)S(1)}, u32[]{:S(2)}, u32[]{:S(2)}) collective-permute-start(bf16[256,896]{1,0:T(8,128)(2,1)S(1)} %bitcast.23), channel_id=1, source_target_pairs={{0,6},{1,7},{2,0},{3,1},{4,2},{5,3},{6,4},{7,5},{8,14},{9,15},{10,... | collective-permute-start | bytes 1376264 | tf_op jit(solution)/shard_map/ppermute | solution.py:302
  52.0 19.7 %collective-permute-start.10 = (bf16[256,896]{1,0:T(8,128)(2,1)S(1)}, bf16[256,896]{1,0:T(8,128)(2,1)S(1)}, u32[]{:S(2)}, u32[]{:S(2)}) collective-permute-start(bf16[256,896]{1,0:T(8,128)(2,1)S(1)} %collective-permute-done.6.refs_1_), channel_id=1, source_target_pairs={{0,6},{1,7},{2,0},{3,1},{4,2},{5,3},{6,4},{7,5},{8,14},{9,15},{10,... | collective-permute-start | bytes 1376264 | tf_op jit(solution)/shard_map/ppermute | solution.py:302
  56.2 18.5 %collective-permute-start.9 = (bf16[256,896]{1,0:T(8,128)(2,1)S(1)}, bf16[256,896]{1,0:T(8,128)(2,1)S(1)}, u32[]{:S(2)}, u32[]{:S(2)}) collective-permute-start(bf16[256,896]{1,0:T(8,128)(2,1)S(1)} %collective-permute-done.5.refs_0_), channel_id=1, source_target_pairs={{0,2},{1,3},{2,4},{3,5},{4,6},{5,7},{6,0},{7,1},{8,10},{9,11},{10,... | collective-permute-start | bytes 1376264 | tf_op jit(solution)/shard_map/ppermute | solution.py:302
  56.2 12.5 %collective-permute-start.11 = (bf16[64,1024]{1,0:T(8,128)(2,1)S(1)}, bf16[64,1024]{1,0:T(8,128)(2,1)S(1)}, u32[]{:S(2)}, u32[]{:S(2)}) collective-permute-start(bf16[64,1024]{1,0:T(8,128)(2,1)S(1)} %copy-done.8), channel_id=1, source_target_pairs={{8,1},{16,9},{24,17},{32,25},{40,33},{48,41},{56,49},{64,57},{72,6... | collective-permute-start | bytes 393224 | tf_op jit(solution)/shard_map/ppermute | solution.py:319
  57.5 17.2 %copy-start.6 = (bf16[4,64,1024]{2,1,0:T(8,128)(2,1)S(1)}, bf16[4,64,1024]{2,1,0:T(8,128)(2,1)}, u32[]{:S(2)}) copy-start(bf16[4,64,1024]{2,1,0:T(8,128)(2,1)} %get-tuple-element.99.refs_18_) | copy-start | bytes 1572868
  59.9 14.8 %copy-start.2 = (bf16[512,4096]{1,0:T(8,128)(2,1)S(1)}, bf16[512,4096]{1,0:T(8,128)(2,1)}, u32[]{:S(2)}) copy-start(bf16[512,4096]{1,0:T(8,128)(2,1)} %refs_20_.1) | copy-start | bytes 12582916
  74.7 8.8 %copy-start.5 = (bf16[4,64,1024]{2,1,0:T(8,128)(2,1)S(1)}, bf16[4,64,1024]{2,1,0:T(8,128)(2,1)}, u32[]{:S(2)}) copy-start(bf16[4,64,1024]{2,1,0:T(8,128)(2,1)} %get-tuple-element.107.refs_18_) | copy-start | bytes 1572868
  80.8 13.4 %collective-permute-start.12 = (bf16[64,4096]{1,0:T(8,128)(2,1)S(1)}, bf16[64,4096]{1,0:T(8,128)(2,1)S(1)}, u32[]{:S(2)}, u32[]{:S(2)}) collective-permute-start(bf16[64,4096]{1,0:T(8,128)(2,1)S(1)} %get-tuple-element.104), channel_id=1, source_target_pairs={{0,2},{2,4},{4,6},{6,0},{1,3},{3,5},{5,7},{7,1},{8,10},{10,12},{12... | collective-permute-start | bytes 1572872 | tf_op jit(solution)/shard_map/ppermute | solution.py:27
  80.9 13.3 %collective-permute-start.13 = (bf16[64,4096]{1,0:T(8,128)(2,1)S(1)}, bf16[64,4096]{1,0:T(8,128)(2,1)S(1)}, u32[]{:S(2)}, u32[]{:S(2)}) collective-permute-start(bf16[64,4096]{1,0:T(8,128)(2,1)S(1)} %get-tuple-element.105), channel_id=1, source_target_pairs={{0,6},{2,0},{4,2},{6,4},{1,7},{3,1},{5,3},{7,5},{8,14},{10,8},{12,... | collective-permute-start | bytes 1572872 | tf_op jit(solution)/shard_map/ppermute | solution.py:27
  83.5 2.2 %copy-start.4 = (bf16[512,4096]{1,0:T(8,128)(2,1)S(1)}, bf16[512,4096]{1,0:T(8,128)(2,1)}, u32[]{:S(2)}) copy-start(bf16[512,4096]{1,0:T(8,128)(2,1)} %copy-done.3) | copy-start | bytes 12582916
  94.3 7.8 %collective-permute-start.15 = (bf16[64,2048]{1,0:T(8,128)(2,1)S(1)}, bf16[64,2048]{1,0:T(8,128)(2,1)S(1)}, u32[]{:S(2)}, u32[]{:S(2)}) collective-permute-start(bf16[64,2048]{1,0:T(8,128)(2,1)S(1)} %get-tuple-element.122), channel_id=1, source_target_pairs={{0,6},{2,0},{4,2},{6,4},{1,7},{3,1},{5,3},{7,5},{8,14},{10,8},{12,... | collective-permute-start | bytes 786440 | tf_op jit(solution)/shard_map/ppermute | solution.py:27
  96.8 6.4 %collective-permute-start.14 = (bf16[64,2048]{1,0:T(8,128)(2,1)S(1)}, bf16[64,2048]{1,0:T(8,128)(2,1)S(1)}, u32[]{:S(2)}, u32[]{:S(2)}) collective-permute-start(bf16[64,2048]{1,0:T(8,128)(2,1)S(1)} %get-tuple-element.120), channel_id=1, source_target_pairs={{0,2},{2,4},{4,6},{6,0},{1,3},{3,5},{5,7},{7,1},{8,10},{10,12},{12... | collective-permute-start | bytes 786440 | tf_op jit(solution)/shard_map/ppermute | solution.py:27
  96.8 15.5 %collective-permute-start.19 = (bf16[64,2048]{1,0:T(8,128)(2,1)S(1)}, bf16[64,2048]{1,0:T(8,128)(2,1)S(1)}, u32[]{:S(2)}, u32[]{:S(2)}) collective-permute-start(bf16[64,2048]{1,0:T(8,128)(2,1)S(1)} %get-tuple-element.128), channel_id=1, source_target_pairs={{0,6},{2,0},{4,2},{6,4},{1,7},{3,1},{5,3},{7,5},{8,14},{10,8},{12,... | collective-permute-start | bytes 786440 | tf_op jit(solution)/shard_map/ppermute | solution.py:27
  99.5 12.9 %collective-permute-start.18 = (bf16[64,2048]{1,0:T(8,128)(2,1)S(1)}, bf16[64,2048]{1,0:T(8,128)(2,1)S(1)}, u32[]{:S(2)}, u32[]{:S(2)}) collective-permute-start(bf16[64,2048]{1,0:T(8,128)(2,1)S(1)} %get-tuple-element.126), channel_id=1, source_target_pairs={{0,2},{2,4},{4,6},{6,0},{1,3},{3,5},{5,7},{7,1},{8,10},{10,12},{12... | collective-permute-start | bytes 786440 | tf_op jit(solution)/shard_map/ppermute | solution.py:27
  99.5 15.7 %collective-permute-start.17 = (bf16[64,2048]{1,0:T(8,128)(2,1)S(1)}, bf16[64,2048]{1,0:T(8,128)(2,1)S(1)}, u32[]{:S(2)}, u32[]{:S(2)}) collective-permute-start(bf16[64,2048]{1,0:T(8,128)(2,1)S(1)} %get-tuple-element.124), channel_id=1, source_target_pairs={{0,6},{2,0},{4,2},{6,4},{1,7},{3,1},{5,3},{7,5},{8,14},{10,8},{12,... | collective-permute-start | bytes 786440 | tf_op jit(solution)/shard_map/ppermute | solution.py:27
  102.2 18.9 %collective-permute-start.21 = (bf16[64,2048]{1,0:T(8,128)(2,1)S(1)}, bf16[64,2048]{1,0:T(8,128)(2,1)S(1)}, u32[]{:S(2)}, u32[]{:S(2)}) collective-permute-start(bf16[64,2048]{1,0:T(8,128)(2,1)S(1)} %get-tuple-element.131), channel_id=1, source_target_pairs={{0,2},{2,4},{4,6},{6,0},{1,3},{3,5},{5,7},{7,1},{8,10},{10,12},{12... | collective-permute-start | bytes 786440 | tf_op jit(solution)/shard_map/ppermute | solution.py:27
  103.4 17.9 %collective-permute-start.16 = (bf16[64,4096]{1,0:T(8,128)(2,1)S(1)}, bf16[64,4096]{1,0:T(8,128)(2,1)S(1)}, u32[]{:S(2)}, u32[]{:S(2)}) collective-permute-start(bf16[64,4096]{1,0:T(8,128)(2,1)S(1)} %pad_maximum_fusion.1), channel_id=1, source_target_pairs={{0,1},{1,8},{2,3},{3,2},{4,5},{5,4},{6,7},{7,6},{8,9},{9,16},{10,1... | collective-permute-start | bytes 1572872 | tf_op jit(solution)/shard_map/ppermute | solution.py:340
  112.4 8.6 %collective-permute-start.20 = (bf16[64,2048]{1,0:T(8,128)(2,1)S(1)}, bf16[64,2048]{1,0:T(8,128)(2,1)S(1)}, u32[]{:S(2)}, u32[]{:S(2)}) collective-permute-start(bf16[64,2048]{1,0:T(8,128)(2,1)S(1)} %add_convert_fusion.3), channel_id=1, source_target_pairs={{0,2},{2,4},{4,6},{6,0},{1,3},{3,5},{5,7},{7,1},{8,10},{10,12},{12... | collective-permute-start | bytes 786440 | tf_op jit(solution)/shard_map/ppermute | solution.py:27
  112.5 8.6 %collective-permute-start.22 = (bf16[64,2048]{1,0:T(8,128)(2,1)S(1)}, bf16[64,2048]{1,0:T(8,128)(2,1)S(1)}, u32[]{:S(2)}, u32[]{:S(2)}) collective-permute-start(bf16[64,2048]{1,0:T(8,128)(2,1)S(1)} %add_convert_fusion.2), channel_id=1, source_target_pairs={{0,6},{2,0},{4,2},{6,4},{1,7},{3,1},{5,3},{7,5},{8,14},{10,8},{12,... | collective-permute-start | bytes 786440 | tf_op jit(solution)/shard_map/ppermute | solution.py:27

commit v8 on v7

--- a/solution.py
+++ b/solution.py
@@ -170,8 +170,7 @@
     near_refs, row_refs, weight_refs = take(12), take(2), take(4)
     q_ref, crossing_ref = take(2)
     out_weight_refs, out_refs, far_kv_refs = take(2), take(6 if group == 0 else 8), take(4)
-    count = row_refs[0].shape[0] // 2
-    rows = jnp.concatenate([ref[group * count : (group + 1) * count] for ref in row_refs], axis=0)
+    rows = jnp.concatenate([ref[...] for ref in row_refs], axis=0)
     for weight_ref, far_kv_ref in zip(weight_refs, far_kv_refs):
         far_kv_ref[...] = dot(rows, weight_ref[...]).astype(BF16).reshape(far_kv_ref.shape)
     (context_ref,) = refs
@@ -317,12 +316,17 @@
     near, mine, theirs, crossing = lax.optimization_barrier((near, mine, theirs, crossing))
     ring_after = hop(theirs, 1, 1), hop(mine, -1, 0)
     crossing = lax.ppermute(crossing, ("seq", "core"), [(2 * i + 2, 2 * i + 1) for i in range(n_seq - 1)])
-    far = hop(ring[0], 1, 0), hop(ring[1], -1, 0)
+    half_rows = mine.shape[0] // 2
+    far_a = hop(ring[0][:half_rows], 1, 0), hop(ring[1][:half_rows], -1, 0)
     near = (*near, *project(weights[:4], ring), *project(weights[:4], ring_after))
-
-    up_a, down_a, above_a, below_a, *here_a = attend(0, places_a, second_queries, crossing, near, far, weights)
+    far_a, near, later = lax.optimization_barrier((far_a, near, (ring[0][half_rows:], ring[1][half_rows:])))
+    far_b = hop(later[0], 1, 0), hop(later[1], -1, 0)
+
+    sums_a = attend(0, places_a, second_queries, crossing, near, far_a, weights)
+    sums_a, far_b = lax.optimization_barrier((sums_a, far_b))
+    up_a, down_a, above_a, below_a, *here_a = sums_a
     up_a, down_a = step(up_a, "z", 1), step(down_a, "z", -1)
-    sums_b = attend(1, places_b, first_queries, crossing, near, far, weights)
+    sums_b = attend(1, places_b, first_queries, crossing, near, far_b, weights)
     up_a, down_a, sums_b = lax.optimization_barrier((up_a, down_a, sums_b))
     above_a, below_a = lax.optimization_barrier((add(above_a, up_a[:, :side]), add(below_a, down_a[:, side:])))
     up_left_a, down_right_a = step(above_a, "z", 1), step(below_a, "z", -1)

time: 124 us -> 120 us (0.968)
  waiting for transfers between devices: 29.9 us -> 25.1 us
    ppermute x7 -> x9, waiting for transfers between devices: 15.4 us -> 10.5 us  [hop(): return lax.ppermute(value, ('z', 'core'), pairs)]
    ppermute x7 -> x9, starting transfers between devices: 14.7 us -> 15.4 us  [hop(): return lax.ppermute(value, ('z', 'core'), pairs)]
  transfers between devices with their start and end apart: 24 -> 26, of which waited for: 8 -> 8; matrix products, arithmetic and copies ran while one was open for 3% -> 3% of each run, Pallas kernels for 24% -> 30%
where the time goes in v8:
time: 120 us; the launch traced here: 118 us
  starting transfers between devices  48.2 us (40%)
  Pallas kernels  37.3 us (31%)
  waiting for transfers between devices  25.1 us (21%)
  local copies, waits for them, and re-layouts  3.99 us (3%)
  other arithmetic  3.29 us (3%)
    ppermute x14, starting transfers between devices, step(): lax.ppermute(value, axis, [(i, (i + steps) % count) for i in range(count)])  15.7 us
    ppermute x9, starting transfers between devices, hop(): return lax.ppermute(value, ('z', 'core'), pairs)  15.4 us
    pallas_call x1, Pallas kernels, project_queries(): pl.pallas_call(query_kernel, grid_spec=pltpu.PrefetchScalarGridSpec(num_s...  12 us
    pallas_call x2, Pallas kernels, attend(): pl.pallas_call(functools.partial(span_kernel, group), grid_spec=pltpu.Pre...  12 us
    ppermute x9, waiting for transfers between devices, hop(): return lax.ppermute(value, ('z', 'core'), pairs)  10.5 us
    ppermute x14, waiting for transfers between devices, step(): lax.ppermute(value, axis, [(i, (i + steps) % count) for i in range(count)])  9.4 us
    ppermute x1, starting transfers between devices, body(): head = lax.ppermute(out_a, ('seq', 'z', 'core'), pairs)  8.81 us
    pallas_call x3, Pallas kernels, project(): pl.pallas_call(functools.partial(project_kernel, len(carried)), in_specs=...  8.38 us
  transfers between devices with their start and end apart: 26, of which 8 were waited for; matrix products, arithmetic and copies ran while one was open for 3% of the time, Pallas kernels for 30%

profile of v8, /device:TPU:1, one launch (start us, length us, event | category | flops | bytes accessed | tf_op | source)
XLA Modules:
  0.0 118.3 jit_solution(14758347569678047392)
XLA Ops:
  0.0 1.4 %collective-permute-start.3 = (bf16[4096,512]{1,0:T(8,128)(2,1)}, bf16[4096,512]{1,0:T(8,128)(2,1)}, u32[]{:S(2)}, u32[]{:S(2)}) collective-permute-start(bf16[4096,512]{1,0:T(8,128)(2,1)} %wa_hbm.1), channel_id=1, source_target_pairs={{0,1},{1,0},{2,3},{3,2},{4,5},{5,4},{6,7},{7,6},{8,9},{9,8},{10,11... | collective-permute-start | bytes 12582920 | tf_op jit(solution)/shard_map/ppermute | solution.py:27
  1.4 0.7 shift-right-arithmetic_bitcast_fusion
  2.5 0.5 convert_reduce_fusion
  3.0 0.1 select_reduce_fusion
  3.2 0.6 reshape.76.index_ref
  3.8 3.0 %shard_map.91 = bf16[48,16,896]{2,1,0:T(8,128)(2,1)} custom-call(s32[48]{0:T(128)} %reshape.76.index_ref, s32[1]{0:T(128)} %bitcast.4.start_ref, bf16[24,128,896]{2,1,0:T(8,128)(2,1)} %source_ref.1), custom_call_target="tpu_custom_call" | custom-call | flops 400000000 | bytes 400000 | tf_op jit(solution)/shard_map/pallas_call | solution.py:61
  6.8 7.0 %all-to-all-start = ((bf16[16,3,16,896]{3,2,1,0:T(8,128)(2,1)}), bf16[16,3,16,896]{3,2,1,0:T(8,128)(2,1)}, u32[]{:S(2)}, u32[]{:S(2)}) async-start(bf16[16,3,16,896]{3,2,1,0:T(8,128)(2,1)} %bitcast.28), calls=%async_computation | async-start | bytes 2752512 | tf_op jit(solution)/shard_map/all_to_all | solution.py:270
  13.9 0.9 collective-permute-start
  14.7 0.1 collective-permute-start.1
  15.0 0.1 rev.6
  15.1 0.1 rev.7
  15.2 0.1 copy.18
  15.5 12.0 %shard_map.92 = (bf16[4,64,1024]{2,1,0:T(8,128)(2,1)}, bf16[4,64,1024]{2,1,0:T(8,128)(2,1)}, bf16[64,1024]{1,0:T(8,128)(2,1)}) custom-call(s32[1]{0:T(128)} %bitcast.7.core_ref, bf16[8,128,4096]{2,1,0:T(8,128)(2,1)} %bitcast.27, bf16[4096,512]{1,0:T(8,128)(2,1)} %wa_hbm.1, bf16[4096,512]{1,0:T(8,128)(2,1)} %collective-permute-done.3.wb_hbm), custom_call_target="tpu_custom_call" | custom-call | flops 1200000000 | bytes 1200000 | tf_op jit(solution)/shard_map/pallas_call | solution.py:112
  27.6 5.2 %all-to-all-done = bf16[16,3,16,896]{3,2,1,0:T(8,128)(2,1)} async-done(((bf16[16,3,16,896]{3,2,1,0:T(8,128)(2,1)}), bf16[16,3,16,896]{3,2,1,0:T(8,128)(2,1)}, u32[]{:S(2)}, u32[]{:S(2)}) %all-to-all-start) | async-done | bytes 1376288 | tf_op jit(solution)/shard_map/all_to_all | solution.py:270
  32.8 2.0 %shard_map.93 = (bf16[16,16,896]{2,1,0:T(8,128)(2,1)S(1)}, bf16[16,16,896]{2,1,0:T(8,128)(2,1)S(1)}) custom-call(s32[32]{0:T(128)S(1)} %reshape.82.index_ref, s32[1]{0:T(128)} %constant.53.clone.1.start_ref, bf16[48,16,896]{2,1,0:T(8,128)(2,1)} %bitcast.6.source_ref), custom_call_target="tpu_custom_call" | custom-call | flops 400000000 | bytes 400000 | tf_op jit(solution)/shard_map/pallas_call | solution.py:61
  34.8 3.7 %collective-permute-start.8 = (bf16[256,896]{1,0:T(8,128)(2,1)S(1)}, bf16[256,896]{1,0:T(8,128)(2,1)S(1)}, u32[]{:S(2)}, u32[]{:S(2)}) collective-permute-start(bf16[256,896]{1,0:T(8,128)(2,1)S(1)} %bitcast.24), channel_id=1, source_target_pairs={{0,1},{1,0},{2,3},{3,2},{4,5},{5,4},{6,7},{7,6},{8,9},{9,8},{10,11... | collective-permute-start | bytes 1376264 | tf_op jit(solution)/shard_map/ppermute | solution.py:301
  38.5 1.7 %collective-permute-start.4 = (bf16[256,896]{1,0:T(8,128)(2,1)S(1)}, bf16[256,896]{1,0:T(8,128)(2,1)S(1)}, u32[]{:S(2)}, u32[]{:S(2)}) collective-permute-start(bf16[256,896]{1,0:T(8,128)(2,1)S(1)} %bitcast.21), channel_id=1, source_target_pairs={{0,2},{1,3},{2,4},{3,5},{4,6},{5,7},{6,0},{7,1},{8,10},{9,11},{10,... | collective-permute-start | bytes 1376264 | tf_op jit(solution)/shard_map/ppermute | solution.py:301
  40.1 2.2 %collective-permute-start.6 = (bf16[256,896]{1,0:T(8,128)(2,1)S(1)}, bf16[256,896]{1,0:T(8,128)(2,1)S(1)}, u32[]{:S(2)}, u32[]{:S(2)}) collective-permute-start(bf16[256,896]{1,0:T(8,128)(2,1)S(1)} %bitcast.25), channel_id=1, source_target_pairs={{0,7},{1,6},{2,1},{3,0},{4,3},{5,2},{6,5},{7,4},{8,15},{9,14},{10,... | collective-permute-start | bytes 1376264 | tf_op jit(solution)/shard_map/ppermute | solution.py:301
  42.3 3.7 %shard_map.94 = (bf16[2,2,4,32,512]{4,3,2,1,0:T(8,128)(2,1)S(1)}, bf16[2,2,4,32,512]{4,3,2,1,0:T(8,128)(2,1)S(1)}, bf16[2,2,4,32,512]{4,3,2,1,0:T(8,128)(2,1)S(1...) custom-call(bf16[256,896]{1,0:T(8,128)(2,1)S(1)} %bitcast.22, ...), custom_call_target="tpu_custom_call" | custom-call | flops 800000000 | bytes 800000 | tf_op jit(solution)/shard_map/pallas_call | solution.py:150
  46.0 1.7 %collective-permute-start.10 = (bf16[256,896]{1,0:T(8,128)(2,1)S(1)}, bf16[256,896]{1,0:T(8,128)(2,1)S(1)}, u32[]{:S(2)}, u32[]{:S(2)}) collective-permute-start(bf16[256,896]{1,0:T(8,128)(2,1)S(1)} %bitcast.23), channel_id=1, source_target_pairs={{0,6},{1,7},{2,0},{3,1},{4,2},{5,3},{6,4},{7,5},{8,14},{9,15},{10,... | collective-permute-start | bytes 1376264 | tf_op jit(solution)/shard_map/ppermute | solution.py:301
  47.7 0.3 collective-permute-start.9
  48.0 5.0 %collective-permute-done.4.refs_0_ = bf16[256,896]{1,0:T(8,128)(2,1)S(1)} collective-permute-done((bf16[256,896]{1,0:T(8,128)(2,1)S(1)}, bf16[256,896]{1,0:T(8,128)(2,1)S(1)}, u32[]{:S(2)}, u32[]{:S(2)}) %collective-permute-start.4) | collective-permute-done | bytes 458784 | tf_op jit(solution)/shard_map/ppermute | solution.py:301
  53.1 0.3 collective-permute-start.5
  53.4 2.9 %collective-permute-start.7 = (bf16[128,896]{1,0:T(8,128)(2,1)S(1)}, bf16[128,896]{1,0:T(8,128)(2,1)S(1)}, u32[]{:S(2)}, u32[]{:S(2)}) collective-permute-start(bf16[128,896]{1,0:T(8,128)(2,1)S(1)} %get-tuple-element.182), channel_id=1, source_target_pairs={{0,6},{1,7},{2,0},{3,1},{4,2},{5,3},{6,4},{7,5},{8,14},{9,15},{10,... | collective-permute-start | bytes 688136 | tf_op jit(solution)/shard_map/ppermute | solution.py:301
  56.3 1.3 %collective-permute-start.11 = (bf16[64,1024]{1,0:T(8,128)(2,1)S(1)}, bf16[64,1024]{1,0:T(8,128)(2,1)S(1)}, u32[]{:S(2)}, u32[]{:S(2)}) collective-permute-start(bf16[64,1024]{1,0:T(8,128)(2,1)S(1)} %copy-done.8), channel_id=1, source_target_pairs={{8,1},{16,9},{24,17},{32,25},{40,33},{48,41},{56,49},{64,57},{72,6... | collective-permute-start | bytes 393224 | tf_op jit(solution)/shard_map/ppermute | solution.py:318
  57.6 2.3 %shard_map.95 = (bf16[2,2,4,32,512]{4,3,2,1,0:T(8,128)(2,1)S(1)}, bf16[2,2,4,32,512]{4,3,2,1,0:T(8,128)(2,1)S(1)}, bf16[2,2,4,32,512]{4,3,2,1,0:T(8,128)(2,1)S(1)}, bf16[2,2,4,32,512]{4,3,2,1,0:T(8,128)(2,1)S(1)}) custom-call(bf16[256,896]{1,0:T(8,128)(2,1)S(1)} %collective-permute-done.4.refs_0_, bf16[256,896]{1,0:T(8,128)(2,1)S(1)} %collective-permute-done.6.refs_1_, ...), custom_call_target="tpu_custom_call" | custom-call | flops 800000000 | bytes 800000 | tf_op jit(solution)/shard_map/pallas_call | solution.py:150
  60.0 2.4 %collective-permute-done.10.refs_1_ = bf16[256,896]{1,0:T(8,128)(2,1)S(1)} collective-permute-done((bf16[256,896]{1,0:T(8,128)(2,1)S(1)}, bf16[256,896]{1,0:T(8,128)(2,1)S(1)}, u32[]{:S(2)}, u32[]{:S(2)}) %collective-permute-start.10) | collective-permute-done | bytes 458784 | tf_op jit(solution)/shard_map/ppermute | solution.py:301
  62.3 0.8 collective-permute-done.9.refs_0_
  63.1 2.3 %shard_map.96 = (bf16[2,2,4,32,512]{4,3,2,1,0:T(8,128)(2,1)S(1)}, bf16[2,2,4,32,512]{4,3,2,1,0:T(8,128)(2,1)S(1)}, bf16[2,2,4,32,512]{4,3,2,1,0:T(8,128)(2,1)S(1)}, bf16[2,2,4,32,512]{4,3,2,1,0:T(8,128)(2,1)S(1)}) custom-call(bf16[256,896]{1,0:T(8,128)(2,1)S(1)} %collective-permute-done.9.refs_0_, bf16[256,896]{1,0:T(8,128)(2,1)S(1)} %collective-permute-done.10.refs_1_, ...), custom_call_target="tpu_custom_call" | custom-call | flops 800000000 | bytes 800000 | tf_op jit(solution)/shard_map/pallas_call | solution.py:150
  65.5 2.3 %collective-permute-done.5.refs_12_ = bf16[128,896]{1,0:T(8,128)(2,1)S(1)} collective-permute-done((bf16[128,896]{1,0:T(8,128)(2,1)S(1)}, bf16[128,896]{1,0:T(8,128)(2,1)S(1)}, u32[]{:S(2)}, u32[]{:S(2)}) %collective-permute-start.5) | collective-permute-done | bytes 229408 | tf_op jit(solution)/shard_map/ppermute | solution.py:301
  67.8 1.2 collective-permute-start.12
  69.0 1.5 %collective-permute-start.13 = (bf16[128,896]{1,0:T(8,128)(2,1)S(1)}, bf16[128,896]{1,0:T(8,128)(2,1)S(1)}, u32[]{:S(2)}, u32[]{:S(2)}) collective-permute-start(bf16[128,896]{1,0:T(8,128)(2,1)S(1)} %get-tuple-element.148), channel_id=1, source_target_pairs={{0,6},{1,7},{2,0},{3,1},{4,2},{5,3},{6,4},{7,5},{8,14},{9,15},{10,... | collective-permute-start | bytes 688136 | tf_op jit(solution)/shard_map/ppermute | solution.py:301
  70.5 6.0 %shard_map.97 = (bf16[64,4096]{1,0:T(8,128)(2,1)S(1)}, bf16[64,4096]{1,0:T(8,128)(2,1)S(1)}, bf16[64,2048]{1,0:T(8,128)(2,1)S(1)}, bf16[64,2048]{1,0:T(8,128)(2,...) custom-call(s32[9]{0:T(128)S(1)} %pad_add_fusion.place_ref, ...), custom_call_target="tpu_custom_call" | custom-call | flops 2000000000 | bytes 2000000 | tf_op jit(solution)/shard_map/pallas_call | solution.py:237
  76.6 2.7 %collective-permute-start.15 = (bf16[64,4096]{1,0:T(8,128)(2,1)S(1)}, bf16[64,4096]{1,0:T(8,128)(2,1)S(1)}, u32[]{:S(2)}, u32[]{:S(2)}) collective-permute-start(bf16[64,4096]{1,0:T(8,128)(2,1)S(1)} %get-tuple-element.151), channel_id=1, source_target_pairs={{0,6},{2,0},{4,2},{6,4},{1,7},{3,1},{5,3},{7,5},{8,14},{10,8},{12,... | collective-permute-start | bytes 1572872 | tf_op jit(solution)/shard_map/ppermute | solution.py:27
  79.3 2.2 %copy-done.4 = bf16[512,4096]{1,0:T(8,128)(2,1)S(1)} copy-done((bf16[512,4096]{1,0:T(8,128)(2,1)S(1)}, bf16[512,4096]{1,0:T(8,128)(2,1)}, u32[]{:S(2)}) %copy-start.4) | copy-done | bytes 4194328
  81.5 6.0 %shard_map.98 = (bf16[64,2048]{1,0:T(8,128)(2,1)S(1)}, bf16[64,2048]{1,0:T(8,128)(2,1)S(1)}, bf16[64,2048]{1,0:T(8,128)(2,1)S(1)}, bf16[64,2048]{1,0:T(8,128)(2,...) custom-call(s32[4]{0:T(128)S(1)} %get-tuple-element.152.place_ref, ...), custom_call_target="tpu_custom_call" | custom-call | flops 2000000000 | bytes 2000000 | tf_op jit(solution)/shard_map/pallas_call | solution.py:237
  87.5 2.5 %collective-permute-done.14 = bf16[64,4096]{1,0:T(8,128)(2,1)S(1)} collective-permute-done((bf16[64,4096]{1,0:T(8,128)(2,1)S(1)}, bf16[64,4096]{1,0:T(8,128)(2,1)S(1)}, u32[]{:S(2)}, u32[]{:S(2)}) %collective-permute-start.14) | collective-permute-done | bytes 524320 | tf_op jit(solution)/shard_map/ppermute | solution.py:27
  90.0 0.1 add_convert_fusion.6
  90.1 2.5 %collective-permute-start.17 = (bf16[64,2048]{1,0:T(8,128)(2,1)S(1)}, bf16[64,2048]{1,0:T(8,128)(2,1)S(1)}, u32[]{:S(2)}, u32[]{:S(2)}) collective-permute-start(bf16[64,2048]{1,0:T(8,128)(2,1)S(1)} %get-tuple-element.170), channel_id=1, source_target_pairs={{0,6},{2,0},{4,2},{6,4},{1,7},{3,1},{5,3},{7,5},{8,14},{10,8},{12,... | collective-permute-start | bytes 786440 | tf_op jit(solution)/shard_map/ppermute | solution.py:27
  92.6 2.7 %collective-permute-start.21 = (bf16[64,2048]{1,0:T(8,128)(2,1)S(1)}, bf16[64,2048]{1,0:T(8,128)(2,1)S(1)}, u32[]{:S(2)}, u32[]{:S(2)}) collective-permute-start(bf16[64,2048]{1,0:T(8,128)(2,1)S(1)} %get-tuple-element.176), channel_id=1, source_target_pairs={{0,6},{2,0},{4,2},{6,4},{1,7},{3,1},{5,3},{7,5},{8,14},{10,8},{12,... | collective-permute-start | bytes 786440 | tf_op jit(solution)/shard_map/ppermute | solution.py:27
  95.3 2.7 %collective-permute-start.19 = (bf16[64,2048]{1,0:T(8,128)(2,1)S(1)}, bf16[64,2048]{1,0:T(8,128)(2,1)S(1)}, u32[]{:S(2)}, u32[]{:S(2)}) collective-permute-start(bf16[64,2048]{1,0:T(8,128)(2,1)S(1)} %get-tuple-element.172), channel_id=1, source_target_pairs={{0,6},{2,0},{4,2},{6,4},{1,7},{3,1},{5,3},{7,5},{8,14},{10,8},{12,... | collective-permute-start | bytes 786440 | tf_op jit(solution)/shard_map/ppermute | solution.py:27
  98.1 1.0 collective-permute-done.16
  99.2 8.8 %collective-permute-start.18 = (bf16[64,4096]{1,0:T(8,128)(2,1)S(1)}, bf16[64,4096]{1,0:T(8,128)(2,1)S(1)}, u32[]{:S(2)}, u32[]{:S(2)}) collective-permute-start(bf16[64,4096]{1,0:T(8,128)(2,1)S(1)} %pad_maximum_fusion.1), channel_id=1, source_target_pairs={{0,1},{1,8},{2,3},{3,2},{4,5},{5,4},{6,7},{7,6},{8,9},{9,16},{10,1... | collective-permute-start | bytes 1572872 | tf_op jit(solution)/shard_map/ppermute | solution.py:344
  108.2 2.7 %collective-permute-start.24 = (bf16[64,2048]{1,0:T(8,128)(2,1)S(1)}, bf16[64,2048]{1,0:T(8,128)(2,1)S(1)}, u32[]{:S(2)}, u32[]{:S(2)}) collective-permute-start(bf16[64,2048]{1,0:T(8,128)(2,1)S(1)} %add_convert_fusion.2), channel_id=1, source_target_pairs={{0,6},{2,0},{4,2},{6,4},{1,7},{3,1},{5,3},{7,5},{8,14},{10,8},{12,... | collective-permute-start | bytes 786440 | tf_op jit(solution)/shard_map/ppermute | solution.py:27
  110.9 5.9 %collective-permute-done.22 = bf16[64,2048]{1,0:T(8,128)(2,1)S(1)} collective-permute-done((bf16[64,2048]{1,0:T(8,128)(2,1)S(1)}, bf16[64,2048]{1,0:T(8,128)(2,1)S(1)}, u32[]{:S(2)}, u32[]{:S(2)}) %collective-permute-start.22) | collective-permute-done | bytes 262176 | tf_op jit(solution)/shard_map/ppermute | solution.py:27
  116.9 0.1 add_convert_fusion
  117.1 0.1 slice.44
  117.2 1.1 pad_maximum_fusion
  (65 shorter events, 1.6 us)
Async XLA Ops:
  0.0 15.5 %collective-permute-start.3 = (bf16[4096,512]{1,0:T(8,128)(2,1)}, bf16[4096,512]{1,0:T(8,128)(2,1)}, u32[]{:S(2)}, u32[]{:S(2)}) collective-permute-start(bf16[4096,512]{1,0:T(8,128)(2,1)} %wa_hbm.1), channel_id=1, source_target_pairs={{0,1},{1,0},{2,3},{3,2},{4,5},{5,4},{6,7},{7,6},{8,9},{9,8},{10,11... | collective-permute-start | bytes 12582920 | tf_op jit(solution)/shard_map/ppermute | solution.py:27
  1.4 31.4 %collective-permute-start.2 = (bf16[512,4096]{1,0:T(8,128)(2,1)}, bf16[512,4096]{1,0:T(8,128)(2,1)}, u32[]{:S(2)}, u32[]{:S(2)}) collective-permute-start(bf16[512,4096]{1,0:T(8,128)(2,1)} %refs_20_.1), channel_id=1, source_target_pairs={{0,1},{1,0},{2,3},{3,2},{4,5},{5,4},{6,7},{7,6},{8,9},{9,8},{10,11... | collective-permute-start | bytes 12582920 | tf_op jit(solution)/shard_map/ppermute | solution.py:27
  6.8 7.1 %copy-start = (bf16[896,512]{1,0:T(8,128)(2,1)S(1)}, bf16[896,512]{1,0:T(8,128)(2,1)}, u32[]{:S(2)}) copy-start(bf16[896,512]{1,0:T(8,128)(2,1)} %refs_14_.1) | copy-start | bytes 2752516
  6.8 7.9 %copy-start.1 = (bf16[896,512]{1,0:T(8,128)(2,1)S(1)}, bf16[896,512]{1,0:T(8,128)(2,1)}, u32[]{:S(2)}) copy-start(bf16[896,512]{1,0:T(8,128)(2,1)} %refs_15_.1) | copy-start | bytes 2752516
  6.8 8.6 %copy-start.7 = (s32[4]{0:T(128)S(1)}, s32[4]{0:T(128)}, u32[]{:S(2)}) copy-start(s32[4]{0:T(128)} %constant.54.clone) | copy-start | bytes 52
  6.8 26.0 %all-to-all-start = ((bf16[16,3,16,896]{3,2,1,0:T(8,128)(2,1)}), bf16[16,3,16,896]{3,2,1,0:T(8,128)(2,1)}, u32[]{:S(2)}, u32[]{:S(2)}) async-start(bf16[16,3,16,896]{3,2,1,0:T(8,128)(2,1)} %bitcast.28), calls=%async_computation | async-start | bytes 2752512 | tf_op jit(solution)/shard_map/all_to_all | solution.py:270
  13.9 13.7 %collective-permute-start = (bf16[896,512]{1,0:T(8,128)(2,1)S(1)}, bf16[896,512]{1,0:T(8,128)(2,1)S(1)}, u32[]{:S(2)}, u32[]{:S(2)}) collective-permute-start(bf16[896,512]{1,0:T(8,128)(2,1)S(1)} %copy-done), channel_id=1, source_target_pairs={{0,1},{1,0},{2,3},{3,2},{4,5},{5,4},{6,7},{7,6},{8,9},{9,8},{10,11... | collective-permute-start | bytes 2752520 | tf_op jit(solution)/shard_map/ppermute | solution.py:27
  14.7 12.8 %collective-permute-start.1 = (bf16[896,512]{1,0:T(8,128)(2,1)S(1)}, bf16[896,512]{1,0:T(8,128)(2,1)}, u32[]{:S(2)}, u32[]{:S(2)}) collective-permute-start(bf16[896,512]{1,0:T(8,128)(2,1)S(1)} %copy-done.1), channel_id=1, source_target_pairs={{0,1},{1,0},{2,3},{3,2},{4,5},{5,4},{6,7},{7,6},{8,9},{9,8},{10,11... | collective-permute-start | bytes 2752520 | tf_op jit(solution)/shard_map/ppermute | solution.py:27
  34.8 7.5 %collective-permute-start.8 = (bf16[256,896]{1,0:T(8,128)(2,1)S(1)}, bf16[256,896]{1,0:T(8,128)(2,1)S(1)}, u32[]{:S(2)}, u32[]{:S(2)}) collective-permute-start(bf16[256,896]{1,0:T(8,128)(2,1)S(1)} %bitcast.24), channel_id=1, source_target_pairs={{0,1},{1,0},{2,3},{3,2},{4,5},{5,4},{6,7},{7,6},{8,9},{9,8},{10,11... | collective-permute-start | bytes 1376264 | tf_op jit(solution)/shard_map/ppermute | solution.py:301
  38.5 17.8 %copy-start.8 = (bf16[64,1024]{1,0:T(8,128)(2,1)S(1)}, bf16[64,1024]{1,0:T(8,128)(2,1)}, u32[]{:S(2)}) copy-start(bf16[64,1024]{1,0:T(8,128)(2,1)} %get-tuple-element.138) | copy-start | bytes 393220
  38.5 14.6 %collective-permute-start.4 = (bf16[256,896]{1,0:T(8,128)(2,1)S(1)}, bf16[256,896]{1,0:T(8,128)(2,1)S(1)}, u32[]{:S(2)}, u32[]{:S(2)}) collective-permute-start(bf16[256,896]{1,0:T(8,128)(2,1)S(1)} %bitcast.21), channel_id=1, source_target_pairs={{0,2},{1,3},{2,4},{3,5},{4,6},{5,7},{6,0},{7,1},{8,10},{9,11},{10,... | collective-permute-start | bytes 1376264 | tf_op jit(solution)/shard_map/ppermute | solution.py:301
  40.1 13.2 %collective-permute-start.6 = (bf16[256,896]{1,0:T(8,128)(2,1)S(1)}, bf16[256,896]{1,0:T(8,128)(2,1)S(1)}, u32[]{:S(2)}, u32[]{:S(2)}) collective-permute-start(bf16[256,896]{1,0:T(8,128)(2,1)S(1)} %bitcast.25), channel_id=1, source_target_pairs={{0,7},{1,6},{2,1},{3,0},{4,3},{5,2},{6,5},{7,4},{8,15},{9,14},{10,... | collective-permute-start | bytes 1376264 | tf_op jit(solution)/shard_map/ppermute | solution.py:301
  46.0 24.5 %copy-start.3 = (bf16[512,4096]{1,0:T(8,128)(2,1)}, bf16[512,4096]{1,0:T(8,128)(2,1)S(1)}, u32[]{:S(2)}) copy-start(bf16[512,4096]{1,0:T(8,128)(2,1)S(1)} %get-tuple-element.140.refs_21_) | copy-start | bytes 12582916
  46.0 16.3 %collective-permute-start.10 = (bf16[256,896]{1,0:T(8,128)(2,1)S(1)}, bf16[256,896]{1,0:T(8,128)(2,1)S(1)}, u32[]{:S(2)}, u32[]{:S(2)}) collective-permute-start(bf16[256,896]{1,0:T(8,128)(2,1)S(1)} %bitcast.23), channel_id=1, source_target_pairs={{0,6},{1,7},{2,0},{3,1},{4,2},{5,3},{6,4},{7,5},{8,14},{9,15},{10,... | collective-permute-start | bytes 1376264 | tf_op jit(solution)/shard_map/ppermute | solution.py:301
  47.7 15.4 %collective-permute-start.9 = (bf16[256,896]{1,0:T(8,128)(2,1)S(1)}, bf16[256,896]{1,0:T(8,128)(2,1)S(1)}, u32[]{:S(2)}, u32[]{:S(2)}) collective-permute-start(bf16[256,896]{1,0:T(8,128)(2,1)S(1)} %bitcast.26), channel_id=1, source_target_pairs={{0,3},{1,2},{2,5},{3,4},{4,7},{5,6},{6,1},{7,0},{8,11},{9,10},{10,... | collective-permute-start | bytes 1376264 | tf_op jit(solution)/shard_map/ppermute | solution.py:301
  53.1 14.7 %collective-permute-start.5 = (bf16[128,896]{1,0:T(8,128)(2,1)S(1)}, bf16[128,896]{1,0:T(8,128)(2,1)S(1)}, u32[]{:S(2)}, u32[]{:S(2)}) collective-permute-start(bf16[128,896]{1,0:T(8,128)(2,1)S(1)} %get-tuple-element.184), channel_id=1, source_target_pairs={{0,2},{1,3},{2,4},{3,5},{4,6},{5,7},{6,0},{7,1},{8,10},{9,11},{10,... | collective-permute-start | bytes 688136 | tf_op jit(solution)/shard_map/ppermute | solution.py:301
  53.4 14.4 %collective-permute-start.7 = (bf16[128,896]{1,0:T(8,128)(2,1)S(1)}, bf16[128,896]{1,0:T(8,128)(2,1)S(1)}, u32[]{:S(2)}, u32[]{:S(2)}) collective-permute-start(bf16[128,896]{1,0:T(8,128)(2,1)S(1)} %get-tuple-element.182), channel_id=1, source_target_pairs={{0,6},{1,7},{2,0},{3,1},{4,2},{5,3},{6,4},{7,5},{8,14},{9,15},{10,... | collective-permute-start | bytes 688136 | tf_op jit(solution)/shard_map/ppermute | solution.py:301
  56.3 14.2 %collective-permute-start.11 = (bf16[64,1024]{1,0:T(8,128)(2,1)S(1)}, bf16[64,1024]{1,0:T(8,128)(2,1)S(1)}, u32[]{:S(2)}, u32[]{:S(2)}) collective-permute-start(bf16[64,1024]{1,0:T(8,128)(2,1)S(1)} %copy-done.8), channel_id=1, source_target_pairs={{8,1},{16,9},{24,17},{32,25},{40,33},{48,41},{56,49},{64,57},{72,6... | collective-permute-start | bytes 393224 | tf_op jit(solution)/shard_map/ppermute | solution.py:318
  57.6 12.9 %copy-start.6 = (bf16[4,64,1024]{2,1,0:T(8,128)(2,1)S(1)}, bf16[4,64,1024]{2,1,0:T(8,128)(2,1)}, u32[]{:S(2)}) copy-start(bf16[4,64,1024]{2,1,0:T(8,128)(2,1)} %get-tuple-element.137.refs_18_) | copy-start | bytes 1572868
  60.0 10.5 %copy-start.2 = (bf16[512,4096]{1,0:T(8,128)(2,1)S(1)}, bf16[512,4096]{1,0:T(8,128)(2,1)}, u32[]{:S(2)}) copy-start(bf16[512,4096]{1,0:T(8,128)(2,1)} %refs_20_.1) | copy-start | bytes 12582916
  67.8 8.7 %collective-permute-start.12 = (bf16[128,896]{1,0:T(8,128)(2,1)S(1)}, bf16[128,896]{1,0:T(8,128)(2,1)S(1)}, u32[]{:S(2)}, u32[]{:S(2)}) collective-permute-start(bf16[128,896]{1,0:T(8,128)(2,1)S(1)} %get-tuple-element.147), channel_id=1, source_target_pairs={{0,2},{1,3},{2,4},{3,5},{4,6},{5,7},{6,0},{7,1},{8,10},{9,11},{10,... | collective-permute-start | bytes 688136 | tf_op jit(solution)/shard_map/ppermute | solution.py:301
  69.0 7.6 %collective-permute-start.13 = (bf16[128,896]{1,0:T(8,128)(2,1)S(1)}, bf16[128,896]{1,0:T(8,128)(2,1)S(1)}, u32[]{:S(2)}, u32[]{:S(2)}) collective-permute-start(bf16[128,896]{1,0:T(8,128)(2,1)S(1)} %get-tuple-element.148), channel_id=1, source_target_pairs={{0,6},{1,7},{2,0},{3,1},{4,2},{5,3},{6,4},{7,5},{8,14},{9,15},{10,... | collective-permute-start | bytes 688136 | tf_op jit(solution)/shard_map/ppermute | solution.py:301
  70.5 8.8 %copy-start.5 = (bf16[4,64,1024]{2,1,0:T(8,128)(2,1)S(1)}, bf16[4,64,1024]{2,1,0:T(8,128)(2,1)}, u32[]{:S(2)}) copy-start(bf16[4,64,1024]{2,1,0:T(8,128)(2,1)} %get-tuple-element.155.refs_18_) | copy-start | bytes 1572868
  76.5 13.5 %collective-permute-start.14 = (bf16[64,4096]{1,0:T(8,128)(2,1)S(1)}, bf16[64,4096]{1,0:T(8,128)(2,1)S(1)}, u32[]{:S(2)}, u32[]{:S(2)}) collective-permute-start(bf16[64,4096]{1,0:T(8,128)(2,1)S(1)} %get-tuple-element.150), channel_id=1, source_target_pairs={{0,2},{2,4},{4,6},{6,0},{1,3},{3,5},{5,7},{7,1},{8,10},{10,12},{12... | collective-permute-start | bytes 1572872 | tf_op jit(solution)/shard_map/ppermute | solution.py:27
  76.6 13.4 %collective-permute-start.15 = (bf16[64,4096]{1,0:T(8,128)(2,1)S(1)}, bf16[64,4096]{1,0:T(8,128)(2,1)S(1)}, u32[]{:S(2)}, u32[]{:S(2)}) collective-permute-start(bf16[64,4096]{1,0:T(8,128)(2,1)S(1)} %get-tuple-element.151), channel_id=1, source_target_pairs={{0,6},{2,0},{4,2},{6,4},{1,7},{3,1},{5,3},{7,5},{8,14},{10,8},{12,... | collective-permute-start | bytes 1572872 | tf_op jit(solution)/shard_map/ppermute | solution.py:27
  79.3 2.2 %copy-start.4 = (bf16[512,4096]{1,0:T(8,128)(2,1)S(1)}, bf16[512,4096]{1,0:T(8,128)(2,1)}, u32[]{:S(2)}) copy-start(bf16[512,4096]{1,0:T(8,128)(2,1)} %copy-done.3) | copy-start | bytes 12582916
  90.1 7.8 %collective-permute-start.17 = (bf16[64,2048]{1,0:T(8,128)(2,1)S(1)}, bf16[64,2048]{1,0:T(8,128)(2,1)S(1)}, u32[]{:S(2)}, u32[]{:S(2)}) collective-permute-start(bf16[64,2048]{1,0:T(8,128)(2,1)S(1)} %get-tuple-element.170), channel_id=1, source_target_pairs={{0,6},{2,0},{4,2},{6,4},{1,7},{3,1},{5,3},{7,5},{8,14},{10,8},{12,... | collective-permute-start | bytes 786440 | tf_op jit(solution)/shard_map/ppermute | solution.py:27
  92.6 6.4 %collective-permute-start.16 = (bf16[64,2048]{1,0:T(8,128)(2,1)S(1)}, bf16[64,2048]{1,0:T(8,128)(2,1)S(1)}, u32[]{:S(2)}, u32[]{:S(2)}) collective-permute-start(bf16[64,2048]{1,0:T(8,128)(2,1)S(1)} %get-tuple-element.168), channel_id=1, source_target_pairs={{0,2},{2,4},{4,6},{6,0},{1,3},{3,5},{5,7},{7,1},{8,10},{10,12},{12... | collective-permute-start | bytes 786440 | tf_op jit(solution)/shard_map/ppermute | solution.py:27
  92.6 15.4 %collective-permute-start.21 = (bf16[64,2048]{1,0:T(8,128)(2,1)S(1)}, bf16[64,2048]{1,0:T(8,128)(2,1)S(1)}, u32[]{:S(2)}, u32[]{:S(2)}) collective-permute-start(bf16[64,2048]{1,0:T(8,128)(2,1)S(1)} %get-tuple-element.176), channel_id=1, source_target_pairs={{0,6},{2,0},{4,2},{6,4},{1,7},{3,1},{5,3},{7,5},{8,14},{10,8},{12,... | collective-permute-start | bytes 786440 | tf_op jit(solution)/shard_map/ppermute | solution.py:27
  95.3 12.8 %collective-permute-start.20 = (bf16[64,2048]{1,0:T(8,128)(2,1)S(1)}, bf16[64,2048]{1,0:T(8,128)(2,1)S(1)}, u32[]{:S(2)}, u32[]{:S(2)}) collective-permute-start(bf16[64,2048]{1,0:T(8,128)(2,1)S(1)} %get-tuple-element.174), channel_id=1, source_target_pairs={{0,2},{2,4},{4,6},{6,0},{1,3},{3,5},{5,7},{7,1},{8,10},{10,12},{12... | collective-permute-start | bytes 786440 | tf_op jit(solution)/shard_map/ppermute | solution.py:27
  95.3 15.6 %collective-permute-start.19 = (bf16[64,2048]{1,0:T(8,128)(2,1)S(1)}, bf16[64,2048]{1,0:T(8,128)(2,1)S(1)}, u32[]{:S(2)}, u32[]{:S(2)}) collective-permute-start(bf16[64,2048]{1,0:T(8,128)(2,1)S(1)} %get-tuple-element.172), channel_id=1, source_target_pairs={{0,6},{2,0},{4,2},{6,4},{1,7},{3,1},{5,3},{7,5},{8,14},{10,8},{12,... | collective-permute-start | bytes 786440 | tf_op jit(solution)/shard_map/ppermute | solution.py:27
  98.0 19.0 %collective-permute-start.23 = (bf16[64,2048]{1,0:T(8,128)(2,1)S(1)}, bf16[64,2048]{1,0:T(8,128)(2,1)S(1)}, u32[]{:S(2)}, u32[]{:S(2)}) collective-permute-start(bf16[64,2048]{1,0:T(8,128)(2,1)S(1)} %get-tuple-element.179), channel_id=1, source_target_pairs={{0,2},{2,4},{4,6},{6,0},{1,3},{3,5},{5,7},{7,1},{8,10},{10,12},{12... | collective-permute-start | bytes 786440 | tf_op jit(solution)/shard_map/ppermute | solution.py:27
  99.2 17.9 %collective-permute-start.18 = (bf16[64,4096]{1,0:T(8,128)(2,1)S(1)}, bf16[64,4096]{1,0:T(8,128)(2,1)S(1)}, u32[]{:S(2)}, u32[]{:S(2)}) collective-permute-start(bf16[64,4096]{1,0:T(8,128)(2,1)S(1)} %pad_maximum_fusion.1), channel_id=1, source_target_pairs={{0,1},{1,8},{2,3},{3,2},{4,5},{5,4},{6,7},{7,6},{8,9},{9,16},{10,1... | collective-permute-start | bytes 1572872 | tf_op jit(solution)/shard_map/ppermute | solution.py:344
  108.2 8.7 %collective-permute-start.22 = (bf16[64,2048]{1,0:T(8,128)(2,1)S(1)}, bf16[64,2048]{1,0:T(8,128)(2,1)S(1)}, u32[]{:S(2)}, u32[]{:S(2)}) collective-permute-start(bf16[64,2048]{1,0:T(8,128)(2,1)S(1)} %add_convert_fusion.3), channel_id=1, source_target_pairs={{0,2},{2,4},{4,6},{6,0},{1,3},{3,5},{5,7},{7,1},{8,10},{10,12},{12... | collective-permute-start | bytes 786440 | tf_op jit(solution)/shard_map/ppermute | solution.py:27
  108.2 8.7 %collective-permute-start.24 = (bf16[64,2048]{1,0:T(8,128)(2,1)S(1)}, bf16[64,2048]{1,0:T(8,128)(2,1)S(1)}, u32[]{:S(2)}, u32[]{:S(2)}) collective-permute-start(bf16[64,2048]{1,0:T(8,128)(2,1)S(1)} %add_convert_fusion.2), channel_id=1, source_target_pairs={{0,6},{2,0},{4,2},{6,4},{1,7},{3,1},{5,3},{7,5},{8,14},{10,8},{12,... | collective-permute-start | bytes 786440 | tf_op jit(solution)/shard_map/ppermute | solution.py:27

commit v9 on v8

--- a/solution.py
+++ b/solution.py
@@ -249,6 +249,29 @@
     )(places, *operands)
 
 
+def assemble_kernel(head_ref, first_ref, *refs):
+    out_ref, side = refs[-1], refs[0].shape[1]
+    rows = lax.broadcasted_iota(jnp.int32, (BLOCK, side), 0)
+    for i in range(2):
+        place = slice(i * side, (i + 1) * side)
+        total = refs[i][...].astype(F32) + refs[2 + i][...].astype(F32) + refs[4 + i][...].astype(F32)
+        both = jnp.concatenate([head_ref[:, place].astype(F32), total], axis=0)
+        rolled = pltpu.roll(both, BLOCK - 1, 0)
+        out_ref[:, place] = jnp.where(rows == BLOCK - 1, first_ref[:1, place].astype(F32), rolled).astype(BF16)
+
+
+def assemble(head, first, here, direct, summed):
+    vmem = pl.BlockSpec(memory_space=pltpu.VMEM)
+    return pl.pallas_call(
+        assemble_kernel,
+        in_specs=[vmem] * 8,
+        out_specs=vmem,
+        out_shape=jax.ShapeDtypeStruct((BLOCK, head.shape[1]), BF16),
+        cost_estimate=cost(1e8),
+        compiler_params=pltpu.CompilerParams(vmem_limit_bytes=24 * 1024 * 1024),
+    )(head, first, *here, *direct, *summed)
+
+
 def body(decoder, w_query, w_key, w_value, w_out, database, nb_shard, nb_slot):
     n_seq = lax.axis_size("seq")
     seq_index, z_index, core = lax.axis_index("seq"), lax.axis_index("z"), lax.axis_index("core")
@@ -344,8 +367,7 @@
     head = lax.ppermute(out_a, ("seq", "z", "core"), pairs)
     above_b, below_b = lax.optimization_barrier((add(sums_b[2], up_b), add(sums_b[5], down_b)))
     up_left_b, down_right_b = step(above_b, "z", 1), step(below_b, "z", -1)
-    out_b = total(*sums_b[6:], down_left_b, up_right_b, up_left_b, down_right_b)
-    return jnp.concatenate([head[1:], out_b, out_a[:1]], axis=0)
+    return assemble(head, out_a, sums_b[6:], (down_left_b, up_right_b), (up_left_b, down_right_b))
 
 
 def solution(mesh):

time: 120 us -> 122 us (1.017); the launches traced: 118 us -> 122 us
  waiting for transfers between devices: 25.1 us -> 30.8 us
  starting transfers between devices: 48.2 us -> 45.8 us
  Pallas kernels: 37.3 us -> 38.9 us
  other arithmetic: 3.29 us -> 1.93 us
    ppermute x14, waiting for transfers between devices: 9.4 us -> 15.1 us  [step(): lax.ppermute(value, axis, [(i, (i + steps) % count) for i in range(count)])]
    ppermute x14, starting transfers between devices: 15.7 us -> 14 us  [step(): lax.ppermute(value, axis, [(i, (i + steps) % count) for i in range(count)])]
    pallas_call x0 -> x1, Pallas kernels: none -> 1.38 us  [assemble(): pl.pallas_call(assemble_kernel, in_specs=[vmem] * 8, out_specs=vmem, out_...]
  transfers between devices with their start and end apart: 26 -> 26, of which waited for: 8 -> 9; matrix products, arithmetic and copies ran while one was open for 3% -> 3% of each run, Pallas kernels for 30% -> 29%
where the time goes in v9:
time: 122 us
  starting transfers between devices  45.8 us (38%)
  Pallas kernels  38.9 us (32%)
  waiting for transfers between devices  30.8 us (25%)
  local copies, waits for them, and re-layouts  3.86 us (3%)
  other arithmetic  1.93 us (2%)
    ppermute x9, starting transfers between devices, hop(): return lax.ppermute(value, ('z', 'core'), pairs)  15.4 us
    ppermute x14, waiting for transfers between devices, step(): lax.ppermute(value, axis, [(i, (i + steps) % count) for i in range(count)])  15.1 us
    ppermute x14, starting transfers between devices, step(): lax.ppermute(value, axis, [(i, (i + steps) % count) for i in range(count)])  14 us
    pallas_call x1, Pallas kernels, project_queries(): pl.pallas_call(query_kernel, grid_spec=pltpu.PrefetchScalarGridSpec(num_s...  12 us
    pallas_call x2, Pallas kernels, attend(): pl.pallas_call(functools.partial(span_kernel, group), grid_spec=pltpu.Pre...  12 us
    ppermute x9, waiting for transfers between devices, hop(): return lax.ppermute(value, ('z', 'core'), pairs)  10.5 us
    pallas_call x3, Pallas kernels, project(): pl.pallas_call(functools.partial(project_kernel, len(carried)), in_specs=...  8.38 us
    ppermute x1, starting transfers between devices, body(): head = lax.ppermute(out_a, ('seq', 'z', 'core'), pairs)  8.24 us
  transfers between devices with their start and end apart: 26, of which 9 were waited for; matrix products, arithmetic and copies ran while one was open for 3% of the time, Pallas kernels for 29%

profile of v9, /device:TPU:1, one launch (start us, length us, event | category | flops | bytes accessed | tf_op | source)
XLA Modules:
  0.0 121.6 jit_solution(10688454161980775595)
XLA Ops:
  0.0 1.4 %collective-permute-start.3 = (bf16[4096,512]{1,0:T(8,128)(2,1)}, bf16[4096,512]{1,0:T(8,128)(2,1)}, u32[]{:S(2)}, u32[]{:S(2)}) collective-permute-start(bf16[4096,512]{1,0:T(8,128)(2,1)} %wa_hbm.1), channel_id=1, source_target_pairs={{0,1},{1,0},{2,3},{3,2},{4,5},{5,4},{6,7},{7,6},{8,9},{9,8},{10,11... | collective-permute-start | bytes 12582920 | tf_op jit(solution)/shard_map/ppermute | solution.py:27
  1.4 0.7 shift-right-arithmetic_bitcast_fusion
  2.5 0.5 convert_reduce_fusion
  3.0 0.1 select_reduce_fusion
  3.2 0.6 reshape.76.index_ref
  3.8 3.1 %shard_map.91 = bf16[48,16,896]{2,1,0:T(8,128)(2,1)} custom-call(s32[48]{0:T(128)} %reshape.76.index_ref, s32[1]{0:T(128)} %bitcast.4.start_ref, bf16[24,128,896]{2,1,0:T(8,128)(2,1)} %source_ref.1), custom_call_target="tpu_custom_call" | custom-call | flops 400000000 | bytes 400000 | tf_op jit(solution)/shard_map/pallas_call | solution.py:61
  6.9 6.9 %all-to-all-start = ((bf16[16,3,16,896]{3,2,1,0:T(8,128)(2,1)}), bf16[16,3,16,896]{3,2,1,0:T(8,128)(2,1)}, u32[]{:S(2)}, u32[]{:S(2)}) async-start(bf16[16,3,16,896]{3,2,1,0:T(8,128)(2,1)} %bitcast.28), calls=%async_computation | async-start | bytes 2752512 | tf_op jit(solution)/shard_map/all_to_all | solution.py:293
  13.8 0.9 collective-permute-start
  14.7 0.1 collective-permute-start.1
  14.9 0.1 rev.6
  15.0 0.1 rev.7
  15.2 0.1 copy.18
  15.5 12.0 %shard_map.92 = (bf16[4,64,1024]{2,1,0:T(8,128)(2,1)}, bf16[4,64,1024]{2,1,0:T(8,128)(2,1)}, bf16[64,1024]{1,0:T(8,128)(2,1)}) custom-call(s32[1]{0:T(128)} %bitcast.7.core_ref, bf16[8,128,4096]{2,1,0:T(8,128)(2,1)} %bitcast.27, bf16[4096,512]{1,0:T(8,128)(2,1)} %wa_hbm.1, bf16[4096,512]{1,0:T(8,128)(2,1)} %collective-permute-done.3.wb_hbm), custom_call_target="tpu_custom_call" | custom-call | flops 1200000000 | bytes 1200000 | tf_op jit(solution)/shard_map/pallas_call | solution.py:112
  27.6 5.2 %all-to-all-done = bf16[16,3,16,896]{3,2,1,0:T(8,128)(2,1)} async-done(((bf16[16,3,16,896]{3,2,1,0:T(8,128)(2,1)}), bf16[16,3,16,896]{3,2,1,0:T(8,128)(2,1)}, u32[]{:S(2)}, u32[]{:S(2)}) %all-to-all-start) | async-done | bytes 1376288 | tf_op jit(solution)/shard_map/all_to_all | solution.py:293
  32.8 2.0 %shard_map.93 = (bf16[16,16,896]{2,1,0:T(8,128)(2,1)S(1)}, bf16[16,16,896]{2,1,0:T(8,128)(2,1)S(1)}) custom-call(s32[32]{0:T(128)S(1)} %reshape.82.index_ref, s32[1]{0:T(128)} %constant.53.clone.1.start_ref, bf16[48,16,896]{2,1,0:T(8,128)(2,1)} %bitcast.6.source_ref), custom_call_target="tpu_custom_call" | custom-call | flops 400000000 | bytes 400000 | tf_op jit(solution)/shard_map/pallas_call | solution.py:61
  34.8 3.7 %collective-permute-start.8 = (bf16[256,896]{1,0:T(8,128)(2,1)S(1)}, bf16[256,896]{1,0:T(8,128)(2,1)S(1)}, u32[]{:S(2)}, u32[]{:S(2)}) collective-permute-start(bf16[256,896]{1,0:T(8,128)(2,1)S(1)} %bitcast.24), channel_id=1, source_target_pairs={{0,1},{1,0},{2,3},{3,2},{4,5},{5,4},{6,7},{7,6},{8,9},{9,8},{10,11... | collective-permute-start | bytes 1376264 | tf_op jit(solution)/shard_map/ppermute | solution.py:324
  38.4 1.7 %collective-permute-start.4 = (bf16[256,896]{1,0:T(8,128)(2,1)S(1)}, bf16[256,896]{1,0:T(8,128)(2,1)S(1)}, u32[]{:S(2)}, u32[]{:S(2)}) collective-permute-start(bf16[256,896]{1,0:T(8,128)(2,1)S(1)} %bitcast.21), channel_id=1, source_target_pairs={{0,2},{1,3},{2,4},{3,5},{4,6},{5,7},{6,0},{7,1},{8,10},{9,11},{10,... | collective-permute-start | bytes 1376264 | tf_op jit(solution)/shard_map/ppermute | solution.py:324
  40.1 2.2 %collective-permute-start.6 = (bf16[256,896]{1,0:T(8,128)(2,1)S(1)}, bf16[256,896]{1,0:T(8,128)(2,1)S(1)}, u32[]{:S(2)}, u32[]{:S(2)}) collective-permute-start(bf16[256,896]{1,0:T(8,128)(2,1)S(1)} %bitcast.25), channel_id=1, source_target_pairs={{0,7},{1,6},{2,1},{3,0},{4,3},{5,2},{6,5},{7,4},{8,15},{9,14},{10,... | collective-permute-start | bytes 1376264 | tf_op jit(solution)/shard_map/ppermute | solution.py:324
  42.3 3.7 %shard_map.94 = (bf16[2,2,4,32,512]{4,3,2,1,0:T(8,128)(2,1)S(1)}, bf16[2,2,4,32,512]{4,3,2,1,0:T(8,128)(2,1)S(1)}, bf16[2,2,4,32,512]{4,3,2,1,0:T(8,128)(2,1)S(1...) custom-call(bf16[256,896]{1,0:T(8,128)(2,1)S(1)} %bitcast.22, ...), custom_call_target="tpu_custom_call" | custom-call | flops 800000000 | bytes 800000 | tf_op jit(solution)/shard_map/pallas_call | solution.py:150
  46.0 1.7 %collective-permute-start.10 = (bf16[256,896]{1,0:T(8,128)(2,1)S(1)}, bf16[256,896]{1,0:T(8,128)(2,1)S(1)}, u32[]{:S(2)}, u32[]{:S(2)}) collective-permute-start(bf16[256,896]{1,0:T(8,128)(2,1)S(1)} %bitcast.23), channel_id=1, source_target_pairs={{0,6},{1,7},{2,0},{3,1},{4,2},{5,3},{6,4},{7,5},{8,14},{9,15},{10,... | collective-permute-start | bytes 1376264 | tf_op jit(solution)/shard_map/ppermute | solution.py:324
  47.7 0.3 collective-permute-start.9
  48.0 5.0 %collective-permute-done.4.refs_0_ = bf16[256,896]{1,0:T(8,128)(2,1)S(1)} collective-permute-done((bf16[256,896]{1,0:T(8,128)(2,1)S(1)}, bf16[256,896]{1,0:T(8,128)(2,1)S(1)}, u32[]{:S(2)}, u32[]{:S(2)}) %collective-permute-start.4) | collective-permute-done | bytes 458784 | tf_op jit(solution)/shard_map/ppermute | solution.py:324
  53.0 0.3 collective-permute-start.5
  53.4 2.9 %collective-permute-start.7 = (bf16[128,896]{1,0:T(8,128)(2,1)S(1)}, bf16[128,896]{1,0:T(8,128)(2,1)S(1)}, u32[]{:S(2)}, u32[]{:S(2)}) collective-permute-start(bf16[128,896]{1,0:T(8,128)(2,1)S(1)} %get-tuple-element.182), channel_id=1, source_target_pairs={{0,6},{1,7},{2,0},{3,1},{4,2},{5,3},{6,4},{7,5},{8,14},{9,15},{10,... | collective-permute-start | bytes 688136 | tf_op jit(solution)/shard_map/ppermute | solution.py:324
  56.3 1.3 %collective-permute-start.11 = (bf16[64,1024]{1,0:T(8,128)(2,1)S(1)}, bf16[64,1024]{1,0:T(8,128)(2,1)S(1)}, u32[]{:S(2)}, u32[]{:S(2)}) collective-permute-start(bf16[64,1024]{1,0:T(8,128)(2,1)S(1)} %copy-done.8), channel_id=1, source_target_pairs={{8,1},{16,9},{24,17},{32,25},{40,33},{48,41},{56,49},{64,57},{72,6... | collective-permute-start | bytes 393224 | tf_op jit(solution)/shard_map/ppermute | solution.py:341
  57.6 2.3 %shard_map.95 = (bf16[2,2,4,32,512]{4,3,2,1,0:T(8,128)(2,1)S(1)}, bf16[2,2,4,32,512]{4,3,2,1,0:T(8,128)(2,1)S(1)}, bf16[2,2,4,32,512]{4,3,2,1,0:T(8,128)(2,1)S(1)}, bf16[2,2,4,32,512]{4,3,2,1,0:T(8,128)(2,1)S(1)}) custom-call(bf16[256,896]{1,0:T(8,128)(2,1)S(1)} %collective-permute-done.4.refs_0_, bf16[256,896]{1,0:T(8,128)(2,1)S(1)} %collective-permute-done.6.refs_1_, ...), custom_call_target="tpu_custom_call" | custom-call | flops 800000000 | bytes 800000 | tf_op jit(solution)/shard_map/pallas_call | solution.py:150
  59.9 2.4 %collective-permute-done.10.refs_1_ = bf16[256,896]{1,0:T(8,128)(2,1)S(1)} collective-permute-done((bf16[256,896]{1,0:T(8,128)(2,1)S(1)}, bf16[256,896]{1,0:T(8,128)(2,1)S(1)}, u32[]{:S(2)}, u32[]{:S(2)}) %collective-permute-start.10) | collective-permute-done | bytes 458784 | tf_op jit(solution)/shard_map/ppermute | solution.py:324
  62.3 0.8 collective-permute-done.9.refs_0_
  63.1 2.3 %shard_map.96 = (bf16[2,2,4,32,512]{4,3,2,1,0:T(8,128)(2,1)S(1)}, bf16[2,2,4,32,512]{4,3,2,1,0:T(8,128)(2,1)S(1)}, bf16[2,2,4,32,512]{4,3,2,1,0:T(8,128)(2,1)S(1)}, bf16[2,2,4,32,512]{4,3,2,1,0:T(8,128)(2,1)S(1)}) custom-call(bf16[256,896]{1,0:T(8,128)(2,1)S(1)} %collective-permute-done.9.refs_0_, bf16[256,896]{1,0:T(8,128)(2,1)S(1)} %collective-permute-done.10.refs_1_, ...), custom_call_target="tpu_custom_call" | custom-call | flops 800000000 | bytes 800000 | tf_op jit(solution)/shard_map/pallas_call | solution.py:150
  65.4 2.3 %collective-permute-done.5.refs_12_ = bf16[128,896]{1,0:T(8,128)(2,1)S(1)} collective-permute-done((bf16[128,896]{1,0:T(8,128)(2,1)S(1)}, bf16[128,896]{1,0:T(8,128)(2,1)S(1)}, u32[]{:S(2)}, u32[]{:S(2)}) %collective-permute-start.5) | collective-permute-done | bytes 229408 | tf_op jit(solution)/shard_map/ppermute | solution.py:324
  67.8 1.2 collective-permute-start.12
  68.9 1.5 %collective-permute-start.13 = (bf16[128,896]{1,0:T(8,128)(2,1)S(1)}, bf16[128,896]{1,0:T(8,128)(2,1)S(1)}, u32[]{:S(2)}, u32[]{:S(2)}) collective-permute-start(bf16[128,896]{1,0:T(8,128)(2,1)S(1)} %get-tuple-element.148), channel_id=1, source_target_pairs={{0,6},{1,7},{2,0},{3,1},{4,2},{5,3},{6,4},{7,5},{8,14},{9,15},{10,... | collective-permute-start | bytes 688136 | tf_op jit(solution)/shard_map/ppermute | solution.py:324
  70.5 6.0 %shard_map.97 = (bf16[64,4096]{1,0:T(8,128)(2,1)S(1)}, bf16[64,4096]{1,0:T(8,128)(2,1)S(1)}, bf16[64,2048]{1,0:T(8,128)(2,1)S(1)}, bf16[64,2048]{1,0:T(8,128)(2,...) custom-call(s32[9]{0:T(128)S(1)} %pad_add_fusion.place_ref, ...), custom_call_target="tpu_custom_call" | custom-call | flops 2000000000 | bytes 2000000 | tf_op jit(solution)/shard_map/pallas_call | solution.py:237
  76.6 2.7 %collective-permute-start.15 = (bf16[64,4096]{1,0:T(8,128)(2,1)S(1)}, bf16[64,4096]{1,0:T(8,128)(2,1)S(1)}, u32[]{:S(2)}, u32[]{:S(2)}) collective-permute-start(bf16[64,4096]{1,0:T(8,128)(2,1)S(1)} %get-tuple-element.151), channel_id=1, source_target_pairs={{0,6},{2,0},{4,2},{6,4},{1,7},{3,1},{5,3},{7,5},{8,14},{10,8},{12,... | collective-permute-start | bytes 1572872 | tf_op jit(solution)/shard_map/ppermute | solution.py:27
  79.3 2.2 %copy-done.4 = bf16[512,4096]{1,0:T(8,128)(2,1)S(1)} copy-done((bf16[512,4096]{1,0:T(8,128)(2,1)S(1)}, bf16[512,4096]{1,0:T(8,128)(2,1)}, u32[]{:S(2)}) %copy-start.4) | copy-done | bytes 4194328
  81.4 6.0 %shard_map.98 = (bf16[64,2048]{1,0:T(8,128)(2,1)S(1)}, bf16[64,2048]{1,0:T(8,128)(2,1)S(1)}, bf16[64,2048]{1,0:T(8,128)(2,1)S(1)}, bf16[64,2048]{1,0:T(8,128)(2,...) custom-call(s32[4]{0:T(128)S(1)} %get-tuple-element.152.place_ref, ...), custom_call_target="tpu_custom_call" | custom-call | flops 2000000000 | bytes 2000000 | tf_op jit(solution)/shard_map/pallas_call | solution.py:237
  87.5 2.5 %collective-permute-done.14 = bf16[64,4096]{1,0:T(8,128)(2,1)S(1)} collective-permute-done((bf16[64,4096]{1,0:T(8,128)(2,1)S(1)}, bf16[64,4096]{1,0:T(8,128)(2,1)S(1)}, u32[]{:S(2)}, u32[]{:S(2)}) %collective-permute-start.14) | collective-permute-done | bytes 524320 | tf_op jit(solution)/shard_map/ppermute | solution.py:27
  90.0 0.1 add_convert_fusion.4
  90.2 2.7 %collective-permute-start.22 = (bf16[64,2048]{1,0:T(8,128)(2,1)S(1)}, bf16[64,2048]{1,0:T(8,128)(2,1)S(1)}, u32[]{:S(2)}, u32[]{:S(2)}) collective-permute-start(bf16[64,2048]{1,0:T(8,128)(2,1)S(1)} %get-tuple-element.178), channel_id=1, source_target_pairs={{0,6},{2,0},{4,2},{6,4},{1,7},{3,1},{5,3},{7,5},{8,14},{10,8},{12,... | collective-permute-start | bytes 786440 | tf_op jit(solution)/shard_map/ppermute | solution.py:27
  92.9 2.7 %collective-permute-start.17 = (bf16[64,2048]{1,0:T(8,128)(2,1)S(1)}, bf16[64,2048]{1,0:T(8,128)(2,1)S(1)}, u32[]{:S(2)}, u32[]{:S(2)}) collective-permute-start(bf16[64,2048]{1,0:T(8,128)(2,1)S(1)} %get-tuple-element.170), channel_id=1, source_target_pairs={{0,6},{2,0},{4,2},{6,4},{1,7},{3,1},{5,3},{7,5},{8,14},{10,8},{12,... | collective-permute-start | bytes 786440 | tf_op jit(solution)/shard_map/ppermute | solution.py:27
  95.6 1.5 %collective-permute-done.16 = bf16[64,2048]{1,0:T(8,128)(2,1)S(1)} collective-permute-done((bf16[64,2048]{1,0:T(8,128)(2,1)S(1)}, bf16[64,2048]{1,0:T(8,128)(2,1)S(1)}, u32[]{:S(2)}, u32[]{:S(2)}) %collective-permute-start.16) | collective-permute-done | bytes 262176 | tf_op jit(solution)/shard_map/ppermute | solution.py:27
  97.0 0.1 add_convert_fusion.3
  97.1 4.5 %collective-permute-done.17 = bf16[64,2048]{1,0:T(8,128)(2,1)S(1)} collective-permute-done((bf16[64,2048]{1,0:T(8,128)(2,1)S(1)}, bf16[64,2048]{1,0:T(8,128)(2,1)S(1)}, u32[]{:S(2)}, u32[]{:S(2)}) %collective-permute-start.17) | collective-permute-done | bytes 262176 | tf_op jit(solution)/shard_map/ppermute | solution.py:27
  101.8 8.2 %collective-permute-start.18 = (bf16[64,4096]{1,0:T(8,128)(2,1)S(1)}, bf16[64,4096]{1,0:T(8,128)(2,1)S(1)}, u32[]{:S(2)}, u32[]{:S(2)}) collective-permute-start(bf16[64,4096]{1,0:T(8,128)(2,1)S(1)} %pad_maximum_fusion.first_ref), channel_id=1, source_target_pairs={{0,1},{1,8},{2,3},{3,2},{4,5},{5,4},{6,7},{7,6},{8,9},{9,16},{10,1... | collective-permute-start | bytes 1572872 | tf_op jit(solution)/shard_map/ppermute | solution.py:367
  110.2 1.2 %collective-permute-start.23 = (bf16[64,2048]{1,0:T(8,128)(2,1)S(1)}, bf16[64,2048]{1,0:T(8,128)(2,1)S(1)}, u32[]{:S(2)}, u32[]{:S(2)}) collective-permute-start(bf16[64,2048]{1,0:T(8,128)(2,1)S(1)} %add_convert_fusion.1), channel_id=1, source_target_pairs={{0,2},{2,4},{4,6},{6,0},{1,3},{3,5},{5,7},{7,1},{8,10},{10,12},{12... | collective-permute-start | bytes 786440 | tf_op jit(solution)/shard_map/ppermute | solution.py:27
  111.4 2.2 %collective-permute-start.24 = (bf16[64,2048]{1,0:T(8,128)(2,1)S(1)}, bf16[64,2048]{1,0:T(8,128)(2,1)S(1)}, u32[]{:S(2)}, u32[]{:S(2)}) collective-permute-start(bf16[64,2048]{1,0:T(8,128)(2,1)S(1)} %add_convert_fusion), channel_id=1, source_target_pairs={{0,6},{2,0},{4,2},{6,4},{1,7},{3,1},{5,3},{7,5},{8,14},{10,8},{12,... | collective-permute-start | bytes 786440 | tf_op jit(solution)/shard_map/ppermute | solution.py:27
  113.6 6.6 %collective-permute-done.23.refs_4_ = bf16[64,2048]{1,0:T(8,128)(2,1)S(1)} collective-permute-done((bf16[64,2048]{1,0:T(8,128)(2,1)S(1)}, bf16[64,2048]{1,0:T(8,128)(2,1)S(1)}, u32[]{:S(2)}, u32[]{:S(2)}) %collective-permute-start.23) | collective-permute-done | bytes 262176 | tf_op jit(solution)/shard_map/ppermute | solution.py:27
  120.2 1.4 %shard_map.99 = bf16[128,4096]{1,0:T(8,128)(2,1)} custom-call(bf16[64,4096]{1,0:T(8,128)(2,1)S(1)} %collective-permute-done.18.head_ref, bf16[64,4096]{1,0:T(8,128)(2,1)S(1)} %pad_maximum_fusion.first_ref, bf16[64,2048]{1,0:T(8,128)(2,1)S(1)} %get-tuple-element.171.refs_0_, bf16[64,2048]{1,0:T(8,128)(2,1)S(1)} %get-tuple-element.172.refs_1_, ...), custom_call_target="tpu_custom_call" | custom-call | flops 40000000 | bytes 40000 | tf_op jit(solution)/shard_map/pallas_call | solution.py:265
  (61 shorter events, 1.4 us)
Async XLA Ops:
  0.0 15.5 %collective-permute-start.3 = (bf16[4096,512]{1,0:T(8,128)(2,1)}, bf16[4096,512]{1,0:T(8,128)(2,1)}, u32[]{:S(2)}, u32[]{:S(2)}) collective-permute-start(bf16[4096,512]{1,0:T(8,128)(2,1)} %wa_hbm.1), channel_id=1, source_target_pairs={{0,1},{1,0},{2,3},{3,2},{4,5},{5,4},{6,7},{7,6},{8,9},{9,8},{10,11... | collective-permute-start | bytes 12582920 | tf_op jit(solution)/shard_map/ppermute | solution.py:27
  1.4 31.4 %collective-permute-start.2 = (bf16[512,4096]{1,0:T(8,128)(2,1)}, bf16[512,4096]{1,0:T(8,128)(2,1)}, u32[]{:S(2)}, u32[]{:S(2)}) collective-permute-start(bf16[512,4096]{1,0:T(8,128)(2,1)} %refs_20_.1), channel_id=1, source_target_pairs={{0,1},{1,0},{2,3},{3,2},{4,5},{5,4},{6,7},{7,6},{8,9},{9,8},{10,11... | collective-permute-start | bytes 12582920 | tf_op jit(solution)/shard_map/ppermute | solution.py:27
  3.8 10.0 %copy-start = (bf16[896,512]{1,0:T(8,128)(2,1)S(1)}, bf16[896,512]{1,0:T(8,128)(2,1)}, u32[]{:S(2)}) copy-start(bf16[896,512]{1,0:T(8,128)(2,1)} %refs_14_.1) | copy-start | bytes 2752516
  3.8 10.9 %copy-start.1 = (bf16[896,512]{1,0:T(8,128)(2,1)S(1)}, bf16[896,512]{1,0:T(8,128)(2,1)}, u32[]{:S(2)}) copy-start(bf16[896,512]{1,0:T(8,128)(2,1)} %refs_15_.1) | copy-start | bytes 2752516
  3.8 11.6 %copy-start.7 = (s32[4]{0:T(128)S(1)}, s32[4]{0:T(128)}, u32[]{:S(2)}) copy-start(s32[4]{0:T(128)} %constant.54.clone) | copy-start | bytes 52
  6.9 25.9 %all-to-all-start = ((bf16[16,3,16,896]{3,2,1,0:T(8,128)(2,1)}), bf16[16,3,16,896]{3,2,1,0:T(8,128)(2,1)}, u32[]{:S(2)}, u32[]{:S(2)}) async-start(bf16[16,3,16,896]{3,2,1,0:T(8,128)(2,1)} %bitcast.28), calls=%async_computation | async-start | bytes 2752512 | tf_op jit(solution)/shard_map/all_to_all | solution.py:293
  13.8 13.7 %collective-permute-start = (bf16[896,512]{1,0:T(8,128)(2,1)S(1)}, bf16[896,512]{1,0:T(8,128)(2,1)S(1)}, u32[]{:S(2)}, u32[]{:S(2)}) collective-permute-start(bf16[896,512]{1,0:T(8,128)(2,1)S(1)} %copy-done), channel_id=1, source_target_pairs={{0,1},{1,0},{2,3},{3,2},{4,5},{5,4},{6,7},{7,6},{8,9},{9,8},{10,11... | collective-permute-start | bytes 2752520 | tf_op jit(solution)/shard_map/ppermute | solution.py:27
  14.7 12.8 %collective-permute-start.1 = (bf16[896,512]{1,0:T(8,128)(2,1)S(1)}, bf16[896,512]{1,0:T(8,128)(2,1)}, u32[]{:S(2)}, u32[]{:S(2)}) collective-permute-start(bf16[896,512]{1,0:T(8,128)(2,1)S(1)} %copy-done.1), channel_id=1, source_target_pairs={{0,1},{1,0},{2,3},{3,2},{4,5},{5,4},{6,7},{7,6},{8,9},{9,8},{10,11... | collective-permute-start | bytes 2752520 | tf_op jit(solution)/shard_map/ppermute | solution.py:27
  34.8 7.5 %collective-permute-start.8 = (bf16[256,896]{1,0:T(8,128)(2,1)S(1)}, bf16[256,896]{1,0:T(8,128)(2,1)S(1)}, u32[]{:S(2)}, u32[]{:S(2)}) collective-permute-start(bf16[256,896]{1,0:T(8,128)(2,1)S(1)} %bitcast.24), channel_id=1, source_target_pairs={{0,1},{1,0},{2,3},{3,2},{4,5},{5,4},{6,7},{7,6},{8,9},{9,8},{10,11... | collective-permute-start | bytes 1376264 | tf_op jit(solution)/shard_map/ppermute | solution.py:324
  38.4 17.8 %copy-start.8 = (bf16[64,1024]{1,0:T(8,128)(2,1)S(1)}, bf16[64,1024]{1,0:T(8,128)(2,1)}, u32[]{:S(2)}) copy-start(bf16[64,1024]{1,0:T(8,128)(2,1)} %get-tuple-element.138) | copy-start | bytes 393220
  38.4 14.6 %collective-permute-start.4 = (bf16[256,896]{1,0:T(8,128)(2,1)S(1)}, bf16[256,896]{1,0:T(8,128)(2,1)S(1)}, u32[]{:S(2)}, u32[]{:S(2)}) collective-permute-start(bf16[256,896]{1,0:T(8,128)(2,1)S(1)} %bitcast.21), channel_id=1, source_target_pairs={{0,2},{1,3},{2,4},{3,5},{4,6},{5,7},{6,0},{7,1},{8,10},{9,11},{10,... | collective-permute-start | bytes 1376264 | tf_op jit(solution)/shard_map/ppermute | solution.py:324
  40.1 13.2 %collective-permute-start.6 = (bf16[256,896]{1,0:T(8,128)(2,1)S(1)}, bf16[256,896]{1,0:T(8,128)(2,1)S(1)}, u32[]{:S(2)}, u32[]{:S(2)}) collective-permute-start(bf16[256,896]{1,0:T(8,128)(2,1)S(1)} %bitcast.25), channel_id=1, source_target_pairs={{0,7},{1,6},{2,1},{3,0},{4,3},{5,2},{6,5},{7,4},{8,15},{9,14},{10,... | collective-permute-start | bytes 1376264 | tf_op jit(solution)/shard_map/ppermute | solution.py:324
  46.0 24.5 %copy-start.3 = (bf16[512,4096]{1,0:T(8,128)(2,1)}, bf16[512,4096]{1,0:T(8,128)(2,1)S(1)}, u32[]{:S(2)}) copy-start(bf16[512,4096]{1,0:T(8,128)(2,1)S(1)} %get-tuple-element.140.refs_21_) | copy-start | bytes 12582916
  46.0 16.3 %collective-permute-start.10 = (bf16[256,896]{1,0:T(8,128)(2,1)S(1)}, bf16[256,896]{1,0:T(8,128)(2,1)S(1)}, u32[]{:S(2)}, u32[]{:S(2)}) collective-permute-start(bf16[256,896]{1,0:T(8,128)(2,1)S(1)} %bitcast.23), channel_id=1, source_target_pairs={{0,6},{1,7},{2,0},{3,1},{4,2},{5,3},{6,4},{7,5},{8,14},{9,15},{10,... | collective-permute-start | bytes 1376264 | tf_op jit(solution)/shard_map/ppermute | solution.py:324
  47.7 15.4 %collective-permute-start.9 = (bf16[256,896]{1,0:T(8,128)(2,1)S(1)}, bf16[256,896]{1,0:T(8,128)(2,1)S(1)}, u32[]{:S(2)}, u32[]{:S(2)}) collective-permute-start(bf16[256,896]{1,0:T(8,128)(2,1)S(1)} %bitcast.26), channel_id=1, source_target_pairs={{0,3},{1,2},{2,5},{3,4},{4,7},{5,6},{6,1},{7,0},{8,11},{9,10},{10,... | collective-permute-start | bytes 1376264 | tf_op jit(solution)/shard_map/ppermute | solution.py:324
  53.0 14.7 %collective-permute-start.5 = (bf16[128,896]{1,0:T(8,128)(2,1)S(1)}, bf16[128,896]{1,0:T(8,128)(2,1)S(1)}, u32[]{:S(2)}, u32[]{:S(2)}) collective-permute-start(bf16[128,896]{1,0:T(8,128)(2,1)S(1)} %get-tuple-element.184), channel_id=1, source_target_pairs={{0,2},{1,3},{2,4},{3,5},{4,6},{5,7},{6,0},{7,1},{8,10},{9,11},{10,... | collective-permute-start | bytes 688136 | tf_op jit(solution)/shard_map/ppermute | solution.py:324
  53.4 14.4 %collective-permute-start.7 = (bf16[128,896]{1,0:T(8,128)(2,1)S(1)}, bf16[128,896]{1,0:T(8,128)(2,1)S(1)}, u32[]{:S(2)}, u32[]{:S(2)}) collective-permute-start(bf16[128,896]{1,0:T(8,128)(2,1)S(1)} %get-tuple-element.182), channel_id=1, source_target_pairs={{0,6},{1,7},{2,0},{3,1},{4,2},{5,3},{6,4},{7,5},{8,14},{9,15},{10,... | collective-permute-start | bytes 688136 | tf_op jit(solution)/shard_map/ppermute | solution.py:324
  56.3 14.2 %collective-permute-start.11 = (bf16[64,1024]{1,0:T(8,128)(2,1)S(1)}, bf16[64,1024]{1,0:T(8,128)(2,1)S(1)}, u32[]{:S(2)}, u32[]{:S(2)}) collective-permute-start(bf16[64,1024]{1,0:T(8,128)(2,1)S(1)} %copy-done.8), channel_id=1, source_target_pairs={{8,1},{16,9},{24,17},{32,25},{40,33},{48,41},{56,49},{64,57},{72,6... | collective-permute-start | bytes 393224 | tf_op jit(solution)/shard_map/ppermute | solution.py:341
  57.6 12.9 %copy-start.2 = (bf16[512,4096]{1,0:T(8,128)(2,1)S(1)}, bf16[512,4096]{1,0:T(8,128)(2,1)}, u32[]{:S(2)}) copy-start(bf16[512,4096]{1,0:T(8,128)(2,1)} %refs_20_.1) | copy-start | bytes 12582916
  57.6 12.9 %copy-start.6 = (bf16[4,64,1024]{2,1,0:T(8,128)(2,1)S(1)}, bf16[4,64,1024]{2,1,0:T(8,128)(2,1)}, u32[]{:S(2)}) copy-start(bf16[4,64,1024]{2,1,0:T(8,128)(2,1)} %get-tuple-element.137.refs_18_) | copy-start | bytes 1572868
  67.8 8.7 %collective-permute-start.12 = (bf16[128,896]{1,0:T(8,128)(2,1)S(1)}, bf16[128,896]{1,0:T(8,128)(2,1)S(1)}, u32[]{:S(2)}, u32[]{:S(2)}) collective-permute-start(bf16[128,896]{1,0:T(8,128)(2,1)S(1)} %get-tuple-element.147), channel_id=1, source_target_pairs={{0,2},{1,3},{2,4},{3,5},{4,6},{5,7},{6,0},{7,1},{8,10},{9,11},{10,... | collective-permute-start | bytes 688136 | tf_op jit(solution)/shard_map/ppermute | solution.py:324
  68.9 7.6 %collective-permute-start.13 = (bf16[128,896]{1,0:T(8,128)(2,1)S(1)}, bf16[128,896]{1,0:T(8,128)(2,1)S(1)}, u32[]{:S(2)}, u32[]{:S(2)}) collective-permute-start(bf16[128,896]{1,0:T(8,128)(2,1)S(1)} %get-tuple-element.148), channel_id=1, source_target_pairs={{0,6},{1,7},{2,0},{3,1},{4,2},{5,3},{6,4},{7,5},{8,14},{9,15},{10,... | collective-permute-start | bytes 688136 | tf_op jit(solution)/shard_map/ppermute | solution.py:324
  70.5 8.8 %copy-start.5 = (bf16[4,64,1024]{2,1,0:T(8,128)(2,1)S(1)}, bf16[4,64,1024]{2,1,0:T(8,128)(2,1)}, u32[]{:S(2)}) copy-start(bf16[4,64,1024]{2,1,0:T(8,128)(2,1)} %get-tuple-element.155.refs_18_) | copy-start | bytes 1572868
  76.5 13.5 %collective-permute-start.14 = (bf16[64,4096]{1,0:T(8,128)(2,1)S(1)}, bf16[64,4096]{1,0:T(8,128)(2,1)S(1)}, u32[]{:S(2)}, u32[]{:S(2)}) collective-permute-start(bf16[64,4096]{1,0:T(8,128)(2,1)S(1)} %get-tuple-element.150), channel_id=1, source_target_pairs={{0,2},{2,4},{4,6},{6,0},{1,3},{3,5},{5,7},{7,1},{8,10},{10,12},{12... | collective-permute-start | bytes 1572872 | tf_op jit(solution)/shard_map/ppermute | solution.py:27
  76.6 13.4 %collective-permute-start.15 = (bf16[64,4096]{1,0:T(8,128)(2,1)S(1)}, bf16[64,4096]{1,0:T(8,128)(2,1)S(1)}, u32[]{:S(2)}, u32[]{:S(2)}) collective-permute-start(bf16[64,4096]{1,0:T(8,128)(2,1)S(1)} %get-tuple-element.151), channel_id=1, source_target_pairs={{0,6},{2,0},{4,2},{6,4},{1,7},{3,1},{5,3},{7,5},{8,14},{10,8},{12,... | collective-permute-start | bytes 1572872 | tf_op jit(solution)/shard_map/ppermute | solution.py:27
  79.3 2.2 %copy-start.4 = (bf16[512,4096]{1,0:T(8,128)(2,1)S(1)}, bf16[512,4096]{1,0:T(8,128)(2,1)}, u32[]{:S(2)}) copy-start(bf16[512,4096]{1,0:T(8,128)(2,1)} %copy-done.3) | copy-start | bytes 12582916
  90.1 6.9 %collective-permute-start.16 = (bf16[64,2048]{1,0:T(8,128)(2,1)S(1)}, bf16[64,2048]{1,0:T(8,128)(2,1)S(1)}, u32[]{:S(2)}, u32[]{:S(2)}) collective-permute-start(bf16[64,2048]{1,0:T(8,128)(2,1)S(1)} %get-tuple-element.168), channel_id=1, source_target_pairs={{0,2},{2,4},{4,6},{6,0},{1,3},{3,5},{5,7},{7,1},{8,10},{10,12},{12... | collective-permute-start | bytes 786440 | tf_op jit(solution)/shard_map/ppermute | solution.py:27
  90.2 19.8 %collective-permute-start.22 = (bf16[64,2048]{1,0:T(8,128)(2,1)S(1)}, bf16[64,2048]{1,0:T(8,128)(2,1)S(1)}, u32[]{:S(2)}, u32[]{:S(2)}) collective-permute-start(bf16[64,2048]{1,0:T(8,128)(2,1)S(1)} %get-tuple-element.178), channel_id=1, source_target_pairs={{0,6},{2,0},{4,2},{6,4},{1,7},{3,1},{5,3},{7,5},{8,14},{10,8},{12,... | collective-permute-start | bytes 786440 | tf_op jit(solution)/shard_map/ppermute | solution.py:27
  92.9 17.3 %collective-permute-start.21 = (bf16[64,2048]{1,0:T(8,128)(2,1)S(1)}, bf16[64,2048]{1,0:T(8,128)(2,1)S(1)}, u32[]{:S(2)}, u32[]{:S(2)}) collective-permute-start(bf16[64,2048]{1,0:T(8,128)(2,1)S(1)} %get-tuple-element.176), channel_id=1, source_target_pairs={{0,2},{2,4},{4,6},{6,0},{1,3},{3,5},{5,7},{7,1},{8,10},{10,12},{12... | collective-permute-start | bytes 786440 | tf_op jit(solution)/shard_map/ppermute | solution.py:27
  92.9 8.8 %collective-permute-start.17 = (bf16[64,2048]{1,0:T(8,128)(2,1)S(1)}, bf16[64,2048]{1,0:T(8,128)(2,1)S(1)}, u32[]{:S(2)}, u32[]{:S(2)}) collective-permute-start(bf16[64,2048]{1,0:T(8,128)(2,1)S(1)} %get-tuple-element.170), channel_id=1, source_target_pairs={{0,6},{2,0},{4,2},{6,4},{1,7},{3,1},{5,3},{7,5},{8,14},{10,8},{12,... | collective-permute-start | bytes 786440 | tf_op jit(solution)/shard_map/ppermute | solution.py:27
  95.5 18.1 %collective-permute-start.19 = (bf16[64,2048]{1,0:T(8,128)(2,1)S(1)}, bf16[64,2048]{1,0:T(8,128)(2,1)S(1)}, u32[]{:S(2)}, u32[]{:S(2)}) collective-permute-start(bf16[64,2048]{1,0:T(8,128)(2,1)S(1)} %get-tuple-element.173), channel_id=1, source_target_pairs={{0,6},{2,0},{4,2},{6,4},{1,7},{3,1},{5,3},{7,5},{8,14},{10,8},{12,... | collective-permute-start | bytes 786440 | tf_op jit(solution)/shard_map/ppermute | solution.py:27
  97.0 16.6 %collective-permute-start.20 = (bf16[64,2048]{1,0:T(8,128)(2,1)S(1)}, bf16[64,2048]{1,0:T(8,128)(2,1)S(1)}, u32[]{:S(2)}, u32[]{:S(2)}) collective-permute-start(bf16[64,2048]{1,0:T(8,128)(2,1)S(1)} %get-tuple-element.174), channel_id=1, source_target_pairs={{0,2},{2,4},{4,6},{6,0},{1,3},{3,5},{5,7},{7,1},{8,10},{10,12},{12... | collective-permute-start | bytes 786440 | tf_op jit(solution)/shard_map/ppermute | solution.py:27
  101.8 18.4 %collective-permute-start.18 = (bf16[64,4096]{1,0:T(8,128)(2,1)S(1)}, bf16[64,4096]{1,0:T(8,128)(2,1)S(1)}, u32[]{:S(2)}, u32[]{:S(2)}) collective-permute-start(bf16[64,4096]{1,0:T(8,128)(2,1)S(1)} %pad_maximum_fusion.first_ref), channel_id=1, source_target_pairs={{0,1},{1,8},{2,3},{3,2},{4,5},{5,4},{6,7},{7,6},{8,9},{9,16},{10,1... | collective-permute-start | bytes 1572872 | tf_op jit(solution)/shard_map/ppermute | solution.py:367
  110.2 10.0 %collective-permute-start.23 = (bf16[64,2048]{1,0:T(8,128)(2,1)S(1)}, bf16[64,2048]{1,0:T(8,128)(2,1)S(1)}, u32[]{:S(2)}, u32[]{:S(2)}) collective-permute-start(bf16[64,2048]{1,0:T(8,128)(2,1)S(1)} %add_convert_fusion.1), channel_id=1, source_target_pairs={{0,2},{2,4},{4,6},{6,0},{1,3},{3,5},{5,7},{7,1},{8,10},{10,12},{12... | collective-permute-start | bytes 786440 | tf_op jit(solution)/shard_map/ppermute | solution.py:27
  111.4 8.8 %collective-permute-start.24 = (bf16[64,2048]{1,0:T(8,128)(2,1)S(1)}, bf16[64,2048]{1,0:T(8,128)(2,1)S(1)}, u32[]{:S(2)}, u32[]{:S(2)}) collective-permute-start(bf16[64,2048]{1,0:T(8,128)(2,1)S(1)} %add_convert_fusion), channel_id=1, source_target_pairs={{0,6},{2,0},{4,2},{6,4},{1,7},{3,1},{5,3},{7,5},{8,14},{10,8},{12,... | collective-permute-start | bytes 786440 | tf_op jit(solution)/shard_map/ppermute | solution.py:27

commit v10 on v8

--- a/solution.py
+++ b/solution.py
@@ -19,7 +19,7 @@
 BF16 = jnp.bfloat16
 SHARE = 0.4
 LIMIT = 60 * 1024 * 1024
-GRANT = 32 * 1024 * 1024
+GRANT = 26 * 1024 * 1024
 
 
 def step(value, axis, steps):
@@ -155,7 +155,7 @@
         + [jax.ShapeDtypeStruct(value.shape, value.dtype) for value in carried],
         scratch_shapes=[pltpu.SemaphoreType.DMA((max(1, len(carried)),))],
         cost_estimate=cost(2e9),
-        compiler_params=pltpu.CompilerParams(vmem_limit_bytes=GRANT),
+        compiler_params=pltpu.CompilerParams(vmem_limit_bytes=18 * 1024 * 1024),
     )(*parts, *weights, *carried)
 
 
@@ -289,7 +289,7 @@
     row_index = row_index.transpose(2, 3, 1, 0)[:, ::-1]
     row_index = jnp.where(core == 0, row_index, row_index[::-1]).reshape(-1)
     count = row_index.shape[0] // 2
-    mine, theirs = pick(received, row_index, jnp.zeros((), jnp.int32), piece, [count] * 2, 30)
+    mine, theirs = pick(received, row_index, jnp.zeros((), jnp.int32), piece, [count] * 2, 10)
     mine, theirs = mine.reshape(-1, enc), theirs.reshape(-1, enc)
 
     def hop(value, steps, cross):

time: 120 us -> 120 us (level)
  waiting for transfers between devices: 25.1 us -> 27.3 us
  local copies, waits for them, and re-layouts: 3.99 us -> 1.8 us
    unnamed x18 -> x14, local copies, waits for them, and re-layouts: 2.23 us -> 0.04 us
    ppermute x14, waiting for transfers between devices: 9.4 us -> 11.6 us  [step(): lax.ppermute(value, axis, [(i, (i + steps) % count) for i in range(count)])]
where the time goes in v10:
time: 120 us; the launch traced here: 118 us
  starting transfers between devices  48.2 us (40%)
  Pallas kernels  37.3 us (31%)
  waiting for transfers between devices  27.3 us (23%)
  other arithmetic  3.29 us (3%)
  local copies, waits for them, and re-layouts  1.8 us (2%)
    ppermute x14, starting transfers between devices, step(): lax.ppermute(value, axis, [(i, (i + steps) % count) for i in range(count)])  15.7 us
    ppermute x9, starting transfers between devices, hop(): return lax.ppermute(value, ('z', 'core'), pairs)  15.4 us
    pallas_call x1, Pallas kernels, project_queries(): pl.pallas_call(query_kernel, grid_spec=pltpu.PrefetchScalarGridSpec(num_s...  12 us
    pallas_call x2, Pallas kernels, attend(): pl.pallas_call(functools.partial(span_kernel, group), grid_spec=pltpu.Pre...  12 us
    ppermute x14, waiting for transfers between devices, step(): lax.ppermute(value, axis, [(i, (i + steps) % count) for i in range(count)])  11.6 us
    ppermute x9, waiting for transfers between devices, hop(): return lax.ppermute(value, ('z', 'core'), pairs)  10.5 us
    ppermute x1, starting transfers between devices, body(): head = lax.ppermute(out_a, ('seq', 'z', 'core'), pairs)  8.81 us
    pallas_call x3, Pallas kernels, project(): pl.pallas_call(functools.partial(project_kernel, len(carried)), in_specs=...  8.38 us
  transfers between devices with their start and end apart: 26, of which 8 were waited for; matrix products, arithmetic and copies ran while one was open for 3% of the time, Pallas kernels for 30%

profile of v10, /device:TPU:1, one launch (start us, length us, event | category | flops | bytes accessed | tf_op | source)
XLA Modules:
  0.0 118.3 jit_solution(11386610656416840881)
XLA Ops:
  0.0 1.4 %collective-permute-start.3 = (bf16[4096,512]{1,0:T(8,128)(2,1)}, bf16[4096,512]{1,0:T(8,128)(2,1)}, u32[]{:S(2)}, u32[]{:S(2)}) collective-permute-start(bf16[4096,512]{1,0:T(8,128)(2,1)} %wa_hbm.1), channel_id=1, source_target_pairs={{0,1},{1,0},{2,3},{3,2},{4,5},{5,4},{6,7},{7,6},{8,9},{9,8},{10,11... | collective-permute-start | bytes 12582920 | tf_op jit(solution)/shard_map/ppermute | solution.py:27
  1.4 0.7 shift-right-arithmetic_bitcast_fusion
  2.5 0.5 convert_reduce_fusion
  3.0 0.1 select_reduce_fusion
  3.2 0.6 reshape.76.index_ref
  3.8 3.0 %shard_map.91 = bf16[48,16,896]{2,1,0:T(8,128)(2,1)} custom-call(s32[48]{0:T(128)} %reshape.76.index_ref, s32[1]{0:T(128)} %bitcast.4.start_ref, bf16[24,128,896]{2,1,0:T(8,128)(2,1)} %source_ref.1), custom_call_target="tpu_custom_call" | custom-call | flops 400000000 | bytes 400000 | tf_op jit(solution)/shard_map/pallas_call | solution.py:61
  6.8 7.0 %all-to-all-start = ((bf16[16,3,16,896]{3,2,1,0:T(8,128)(2,1)}), bf16[16,3,16,896]{3,2,1,0:T(8,128)(2,1)}, u32[]{:S(2)}, u32[]{:S(2)}) async-start(bf16[16,3,16,896]{3,2,1,0:T(8,128)(2,1)} %bitcast.28), calls=%async_computation | async-start | bytes 2752512 | tf_op jit(solution)/shard_map/all_to_all | solution.py:270
  13.9 0.9 collective-permute-start
  14.7 0.1 collective-permute-start.1
  15.0 0.1 rev.6
  15.1 0.1 rev.7
  15.2 0.1 copy.18
  15.5 12.0 %shard_map.92 = (bf16[4,64,1024]{2,1,0:T(8,128)(2,1)}, bf16[4,64,1024]{2,1,0:T(8,128)(2,1)}, bf16[64,1024]{1,0:T(8,128)(2,1)}) custom-call(s32[1]{0:T(128)} %bitcast.7.core_ref, bf16[8,128,4096]{2,1,0:T(8,128)(2,1)} %bitcast.27, bf16[4096,512]{1,0:T(8,128)(2,1)} %wa_hbm.1, bf16[4096,512]{1,0:T(8,128)(2,1)} %collective-permute-done.3.wb_hbm), custom_call_target="tpu_custom_call" | custom-call | flops 1200000000 | bytes 1200000 | tf_op jit(solution)/shard_map/pallas_call | solution.py:112
  27.6 5.2 %all-to-all-done = bf16[16,3,16,896]{3,2,1,0:T(8,128)(2,1)} async-done(((bf16[16,3,16,896]{3,2,1,0:T(8,128)(2,1)}), bf16[16,3,16,896]{3,2,1,0:T(8,128)(2,1)}, u32[]{:S(2)}, u32[]{:S(2)}) %all-to-all-start) | async-done | bytes 1376288 | tf_op jit(solution)/shard_map/all_to_all | solution.py:270
  32.8 2.0 %shard_map.93 = (bf16[16,16,896]{2,1,0:T(8,128)(2,1)S(1)}, bf16[16,16,896]{2,1,0:T(8,128)(2,1)S(1)}) custom-call(s32[32]{0:T(128)S(1)} %reshape.82.index_ref, s32[1]{0:T(128)} %constant.53.clone.1.start_ref, bf16[48,16,896]{2,1,0:T(8,128)(2,1)} %bitcast.6.source_ref), custom_call_target="tpu_custom_call" | custom-call | flops 400000000 | bytes 400000 | tf_op jit(solution)/shard_map/pallas_call | solution.py:61
  34.8 3.7 %collective-permute-start.8 = (bf16[256,896]{1,0:T(8,128)(2,1)S(1)}, bf16[256,896]{1,0:T(8,128)(2,1)S(1)}, u32[]{:S(2)}, u32[]{:S(2)}) collective-permute-start(bf16[256,896]{1,0:T(8,128)(2,1)S(1)} %bitcast.24), channel_id=1, source_target_pairs={{0,1},{1,0},{2,3},{3,2},{4,5},{5,4},{6,7},{7,6},{8,9},{9,8},{10,11... | collective-permute-start | bytes 1376264 | tf_op jit(solution)/shard_map/ppermute | solution.py:301
  38.5 1.7 %collective-permute-start.4 = (bf16[256,896]{1,0:T(8,128)(2,1)S(1)}, bf16[256,896]{1,0:T(8,128)(2,1)S(1)}, u32[]{:S(2)}, u32[]{:S(2)}) collective-permute-start(bf16[256,896]{1,0:T(8,128)(2,1)S(1)} %bitcast.21), channel_id=1, source_target_pairs={{0,2},{1,3},{2,4},{3,5},{4,6},{5,7},{6,0},{7,1},{8,10},{9,11},{10,... | collective-permute-start | bytes 1376264 | tf_op jit(solution)/shard_map/ppermute | solution.py:301
  40.1 2.2 %collective-permute-start.6 = (bf16[256,896]{1,0:T(8,128)(2,1)S(1)}, bf16[256,896]{1,0:T(8,128)(2,1)S(1)}, u32[]{:S(2)}, u32[]{:S(2)}) collective-permute-start(bf16[256,896]{1,0:T(8,128)(2,1)S(1)} %bitcast.25), channel_id=1, source_target_pairs={{0,7},{1,6},{2,1},{3,0},{4,3},{5,2},{6,5},{7,4},{8,15},{9,14},{10,... | collective-permute-start | bytes 1376264 | tf_op jit(solution)/shard_map/ppermute | solution.py:301
  42.3 3.7 %shard_map.94 = (bf16[2,2,4,32,512]{4,3,2,1,0:T(8,128)(2,1)S(1)}, bf16[2,2,4,32,512]{4,3,2,1,0:T(8,128)(2,1)S(1)}, bf16[2,2,4,32,512]{4,3,2,1,0:T(8,128)(2,1)S(1...) custom-call(bf16[256,896]{1,0:T(8,128)(2,1)S(1)} %bitcast.22, ...), custom_call_target="tpu_custom_call" | custom-call | flops 800000000 | bytes 800000 | tf_op jit(solution)/shard_map/pallas_call | solution.py:150
  46.0 1.7 %collective-permute-start.10 = (bf16[256,896]{1,0:T(8,128)(2,1)S(1)}, bf16[256,896]{1,0:T(8,128)(2,1)S(1)}, u32[]{:S(2)}, u32[]{:S(2)}) collective-permute-start(bf16[256,896]{1,0:T(8,128)(2,1)S(1)} %bitcast.23), channel_id=1, source_target_pairs={{0,6},{1,7},{2,0},{3,1},{4,2},{5,3},{6,4},{7,5},{8,14},{9,15},{10,... | collective-permute-start | bytes 1376264 | tf_op jit(solution)/shard_map/ppermute | solution.py:301
  47.7 0.3 collective-permute-start.9
  48.0 5.0 %collective-permute-done.4.refs_0_ = bf16[256,896]{1,0:T(8,128)(2,1)S(1)} collective-permute-done((bf16[256,896]{1,0:T(8,128)(2,1)S(1)}, bf16[256,896]{1,0:T(8,128)(2,1)S(1)}, u32[]{:S(2)}, u32[]{:S(2)}) %collective-permute-start.4) | collective-permute-done | bytes 458784 | tf_op jit(solution)/shard_map/ppermute | solution.py:301
  53.1 0.3 collective-permute-start.5
  53.4 2.9 %collective-permute-start.7 = (bf16[128,896]{1,0:T(8,128)(2,1)S(1)}, bf16[128,896]{1,0:T(8,128)(2,1)S(1)}, u32[]{:S(2)}, u32[]{:S(2)}) collective-permute-start(bf16[128,896]{1,0:T(8,128)(2,1)S(1)} %get-tuple-element.182), channel_id=1, source_target_pairs={{0,6},{1,7},{2,0},{3,1},{4,2},{5,3},{6,4},{7,5},{8,14},{9,15},{10,... | collective-permute-start | bytes 688136 | tf_op jit(solution)/shard_map/ppermute | solution.py:301
  56.3 1.3 %collective-permute-start.11 = (bf16[64,1024]{1,0:T(8,128)(2,1)S(1)}, bf16[64,1024]{1,0:T(8,128)(2,1)S(1)}, u32[]{:S(2)}, u32[]{:S(2)}) collective-permute-start(bf16[64,1024]{1,0:T(8,128)(2,1)S(1)} %copy-done.6), channel_id=1, source_target_pairs={{8,1},{16,9},{24,17},{32,25},{40,33},{48,41},{56,49},{64,57},{72,6... | collective-permute-start | bytes 393224 | tf_op jit(solution)/shard_map/ppermute | solution.py:318
  57.6 2.3 %shard_map.95 = (bf16[2,2,4,32,512]{4,3,2,1,0:T(8,128)(2,1)S(1)}, bf16[2,2,4,32,512]{4,3,2,1,0:T(8,128)(2,1)S(1)}, bf16[2,2,4,32,512]{4,3,2,1,0:T(8,128)(2,1)S(1)}, bf16[2,2,4,32,512]{4,3,2,1,0:T(8,128)(2,1)S(1)}) custom-call(bf16[256,896]{1,0:T(8,128)(2,1)S(1)} %collective-permute-done.4.refs_0_, bf16[256,896]{1,0:T(8,128)(2,1)S(1)} %collective-permute-done.6.refs_1_, ...), custom_call_target="tpu_custom_call" | custom-call | flops 800000000 | bytes 800000 | tf_op jit(solution)/shard_map/pallas_call | solution.py:150
  60.0 2.4 %collective-permute-done.10.refs_1_ = bf16[256,896]{1,0:T(8,128)(2,1)S(1)} collective-permute-done((bf16[256,896]{1,0:T(8,128)(2,1)S(1)}, bf16[256,896]{1,0:T(8,128)(2,1)S(1)}, u32[]{:S(2)}, u32[]{:S(2)}) %collective-permute-start.10) | collective-permute-done | bytes 458784 | tf_op jit(solution)/shard_map/ppermute | solution.py:301
  62.3 0.8 collective-permute-done.9.refs_0_
  63.1 2.3 %shard_map.96 = (bf16[2,2,4,32,512]{4,3,2,1,0:T(8,128)(2,1)S(1)}, bf16[2,2,4,32,512]{4,3,2,1,0:T(8,128)(2,1)S(1)}, bf16[2,2,4,32,512]{4,3,2,1,0:T(8,128)(2,1)S(1)}, bf16[2,2,4,32,512]{4,3,2,1,0:T(8,128)(2,1)S(1)}) custom-call(bf16[256,896]{1,0:T(8,128)(2,1)S(1)} %collective-permute-done.9.refs_0_, bf16[256,896]{1,0:T(8,128)(2,1)S(1)} %collective-permute-done.10.refs_1_, ...), custom_call_target="tpu_custom_call" | custom-call | flops 800000000 | bytes 800000 | tf_op jit(solution)/shard_map/pallas_call | solution.py:150
  65.5 2.3 %collective-permute-done.5.refs_12_ = bf16[128,896]{1,0:T(8,128)(2,1)S(1)} collective-permute-done((bf16[128,896]{1,0:T(8,128)(2,1)S(1)}, bf16[128,896]{1,0:T(8,128)(2,1)S(1)}, u32[]{:S(2)}, u32[]{:S(2)}) %collective-permute-start.5) | collective-permute-done | bytes 229408 | tf_op jit(solution)/shard_map/ppermute | solution.py:301
  67.8 1.2 collective-permute-start.12
  69.0 1.5 %collective-permute-start.13 = (bf16[128,896]{1,0:T(8,128)(2,1)S(1)}, bf16[128,896]{1,0:T(8,128)(2,1)S(1)}, u32[]{:S(2)}, u32[]{:S(2)}) collective-permute-start(bf16[128,896]{1,0:T(8,128)(2,1)S(1)} %get-tuple-element.148), channel_id=1, source_target_pairs={{0,6},{1,7},{2,0},{3,1},{4,2},{5,3},{6,4},{7,5},{8,14},{9,15},{10,... | collective-permute-start | bytes 688136 | tf_op jit(solution)/shard_map/ppermute | solution.py:301
  70.5 6.0 %shard_map.97 = (bf16[64,4096]{1,0:T(8,128)(2,1)S(1)}, bf16[64,4096]{1,0:T(8,128)(2,1)S(1)}, bf16[64,2048]{1,0:T(8,128)(2,1)S(1)}, bf16[64,2048]{1,0:T(8,128)(2,...) custom-call(s32[9]{0:T(128)S(1)} %pad_add_fusion.place_ref, ...), custom_call_target="tpu_custom_call" | custom-call | flops 2000000000 | bytes 2000000 | tf_op jit(solution)/shard_map/pallas_call | solution.py:237
  76.6 2.7 %collective-permute-start.15 = (bf16[64,4096]{1,0:T(8,128)(2,1)S(1)}, bf16[64,4096]{1,0:T(8,128)(2,1)S(1)}, u32[]{:S(2)}, u32[]{:S(2)}) collective-permute-start(bf16[64,4096]{1,0:T(8,128)(2,1)S(1)} %get-tuple-element.151), channel_id=1, source_target_pairs={{0,6},{2,0},{4,2},{6,4},{1,7},{3,1},{5,3},{7,5},{8,14},{10,8},{12,... | collective-permute-start | bytes 1572872 | tf_op jit(solution)/shard_map/ppermute | solution.py:27
  79.3 6.0 %shard_map.98 = (bf16[64,2048]{1,0:T(8,128)(2,1)S(1)}, bf16[64,2048]{1,0:T(8,128)(2,1)S(1)}, bf16[64,2048]{1,0:T(8,128)(2,1)S(1)}, bf16[64,2048]{1,0:T(8,128)(2,...) custom-call(s32[4]{0:T(128)S(1)} %get-tuple-element.152.place_ref, ...), custom_call_target="tpu_custom_call" | custom-call | flops 2000000000 | bytes 2000000 | tf_op jit(solution)/shard_map/pallas_call | solution.py:237
  85.3 4.7 %collective-permute-done.14 = bf16[64,4096]{1,0:T(8,128)(2,1)S(1)} collective-permute-done((bf16[64,4096]{1,0:T(8,128)(2,1)S(1)}, bf16[64,4096]{1,0:T(8,128)(2,1)S(1)}, u32[]{:S(2)}, u32[]{:S(2)}) %collective-permute-start.14) | collective-permute-done | bytes 524320 | tf_op jit(solution)/shard_map/ppermute | solution.py:27
  90.0 0.1 add_convert_fusion.6
  90.1 2.5 %collective-permute-start.17 = (bf16[64,2048]{1,0:T(8,128)(2,1)S(1)}, bf16[64,2048]{1,0:T(8,128)(2,1)S(1)}, u32[]{:S(2)}, u32[]{:S(2)}) collective-permute-start(bf16[64,2048]{1,0:T(8,128)(2,1)S(1)} %get-tuple-element.170), channel_id=1, source_target_pairs={{0,6},{2,0},{4,2},{6,4},{1,7},{3,1},{5,3},{7,5},{8,14},{10,8},{12,... | collective-permute-start | bytes 786440 | tf_op jit(solution)/shard_map/ppermute | solution.py:27
  92.6 2.7 %collective-permute-start.21 = (bf16[64,2048]{1,0:T(8,128)(2,1)S(1)}, bf16[64,2048]{1,0:T(8,128)(2,1)S(1)}, u32[]{:S(2)}, u32[]{:S(2)}) collective-permute-start(bf16[64,2048]{1,0:T(8,128)(2,1)S(1)} %get-tuple-element.176), channel_id=1, source_target_pairs={{0,6},{2,0},{4,2},{6,4},{1,7},{3,1},{5,3},{7,5},{8,14},{10,8},{12,... | collective-permute-start | bytes 786440 | tf_op jit(solution)/shard_map/ppermute | solution.py:27
  95.3 2.7 %collective-permute-start.19 = (bf16[64,2048]{1,0:T(8,128)(2,1)S(1)}, bf16[64,2048]{1,0:T(8,128)(2,1)S(1)}, u32[]{:S(2)}, u32[]{:S(2)}) collective-permute-start(bf16[64,2048]{1,0:T(8,128)(2,1)S(1)} %get-tuple-element.172), channel_id=1, source_target_pairs={{0,6},{2,0},{4,2},{6,4},{1,7},{3,1},{5,3},{7,5},{8,14},{10,8},{12,... | collective-permute-start | bytes 786440 | tf_op jit(solution)/shard_map/ppermute | solution.py:27
  98.0 0.1 add_convert_fusion.4
  98.1 1.0 collective-permute-done.16
  99.2 8.8 %collective-permute-start.18 = (bf16[64,4096]{1,0:T(8,128)(2,1)S(1)}, bf16[64,4096]{1,0:T(8,128)(2,1)S(1)}, u32[]{:S(2)}, u32[]{:S(2)}) collective-permute-start(bf16[64,4096]{1,0:T(8,128)(2,1)S(1)} %pad_maximum_fusion.1), channel_id=1, source_target_pairs={{0,1},{1,8},{2,3},{3,2},{4,5},{5,4},{6,7},{7,6},{8,9},{9,16},{10,1... | collective-permute-start | bytes 1572872 | tf_op jit(solution)/shard_map/ppermute | solution.py:344
  108.2 2.7 %collective-permute-start.24 = (bf16[64,2048]{1,0:T(8,128)(2,1)S(1)}, bf16[64,2048]{1,0:T(8,128)(2,1)S(1)}, u32[]{:S(2)}, u32[]{:S(2)}) collective-permute-start(bf16[64,2048]{1,0:T(8,128)(2,1)S(1)} %add_convert_fusion.2), channel_id=1, source_target_pairs={{0,6},{2,0},{4,2},{6,4},{1,7},{3,1},{5,3},{7,5},{8,14},{10,8},{12,... | collective-permute-start | bytes 786440 | tf_op jit(solution)/shard_map/ppermute | solution.py:27
  110.9 5.9 %collective-permute-done.22 = bf16[64,2048]{1,0:T(8,128)(2,1)S(1)} collective-permute-done((bf16[64,2048]{1,0:T(8,128)(2,1)S(1)}, bf16[64,2048]{1,0:T(8,128)(2,1)S(1)}, u32[]{:S(2)}, u32[]{:S(2)}) %collective-permute-start.22) | collective-permute-done | bytes 262176 | tf_op jit(solution)/shard_map/ppermute | solution.py:27
  116.9 0.1 add_convert_fusion
  117.1 0.1 slice.44
  117.2 1.1 pad_maximum_fusion
  (61 shorter events, 1.5 us)
Async XLA Ops:
  0.0 15.5 %collective-permute-start.3 = (bf16[4096,512]{1,0:T(8,128)(2,1)}, bf16[4096,512]{1,0:T(8,128)(2,1)}, u32[]{:S(2)}, u32[]{:S(2)}) collective-permute-start(bf16[4096,512]{1,0:T(8,128)(2,1)} %wa_hbm.1), channel_id=1, source_target_pairs={{0,1},{1,0},{2,3},{3,2},{4,5},{5,4},{6,7},{7,6},{8,9},{9,8},{10,11... | collective-permute-start | bytes 12582920 | tf_op jit(solution)/shard_map/ppermute | solution.py:27
  1.4 31.4 %collective-permute-start.2 = (bf16[512,4096]{1,0:T(8,128)(2,1)}, bf16[512,4096]{1,0:T(8,128)(2,1)}, u32[]{:S(2)}, u32[]{:S(2)}) collective-permute-start(bf16[512,4096]{1,0:T(8,128)(2,1)} %refs_20_.1), channel_id=1, source_target_pairs={{0,1},{1,0},{2,3},{3,2},{4,5},{5,4},{6,7},{7,6},{8,9},{9,8},{10,11... | collective-permute-start | bytes 12582920 | tf_op jit(solution)/shard_map/ppermute | solution.py:27
  6.8 7.1 %copy-start = (bf16[896,512]{1,0:T(8,128)(2,1)S(1)}, bf16[896,512]{1,0:T(8,128)(2,1)}, u32[]{:S(2)}) copy-start(bf16[896,512]{1,0:T(8,128)(2,1)} %refs_14_.1) | copy-start | bytes 2752516
  6.8 7.9 %copy-start.1 = (bf16[896,512]{1,0:T(8,128)(2,1)S(1)}, bf16[896,512]{1,0:T(8,128)(2,1)}, u32[]{:S(2)}) copy-start(bf16[896,512]{1,0:T(8,128)(2,1)} %refs_15_.1) | copy-start | bytes 2752516
  6.8 8.6 %copy-start.5 = (s32[4]{0:T(128)S(1)}, s32[4]{0:T(128)}, u32[]{:S(2)}) copy-start(s32[4]{0:T(128)} %constant.54.clone) | copy-start | bytes 52
  6.8 26.0 %all-to-all-start = ((bf16[16,3,16,896]{3,2,1,0:T(8,128)(2,1)}), bf16[16,3,16,896]{3,2,1,0:T(8,128)(2,1)}, u32[]{:S(2)}, u32[]{:S(2)}) async-start(bf16[16,3,16,896]{3,2,1,0:T(8,128)(2,1)} %bitcast.28), calls=%async_computation | async-start | bytes 2752512 | tf_op jit(solution)/shard_map/all_to_all | solution.py:270
  13.9 13.7 %collective-permute-start = (bf16[896,512]{1,0:T(8,128)(2,1)S(1)}, bf16[896,512]{1,0:T(8,128)(2,1)S(1)}, u32[]{:S(2)}, u32[]{:S(2)}) collective-permute-start(bf16[896,512]{1,0:T(8,128)(2,1)S(1)} %copy-done), channel_id=1, source_target_pairs={{0,1},{1,0},{2,3},{3,2},{4,5},{5,4},{6,7},{7,6},{8,9},{9,8},{10,11... | collective-permute-start | bytes 2752520 | tf_op jit(solution)/shard_map/ppermute | solution.py:27
  14.7 12.8 %collective-permute-start.1 = (bf16[896,512]{1,0:T(8,128)(2,1)S(1)}, bf16[896,512]{1,0:T(8,128)(2,1)}, u32[]{:S(2)}, u32[]{:S(2)}) collective-permute-start(bf16[896,512]{1,0:T(8,128)(2,1)S(1)} %copy-done.1), channel_id=1, source_target_pairs={{0,1},{1,0},{2,3},{3,2},{4,5},{5,4},{6,7},{7,6},{8,9},{9,8},{10,11... | collective-permute-start | bytes 2752520 | tf_op jit(solution)/shard_map/ppermute | solution.py:27
  34.8 7.5 %collective-permute-start.8 = (bf16[256,896]{1,0:T(8,128)(2,1)S(1)}, bf16[256,896]{1,0:T(8,128)(2,1)S(1)}, u32[]{:S(2)}, u32[]{:S(2)}) collective-permute-start(bf16[256,896]{1,0:T(8,128)(2,1)S(1)} %bitcast.24), channel_id=1, source_target_pairs={{0,1},{1,0},{2,3},{3,2},{4,5},{5,4},{6,7},{7,6},{8,9},{9,8},{10,11... | collective-permute-start | bytes 1376264 | tf_op jit(solution)/shard_map/ppermute | solution.py:301
  38.5 17.8 %copy-start.6 = (bf16[64,1024]{1,0:T(8,128)(2,1)S(1)}, bf16[64,1024]{1,0:T(8,128)(2,1)}, u32[]{:S(2)}) copy-start(bf16[64,1024]{1,0:T(8,128)(2,1)} %get-tuple-element.138) | copy-start | bytes 393220
  38.5 14.6 %collective-permute-start.4 = (bf16[256,896]{1,0:T(8,128)(2,1)S(1)}, bf16[256,896]{1,0:T(8,128)(2,1)S(1)}, u32[]{:S(2)}, u32[]{:S(2)}) collective-permute-start(bf16[256,896]{1,0:T(8,128)(2,1)S(1)} %bitcast.21), channel_id=1, source_target_pairs={{0,2},{1,3},{2,4},{3,5},{4,6},{5,7},{6,0},{7,1},{8,10},{9,11},{10,... | collective-permute-start | bytes 1376264 | tf_op jit(solution)/shard_map/ppermute | solution.py:301
  40.1 13.2 %collective-permute-start.6 = (bf16[256,896]{1,0:T(8,128)(2,1)S(1)}, bf16[256,896]{1,0:T(8,128)(2,1)S(1)}, u32[]{:S(2)}, u32[]{:S(2)}) collective-permute-start(bf16[256,896]{1,0:T(8,128)(2,1)S(1)} %bitcast.25), channel_id=1, source_target_pairs={{0,7},{1,6},{2,1},{3,0},{4,3},{5,2},{6,5},{7,4},{8,15},{9,14},{10,... | collective-permute-start | bytes 1376264 | tf_op jit(solution)/shard_map/ppermute | solution.py:301
  46.0 16.4 %collective-permute-start.10 = (bf16[256,896]{1,0:T(8,128)(2,1)S(1)}, bf16[256,896]{1,0:T(8,128)(2,1)S(1)}, u32[]{:S(2)}, u32[]{:S(2)}) collective-permute-start(bf16[256,896]{1,0:T(8,128)(2,1)S(1)} %bitcast.23), channel_id=1, source_target_pairs={{0,6},{1,7},{2,0},{3,1},{4,2},{5,3},{6,4},{7,5},{8,14},{9,15},{10,... | collective-permute-start | bytes 1376264 | tf_op jit(solution)/shard_map/ppermute | solution.py:301
  47.7 15.4 %collective-permute-start.9 = (bf16[256,896]{1,0:T(8,128)(2,1)S(1)}, bf16[256,896]{1,0:T(8,128)(2,1)S(1)}, u32[]{:S(2)}, u32[]{:S(2)}) collective-permute-start(bf16[256,896]{1,0:T(8,128)(2,1)S(1)} %bitcast.26), channel_id=1, source_target_pairs={{0,3},{1,2},{2,5},{3,4},{4,7},{5,6},{6,1},{7,0},{8,11},{9,10},{10,... | collective-permute-start | bytes 1376264 | tf_op jit(solution)/shard_map/ppermute | solution.py:301
  53.1 14.7 %collective-permute-start.5 = (bf16[128,896]{1,0:T(8,128)(2,1)S(1)}, bf16[128,896]{1,0:T(8,128)(2,1)S(1)}, u32[]{:S(2)}, u32[]{:S(2)}) collective-permute-start(bf16[128,896]{1,0:T(8,128)(2,1)S(1)} %get-tuple-element.184), channel_id=1, source_target_pairs={{0,2},{1,3},{2,4},{3,5},{4,6},{5,7},{6,0},{7,1},{8,10},{9,11},{10,... | collective-permute-start | bytes 688136 | tf_op jit(solution)/shard_map/ppermute | solution.py:301
  53.4 14.4 %collective-permute-start.7 = (bf16[128,896]{1,0:T(8,128)(2,1)S(1)}, bf16[128,896]{1,0:T(8,128)(2,1)S(1)}, u32[]{:S(2)}, u32[]{:S(2)}) collective-permute-start(bf16[128,896]{1,0:T(8,128)(2,1)S(1)} %get-tuple-element.182), channel_id=1, source_target_pairs={{0,6},{1,7},{2,0},{3,1},{4,2},{5,3},{6,4},{7,5},{8,14},{9,15},{10,... | collective-permute-start | bytes 688136 | tf_op jit(solution)/shard_map/ppermute | solution.py:301
  56.3 14.2 %collective-permute-start.11 = (bf16[64,1024]{1,0:T(8,128)(2,1)S(1)}, bf16[64,1024]{1,0:T(8,128)(2,1)S(1)}, u32[]{:S(2)}, u32[]{:S(2)}) collective-permute-start(bf16[64,1024]{1,0:T(8,128)(2,1)S(1)} %copy-done.6), channel_id=1, source_target_pairs={{8,1},{16,9},{24,17},{32,25},{40,33},{48,41},{56,49},{64,57},{72,6... | collective-permute-start | bytes 393224 | tf_op jit(solution)/shard_map/ppermute | solution.py:318
  57.6 12.9 %copy-start.4 = (bf16[4,64,1024]{2,1,0:T(8,128)(2,1)S(1)}, bf16[4,64,1024]{2,1,0:T(8,128)(2,1)}, u32[]{:S(2)}) copy-start(bf16[4,64,1024]{2,1,0:T(8,128)(2,1)} %get-tuple-element.137.refs_18_) | copy-start | bytes 1572868
  60.0 10.5 %copy-start.2 = (bf16[512,4096]{1,0:T(8,128)(2,1)S(1)}, bf16[512,4096]{1,0:T(8,128)(2,1)}, u32[]{:S(2)}) copy-start(bf16[512,4096]{1,0:T(8,128)(2,1)} %refs_20_.1) | copy-start | bytes 12582916
  67.8 8.7 %collective-permute-start.12 = (bf16[128,896]{1,0:T(8,128)(2,1)S(1)}, bf16[128,896]{1,0:T(8,128)(2,1)S(1)}, u32[]{:S(2)}, u32[]{:S(2)}) collective-permute-start(bf16[128,896]{1,0:T(8,128)(2,1)S(1)} %get-tuple-element.147), channel_id=1, source_target_pairs={{0,2},{1,3},{2,4},{3,5},{4,6},{5,7},{6,0},{7,1},{8,10},{9,11},{10,... | collective-permute-start | bytes 688136 | tf_op jit(solution)/shard_map/ppermute | solution.py:301
  69.0 7.6 %collective-permute-start.13 = (bf16[128,896]{1,0:T(8,128)(2,1)S(1)}, bf16[128,896]{1,0:T(8,128)(2,1)S(1)}, u32[]{:S(2)}, u32[]{:S(2)}) collective-permute-start(bf16[128,896]{1,0:T(8,128)(2,1)S(1)} %get-tuple-element.148), channel_id=1, source_target_pairs={{0,6},{1,7},{2,0},{3,1},{4,2},{5,3},{6,4},{7,5},{8,14},{9,15},{10,... | collective-permute-start | bytes 688136 | tf_op jit(solution)/shard_map/ppermute | solution.py:301
  70.5 8.8 %copy-start.3 = (bf16[4,64,1024]{2,1,0:T(8,128)(2,1)S(1)}, bf16[4,64,1024]{2,1,0:T(8,128)(2,1)}, u32[]{:S(2)}) copy-start(bf16[4,64,1024]{2,1,0:T(8,128)(2,1)} %get-tuple-element.155.refs_18_) | copy-start | bytes 1572868
  76.5 13.5 %collective-permute-start.14 = (bf16[64,4096]{1,0:T(8,128)(2,1)S(1)}, bf16[64,4096]{1,0:T(8,128)(2,1)S(1)}, u32[]{:S(2)}, u32[]{:S(2)}) collective-permute-start(bf16[64,4096]{1,0:T(8,128)(2,1)S(1)} %get-tuple-element.150), channel_id=1, source_target_pairs={{0,2},{2,4},{4,6},{6,0},{1,3},{3,5},{5,7},{7,1},{8,10},{10,12},{12... | collective-permute-start | bytes 1572872 | tf_op jit(solution)/shard_map/ppermute | solution.py:27
  76.6 13.4 %collective-permute-start.15 = (bf16[64,4096]{1,0:T(8,128)(2,1)S(1)}, bf16[64,4096]{1,0:T(8,128)(2,1)S(1)}, u32[]{:S(2)}, u32[]{:S(2)}) collective-permute-start(bf16[64,4096]{1,0:T(8,128)(2,1)S(1)} %get-tuple-element.151), channel_id=1, source_target_pairs={{0,6},{2,0},{4,2},{6,4},{1,7},{3,1},{5,3},{7,5},{8,14},{10,8},{12,... | collective-permute-start | bytes 1572872 | tf_op jit(solution)/shard_map/ppermute | solution.py:27
  90.1 7.8 %collective-permute-start.17 = (bf16[64,2048]{1,0:T(8,128)(2,1)S(1)}, bf16[64,2048]{1,0:T(8,128)(2,1)S(1)}, u32[]{:S(2)}, u32[]{:S(2)}) collective-permute-start(bf16[64,2048]{1,0:T(8,128)(2,1)S(1)} %get-tuple-element.170), channel_id=1, source_target_pairs={{0,6},{2,0},{4,2},{6,4},{1,7},{3,1},{5,3},{7,5},{8,14},{10,8},{12,... | collective-permute-start | bytes 786440 | tf_op jit(solution)/shard_map/ppermute | solution.py:27
  92.6 6.4 %collective-permute-start.16 = (bf16[64,2048]{1,0:T(8,128)(2,1)S(1)}, bf16[64,2048]{1,0:T(8,128)(2,1)S(1)}, u32[]{:S(2)}, u32[]{:S(2)}) collective-permute-start(bf16[64,2048]{1,0:T(8,128)(2,1)S(1)} %get-tuple-element.168), channel_id=1, source_target_pairs={{0,2},{2,4},{4,6},{6,0},{1,3},{3,5},{5,7},{7,1},{8,10},{10,12},{12... | collective-permute-start | bytes 786440 | tf_op jit(solution)/shard_map/ppermute | solution.py:27
  92.6 15.4 %collective-permute-start.21 = (bf16[64,2048]{1,0:T(8,128)(2,1)S(1)}, bf16[64,2048]{1,0:T(8,128)(2,1)S(1)}, u32[]{:S(2)}, u32[]{:S(2)}) collective-permute-start(bf16[64,2048]{1,0:T(8,128)(2,1)S(1)} %get-tuple-element.176), channel_id=1, source_target_pairs={{0,6},{2,0},{4,2},{6,4},{1,7},{3,1},{5,3},{7,5},{8,14},{10,8},{12,... | collective-permute-start | bytes 786440 | tf_op jit(solution)/shard_map/ppermute | solution.py:27
  95.3 12.8 %collective-permute-start.20 = (bf16[64,2048]{1,0:T(8,128)(2,1)S(1)}, bf16[64,2048]{1,0:T(8,128)(2,1)S(1)}, u32[]{:S(2)}, u32[]{:S(2)}) collective-permute-start(bf16[64,2048]{1,0:T(8,128)(2,1)S(1)} %get-tuple-element.174), channel_id=1, source_target_pairs={{0,2},{2,4},{4,6},{6,0},{1,3},{3,5},{5,7},{7,1},{8,10},{10,12},{12... | collective-permute-start | bytes 786440 | tf_op jit(solution)/shard_map/ppermute | solution.py:27
  95.3 15.6 %collective-permute-start.19 = (bf16[64,2048]{1,0:T(8,128)(2,1)S(1)}, bf16[64,2048]{1,0:T(8,128)(2,1)S(1)}, u32[]{:S(2)}, u32[]{:S(2)}) collective-permute-start(bf16[64,2048]{1,0:T(8,128)(2,1)S(1)} %get-tuple-element.172), channel_id=1, source_target_pairs={{0,6},{2,0},{4,2},{6,4},{1,7},{3,1},{5,3},{7,5},{8,14},{10,8},{12,... | collective-permute-start | bytes 786440 | tf_op jit(solution)/shard_map/ppermute | solution.py:27
  98.0 19.0 %collective-permute-start.23 = (bf16[64,2048]{1,0:T(8,128)(2,1)S(1)}, bf16[64,2048]{1,0:T(8,128)(2,1)S(1)}, u32[]{:S(2)}, u32[]{:S(2)}) collective-permute-start(bf16[64,2048]{1,0:T(8,128)(2,1)S(1)} %get-tuple-element.179), channel_id=1, source_target_pairs={{0,2},{2,4},{4,6},{6,0},{1,3},{3,5},{5,7},{7,1},{8,10},{10,12},{12... | collective-permute-start | bytes 786440 | tf_op jit(solution)/shard_map/ppermute | solution.py:27
  99.2 17.9 %collective-permute-start.18 = (bf16[64,4096]{1,0:T(8,128)(2,1)S(1)}, bf16[64,4096]{1,0:T(8,128)(2,1)S(1)}, u32[]{:S(2)}, u32[]{:S(2)}) collective-permute-start(bf16[64,4096]{1,0:T(8,128)(2,1)S(1)} %pad_maximum_fusion.1), channel_id=1, source_target_pairs={{0,1},{1,8},{2,3},{3,2},{4,5},{5,4},{6,7},{7,6},{8,9},{9,16},{10,1... | collective-permute-start | bytes 1572872 | tf_op jit(solution)/shard_map/ppermute | solution.py:344
  108.2 8.7 %collective-permute-start.22 = (bf16[64,2048]{1,0:T(8,128)(2,1)S(1)}, bf16[64,2048]{1,0:T(8,128)(2,1)S(1)}, u32[]{:S(2)}, u32[]{:S(2)}) collective-permute-start(bf16[64,2048]{1,0:T(8,128)(2,1)S(1)} %add_convert_fusion.3), channel_id=1, source_target_pairs={{0,2},{2,4},{4,6},{6,0},{1,3},{3,5},{5,7},{7,1},{8,10},{10,12},{12... | collective-permute-start | bytes 786440 | tf_op jit(solution)/shard_map/ppermute | solution.py:27
  108.2 8.7 %collective-permute-start.24 = (bf16[64,2048]{1,0:T(8,128)(2,1)S(1)}, bf16[64,2048]{1,0:T(8,128)(2,1)S(1)}, u32[]{:S(2)}, u32[]{:S(2)}) collective-permute-start(bf16[64,2048]{1,0:T(8,128)(2,1)S(1)} %add_convert_fusion.2), channel_id=1, source_target_pairs={{0,6},{2,0},{4,2},{6,4},{1,7},{3,1},{5,3},{7,5},{8,14},{10,8},{12,... | collective-permute-start | bytes 786440 | tf_op jit(solution)/shard_map/ppermute | solution.py:27
